TPU v7x, 32 devices: a whole 2x2x4 slice. The times are simulated.
32 devices in a mesh: zone: 2 (over core), gx: 4 (over y, x), yz: 4 (over z).
Axes of the slice: x: 2, y: 2, z: 4, core: 2. Of those that a mesh axis runs over, the one named last changes fastest.
Arguments:
- adjoint: float32 [2, 27, 32, 16, 512], P('zone', None, 'gx', None, 'yz'), may hold values from -6 to 6
- saved: float32 [2, 2, 27, 32, 16, 512], P(None, 'zone', None, 'gx', None, 'yz')
- solid: int32 [2, 32, 16, 512], P('zone', 'gx', None, 'yz'), may hold values 0 or 1
- band_device: int32 [2, 16, 512, 2], P('zone', None, 'yz'), may hold values from 0 to 3, as said below
- band_cell: int32 [2, 16, 512, 2], P('zone', None, 'yz'), may hold values from 0 to 127
- band_weight: float32 [2, 16, 512, 2], P('zone', None, 'yz'), may hold values from 0.1 to 0.9
Outputs:
- adjoint_out: float32 [2, 27, 32, 16, 512], P('zone', None, 'gx', None, 'yz')
Inputs may be any that keep to these rules, and one draw needn't show every extreme that they name: band_device and band_cell name, for each band cell and partner, a cell of the other zone's interface plane in the same radial row; within a radial row, the target of cell z and partner k is (z + s + d + k) mod 512 for one shift s of that row and a jitter d from -2 to 2.
All inputs are finite; a program needn't handle non-finite values. No bound on the sum of `solid` on one device may be relied on, other than what follows from the above.
Results may differ from a plain program's by a relative error of at most 0.0001.
Values sent between devices are 32-bit elements; how exact they have to be, the bound alone decides.
No kernel may reach another device: no remote copies, remote signals or barrier semaphores. Data moves between devices by JAX's collectives and lax.ppermute only.
A program may use at most 64 MiB of HBM per device.

v0:
```python
import jax
import jax.numpy as jnp
import numpy as np
from jax import lax
from jax.sharding import PartitionSpec as P

OMEGA = 1.6


def extended(array, sides, width):
    for axis, dim in sides:
        count, length = (lax.axis_size(axis), array.shape[dim])
        up = [(i, (i + 1) % count) for i in range(count - 1)]
        down = [(j, i) for i, j in up]
        last = lax.slice_in_dim(array, length - width, length, axis=dim)
        initial = lax.slice_in_dim(array, 0, width, axis=dim)
        before = lax.ppermute(last, axis, up)
        after = lax.ppermute(initial, axis, down)
        array = jnp.concatenate([before, array, after], axis=dim)
    return array


def lattice_vectors():
    velocities = np.array(
        [
            [along_x, along_y, along_z]
            for along_x in (-1, 0, 1)
            for along_y in (-1, 0, 1)
            for along_z in (-1, 0, 1)
        ]
    )
    lookup = np.array([8.0 / 27.0, 2.0 / 27.0, 1.0 / 54.0, 1.0 / 216.0])
    weights = lookup[np.sum(np.abs(velocities), axis=1)]
    return (velocities, weights)


def moment_table():
    velocities, weights = lattice_vectors()
    speeds = velocities * 1.0
    table_rows = [
        weights,
        weights * speeds[:, 0],
        weights * speeds[:, 1],
        weights * speeds[:, 2],
        weights * speeds[:, 0] * speeds[:, 0],
        weights * speeds[:, 1] * speeds[:, 1],
        weights * speeds[:, 2] * speeds[:, 2],
        weights * speeds[:, 0] * speeds[:, 1],
        weights * speeds[:, 0] * speeds[:, 2],
        weights * speeds[:, 1] * speeds[:, 2],
    ]
    return np.stack(table_rows)


def finish_collision(pulled, moments, velocity, solid_now):
    speeds = jnp.asarray(lattice_vectors()[0], dtype=jnp.float32)
    vel_x, vel_y, vel_z = (velocity[0], velocity[1], velocity[2])
    zeroth = moments[0]
    quadratic = (
        vel_x * vel_x * moments[4]
        + vel_y * vel_y * moments[5]
        + vel_z * vel_z * moments[6]
        + 2.0
        * (vel_x * vel_y * moments[7] + vel_x * vel_z * moments[8] + vel_y * vel_z * moments[9])
    )
    squared = vel_x * vel_x + vel_y * vel_y + vel_z * vel_z
    scalar_part = zeroth * (1.0 + 1.5 * squared) - 4.5 * quadratic
    vector_x = (
        3.0 * moments[1]
        + 9.0 * (moments[4] * vel_x + moments[7] * vel_y + moments[8] * vel_z)
        - 3.0 * vel_x * zeroth
    )
    vector_y = (
        3.0 * moments[2]
        + 9.0 * (moments[7] * vel_x + moments[5] * vel_y + moments[9] * vel_z)
        - 3.0 * vel_y * zeroth
    )
    vector_z = (
        3.0 * moments[3]
        + 9.0 * (moments[8] * vel_x + moments[9] * vel_y + moments[6] * vel_z)
        - 3.0 * vel_z * zeroth
    )
    projected = (
        scalar_part[None]
        + speeds[:, 0, None, None, None] * vector_x[None]
        + speeds[:, 1, None, None, None] * vector_y[None]
        + speeds[:, 2, None, None, None] * vector_z[None]
    )
    relaxed = (1.0 - OMEGA) * pulled + OMEGA * projected
    bounced = pulled[::-1]
    return jnp.where(solid_now[None] == 1, bounced, relaxed)


def collide_adjoint(pulled, saved_now, solid_now):
    speeds = jnp.asarray(lattice_vectors()[0], dtype=jnp.float32)
    moment_rows = jnp.asarray(moment_table(), dtype=jnp.float32)
    density = jnp.sum(saved_now, axis=0)
    momentum = jnp.einsum("qa,qxyz->axyz", speeds, saved_now, precision=lax.Precision.HIGHEST)
    velocity = momentum / density[None]
    moments = jnp.einsum("mq,qxyz->mxyz", moment_rows, pulled, precision=lax.Precision.HIGHEST)
    return finish_collision(pulled, moments, velocity, solid_now)


def padded_block(field_now):
    return extended(field_now, (("gx", 1), ("yz", 3)), 1)


def stream_pull(field_now):
    velocities = lattice_vectors()[0]
    padded = padded_block(field_now)
    padded = jnp.pad(padded, ((0, 0), (0, 0), (1, 1), (0, 0)))
    extent_x, extent_y, extent_z = (field_now.shape[1], field_now.shape[2], field_now.shape[3])
    pieces = []
    for direction in range(27):
        shift_x = 1 + int(velocities[direction, 0])
        shift_y = 1 + int(velocities[direction, 1])
        shift_z = 1 + int(velocities[direction, 2])
        pieces.append(
            padded[
                direction,
                shift_x : shift_x + extent_x,
                shift_y : shift_y + extent_y,
                shift_z : shift_z + extent_z,
            ]
        )
    return jnp.stack(pieces)


def band_ghost(band_values):
    velocities = lattice_vectors()[0]
    extent_y = band_values.shape[1]
    padded = jnp.pad(band_values, ((0, 0), (1, 1), (0, 0)))
    ghosts = []
    for direction in range(9):
        shift_y = 1 + int(velocities[18 + direction, 1])
        ghosts.append(padded[direction, shift_y : shift_y + extent_y])
    zeros_part = jnp.zeros((18,) + band_values.shape[1:], band_values.dtype)
    return jnp.concatenate([zeros_part, jnp.stack(ghosts)], axis=0)


def band_from_partner(field_now, local_target, weight_now):
    extent_x, extent_y, extent_z = (field_now.shape[1], field_now.shape[2], field_now.shape[3])
    taps = weight_now.shape[-1]
    own_plane = field_now[:, extent_x - 1]
    initial = jnp.zeros((9, extent_y, extent_z), jnp.float32)
    zone_now = lax.axis_index("zone")
    target = (1 - zone_now) * (lax.axis_size("yz") * extent_z) + local_target
    shard_piece = lax.all_gather(own_plane, ("zone", "yz"), axis=2, tiled=True)
    span = shard_piece.shape[2]
    shifted = target - jnp.int32(0)
    usable = (shifted >= 0) & (shifted < span)
    clipped = jnp.clip(shifted, 0, span - 1)
    indices = jnp.broadcast_to(
        clipped.reshape(1, extent_y, extent_z * taps), (9, extent_y, extent_z * taps)
    )
    picked = jnp.take_along_axis(shard_piece[0:9], indices, axis=2).reshape(
        9, extent_y, extent_z, taps
    )
    return initial + jnp.sum(jnp.where(usable[None], picked * weight_now[None], 0.0), axis=-1)


def body(adjoint, saved, solid, band_device, band_cell, band_weight):
    current = adjoint[0]
    extent_x, extent_z = (current.shape[1], current.shape[3])
    solid_now = solid[0]
    weight_now = band_weight[0]
    local_target = band_device[0] * extent_z + band_cell[0]
    at_interface = lax.axis_index("gx") == lax.axis_size("gx") - 1
    last_plane = (jnp.arange(extent_x) == extent_x - 1) & at_interface
    for backward in (1, 0):
        band_values = band_from_partner(current, local_target, weight_now)
        pulled = stream_pull(current)
        ghost_plane = band_ghost(band_values)
        pulled = pulled + jnp.where(last_plane[None, :, None, None], ghost_plane[:, None], 0.0)
        current = collide_adjoint(pulled, saved[backward, 0], solid_now)
    return current[None]


def solution(mesh):
    in_specs = (
        P("zone", None, "gx", None, "yz"),
        P(None, "zone", None, "gx", None, "yz"),
        P("zone", "gx", None, "yz"),
        P("zone", None, "yz", None),
        P("zone", None, "yz", None),
        P("zone", None, "yz", None),
    )
    out_specs = P("zone", None, "gx", None, "yz")
    return jax.shard_map(body, mesh=mesh, in_specs=in_specs, out_specs=out_specs, check_vma=False)
```

profile of v0, /device:TPU:0, one launch (start us, length us, event | category | flops | bytes accessed | tf_op | source)
XLA Modules:
  0.0 877.9 jit_solution(7577015662532313864)
XLA Ops:
  9.0 4.9 collective-permute-start
  15.5 4.3 slice_reduce_fusion
  19.8 3.5 fusion.2
  23.4 2.0 collective-permute-done.1
  25.6 2.8 fusion.12
  28.4 2.7 copy.71
  31.1 2.7 copy.72
  35.2 4.7 collective-permute-start.2
  41.7 2.5 copy.73
  44.3 2.5 copy.74
  46.8 5.8 select_maximum_fusion.4
  73.5 361.6 %gather_fusion = f32[36864]{0:T(1024)S(1)} fusion(f32[9,16,1024]{2,1,0:T(8,128)S(1)} %slice_bitcast_fusion.1, s32[36864]{0:T(1024)S(1)} %bitcast.79), kind=kCustom, calls=%fused_computation.clone | custom fusion | bytes 737280 | tf_op jit(solution)/shard_map/jit(take_along_axis)/gather | solution.py:156
  435.5 1.8 select_reduce_fusion.1
  444.2 4.8 collective-permute-start.4
  449.0 3.5 fusion.1
  452.8 2.8 fusion.11
  455.6 2.7 copy.98
  458.3 2.7 copy.99
  462.3 5.1 collective-permute-start.6
  467.4 2.0 collective-permute-done.6
  469.4 2.5 copy.100
  471.9 2.5 copy.101
  474.4 5.8 select_maximum_fusion
  500.3 361.6 %gather_fusion.1 = f32[36864]{0:T(1024)S(1)} fusion(f32[9,16,1024]{2,1,0:T(8,128)S(1)} %slice_bitcast_fusion, s32[36864]{0:T(1024)S(1)} %bitcast.80), kind=kCustom, calls=%fused_computation.1.clone | custom fusion | bytes 737280 | tf_op jit(solution)/shard_map/jit(take_along_axis)/gather | solution.py:156
  (177 shorter events, 66.0 us)
Async XLA Ops:
  6.5 8.6 copy-start.8
  6.5 8.6 copy-start.9
  6.5 8.9 %copy-start.7 = (s32[1,8,16,128]{3,2,1,0:T(8,128)S(1)}, s32[1,8,16,128]{3,2,1,0:T(8,128)}, u32[]{:S(2)}) copy-start(s32[1,8,16,128]{3,2,1,0:T(8,128)} %param.16) | copy-start | bytes 196612
  6.5 65.8 %all-gather.5.cloned.1.call-start = ((), (), s32[]{:S(2)}) async-start(), calls=%async_computation | async-start | bytes 1990656 | tf_op jit(solution)/shard_map/all_gather | solution.py:148
  8.9 490.2 %all-gather.7.cloned.1.call-start = ((), (), s32[]{:S(2)}) async-start(), calls=%async_computation.1 | async-start | bytes 1990656 | tf_op jit(solution)/shard_map/all_gather | solution.py:148
  9.0 16.4 %collective-permute-start = (f32[27,1,16,128]{3,2,0,1:T(8,128)}, f32[27,1,16,128]{3,2,0,1:T(8,128)S(1)}, u32[]{:S(2)}, u32[]{:S(2)}) collective-permute-start(f32[27,1,16,128]{3,2,0,1:T(8,128)} %get-tuple-element.16), channel_id=1, source_target_pairs={{0,4},{4,8},{8,12},{1,5},{5,9},{9,13},{2,6},{6,10},{10,14},{3,7},{... | collective-permute-start | bytes 663560 | tf_op jit(solution)/shard_map/ppermute | solution.py:17
  13.9 11.6 %collective-permute-start.1 = (f32[27,1,16,128]{3,2,0,1:T(8,128)S(1)}, f32[27,1,16,128]{3,2,0,1:T(8,128)S(1)}, u32[]{:S(2)}, u32[]{:S(2)}) collective-permute-start(f32[27,1,16,128]{3,2,0,1:T(8,128)S(1)} %get-tuple-element.17), channel_id=1, source_target_pairs={{4,0},{8,4},{12,8},{5,1},{9,5},{13,9},{6,2},{10,6},{14,10},{7,3},{... | collective-permute-start | bytes 663560 | tf_op jit(solution)/shard_map/ppermute | solution.py:18
  15.4 419.7 %copy-start.10 = (pred[16,256]{1,0:T(8,128)(4,1)}, pred[16,256]{1,0:T(8,128)(4,1)S(1)}, u32[]{:S(2)}) copy-start(pred[16,256]{1,0:T(8,128)(4,1)S(1)} %broadcast_compare_fusion) | copy-start | bytes 12292
  15.5 426.5 %copy-start.5 = (pred[8,16,128]{2,1,0:T(8,128)(4,1)}, pred[8,16,128]{2,1,0:T(8,128)(4,1)S(1)}, u32[]{:S(2)}) copy-start(pred[8,16,128]{2,1,0:T(8,128)(4,1)S(1)} %compare_bitcast_fusion) | copy-start | bytes 49156
  15.5 4.3 copy-start.15
  28.4 11.7 %copy-start.14 = (f32[1,16,128,2]{2,3,1,0:T(2,128)S(1)}, f32[1,16,128,2]{2,3,1,0:T(2,128)}, u32[]{:S(2)}) copy-start(f32[1,16,128,2]{2,3,1,0:T(2,128)} %param.19) | copy-start | bytes 49156
  33.9 10.4 %collective-permute-start.3 = (f32[27,10,16,1]{0,2,3,1:T(8,128)S(1)}, f32[27,10,16,1]{0,2,3,1:T(8,128)S(1)}, u32[]{:S(2)}, u32[]{:S(2)}) collective-permute-start(f32[27,10,16,1]{0,2,3,1:T(8,128)S(1)} %copy.72), channel_id=1, source_target_pairs={{1,0},{2,1},{3,2},{5,4},{6,5},{7,6},{9,8},{10,9},{11,10},{13,12},{... | collective-permute-start | bytes 51848 | tf_op jit(solution)/shard_map/ppermute | solution.py:18
  35.2 6.6 collective-permute-start.2
  39.9 398.0 %copy-start.25 = (pred[8]{0:T(512)(128)(4,1)}, pred[8]{0:T(512)(128)(4,1)S(1)}, u32[]{:S(2)}) copy-start(pred[8]{0:T(512)(128)(4,1)S(1)} %compare_and_fusion) | copy-start | bytes 28
  40.3 397.5 %copy-start.23 = (f32[27]{0:T(128)}, f32[27]{0:T(128)S(1)}, u32[]{:S(2)}) copy-start(f32[27]{0:T(128)S(1)} %pad.42.clone) | copy-start | bytes 328
  46.8 7.8 copy-start.2
  442.0 7.0 copy-start.16
  442.9 9.8 %copy-start.4 = (f32[27,1,16,128]{3,2,0,1:T(8,128)}, f32[27,1,16,128]{3,2,0,1:T(8,128)S(1)}, u32[]{:S(2)}) copy-start(f32[27,1,16,128]{3,2,0,1:T(8,128)S(1)} %get-tuple-element.14) | copy-start | bytes 663556
  442.9 9.6 %collective-permute-start.5 = (f32[27,1,16,128]{3,2,0,1:T(8,128)S(1)}, f32[27,1,16,128]{3,2,0,1:T(8,128)S(1)}, u32[]{:S(2)}, u32[]{:S(2)}) collective-permute-start(f32[27,1,16,128]{3,2,0,1:T(8,128)S(1)} %get-tuple-element.15), channel_id=1, source_target_pairs={{4,0},{8,4},{12,8},{5,1},{9,5},{13,9},{6,2},{10,6},{14,10},{7,3},{... | collective-permute-start | bytes 663560 | tf_op jit(solution)/shard_map/ppermute | solution.py:18
  444.2 8.3 collective-permute-start.4
  461.0 10.9 %collective-permute-start.7 = (f32[27,10,16,1]{0,2,3,1:T(8,128)S(1)}, f32[27,10,16,1]{0,2,3,1:T(8,128)S(1)}, u32[]{:S(2)}, u32[]{:S(2)}) collective-permute-start(f32[27,10,16,1]{0,2,3,1:T(8,128)S(1)} %copy.99), channel_id=1, source_target_pairs={{1,0},{2,1},{3,2},{5,4},{6,5},{7,6},{9,8},{10,9},{11,10},{13,12},{... | collective-permute-start | bytes 51848 | tf_op jit(solution)/shard_map/ppermute | solution.py:18
  462.3 7.1 collective-permute-start.6
  474.4 7.8 copy-start.3
  500.3 361.7 %copy-start.11 = (pred[16,256]{1,0:T(8,128)(4,1)S(1)}, pred[16,256]{1,0:T(8,128)(4,1)}, u32[]{:S(2)}) copy-start(pred[16,256]{1,0:T(8,128)(4,1)} %copy-done.10) | copy-start | bytes 12292
  (13 other events, 16.3 us)
Sparse Core Ops, SparseCore 0:
  9.1 31.5 all-gather.4
  467.5 31.0 all-gather.6
where the time goes:
time: 882 us; the launch traced here: 878 us
  local copies, waits for them, and re-layouts  787 us (89%)
  other arithmetic  36.9 us (4%)
  starting transfers between devices  24.6 us (3%)
  between operations  14.1 us (2%)
  matrix products  10.3 us (1%)
    gather x4, local copies, waits for them, and re-layouts, band_from_partner(): jnp.take_along_axis(shard_piece[0:9], indices, axis=2)  723 us
    unnamed x92, local copies, waits for them, and re-layouts  27.9 us
    ppermute x4, starting transfers between devices, extended(): before = lax.ppermute(last, axis, up)  19.4 us
  transfers between devices with their start and end apart: 10, of which 3 were waited for; matrix products, arithmetic and copies ran while one was open for 9% of the time, Pallas kernels for 0%

commit v1 on v0

v1 whole, which is shorter than its diff:
```python
import jax
import jax.numpy as jnp
import numpy as np
from jax import lax
from jax.experimental import pallas as pl
from jax.experimental.pallas import tpu as pltpu
from jax.sharding import PartitionSpec as P

OMEGA = 1.6
VMEM_LIMIT = 48 * 1024 * 1024
SIGNS = (-1, 0, 1)


def number(cx, cy, cz):
    return 9 * (cx + 1) + 3 * (cy + 1) + (cz + 1)


def lanes():
    return lax.broadcasted_iota(jnp.int32, (16, 128), 1)


def shift_y(tile, cy):
    if cy == 0:
        return tile
    row = lax.broadcasted_iota(jnp.int32, tile.shape, 0)
    if cy == 1:
        return jnp.where(row == 15, 0.0, pltpu.roll(tile, 15, 0))
    return jnp.where(row == 0, 0.0, pltpu.roll(tile, 1, 0))


def pack_columns(planes, x, low, high):
    lane = lanes()
    for slot in range(9):
        place = (x + 1) * 9 + slot
        here = lane == place
        low = jnp.where(here, pltpu.roll(planes(3 * slot + 2), place, 1), low)
        high = jnp.where(here, pltpu.roll(planes(3 * slot), place + 1, 1), high)
    return low, high


def pack_kernel(adj, low_out, high_out, top_out, bottom_out):
    extent_x = adj.shape[1]

    def one(x, carry):
        return pack_columns(lambda i: adj[i, x], x, *carry)

    zero = jnp.zeros((16, 128), jnp.float32)
    low, high = lax.fori_loop(0, extent_x, one, (zero, zero))
    low_out[...] = low
    high_out[...] = high
    for j in range(9):
        top_out[j] = adj[j, extent_x - 1]
        bottom_out[j] = adj[18 + j, 0]


def band_tiles(blocks, device, cell, weight, count):
    me = lax.axis_index("yz")
    hops = [lax.rem(me - device[k] + count, count) for k in range(2)]
    values = []
    for j in range(9):
        halves = []
        for r in (0, 8):
            total = jnp.zeros((8, 128), jnp.float32)
            for k in range(2):
                spot = cell[k, r : r + 8]
                picked = jnp.zeros((8, 128), jnp.float32)
                for m in range(count):
                    got = jnp.take_along_axis(blocks[m][j, r : r + 8], spot, axis=1)
                    picked = jnp.where(hops[k][r : r + 8] == m, got, picked)
                total = total + picked * weight[k, r : r + 8]
            halves.append(total)
        values.append(jnp.concatenate(halves, axis=0))
    return values


def velocity_of(saved):
    totals, along_y, along_z = [], [], []
    for cx in SIGNS:
        sums, diffs = [], []
        for cy in SIGNS:
            lo, mid, hi = [saved(number(cx, cy, cz)) for cz in SIGNS]
            sums.append(lo + mid + hi)
            diffs.append(hi - lo)
        totals.append(sums[0] + sums[1] + sums[2])
        along_y.append(sums[2] - sums[0])
        along_z.append(diffs[0] + diffs[1] + diffs[2])
    density = totals[0] + totals[1] + totals[2]
    momentum = (
        totals[2] - totals[0],
        along_y[0] + along_y[1] + along_y[2],
        along_z[0] + along_z[1] + along_z[2],
    )
    return [part / density for part in momentum]


def moments_of(pull):
    rows = []
    for cx in SIGNS:
        plain, first, second = [], [], []
        for cy in SIGNS:
            lo, mid, hi = [pull(cx, cy, cz) for cz in SIGNS]
            both = lo + hi
            plain.append(mid + 0.25 * both)
            first.append(hi - lo)
            second.append(both)
        pair = plain[0] + plain[2]
        rows.append(
            (
                plain[1] + 0.25 * pair,
                plain[2] - plain[0],
                pair,
                first[1] + 0.25 * (first[0] + first[2]),
                first[2] - first[0],
                second[1] + 0.25 * (second[0] + second[2]),
            )
        )
    even = [rows[1][n] + 0.25 * (rows[0][n] + rows[2][n]) for n in range(6)]
    zero = (8.0 / 27.0) * even[0]
    along = (
        (2.0 / 27.0) * (rows[2][0] - rows[0][0]),
        (2.0 / 27.0) * even[1],
        (2.0 / 27.0) * even[3],
    )
    square = (
        (2.0 / 27.0) * (rows[2][0] + rows[0][0]),
        (2.0 / 27.0) * even[2],
        (2.0 / 27.0) * even[5],
    )
    mixed = (
        (1.0 / 54.0) * (rows[2][1] - rows[0][1]),
        (1.0 / 54.0) * (rows[2][3] - rows[0][3]),
        (1.0 / 54.0) * even[4],
    )
    return zero, along, square, mixed


def collide(pull, velocity, solid, store):
    zero, along, square, mixed = moments_of(lambda cx, cy, cz: pull(number(cx, cy, cz)))
    ux, uy, uz = velocity
    xy, xz, yz = mixed
    quadratic = (
        ux * ux * square[0]
        + uy * uy * square[1]
        + uz * uz * square[2]
        + 2.0 * (ux * uy * xy + ux * uz * xz + uy * uz * yz)
    )
    speed = ux * ux + uy * uy + uz * uz
    scalar = OMEGA * (zero * (1.0 + 1.5 * speed) - 4.5 * quadratic)
    vec_x = OMEGA * (3.0 * along[0] + 9.0 * (square[0] * ux + xy * uy + xz * uz) - 3.0 * ux * zero)
    vec_y = OMEGA * (3.0 * along[1] + 9.0 * (xy * ux + square[1] * uy + yz * uz) - 3.0 * uy * zero)
    vec_z = OMEGA * (3.0 * along[2] + 9.0 * (xz * ux + yz * uy + square[2] * uz) - 3.0 * uz * zero)
    wall = solid == 1
    for cx in SIGNS:
        base = scalar if cx == 0 else (scalar + vec_x if cx > 0 else scalar - vec_x)
        for cy in SIGNS:
            inner = base if cy == 0 else (base + vec_y if cy > 0 else base - vec_y)
            for cz in SIGNS:
                full = inner if cz == 0 else (inner + vec_z if cz > 0 else inner - vec_z)
                i = number(cx, cy, cz)
                store(i, jnp.where(wall, pull(26 - i), (1.0 - OMEGA) * pull(i) + full))


def step_kernel(count, backward, last, *refs):
    refs = list(refs)
    adj, saved, solid, from_low, from_high, edge_low, edge_high = refs[:7]
    blocks = refs[7 : 7 + count]
    device, cell, weight = refs[7 + count : 10 + count]
    rest = refs[10 + count :]
    if last:
        out = rest.pop(0)
    else:
        out, low_out, high_out, top_out, bottom_out = rest[:5]
        rest = rest[5:]
    ext, kept, made, pulled, band, adj_sem, ghost_sem, saved_sem, out_sem = rest
    extent_x = made.shape[1]

    def load(x):
        return pltpu.make_async_copy(saved.at[backward, 0, :, x], kept.at[:, x], saved_sem.at[x])

    def save(x):
        return pltpu.make_async_copy(made.at[:, x], out.at[:, x], out_sem.at[x])

    whole = pltpu.make_async_copy(adj, ext.at[:, pl.ds(1, extent_x)], adj_sem)
    low_copy = pltpu.make_async_copy(from_low.at[pl.ds(0, 9)], ext.at[pl.ds(0, 9), 0], ghost_sem.at[0])
    high_copy = pltpu.make_async_copy(
        from_high.at[pl.ds(0, 9)], ext.at[pl.ds(18, 9), extent_x + 1], ghost_sem.at[1]
    )
    whole.start()
    low_copy.start()
    high_copy.start()
    for x in range(extent_x):
        load(x).start()

    for j, tile in enumerate(band_tiles(blocks, device, cell, weight, count)):
        band[j] = tile
    lane = lanes()
    span = 9 * extent_x
    joined = []
    for side, edge in ((0, edge_low), (1, edge_high)):
        tile = jnp.where(lane < 9, pltpu.roll(from_low[9 + side], 128 - span, 1), edge[...])
        beyond = (lane >= span + 9) & (lane < span + 18)
        joined.append(jnp.where(beyond, pltpu.roll(from_high[9 + side], span, 1), tile))
    low_edge, high_edge = joined
    whole.wait()
    low_copy.wait()
    high_copy.wait()

    def plane(x, final):
        load(x).wait()
        for cx in SIGNS:
            for cy in SIGNS:
                slot = 3 * (cx + 1) + cy + 1
                place = (x + 1 + cx) * 9 + slot
                for cz in SIGNS:
                    i = number(cx, cy, cz)
                    tile = ext[i, x + 1 + cx]
                    if cz == -1:
                        edge = pltpu.roll(low_edge, 128 - place, 1)
                        tile = jnp.where(lane == 0, edge, pltpu.roll(tile, 1, 1))
                    elif cz == 1:
                        edge = pltpu.roll(high_edge, 127 - place, 1)
                        tile = jnp.where(lane == 127, edge, pltpu.roll(tile, 127, 1))
                    if final and cx == 1:
                        tile = tile + band[i - 18]
                    pulled[i] = shift_y(tile, cy)
        velocity = velocity_of(lambda i: kept[i, x])

        def store(i, tile):
            made[i, x] = tile

        collide(lambda i: pulled[i], velocity, solid[0, x], store)
        save(x).start()

    lax.fori_loop(0, extent_x - 1, lambda x, c: (plane(x, False), c)[1], 0)
    plane(extent_x - 1, True)
    if not last:
        zero = jnp.zeros((16, 128), jnp.float32)
        low, high = lax.fori_loop(
            0, extent_x, lambda x, c: pack_columns(lambda i: made[i, x], x, *c), (zero, zero)
        )
        low_out[...] = low
        high_out[...] = high
        for j in range(9):
            top_out[j] = made[j, extent_x - 1]
            bottom_out[j] = made[18 + j, 0]
    for x in range(extent_x):
        save(x).wait()


def tile_shape(*lead):
    return jax.ShapeDtypeStruct(lead + (16, 128), jnp.float32)


def in_vmem(n):
    return [pl.BlockSpec(memory_space=pltpu.VMEM)] * n


def in_any(n):
    return [pl.BlockSpec(memory_space=pl.ANY)] * n


def body(sizes, adjoint, saved, solid, band_device, band_cell, band_weight):
    zones, widths, count = sizes
    field = adjoint[0]
    extent_x = field.shape[1]
    axes = ("zone", "gx", "yz")
    device = jnp.moveaxis(band_device[0], -1, 0)
    cell = jnp.moveaxis(band_cell[0], -1, 0)
    weight = jnp.moveaxis(band_weight[0], -1, 0)
    params = pltpu.CompilerParams(vmem_limit_bytes=VMEM_LIMIT)

    def flat(zone, gx, yz):
        return (zone * widths + gx) * count + yz

    def shifted(values, axis, step):
        size = widths if axis == "gx" else count
        pairs = [(i, i + step) for i in range(size) if 0 <= i + step < size]
        return lax.ppermute(values, axis, pairs)

    def crossed(values, hop):
        pairs = [
            (flat(zone, widths - 1, z), flat(1 - zone, widths - 1, (z + hop) % count))
            for zone in range(zones)
            for z in range(count)
        ]
        return lax.ppermute(values, axes, pairs)

    edges = (tile_shape(), tile_shape(), tile_shape(9), tile_shape(9))
    low, high, top, bottom = pl.pallas_call(
        pack_kernel,
        out_shape=edges,
        in_specs=in_vmem(1),
        out_specs=tuple(in_vmem(4)),
        compiler_params=params,
    )(field)
    for backward in (1, 0):
        last = backward == 0
        edge_low = shifted(high, "yz", 1)
        edge_high = shifted(low, "yz", -1)
        blocks = [crossed(top, hop) for hop in range(count)]
        seams = jnp.stack([edge_low, edge_high])
        from_low = shifted(jnp.concatenate([top, seams]), "gx", 1)
        from_high = shifted(jnp.concatenate([bottom, seams]), "gx", -1)
        result = pl.pallas_call(
            lambda *refs, backward=backward, last=last: step_kernel(count, backward, last, *refs),
            out_shape=(tile_shape(27, extent_x),) + (() if last else edges),
            in_specs=in_any(2) + in_vmem(5 + count + 3),
            out_specs=tuple(in_any(1) + ([] if last else in_vmem(4))),
            scratch_shapes=[
                pltpu.VMEM((27, extent_x + 2, 16, 128), jnp.float32),
                pltpu.VMEM((27, extent_x, 16, 128), jnp.float32),
                pltpu.VMEM((27, extent_x, 16, 128), jnp.float32),
                pltpu.VMEM((27, 16, 128), jnp.float32),
                pltpu.VMEM((9, 16, 128), jnp.float32),
                pltpu.SemaphoreType.DMA(()),
                pltpu.SemaphoreType.DMA((2,)),
                pltpu.SemaphoreType.DMA((extent_x,)),
                pltpu.SemaphoreType.DMA((extent_x,)),
            ],
            compiler_params=params,
        )(field, saved, solid, from_low, from_high, edge_low, edge_high, *blocks, device, cell, weight)
        if last:
            field = result[0]
        else:
            field, low, high, top, bottom = result
    return field[None]


def solution(mesh):
    sizes = tuple(mesh.shape[axis] for axis in ("zone", "gx", "yz"))
    in_specs = (
        P("zone", None, "gx", None, "yz"),
        P(None, "zone", None, "gx", None, "yz"),
        P("zone", "gx", None, "yz"),
        P("zone", None, "yz", None),
        P("zone", None, "yz", None),
        P("zone", None, "yz", None),
    )
    out_specs = P("zone", None, "gx", None, "yz")
    return jax.shard_map(
        lambda *args: body(sizes, *args),
        mesh=mesh,
        in_specs=in_specs,
        out_specs=out_specs,
        check_vma=False,
    )
```

time: 882 us -> 60.8 us (0.07)
  the two profiles are of different devices: /device:TPU:0 before, /device:TPU:7 now
where the time goes in v1:
time: 60.8 us; the launch traced here: 60.3 us
  starting transfers between devices  41.8 us (69%)
  Pallas kernels  8.75 us (14%)
  waiting for transfers between devices  8.01 us (13%)
  local copies, waits for them, and re-layouts  1.5 us (2%)
    ppermute x8, starting transfers between devices, crossed(): return lax.ppermute(values, axes, pairs)  26.7 us
    ppermute x8, starting transfers between devices, shifted(): return lax.ppermute(values, axis, pairs)  15.1 us
    pallas_call x2, Pallas kernels, body(): pl.pallas_call(lambda *refs, backward=backward, last=last: step_kernel(co...  7.9 us
    ppermute x8, waiting for transfers between devices, shifted(): return lax.ppermute(values, axis, pairs)  4.05 us
    ppermute x8, waiting for transfers between devices, crossed(): return lax.ppermute(values, axes, pairs)  3.97 us
    unnamed x13, local copies, waits for them, and re-layouts  1.5 us
  transfers between devices with their start and end apart: 16, of which 5 were waited for; matrix products, arithmetic and copies ran while one was open for 0% of the time, Pallas kernels for 0%

profile of v1, /device:TPU:7, one launch (start us, length us, event | category | flops | bytes accessed | tf_op | source)
XLA Modules:
  0.0 60.3 jit_solution(10522937727212179628)
XLA Ops:
  0.0 1.5 %copy-done.1 = f32[1,27,8,16,128]{4,3,2,1,0:T(8,128)S(1)} copy-done((f32[1,27,8,16,128]{4,3,2,1,0:T(8,128)S(1)}, f32[1,27,8,16,128]{4,3,2,1,0:T(8,128)}, u32[]{:S(2)}) %copy-start.1) | copy-done | bytes 1769496
  1.5 0.9 %shard_map.64 = (f32[16,128]{1,0:T(8,128)S(1)}, f32[16,128]{1,0:T(8,128)S(1)}, f32[9,16,128]{2,1,0:T(8,128)S(1)}, f32[9,16,128]{2,1,0:T(8,128)S(1)}) custom-call(f32[27,8,16,128]{3,2,1,0:T(8,128)S(1)} %bitcast.19), custom_call_target="tpu_custom_call" | custom-call | tf_op jit(solution)/shard_map/pallas_call | solution.py:289
  2.3 3.2 %collective-permute-start = (f32[16,128]{1,0:T(8,128)S(1)}, f32[16,128]{1,0:T(8,128)S(1)}, u32[]{:S(2)}, u32[]{:S(2)}) collective-permute-start(f32[16,128]{1,0:T(8,128)S(1)} %get-tuple-element.15), channel_id=1, source_target_pairs={{0,1},{1,2},{2,3},{4,5},{5,6},{6,7},{8,9},{9,10},{10,11},{12,13},{... | collective-permute-start | bytes 24584 | tf_op jit(solution)/shard_map/ppermute | solution.py:278
  5.6 1.3 %collective-permute-start.1 = (f32[16,128]{1,0:T(8,128)S(1)}, f32[16,128]{1,0:T(8,128)S(1)}, u32[]{:S(2)}, u32[]{:S(2)}) collective-permute-start(f32[16,128]{1,0:T(8,128)S(1)} %get-tuple-element.16), channel_id=1, source_target_pairs={{1,0},{2,1},{3,2},{5,4},{6,5},{7,6},{9,8},{10,9},{11,10},{13,12},{... | collective-permute-start | bytes 24584 | tf_op jit(solution)/shard_map/ppermute | solution.py:278
  6.9 7.1 %collective-permute-start.7 = (f32[9,16,128]{2,1,0:T(8,128)S(1)}, f32[9,16,128]{2,1,0:T(8,128)S(1)}, u32[]{:S(2)}, u32[]{:S(2)}) collective-permute-start(f32[9,16,128]{2,1,0:T(8,128)S(1)} %get-tuple-element.14), channel_id=1, source_target_pairs={{12,31},{13,28},{14,29},{15,30},{28,15},{29,12},{30,13},{31,14}} | collective-permute-start | bytes 221192 | tf_op jit(solution)/shard_map/ppermute | solution.py:286
  14.0 1.9 %collective-permute-start.6 = (f32[9,16,128]{2,1,0:T(8,128)S(1)}, f32[9,16,128]{2,1,0:T(8,128)S(1)}, u32[]{:S(2)}, u32[]{:S(2)}) collective-permute-start(f32[9,16,128]{2,1,0:T(8,128)S(1)} %get-tuple-element.14), channel_id=1, source_target_pairs={{12,30},{13,31},{14,28},{15,29},{28,14},{29,15},{30,12},{31,13}} | collective-permute-start | bytes 221192 | tf_op jit(solution)/shard_map/ppermute | solution.py:286
  15.9 2.6 %collective-permute-start.5 = (f32[9,16,128]{2,1,0:T(8,128)S(1)}, f32[9,16,128]{2,1,0:T(8,128)S(1)}, u32[]{:S(2)}, u32[]{:S(2)}) collective-permute-start(f32[9,16,128]{2,1,0:T(8,128)S(1)} %get-tuple-element.14), channel_id=1, source_target_pairs={{12,29},{13,30},{14,31},{15,28},{28,13},{29,14},{30,15},{31,12}} | collective-permute-start | bytes 221192 | tf_op jit(solution)/shard_map/ppermute | solution.py:286
  18.6 1.9 %collective-permute-start.4 = (f32[9,16,128]{2,1,0:T(8,128)S(1)}, f32[9,16,128]{2,1,0:T(8,128)S(1)}, u32[]{:S(2)}, u32[]{:S(2)}) collective-permute-start(f32[9,16,128]{2,1,0:T(8,128)S(1)} %get-tuple-element.14), channel_id=1, source_target_pairs={{12,28},{13,29},{14,30},{15,31},{28,12},{29,13},{30,14},{31,15}} | collective-permute-start | bytes 221192 | tf_op jit(solution)/shard_map/ppermute | solution.py:286
  20.5 1.3 %collective-permute-start.3 = (f32[11,16,128]{2,1,0:T(8,128)S(1)}, f32[11,16,128]{2,1,0:T(8,128)S(1)}, u32[]{:S(2)}, u32[]{:S(2)}) collective-permute-start(f32[11,16,128]{2,1,0:T(8,128)S(1)} %get-tuple-element.25), channel_id=1, source_target_pairs={{4,0},{8,4},{12,8},{5,1},{9,5},{13,9},{6,2},{10,6},{14,10},{7,3},{... | collective-permute-start | bytes 270344 | tf_op jit(solution)/shard_map/ppermute | solution.py:278
  21.9 1.3 %collective-permute-start.2 = (f32[11,16,128]{2,1,0:T(8,128)S(1)}, f32[11,16,128]{2,1,0:T(8,128)S(1)}, u32[]{:S(2)}, u32[]{:S(2)}) collective-permute-start(f32[11,16,128]{2,1,0:T(8,128)S(1)} %get-tuple-element.26), channel_id=1, source_target_pairs={{0,4},{4,8},{8,12},{1,5},{5,9},{9,13},{2,6},{6,10},{10,14},{3,7},{... | collective-permute-start | bytes 270344 | tf_op jit(solution)/shard_map/ppermute | solution.py:278
  23.4 0.2 collective-permute-done.3.refs_4_
  23.6 3.8 %collective-permute-done.2.refs_3_ = f32[11,16,128]{2,1,0:T(8,128)S(1)} collective-permute-done((f32[11,16,128]{2,1,0:T(8,128)S(1)}, f32[11,16,128]{2,1,0:T(8,128)S(1)}, u32[]{:S(2)}, u32[]{:S(2)}) %collective-permute-start.2) | collective-permute-done | bytes 90144 | tf_op jit(solution)/shard_map/ppermute | solution.py:278
  27.4 4.6 %shard_map.65 = (f32[27,8,16,128]{3,2,1,0:T(8,128)S(1)}, f32[16,128]{1,0:T(8,128)S(1)}, f32[16,128]{1,0:T(8,128)S(1)}, f32[9,16,128]{2,1,0:T(8,128)S(1)}, f32[9,16,128]{2,1,0:T(8,128)S(1)}) custom-call(f32[27,8,16,128]{3,2,1,0:T(8,128)S(1)} %bitcast.20, f32[2,1,27,8,16,128]{5,4,3,2,1,0:T(8,128)} %refs_1_.3, s32[1,8,16,128]{3,2,1,0:T(8,128)S(1)} %copy-done.2, ...), custom_call_target="tpu_custom_call" | custom-call | tf_op jit(solution)/shard_map/pallas_call | solution.py:304
  32.0 4.1 %collective-permute-start.8 = (f32[16,128]{1,0:T(8,128)S(1)}, f32[16,128]{1,0:T(8,128)S(1)}, u32[]{:S(2)}, u32[]{:S(2)}) collective-permute-start(f32[16,128]{1,0:T(8,128)S(1)} %get-tuple-element.20), channel_id=1, source_target_pairs={{0,1},{1,2},{2,3},{4,5},{5,6},{6,7},{8,9},{9,10},{10,11},{12,13},{... | collective-permute-start | bytes 24584 | tf_op jit(solution)/shard_map/ppermute | solution.py:278
  36.1 1.3 %collective-permute-start.9 = (f32[16,128]{1,0:T(8,128)S(1)}, f32[16,128]{1,0:T(8,128)S(1)}, u32[]{:S(2)}, u32[]{:S(2)}) collective-permute-start(f32[16,128]{1,0:T(8,128)S(1)} %get-tuple-element.21), channel_id=1, source_target_pairs={{1,0},{2,1},{3,2},{5,4},{6,5},{7,6},{9,8},{10,9},{11,10},{13,12},{... | collective-permute-start | bytes 24584 | tf_op jit(solution)/shard_map/ppermute | solution.py:278
  37.4 6.5 %collective-permute-start.15 = (f32[9,16,128]{2,1,0:T(8,128)S(1)}, f32[9,16,128]{2,1,0:T(8,128)S(1)}, u32[]{:S(2)}, u32[]{:S(2)}) collective-permute-start(f32[9,16,128]{2,1,0:T(8,128)S(1)} %get-tuple-element.19), channel_id=1, source_target_pairs={{12,31},{13,28},{14,29},{15,30},{28,15},{29,12},{30,13},{31,14}} | collective-permute-start | bytes 221192 | tf_op jit(solution)/shard_map/ppermute | solution.py:286
  44.0 1.3 %collective-permute-start.11 = (f32[11,16,128]{2,1,0:T(8,128)S(1)}, f32[11,16,128]{2,1,0:T(8,128)S(1)}, u32[]{:S(2)}, u32[]{:S(2)}) collective-permute-start(f32[11,16,128]{2,1,0:T(8,128)S(1)} %get-tuple-element.23), channel_id=1, source_target_pairs={{4,0},{8,4},{12,8},{5,1},{9,5},{13,9},{6,2},{10,6},{14,10},{7,3},{... | collective-permute-start | bytes 270344 | tf_op jit(solution)/shard_map/ppermute | solution.py:278
  45.3 1.3 %collective-permute-start.10 = (f32[11,16,128]{2,1,0:T(8,128)S(1)}, f32[11,16,128]{2,1,0:T(8,128)S(1)}, u32[]{:S(2)}, u32[]{:S(2)}) collective-permute-start(f32[11,16,128]{2,1,0:T(8,128)S(1)} %get-tuple-element.24), channel_id=1, source_target_pairs={{0,4},{4,8},{8,12},{1,5},{5,9},{9,13},{2,6},{6,10},{10,14},{3,7},{... | collective-permute-start | bytes 270344 | tf_op jit(solution)/shard_map/ppermute | solution.py:278
  46.6 2.3 %collective-permute-start.14 = (f32[9,16,128]{2,1,0:T(8,128)S(1)}, f32[9,16,128]{2,1,0:T(8,128)S(1)}, u32[]{:S(2)}, u32[]{:S(2)}) collective-permute-start(f32[9,16,128]{2,1,0:T(8,128)S(1)} %get-tuple-element.19), channel_id=1, source_target_pairs={{12,30},{13,31},{14,28},{15,29},{28,14},{29,15},{30,12},{31,13}} | collective-permute-start | bytes 221192 | tf_op jit(solution)/shard_map/ppermute | solution.py:286
  48.9 2.4 %collective-permute-start.13 = (f32[9,16,128]{2,1,0:T(8,128)S(1)}, f32[9,16,128]{2,1,0:T(8,128)S(1)}, u32[]{:S(2)}, u32[]{:S(2)}) collective-permute-start(f32[9,16,128]{2,1,0:T(8,128)S(1)} %get-tuple-element.19), channel_id=1, source_target_pairs={{12,29},{13,30},{14,31},{15,28},{28,13},{29,14},{30,15},{31,12}} | collective-permute-start | bytes 221192 | tf_op jit(solution)/shard_map/ppermute | solution.py:286
  51.3 1.9 %collective-permute-start.12 = (f32[9,16,128]{2,1,0:T(8,128)S(1)}, f32[9,16,128]{2,1,0:T(8,128)S(1)}, u32[]{:S(2)}, u32[]{:S(2)}) collective-permute-start(f32[9,16,128]{2,1,0:T(8,128)S(1)} %get-tuple-element.19), channel_id=1, source_target_pairs={{12,28},{13,29},{14,30},{15,31},{28,12},{29,13},{30,14},{31,15}} | collective-permute-start | bytes 221192 | tf_op jit(solution)/shard_map/ppermute | solution.py:286
  53.2 0.4 collective-permute-done.14.refs_9_
  53.6 3.4 %collective-permute-done.13.refs_8_ = f32[9,16,128]{2,1,0:T(8,128)S(1)} collective-permute-done((f32[9,16,128]{2,1,0:T(8,128)S(1)}, f32[9,16,128]{2,1,0:T(8,128)S(1)}, u32[]{:S(2)}, u32[]{:S(2)}) %collective-permute-start.13) | collective-permute-done | bytes 73760 | tf_op jit(solution)/shard_map/ppermute | solution.py:286
  57.0 3.3 %shard_map.66 = f32[27,8,16,128]{3,2,1,0:T(8,128)} custom-call(f32[27,8,16,128]{3,2,1,0:T(8,128)S(1)} %get-tuple-element.18.refs_0_, f32[2,1,27,8,16,128]{5,4,3,2,1,0:T(8,128)S(1)} %copy-done, s32[1,8,16,128]{3,2,1,0:T(8,128)S(1)} %copy-done.2, f32[11,16,128]{2,1,0:T(8,128)S(1)} %collective-permute-done.10.refs_3_, ...), custom_call_target="tpu_custom_call" | custom-call | tf_op jit(solution)/shard_map/pallas_call | solution.py:304
  (27 shorter events, 0.3 us)
Async XLA Ops:
  0.0 1.5 %copy-start.1 = (f32[1,27,8,16,128]{4,3,2,1,0:T(8,128)S(1)}, f32[1,27,8,16,128]{4,3,2,1,0:T(8,128)}, u32[]{:S(2)}) copy-start(f32[1,27,8,16,128]{4,3,2,1,0:T(8,128)} %param.6) | copy-start | bytes 5308420
  1.5 21.7 %copy-start.4 = (s32[1,16,128,2]{2,3,1,0:T(2,128)S(1)}, s32[1,16,128,2]{2,3,1,0:T(2,128)}, u32[]{:S(2)}) copy-start(s32[1,16,128,2]{2,3,1,0:T(2,128)} %param.10) | copy-start | bytes 49156
  1.5 21.7 %copy-start.5 = (s32[1,16,128,2]{2,3,1,0:T(2,128)S(1)}, s32[1,16,128,2]{2,3,1,0:T(2,128)}, u32[]{:S(2)}) copy-start(s32[1,16,128,2]{2,3,1,0:T(2,128)} %param.9) | copy-start | bytes 49156
  1.5 21.7 %copy-start.3 = (f32[1,16,128,2]{2,3,1,0:T(2,128)S(1)}, f32[1,16,128,2]{2,3,1,0:T(2,128)}, u32[]{:S(2)}) copy-start(f32[1,16,128,2]{2,3,1,0:T(2,128)} %param.11) | copy-start | bytes 49156
  1.5 26.0 %copy-start.2 = (s32[1,8,16,128]{3,2,1,0:T(8,128)S(1)}, s32[1,8,16,128]{3,2,1,0:T(8,128)}, u32[]{:S(2)}) copy-start(s32[1,8,16,128]{3,2,1,0:T(8,128)} %refs_2_.3) | copy-start | bytes 196612
  2.3 16.2 %collective-permute-start = (f32[16,128]{1,0:T(8,128)S(1)}, f32[16,128]{1,0:T(8,128)S(1)}, u32[]{:S(2)}, u32[]{:S(2)}) collective-permute-start(f32[16,128]{1,0:T(8,128)S(1)} %get-tuple-element.15), channel_id=1, source_target_pairs={{0,1},{1,2},{2,3},{4,5},{5,6},{6,7},{8,9},{9,10},{10,11},{12,13},{... | collective-permute-start | bytes 24584 | tf_op jit(solution)/shard_map/ppermute | solution.py:278
  5.6 15.0 %collective-permute-start.1 = (f32[16,128]{1,0:T(8,128)S(1)}, f32[16,128]{1,0:T(8,128)S(1)}, u32[]{:S(2)}, u32[]{:S(2)}) collective-permute-start(f32[16,128]{1,0:T(8,128)S(1)} %get-tuple-element.16), channel_id=1, source_target_pairs={{1,0},{2,1},{3,2},{5,4},{6,5},{7,6},{9,8},{10,9},{11,10},{13,12},{... | collective-permute-start | bytes 24584 | tf_op jit(solution)/shard_map/ppermute | solution.py:278
  6.9 15.0 %collective-permute-start.7 = (f32[9,16,128]{2,1,0:T(8,128)S(1)}, f32[9,16,128]{2,1,0:T(8,128)S(1)}, u32[]{:S(2)}, u32[]{:S(2)}) collective-permute-start(f32[9,16,128]{2,1,0:T(8,128)S(1)} %get-tuple-element.14), channel_id=1, source_target_pairs={{12,31},{13,28},{14,29},{15,30},{28,15},{29,12},{30,13},{31,14}} | collective-permute-start | bytes 221192 | tf_op jit(solution)/shard_map/ppermute | solution.py:286
  14.0 9.2 %collective-permute-start.6 = (f32[9,16,128]{2,1,0:T(8,128)S(1)}, f32[9,16,128]{2,1,0:T(8,128)S(1)}, u32[]{:S(2)}, u32[]{:S(2)}) collective-permute-start(f32[9,16,128]{2,1,0:T(8,128)S(1)} %get-tuple-element.14), channel_id=1, source_target_pairs={{12,30},{13,31},{14,28},{15,29},{28,14},{29,15},{30,12},{31,13}} | collective-permute-start | bytes 221192 | tf_op jit(solution)/shard_map/ppermute | solution.py:286
  15.9 7.5 %collective-permute-start.5 = (f32[9,16,128]{2,1,0:T(8,128)S(1)}, f32[9,16,128]{2,1,0:T(8,128)S(1)}, u32[]{:S(2)}, u32[]{:S(2)}) collective-permute-start(f32[9,16,128]{2,1,0:T(8,128)S(1)} %get-tuple-element.14), channel_id=1, source_target_pairs={{12,29},{13,30},{14,31},{15,28},{28,13},{29,14},{30,15},{31,12}} | collective-permute-start | bytes 221192 | tf_op jit(solution)/shard_map/ppermute | solution.py:286
  18.6 4.8 %collective-permute-start.4 = (f32[9,16,128]{2,1,0:T(8,128)S(1)}, f32[9,16,128]{2,1,0:T(8,128)S(1)}, u32[]{:S(2)}, u32[]{:S(2)}) collective-permute-start(f32[9,16,128]{2,1,0:T(8,128)S(1)} %get-tuple-element.14), channel_id=1, source_target_pairs={{12,28},{13,29},{14,30},{15,31},{28,12},{29,13},{30,14},{31,15}} | collective-permute-start | bytes 221192 | tf_op jit(solution)/shard_map/ppermute | solution.py:286
  20.5 3.1 %collective-permute-start.3 = (f32[11,16,128]{2,1,0:T(8,128)S(1)}, f32[11,16,128]{2,1,0:T(8,128)S(1)}, u32[]{:S(2)}, u32[]{:S(2)}) collective-permute-start(f32[11,16,128]{2,1,0:T(8,128)S(1)} %get-tuple-element.25), channel_id=1, source_target_pairs={{4,0},{8,4},{12,8},{5,1},{9,5},{13,9},{6,2},{10,6},{14,10},{7,3},{... | collective-permute-start | bytes 270344 | tf_op jit(solution)/shard_map/ppermute | solution.py:278
  21.9 5.6 %collective-permute-start.2 = (f32[11,16,128]{2,1,0:T(8,128)S(1)}, f32[11,16,128]{2,1,0:T(8,128)S(1)}, u32[]{:S(2)}, u32[]{:S(2)}) collective-permute-start(f32[11,16,128]{2,1,0:T(8,128)S(1)} %get-tuple-element.26), channel_id=1, source_target_pairs={{0,4},{4,8},{8,12},{1,5},{5,9},{9,13},{2,6},{6,10},{10,14},{3,7},{... | collective-permute-start | bytes 270344 | tf_op jit(solution)/shard_map/ppermute | solution.py:278
  27.4 29.6 %copy-start = (f32[2,1,27,8,16,128]{5,4,3,2,1,0:T(8,128)S(1)}, f32[2,1,27,8,16,128]{5,4,3,2,1,0:T(8,128)}, u32[]{:S(2)}) copy-start(f32[2,1,27,8,16,128]{5,4,3,2,1,0:T(8,128)} %refs_1_.3) | copy-start | bytes 10616836
  32.0 11.9 %collective-permute-start.8 = (f32[16,128]{1,0:T(8,128)S(1)}, f32[16,128]{1,0:T(8,128)S(1)}, u32[]{:S(2)}, u32[]{:S(2)}) collective-permute-start(f32[16,128]{1,0:T(8,128)S(1)} %get-tuple-element.20), channel_id=1, source_target_pairs={{0,1},{1,2},{2,3},{4,5},{5,6},{6,7},{8,9},{9,10},{10,11},{12,13},{... | collective-permute-start | bytes 24584 | tf_op jit(solution)/shard_map/ppermute | solution.py:278
  36.1 7.8 %collective-permute-start.9 = (f32[16,128]{1,0:T(8,128)S(1)}, f32[16,128]{1,0:T(8,128)S(1)}, u32[]{:S(2)}, u32[]{:S(2)}) collective-permute-start(f32[16,128]{1,0:T(8,128)S(1)} %get-tuple-element.21), channel_id=1, source_target_pairs={{1,0},{2,1},{3,2},{5,4},{6,5},{7,6},{9,8},{10,9},{11,10},{13,12},{... | collective-permute-start | bytes 24584 | tf_op jit(solution)/shard_map/ppermute | solution.py:278
  37.4 13.9 %collective-permute-start.15 = (f32[9,16,128]{2,1,0:T(8,128)S(1)}, f32[9,16,128]{2,1,0:T(8,128)S(1)}, u32[]{:S(2)}, u32[]{:S(2)}) collective-permute-start(f32[9,16,128]{2,1,0:T(8,128)S(1)} %get-tuple-element.19), channel_id=1, source_target_pairs={{12,31},{13,28},{14,29},{15,30},{28,15},{29,12},{30,13},{31,14}} | collective-permute-start | bytes 221192 | tf_op jit(solution)/shard_map/ppermute | solution.py:286
  44.0 13.0 %collective-permute-start.11 = (f32[11,16,128]{2,1,0:T(8,128)S(1)}, f32[11,16,128]{2,1,0:T(8,128)S(1)}, u32[]{:S(2)}, u32[]{:S(2)}) collective-permute-start(f32[11,16,128]{2,1,0:T(8,128)S(1)} %get-tuple-element.23), channel_id=1, source_target_pairs={{4,0},{8,4},{12,8},{5,1},{9,5},{13,9},{6,2},{10,6},{14,10},{7,3},{... | collective-permute-start | bytes 270344 | tf_op jit(solution)/shard_map/ppermute | solution.py:278
  45.3 11.7 %collective-permute-start.10 = (f32[11,16,128]{2,1,0:T(8,128)S(1)}, f32[11,16,128]{2,1,0:T(8,128)S(1)}, u32[]{:S(2)}, u32[]{:S(2)}) collective-permute-start(f32[11,16,128]{2,1,0:T(8,128)S(1)} %get-tuple-element.24), channel_id=1, source_target_pairs={{0,4},{4,8},{8,12},{1,5},{5,9},{9,13},{2,6},{6,10},{10,14},{3,7},{... | collective-permute-start | bytes 270344 | tf_op jit(solution)/shard_map/ppermute | solution.py:278
  46.6 7.0 %collective-permute-start.14 = (f32[9,16,128]{2,1,0:T(8,128)S(1)}, f32[9,16,128]{2,1,0:T(8,128)S(1)}, u32[]{:S(2)}, u32[]{:S(2)}) collective-permute-start(f32[9,16,128]{2,1,0:T(8,128)S(1)} %get-tuple-element.19), channel_id=1, source_target_pairs={{12,30},{13,31},{14,28},{15,29},{28,14},{29,15},{30,12},{31,13}} | collective-permute-start | bytes 221192 | tf_op jit(solution)/shard_map/ppermute | solution.py:286
  48.9 8.1 %collective-permute-start.13 = (f32[9,16,128]{2,1,0:T(8,128)S(1)}, f32[9,16,128]{2,1,0:T(8,128)S(1)}, u32[]{:S(2)}, u32[]{:S(2)}) collective-permute-start(f32[9,16,128]{2,1,0:T(8,128)S(1)} %get-tuple-element.19), channel_id=1, source_target_pairs={{12,29},{13,30},{14,31},{15,28},{28,13},{29,14},{30,15},{31,12}} | collective-permute-start | bytes 221192 | tf_op jit(solution)/shard_map/ppermute | solution.py:286
  51.3 5.7 %collective-permute-start.12 = (f32[9,16,128]{2,1,0:T(8,128)S(1)}, f32[9,16,128]{2,1,0:T(8,128)S(1)}, u32[]{:S(2)}, u32[]{:S(2)}) collective-permute-start(f32[9,16,128]{2,1,0:T(8,128)S(1)} %get-tuple-element.19), channel_id=1, source_target_pairs={{12,28},{13,29},{14,30},{15,31},{28,12},{29,13},{30,14},{31,15}} | collective-permute-start | bytes 221192 | tf_op jit(solution)/shard_map/ppermute | solution.py:286

commit v2 on v1

--- a/solution.py
+++ b/solution.py
@@ -54,8 +54,6 @@
 
 
 def band_tiles(blocks, device, cell, weight, count):
-    me = lax.axis_index("yz")
-    hops = [lax.rem(me - device[k] + count, count) for k in range(2)]
     values = []
     for j in range(9):
         halves = []
@@ -65,8 +63,8 @@
                 spot = cell[k, r : r + 8]
                 picked = jnp.zeros((8, 128), jnp.float32)
                 for m in range(count):
-                    got = jnp.take_along_axis(blocks[m][j, r : r + 8], spot, axis=1)
-                    picked = jnp.where(hops[k][r : r + 8] == m, got, picked)
+                    got = jnp.take_along_axis(blocks[m, j, r : r + 8], spot, axis=1)
+                    picked = jnp.where(device[k, r : r + 8] == m, got, picked)
                 total = total + picked * weight[k, r : r + 8]
             halves.append(total)
         values.append(jnp.concatenate(halves, axis=0))
@@ -163,9 +161,8 @@
 def step_kernel(count, backward, last, *refs):
     refs = list(refs)
     adj, saved, solid, from_low, from_high, edge_low, edge_high = refs[:7]
-    blocks = refs[7 : 7 + count]
-    device, cell, weight = refs[7 + count : 10 + count]
-    rest = refs[10 + count :]
+    blocks, device, cell, weight = refs[7:11]
+    rest = refs[11:]
     if last:
         out = rest.pop(0)
     else:
@@ -277,13 +274,15 @@
         pairs = [(i, i + step) for i in range(size) if 0 <= i + step < size]
         return lax.ppermute(values, axis, pairs)
 
-    def crossed(values, hop):
+    def crossed(values):
         pairs = [
-            (flat(zone, widths - 1, z), flat(1 - zone, widths - 1, (z + hop) % count))
+            (flat(zone, widths - 1, z), flat(1 - zone, widths - 1, z))
             for zone in range(zones)
             for z in range(count)
         ]
-        return lax.ppermute(values, axes, pairs)
+        partner = lax.ppermute(values, axes, pairs)
+        slots = jnp.broadcast_to(partner[None], (count,) + partner.shape)
+        return lax.all_to_all(slots, "yz", 0, 0)
 
     edges = (tile_shape(), tile_shape(), tile_shape(9), tile_shape(9))
     low, high, top, bottom = pl.pallas_call(
@@ -297,14 +296,14 @@
         last = backward == 0
         edge_low = shifted(high, "yz", 1)
         edge_high = shifted(low, "yz", -1)
-        blocks = [crossed(top, hop) for hop in range(count)]
+        blocks = crossed(top)
         seams = jnp.stack([edge_low, edge_high])
         from_low = shifted(jnp.concatenate([top, seams]), "gx", 1)
         from_high = shifted(jnp.concatenate([bottom, seams]), "gx", -1)
         result = pl.pallas_call(
             lambda *refs, backward=backward, last=last: step_kernel(count, backward, last, *refs),
             out_shape=(tile_shape(27, extent_x),) + (() if last else edges),
-            in_specs=in_any(2) + in_vmem(5 + count + 3),
+            in_specs=in_any(2) + in_vmem(9),
             out_specs=tuple(in_any(1) + ([] if last else in_vmem(4))),
             scratch_shapes=[
                 pltpu.VMEM((27, extent_x + 2, 16, 128), jnp.float32),
@@ -318,7 +317,7 @@
                 pltpu.SemaphoreType.DMA((extent_x,)),
             ],
             compiler_params=params,
-        )(field, saved, solid, from_low, from_high, edge_low, edge_high, *blocks, device, cell, weight)
+        )(field, saved, solid, from_low, from_high, edge_low, edge_high, blocks, device, cell, weight)
         if last:
             field = result[0]
         else:

time: 60.8 us -> 85.2 us (1.40)
  the two profiles are of different devices: /device:TPU:7 before, /device:TPU:6 now
where the time goes in v2:
time: 85.2 us; the launch traced here: 83.9 us
  starting transfers between devices  28.3 us (33%)
  local copies, waits for them, and re-layouts  25.3 us (30%)
  waiting for transfers between devices  19.6 us (23%)
  Pallas kernels  9.58 us (11%)
  other arithmetic  0.95 us (1%)
    unnamed x73, local copies, waits for them, and re-layouts  23.2 us
    ppermute x8, waiting for transfers between devices, shifted(): return lax.ppermute(values, axis, pairs)  17.1 us
    ppermute x8, starting transfers between devices, shifted(): return lax.ppermute(values, axis, pairs)  15.5 us
    all_to_all x2, starting transfers between devices, crossed(): return lax.all_to_all(slots, 'yz', 0, 0)  8.96 us
    pallas_call x2, Pallas kernels, body(): pl.pallas_call(lambda *refs, backward=backward, last=last: step_kernel(co...  8.72 us
    ppermute x2, starting transfers between devices, crossed(): partner = lax.ppermute(values, axes, pairs)  3.83 us
    ppermute x2, waiting for transfers between devices, crossed(): partner = lax.ppermute(values, axes, pairs)  2.46 us
  transfers between devices with their start and end apart: 12, of which 10 were waited for; matrix products, arithmetic and copies ran while one was open for 2% of the time, Pallas kernels for 0%

profile of v2, /device:TPU:6, one launch (start us, length us, event | category | flops | bytes accessed | tf_op | source)
XLA Modules:
  0.0 83.9 jit_solution(649428327341255645)
XLA Ops:
  0.0 1.5 %copy-done.1 = f32[1,27,8,16,128]{4,3,2,1,0:T(8,128)S(1)} copy-done((f32[1,27,8,16,128]{4,3,2,1,0:T(8,128)S(1)}, f32[1,27,8,16,128]{4,3,2,1,0:T(8,128)}, u32[]{:S(2)}) %copy-start.1) | copy-done | bytes 1769496
  2.3 1.9 %collective-permute-start.4 = (f32[9,16,128]{2,1,0:T(8,128)S(1)}, f32[9,16,128]{2,1,0:T(8,128)S(1)}, u32[]{:S(2)}, u32[]{:S(2)}) collective-permute-start(f32[9,16,128]{2,1,0:T(8,128)S(1)} %get-tuple-element.14), channel_id=1, source_target_pairs={{12,28},{13,29},{14,30},{15,31},{28,12},{29,13},{30,14},{31,15}} | collective-permute-start | bytes 221192 | tf_op jit(solution)/shard_map/ppermute | solution.py:283
  4.3 1.2 %collective-permute-done.4 = f32[9,16,128]{2,1,0:T(8,128)S(1)} collective-permute-done((f32[9,16,128]{2,1,0:T(8,128)S(1)}, f32[9,16,128]{2,1,0:T(8,128)S(1)}, u32[]{:S(2)}, u32[]{:S(2)}) %collective-permute-start.4) | collective-permute-done | bytes 73760 | tf_op jit(solution)/shard_map/ppermute | solution.py:283
  6.2 4.9 %all-to-all-start = ((f32[4,9,16,128]{3,2,1,0:T(8,128)}), f32[4,9,16,128]{3,2,1,0:T(8,128)S(1)}, u32[]{:S(2)}, u32[]{:S(2)}) async-start(f32[4,9,16,128]{3,2,1,0:T(8,128)} %broadcast_in_dim.6), calls=%async_computation | async-start | bytes 589824 | tf_op jit(solution)/shard_map/all_to_all | solution.py:285
  11.1 3.9 %collective-permute-start = (f32[16,128]{1,0:T(8,128)S(1)}, f32[16,128]{1,0:T(8,128)S(1)}, u32[]{:S(2)}, u32[]{:S(2)}) collective-permute-start(f32[16,128]{1,0:T(8,128)S(1)} %get-tuple-element.15), channel_id=1, source_target_pairs={{0,1},{1,2},{2,3},{4,5},{5,6},{6,7},{8,9},{9,10},{10,11},{12,13},{... | collective-permute-start | bytes 24584 | tf_op jit(solution)/shard_map/ppermute | solution.py:275
  15.0 1.3 %collective-permute-start.1 = (f32[16,128]{1,0:T(8,128)S(1)}, f32[16,128]{1,0:T(8,128)S(1)}, u32[]{:S(2)}, u32[]{:S(2)}) collective-permute-start(f32[16,128]{1,0:T(8,128)S(1)} %get-tuple-element.16), channel_id=1, source_target_pairs={{1,0},{2,1},{3,2},{5,4},{6,5},{7,6},{9,8},{10,9},{11,10},{13,12},{... | collective-permute-start | bytes 24584 | tf_op jit(solution)/shard_map/ppermute | solution.py:275
  16.5 4.1 %collective-permute-done.1.refs_6_ = f32[16,128]{1,0:T(8,128)S(1)} collective-permute-done((f32[16,128]{1,0:T(8,128)S(1)}, f32[16,128]{1,0:T(8,128)S(1)}, u32[]{:S(2)}, u32[]{:S(2)}) %collective-permute-start.1) | collective-permute-done | bytes 8224 | tf_op jit(solution)/shard_map/ppermute | solution.py:275
  20.6 1.3 %collective-permute-start.3 = (f32[11,16,128]{2,1,0:T(8,128)S(1)}, f32[11,16,128]{2,1,0:T(8,128)S(1)}, u32[]{:S(2)}, u32[]{:S(2)}) collective-permute-start(f32[11,16,128]{2,1,0:T(8,128)S(1)} %get-tuple-element.25), channel_id=1, source_target_pairs={{4,0},{8,4},{12,8},{5,1},{9,5},{13,9},{6,2},{10,6},{14,10},{7,3},{... | collective-permute-start | bytes 270344 | tf_op jit(solution)/shard_map/ppermute | solution.py:275
  21.9 1.3 %collective-permute-start.2 = (f32[11,16,128]{2,1,0:T(8,128)S(1)}, f32[11,16,128]{2,1,0:T(8,128)S(1)}, u32[]{:S(2)}, u32[]{:S(2)}) collective-permute-start(f32[11,16,128]{2,1,0:T(8,128)S(1)} %get-tuple-element.26), channel_id=1, source_target_pairs={{0,4},{4,8},{8,12},{1,5},{5,9},{9,13},{2,6},{6,10},{10,14},{3,7},{... | collective-permute-start | bytes 270344 | tf_op jit(solution)/shard_map/ppermute | solution.py:275
  24.7 3.7 %collective-permute-done.2.refs_3_ = f32[11,16,128]{2,1,0:T(8,128)S(1)} collective-permute-done((f32[11,16,128]{2,1,0:T(8,128)S(1)}, f32[11,16,128]{2,1,0:T(8,128)S(1)}, u32[]{:S(2)}, u32[]{:S(2)}) %collective-permute-start.2) | collective-permute-done | bytes 90144 | tf_op jit(solution)/shard_map/ppermute | solution.py:275
  29.7 1.5 %copy-done.2 = f32[1,27,8,16,128]{4,3,2,1,0:T(8,128)S(1)} copy-done((f32[1,27,8,16,128]{4,3,2,1,0:T(8,128)S(1)}, f32[1,27,8,16,128]{4,3,2,1,0:T(8,128)}, u32[]{:S(2)}) %copy-start.2) | copy-done | bytes 1769496
  37.6 4.4 %shard_map.65 = (f32[27,8,16,128]{3,2,1,0:T(8,128)S(1)}, f32[16,128]{1,0:T(8,128)S(1)}, f32[16,128]{1,0:T(8,128)S(1)}, f32[9,16,128]{2,1,0:T(8,128)S(1)}, f32[9,16,128]{2,1,0:T(8,128)S(1)}) custom-call(f32[27,8,16,128]{3,2,1,0:T(8,128)S(1)} %bitcast.20, f32[2,1,27,8,16,128]{5,4,3,2,1,0:T(8,128)} %refs_1_.3, s32[1,8,16,128]{3,2,1,0:T(8,128)S(1)} %copy-done.7, ...), custom_call_target="tpu_custom_call" | custom-call | tf_op jit(solution)/shard_map/pallas_call | solution.py:303
  42.1 1.2 %copy-done.3 = f32[27,8,16,128]{3,2,1,0:T(8,128)} copy-done((f32[27,8,16,128]{3,2,1,0:T(8,128)}, f32[27,8,16,128]{3,2,1,0:T(8,128)S(1)}, u32[]{:S(2)}) %copy-start.3) | copy-done | bytes 1769496
  45.7 1.9 %collective-permute-start.9 = (f32[9,16,128]{2,1,0:T(8,128)S(1)}, f32[9,16,128]{2,1,0:T(8,128)S(1)}, u32[]{:S(2)}, u32[]{:S(2)}) collective-permute-start(f32[9,16,128]{2,1,0:T(8,128)S(1)} %get-tuple-element.19), channel_id=1, source_target_pairs={{12,28},{13,29},{14,30},{15,31},{28,12},{29,13},{30,14},{31,15}} | collective-permute-start | bytes 221192 | tf_op jit(solution)/shard_map/ppermute | solution.py:283
  47.6 1.2 %collective-permute-done.9 = f32[9,16,128]{2,1,0:T(8,128)S(1)} collective-permute-done((f32[9,16,128]{2,1,0:T(8,128)S(1)}, f32[9,16,128]{2,1,0:T(8,128)S(1)}, u32[]{:S(2)}, u32[]{:S(2)}) %collective-permute-start.9) | collective-permute-done | bytes 73760 | tf_op jit(solution)/shard_map/ppermute | solution.py:283
  49.6 4.1 %all-to-all-start.1 = ((f32[4,9,16,128]{3,2,1,0:T(8,128)}), f32[4,9,16,128]{3,2,1,0:T(8,128)}, u32[]{:S(2)}, u32[]{:S(2)}) async-start(f32[4,9,16,128]{3,2,1,0:T(8,128)} %broadcast_in_dim.7), calls=%async_computation.1 | async-start | bytes 589824 | tf_op jit(solution)/shard_map/all_to_all | solution.py:285
  53.7 3.9 %collective-permute-start.5 = (f32[16,128]{1,0:T(8,128)}, f32[16,128]{1,0:T(8,128)S(1)}, u32[]{:S(2)}, u32[]{:S(2)}) collective-permute-start(f32[16,128]{1,0:T(8,128)} %copy-done.32), channel_id=1, source_target_pairs={{0,1},{1,2},{2,3},{4,5},{5,6},{6,7},{8,9},{9,10},{10,11},{12,13},{... | collective-permute-start | bytes 24584 | tf_op jit(solution)/shard_map/ppermute | solution.py:275
  57.6 1.3 %collective-permute-start.6 = (f32[16,128]{1,0:T(8,128)}, f32[16,128]{1,0:T(8,128)S(1)}, u32[]{:S(2)}, u32[]{:S(2)}) collective-permute-start(f32[16,128]{1,0:T(8,128)} %copy-done.31), channel_id=1, source_target_pairs={{1,0},{2,1},{3,2},{5,4},{6,5},{7,6},{9,8},{10,9},{11,10},{13,12},{... | collective-permute-start | bytes 24584 | tf_op jit(solution)/shard_map/ppermute | solution.py:275
  59.4 4.0 %collective-permute-done.6.refs_6_ = f32[16,128]{1,0:T(8,128)S(1)} collective-permute-done((f32[16,128]{1,0:T(8,128)}, f32[16,128]{1,0:T(8,128)S(1)}, u32[]{:S(2)}, u32[]{:S(2)}) %collective-permute-start.6) | collective-permute-done | bytes 8224 | tf_op jit(solution)/shard_map/ppermute | solution.py:275
  64.4 1.3 %collective-permute-start.8 = (f32[11,16,128]{2,1,0:T(8,128)S(1)}, f32[11,16,128]{2,1,0:T(8,128)S(1)}, u32[]{:S(2)}, u32[]{:S(2)}) collective-permute-start(f32[11,16,128]{2,1,0:T(8,128)S(1)} %get-tuple-element.23), channel_id=1, source_target_pairs={{4,0},{8,4},{12,8},{5,1},{9,5},{13,9},{6,2},{10,6},{14,10},{7,3},{... | collective-permute-start | bytes 270344 | tf_op jit(solution)/shard_map/ppermute | solution.py:275
  65.7 1.3 %collective-permute-start.7 = (f32[11,16,128]{2,1,0:T(8,128)S(1)}, f32[11,16,128]{2,1,0:T(8,128)S(1)}, u32[]{:S(2)}, u32[]{:S(2)}) collective-permute-start(f32[11,16,128]{2,1,0:T(8,128)S(1)} %get-tuple-element.24), channel_id=1, source_target_pairs={{0,4},{4,8},{8,12},{1,5},{5,9},{9,13},{2,6},{6,10},{10,14},{3,7},{... | collective-permute-start | bytes 270344 | tf_op jit(solution)/shard_map/ppermute | solution.py:275
  68.4 3.7 %collective-permute-done.7.refs_3_ = f32[11,16,128]{2,1,0:T(8,128)S(1)} collective-permute-done((f32[11,16,128]{2,1,0:T(8,128)S(1)}, f32[11,16,128]{2,1,0:T(8,128)S(1)}, u32[]{:S(2)}, u32[]{:S(2)}) %collective-permute-start.7) | collective-permute-done | bytes 90144 | tf_op jit(solution)/shard_map/ppermute | solution.py:275
  72.7 1.5 %copy-done.4 = f32[27,8,16,128]{3,2,1,0:T(8,128)S(1)} copy-done((f32[27,8,16,128]{3,2,1,0:T(8,128)S(1)}, f32[27,8,16,128]{3,2,1,0:T(8,128)}, u32[]{:S(2)}) %copy-start.4) | copy-done | bytes 1769496
  79.7 4.3 %shard_map.66 = f32[27,8,16,128]{3,2,1,0:T(8,128)} custom-call(f32[27,8,16,128]{3,2,1,0:T(8,128)S(1)} %copy-done.4, f32[2,1,27,8,16,128]{5,4,3,2,1,0:T(8,128)S(1)} %copy-done, s32[1,8,16,128]{3,2,1,0:T(8,128)S(1)} %copy-done.8, f32[11,16,128]{2,1,0:T(8,128)S(1)} %copy-done.20, f32[11,16,128]{2,1,0:T(8,128)S(1)} %copy-done.18, f32[16,128]{1,0:T(8,128)S(1)} %copy-done.28, ...), custom_call_target="tpu_custom_call" | custom-call | tf_op jit(solution)/shard_map/pallas_call | solution.py:303
  (81 shorter events, 23.2 us)
Async XLA Ops:
  0.0 1.5 %copy-start.1 = (f32[1,27,8,16,128]{4,3,2,1,0:T(8,128)S(1)}, f32[1,27,8,16,128]{4,3,2,1,0:T(8,128)}, u32[]{:S(2)}) copy-start(f32[1,27,8,16,128]{4,3,2,1,0:T(8,128)} %param.6) | copy-start | bytes 5308420
  1.5 21.8 %copy-start.34 = (s32[1,16,128,2]{2,3,1,0:T(2,128)S(1)}, s32[1,16,128,2]{2,3,1,0:T(2,128)}, u32[]{:S(2)}) copy-start(s32[1,16,128,2]{2,3,1,0:T(2,128)} %param.10) | copy-start | bytes 49156
  1.5 21.8 %copy-start.35 = (s32[1,16,128,2]{2,3,1,0:T(2,128)S(1)}, s32[1,16,128,2]{2,3,1,0:T(2,128)}, u32[]{:S(2)}) copy-start(s32[1,16,128,2]{2,3,1,0:T(2,128)} %param.9) | copy-start | bytes 49156
  1.5 22.4 %copy-start.33 = (f32[1,16,128,2]{2,3,1,0:T(2,128)S(1)}, f32[1,16,128,2]{2,3,1,0:T(2,128)}, u32[]{:S(2)}) copy-start(f32[1,16,128,2]{2,3,1,0:T(2,128)} %param.11) | copy-start | bytes 49156
  2.3 3.2 %collective-permute-start.4 = (f32[9,16,128]{2,1,0:T(8,128)S(1)}, f32[9,16,128]{2,1,0:T(8,128)S(1)}, u32[]{:S(2)}, u32[]{:S(2)}) collective-permute-start(f32[9,16,128]{2,1,0:T(8,128)S(1)} %get-tuple-element.14), channel_id=1, source_target_pairs={{12,28},{13,29},{14,30},{15,31},{28,12},{29,13},{30,14},{31,15}} | collective-permute-start | bytes 221192 | tf_op jit(solution)/shard_map/ppermute | solution.py:283
  6.2 22.8 %all-to-all-start = ((f32[4,9,16,128]{3,2,1,0:T(8,128)}), f32[4,9,16,128]{3,2,1,0:T(8,128)S(1)}, u32[]{:S(2)}, u32[]{:S(2)}) async-start(f32[4,9,16,128]{3,2,1,0:T(8,128)} %broadcast_in_dim.6), calls=%async_computation | async-start | bytes 589824 | tf_op jit(solution)/shard_map/all_to_all | solution.py:285
  11.1 5.4 %collective-permute-start = (f32[16,128]{1,0:T(8,128)S(1)}, f32[16,128]{1,0:T(8,128)S(1)}, u32[]{:S(2)}, u32[]{:S(2)}) collective-permute-start(f32[16,128]{1,0:T(8,128)S(1)} %get-tuple-element.15), channel_id=1, source_target_pairs={{0,1},{1,2},{2,3},{4,5},{5,6},{6,7},{8,9},{9,10},{10,11},{12,13},{... | collective-permute-start | bytes 24584 | tf_op jit(solution)/shard_map/ppermute | solution.py:275
  15.0 5.6 %collective-permute-start.1 = (f32[16,128]{1,0:T(8,128)S(1)}, f32[16,128]{1,0:T(8,128)S(1)}, u32[]{:S(2)}, u32[]{:S(2)}) collective-permute-start(f32[16,128]{1,0:T(8,128)S(1)} %get-tuple-element.16), channel_id=1, source_target_pairs={{1,0},{2,1},{3,2},{5,4},{6,5},{7,6},{9,8},{10,9},{11,10},{13,12},{... | collective-permute-start | bytes 24584 | tf_op jit(solution)/shard_map/ppermute | solution.py:275
  16.5 6.7 %copy-start.23 = (f32[16,128]{1,0:T(8,128)}, f32[16,128]{1,0:T(8,128)S(1)}, u32[]{:S(2)}) copy-start(f32[16,128]{1,0:T(8,128)S(1)} %collective-permute-done.refs_5_) | copy-start | bytes 24580
  20.6 2.6 %copy-start.25 = (f32[16,128]{1,0:T(8,128)}, f32[16,128]{1,0:T(8,128)S(1)}, u32[]{:S(2)}) copy-start(f32[16,128]{1,0:T(8,128)S(1)} %collective-permute-done.1.refs_6_) | copy-start | bytes 24580
  20.6 3.4 %collective-permute-start.3 = (f32[11,16,128]{2,1,0:T(8,128)S(1)}, f32[11,16,128]{2,1,0:T(8,128)S(1)}, u32[]{:S(2)}, u32[]{:S(2)}) collective-permute-start(f32[11,16,128]{2,1,0:T(8,128)S(1)} %get-tuple-element.25), channel_id=1, source_target_pairs={{4,0},{8,4},{12,8},{5,1},{9,5},{13,9},{6,2},{10,6},{14,10},{7,3},{... | collective-permute-start | bytes 270344 | tf_op jit(solution)/shard_map/ppermute | solution.py:275
  21.9 6.4 %collective-permute-start.2 = (f32[11,16,128]{2,1,0:T(8,128)S(1)}, f32[11,16,128]{2,1,0:T(8,128)S(1)}, u32[]{:S(2)}, u32[]{:S(2)}) collective-permute-start(f32[11,16,128]{2,1,0:T(8,128)S(1)} %get-tuple-element.26), channel_id=1, source_target_pairs={{0,4},{4,8},{8,12},{1,5},{5,9},{9,13},{2,6},{6,10},{10,14},{3,7},{... | collective-permute-start | bytes 270344 | tf_op jit(solution)/shard_map/ppermute | solution.py:275
  29.7 1.5 %copy-start.2 = (f32[1,27,8,16,128]{4,3,2,1,0:T(8,128)S(1)}, f32[1,27,8,16,128]{4,3,2,1,0:T(8,128)}, u32[]{:S(2)}) copy-start(f32[1,27,8,16,128]{4,3,2,1,0:T(8,128)} %param.6) | copy-start | bytes 5308420
  37.6 35.1 %copy-start = (f32[2,1,27,8,16,128]{5,4,3,2,1,0:T(8,128)S(1)}, f32[2,1,27,8,16,128]{5,4,3,2,1,0:T(8,128)}, u32[]{:S(2)}) copy-start(f32[2,1,27,8,16,128]{5,4,3,2,1,0:T(8,128)} %refs_1_.3) | copy-start | bytes 10616836
  42.1 1.2 %copy-start.3 = (f32[27,8,16,128]{3,2,1,0:T(8,128)}, f32[27,8,16,128]{3,2,1,0:T(8,128)S(1)}, u32[]{:S(2)}) copy-start(f32[27,8,16,128]{3,2,1,0:T(8,128)S(1)} %get-tuple-element.18.refs_0_) | copy-start | bytes 5308420
  45.7 3.1 %collective-permute-start.9 = (f32[9,16,128]{2,1,0:T(8,128)S(1)}, f32[9,16,128]{2,1,0:T(8,128)S(1)}, u32[]{:S(2)}, u32[]{:S(2)}) collective-permute-start(f32[9,16,128]{2,1,0:T(8,128)S(1)} %get-tuple-element.19), channel_id=1, source_target_pairs={{12,28},{13,29},{14,30},{15,31},{28,12},{29,13},{30,14},{31,15}} | collective-permute-start | bytes 221192 | tf_op jit(solution)/shard_map/ppermute | solution.py:283
  49.6 23.1 %all-to-all-start.1 = ((f32[4,9,16,128]{3,2,1,0:T(8,128)}), f32[4,9,16,128]{3,2,1,0:T(8,128)}, u32[]{:S(2)}, u32[]{:S(2)}) async-start(f32[4,9,16,128]{3,2,1,0:T(8,128)} %broadcast_in_dim.7), calls=%async_computation.1 | async-start | bytes 589824 | tf_op jit(solution)/shard_map/all_to_all | solution.py:285
  53.7 5.7 %collective-permute-start.5 = (f32[16,128]{1,0:T(8,128)}, f32[16,128]{1,0:T(8,128)S(1)}, u32[]{:S(2)}, u32[]{:S(2)}) collective-permute-start(f32[16,128]{1,0:T(8,128)} %copy-done.32), channel_id=1, source_target_pairs={{0,1},{1,2},{2,3},{4,5},{5,6},{6,7},{8,9},{9,10},{10,11},{12,13},{... | collective-permute-start | bytes 24584 | tf_op jit(solution)/shard_map/ppermute | solution.py:275
  57.6 5.8 %collective-permute-start.6 = (f32[16,128]{1,0:T(8,128)}, f32[16,128]{1,0:T(8,128)S(1)}, u32[]{:S(2)}, u32[]{:S(2)}) collective-permute-start(f32[16,128]{1,0:T(8,128)} %copy-done.31), channel_id=1, source_target_pairs={{1,0},{2,1},{3,2},{5,4},{6,5},{7,6},{9,8},{10,9},{11,10},{13,12},{... | collective-permute-start | bytes 24584 | tf_op jit(solution)/shard_map/ppermute | solution.py:275
  59.4 8.4 %copy-start.27 = (f32[16,128]{1,0:T(8,128)}, f32[16,128]{1,0:T(8,128)S(1)}, u32[]{:S(2)}) copy-start(f32[16,128]{1,0:T(8,128)S(1)} %collective-permute-done.5.refs_5_) | copy-start | bytes 24580
  63.4 4.4 %copy-start.29 = (f32[16,128]{1,0:T(8,128)}, f32[16,128]{1,0:T(8,128)S(1)}, u32[]{:S(2)}) copy-start(f32[16,128]{1,0:T(8,128)S(1)} %collective-permute-done.6.refs_6_) | copy-start | bytes 24580
  64.4 3.4 %collective-permute-start.8 = (f32[11,16,128]{2,1,0:T(8,128)S(1)}, f32[11,16,128]{2,1,0:T(8,128)S(1)}, u32[]{:S(2)}, u32[]{:S(2)}) collective-permute-start(f32[11,16,128]{2,1,0:T(8,128)S(1)} %get-tuple-element.23), channel_id=1, source_target_pairs={{4,0},{8,4},{12,8},{5,1},{9,5},{13,9},{6,2},{10,6},{14,10},{7,3},{... | collective-permute-start | bytes 270344 | tf_op jit(solution)/shard_map/ppermute | solution.py:275
  65.7 6.4 %collective-permute-start.7 = (f32[11,16,128]{2,1,0:T(8,128)S(1)}, f32[11,16,128]{2,1,0:T(8,128)S(1)}, u32[]{:S(2)}, u32[]{:S(2)}) collective-permute-start(f32[11,16,128]{2,1,0:T(8,128)S(1)} %get-tuple-element.24), channel_id=1, source_target_pairs={{0,4},{4,8},{8,12},{1,5},{5,9},{9,13},{2,6},{6,10},{10,14},{3,7},{... | collective-permute-start | bytes 270344 | tf_op jit(solution)/shard_map/ppermute | solution.py:275
  72.7 1.5 %copy-start.4 = (f32[27,8,16,128]{3,2,1,0:T(8,128)S(1)}, f32[27,8,16,128]{3,2,1,0:T(8,128)}, u32[]{:S(2)}) copy-start(f32[27,8,16,128]{3,2,1,0:T(8,128)} %copy-done.3) | copy-start | bytes 5308420
  (24 other events, 17.6 us)

commit v3 on v1

v3 whole, which is shorter than its diff:
```python
import jax
import jax.numpy as jnp
import numpy as np
from jax import lax
from jax.experimental import pallas as pl
from jax.experimental.pallas import tpu as pltpu
from jax.sharding import PartitionSpec as P

OMEGA = 1.6
VMEM_LIMIT = 20 * 1024 * 1024
SIGNS = (-1, 0, 1)


def number(cx, cy, cz):
    return 9 * (cx + 1) + 3 * (cy + 1) + (cz + 1)


def lanes():
    return lax.broadcasted_iota(jnp.int32, (16, 128), 1)


def shift_y(tile, cy):
    if cy == 0:
        return tile
    row = lax.broadcasted_iota(jnp.int32, tile.shape, 0)
    if cy == 1:
        return jnp.where(row == 15, 0.0, pltpu.roll(tile, 15, 0))
    return jnp.where(row == 0, 0.0, pltpu.roll(tile, 1, 0))


def pack_columns(planes, x, low, high):
    lane = lanes()
    for slot in range(9):
        place = (x + 1) * 9 + slot
        here = lane == place
        low = jnp.where(here, pltpu.roll(planes(3 * slot + 2), place, 1), low)
        high = jnp.where(here, pltpu.roll(planes(3 * slot), place + 1, 1), high)
    return low, high


def is_even(axis):
    return lax.rem(lax.axis_index(axis), 2) == 0


def write_messages(top, low, high, first, second):
    even = is_even("yz")
    for j in range(9):
        tile = top(j)
        first[j] = tile
        second[j] = tile
    first[9] = jnp.where(even, high, low)
    second[9] = jnp.where(even, low, high)


def edges_from(first, second):
    even = is_even("yz")
    me, count = lax.axis_index("yz"), lax.axis_size("yz")
    low = jnp.where(me == 0, 0.0, jnp.where(even, second[9], first[9]))
    high = jnp.where(me == count - 1, 0.0, jnp.where(even, first[9], second[9]))
    return low, high


def pack_kernel(adj, first_out, second_out):
    extent_x = adj.shape[1]
    zero = jnp.zeros((16, 128), jnp.float32)
    low, high = lax.fori_loop(
        0, extent_x, lambda x, c: pack_columns(lambda i: adj[i, x], x, *c), (zero, zero)
    )
    write_messages(lambda j: adj[j, extent_x - 1], low, high, first_out, second_out)


def velocity_kernel(saved, out, kept, sems):
    steps, _, _, extent_x = saved.shape[:4]

    def load(n):
        step, x = n // extent_x, lax.rem(n, extent_x)
        return pltpu.make_async_copy(saved.at[step, 0, :, x], kept.at[n], sems.at[n])

    total = steps * extent_x
    lax.fori_loop(0, total, lambda n, c: (load(n).start(), c)[1], 0)

    def one(n, carry):
        load(n).wait()
        for a, tile in enumerate(velocity_of(lambda i: kept[n, i])):
            out[n // extent_x, a, lax.rem(n, extent_x)] = tile
        return carry

    lax.fori_loop(0, total, one, 0)


def side_kernel(adj, first, second, out):
    extent_x = adj.shape[1]
    even = is_even("gx")
    for j in range(9):
        out[j] = jnp.where(even, adj[j, extent_x - 1], adj[18 + j, 0])
    out[9], out[10] = edges_from(first, second)


def cross_kernel(count, *refs):
    adj, own, first, second = refs[:4]
    others = refs[4 : 4 + count - 3]
    info, out = refs[4 + count - 3 :]
    extent_x = adj.shape[1]
    interface = lax.axis_index("gx") == lax.axis_size("gx") - 1
    out[9], out[10] = edges_from(first, second)

    @pl.when(jnp.logical_not(interface))
    def _():
        even = is_even("gx")
        for j in range(9):
            out[j] = jnp.where(even, adj[18 + j, 0], adj[j, extent_x - 1])

    @pl.when(interface)
    def _():
        me = lax.axis_index("yz")
        even = is_even("yz")
        rows = (0, 8)
        spots, picks = {}, {}
        for r in rows:
            for k in range(2):
                code = info[k, r : r + 8].astype(jnp.int32)
                ahead = lax.rem(code // 128 - me + count, count)
                spots[r, k] = lax.rem(code, 128)
                turned = jnp.where(even, ahead, lax.rem(count - ahead, count))
                masks = [turned == 1, turned == count - 1]
                masks += [ahead == count - hop for hop in range(2, count - 1)]
                picks[r, k] = masks
        for j in range(9):
            halves = []
            for r in rows:
                total = jnp.zeros((8, 128), jnp.float32)
                for k in range(2):
                    tiles = [ref[j, r : r + 8] for ref in (own, first, second, *others)]
                    got = [jnp.take_along_axis(tile, spots[r, k], axis=1) for tile in tiles]
                    picked = got[0]
                    for mask, value in zip(picks[r, k], got[1:]):
                        picked = jnp.where(mask, value, picked)
                    total = total + picked * info[2 + k, r : r + 8]
                halves.append(total)
            out[j] = jnp.concatenate(halves, axis=0)


def velocity_of(saved):
    totals, along_y, along_z = [], [], []
    for cx in SIGNS:
        sums, diffs = [], []
        for cy in SIGNS:
            lo, mid, hi = [saved(number(cx, cy, cz)) for cz in SIGNS]
            sums.append(lo + mid + hi)
            diffs.append(hi - lo)
        totals.append(sums[0] + sums[1] + sums[2])
        along_y.append(sums[2] - sums[0])
        along_z.append(diffs[0] + diffs[1] + diffs[2])
    density = totals[0] + totals[1] + totals[2]
    momentum = (
        totals[2] - totals[0],
        along_y[0] + along_y[1] + along_y[2],
        along_z[0] + along_z[1] + along_z[2],
    )
    return [part / density for part in momentum]


def moments_of(pull):
    rows = []
    for cx in SIGNS:
        plain, first, second = [], [], []
        for cy in SIGNS:
            lo, mid, hi = [pull(cx, cy, cz) for cz in SIGNS]
            both = lo + hi
            plain.append(mid + 0.25 * both)
            first.append(hi - lo)
            second.append(both)
        pair = plain[0] + plain[2]
        rows.append(
            (
                plain[1] + 0.25 * pair,
                plain[2] - plain[0],
                pair,
                first[1] + 0.25 * (first[0] + first[2]),
                first[2] - first[0],
                second[1] + 0.25 * (second[0] + second[2]),
            )
        )
    even = [rows[1][n] + 0.25 * (rows[0][n] + rows[2][n]) for n in range(6)]
    zero = (8.0 / 27.0) * even[0]
    along = (
        (2.0 / 27.0) * (rows[2][0] - rows[0][0]),
        (2.0 / 27.0) * even[1],
        (2.0 / 27.0) * even[3],
    )
    square = (
        (2.0 / 27.0) * (rows[2][0] + rows[0][0]),
        (2.0 / 27.0) * even[2],
        (2.0 / 27.0) * even[5],
    )
    mixed = (
        (1.0 / 54.0) * (rows[2][1] - rows[0][1]),
        (1.0 / 54.0) * (rows[2][3] - rows[0][3]),
        (1.0 / 54.0) * even[4],
    )
    return zero, along, square, mixed


def collide(pull, velocity, solid, store):
    zero, along, square, mixed = moments_of(lambda cx, cy, cz: pull(number(cx, cy, cz)))
    ux, uy, uz = velocity
    xy, xz, yz = mixed
    quadratic = (
        ux * ux * square[0]
        + uy * uy * square[1]
        + uz * uz * square[2]
        + 2.0 * (ux * uy * xy + ux * uz * xz + uy * uz * yz)
    )
    speed = ux * ux + uy * uy + uz * uz
    scalar = OMEGA * (zero * (1.0 + 1.5 * speed) - 4.5 * quadratic)
    vec_x = OMEGA * (3.0 * along[0] + 9.0 * (square[0] * ux + xy * uy + xz * uz) - 3.0 * ux * zero)
    vec_y = OMEGA * (3.0 * along[1] + 9.0 * (xy * ux + square[1] * uy + yz * uz) - 3.0 * uy * zero)
    vec_z = OMEGA * (3.0 * along[2] + 9.0 * (xz * ux + yz * uy + square[2] * uz) - 3.0 * uz * zero)
    wall = solid == 1
    for cx in SIGNS:
        base = scalar if cx == 0 else (scalar + vec_x if cx > 0 else scalar - vec_x)
        for cy in SIGNS:
            inner = base if cy == 0 else (base + vec_y if cy > 0 else base - vec_y)
            for cz in SIGNS:
                full = inner if cz == 0 else (inner + vec_z if cz > 0 else inner - vec_z)
                i = number(cx, cy, cz)
                store(i, jnp.where(wall, pull(26 - i), (1.0 - OMEGA) * pull(i) + full))


def pull_plane(tile_of, edges_of, pulled, raw=None):
    lane = lanes()
    for cx in SIGNS:
        low_edge, high_edge, start = edges_of(cx)
        for cy in SIGNS:
            place = start + 3 * (cx + 1) + cy + 1
            for cz in SIGNS:
                i = number(cx, cy, cz)
                source = tile_of(i, cx)
                tile = source
                if cz == -1:
                    edge = pltpu.roll(low_edge, 128 - place, 1)
                    tile = jnp.where(lane == 0, edge, pltpu.roll(source, 1, 1))
                elif cz == 1:
                    edge = pltpu.roll(high_edge, 127 - place, 1)
                    tile = jnp.where(lane == 127, edge, pltpu.roll(source, 127, 1))
                if raw is not None and cx == 1:
                    tile = jnp.where(raw, source, tile)
                pulled[i] = shift_y(tile, cy)


def inner_kernel(step, last, adj, vel, solid, first, second, *rest):
    if last:
        out, made, pulled, sems = rest
    else:
        out, low_out, high_out, made, pulled, sems = rest
    extent_x = adj.shape[1]
    low_edge, high_edge = edges_from(first, second)

    def save(x):
        return pltpu.make_async_copy(made.at[x - 1], out.at[:, x], sems.at[x - 1])

    def plane(x, carry):
        pull_plane(
            lambda i, cx: adj[i, x + cx],
            lambda cx: (low_edge, high_edge, (x + 1 + cx) * 9),
            pulled,
        )

        def store(i, tile):
            made[x - 1, i] = tile

        velocity = [vel[step, a, x] for a in range(3)]
        collide(lambda i: pulled[i], velocity, solid[0, x], store)
        save(x).start()
        if last:
            return carry
        return pack_columns(lambda i: made[x - 1, i], x, *carry)

    zero = jnp.zeros((16, 128), jnp.float32)
    carry = lax.fori_loop(1, extent_x - 1, plane, 0 if last else (zero, zero))
    if not last:
        low_out[...], high_out[...] = carry
    lax.fori_loop(1, extent_x - 1, lambda x, c: (save(x).wait(), c)[1], 0)


def outer_kernel(step, last, adj, vel, solid, first, second, side, cross, *rest):
    if last:
        _, out, made, pulled, sems = rest
    else:
        _, low_in, high_in, out, first_out, second_out, made, pulled, sems = rest
    extent_x = adj.shape[1]
    low_edge, high_edge = edges_from(first, second)
    even = is_even("gx")
    interface = lax.axis_index("gx") == lax.axis_size("gx") - 1
    below = lambda j: jnp.where(even, cross[j], side[j])
    above = lambda j: jnp.where(even, side[j], cross[j])

    def plane(n, x, tile_of, edges_of, raw):
        pull_plane(tile_of, edges_of, pulled, raw)

        def store(i, tile):
            made[n, i] = tile

        velocity = [vel[step, a, x] for a in range(3)]
        collide(lambda i: pulled[i], velocity, solid[0, x], store)
        save = pltpu.make_async_copy(made.at[n], out.at[:, x], sems.at[n])
        save.start()
        return save

    final = extent_x - 1
    saves = [
        plane(
            0,
            0,
            lambda i, cx: below(i) if cx == -1 else adj[i, cx],
            lambda cx: (
                (below(9), below(10), extent_x * 9)
                if cx == -1
                else (low_edge, high_edge, (1 + cx) * 9)
            ),
            None,
        ),
        plane(
            1,
            final,
            lambda i, cx: above(i - 18) if cx == 1 else adj[i, final + cx],
            lambda cx: (
                (above(9), above(10), 9)
                if cx == 1
                else (low_edge, high_edge, (final + 1 + cx) * 9)
            ),
            interface,
        ),
    ]
    if not last:
        low, high = low_in[...], high_in[...]
        low, high = pack_columns(lambda i: made[0, i], 0, low, high)
        low, high = pack_columns(lambda i: made[1, i], final, low, high)
        write_messages(lambda j: made[1, j], low, high, first_out, second_out)
    for save in saves:
        save.wait()


def tile_shape(*lead):
    return jax.ShapeDtypeStruct(lead + (16, 128), jnp.float32)


def in_vmem(n):
    return [pl.BlockSpec(memory_space=pltpu.VMEM)] * n


def in_any(n):
    return [pl.BlockSpec(memory_space=pl.ANY)] * n


def body(sizes, adjoint, saved, solid, band_device, band_cell, band_weight):
    zones, widths, count = sizes
    field = adjoint[0]
    extent_x = field.shape[1]
    axes = ("zone", "gx", "yz")
    params = pltpu.CompilerParams(vmem_limit_bytes=VMEM_LIMIT)

    def send(values, target):
        flat = lambda zone, gx, yz: (zone * widths + gx) * count + yz
        pairs = []
        for zone in range(zones):
            for gx in range(widths):
                for yz in range(count):
                    to = target(zone, gx, yz)
                    if to is not None:
                        pairs.append((flat(zone, gx, yz), flat(*to)))
        return lax.ppermute(values, axes, pairs)

    def partner_of(place, shift):
        return place + 1 if (place + shift) % 2 == 0 else place - 1

    def along_z(shift):
        return lambda zone, gx, yz: (zone, gx, partner_of(yz, shift) % count)

    def hop_z(hop):
        return lambda zone, gx, yz: (zone, gx, (yz + hop) % count) if gx == widths - 1 else None

    def flip(zone, gx, yz):
        return (1 - zone, gx, yz) if gx == widths - 1 else None

    def along_x(zone, gx, yz):
        return (zone, partner_of(gx, 0), yz)

    def along_x_or_flip(zone, gx, yz):
        if gx == widths - 1:
            return (1 - zone, gx, yz)
        return None if gx == 0 else (zone, partner_of(gx, 1), yz)

    code = band_device[0] * 128 + band_cell[0]
    info = jnp.concatenate(
        [jnp.moveaxis(code.astype(jnp.float32), -1, 0), jnp.moveaxis(band_weight[0], -1, 0)]
    )
    info = send(info, flip)
    first, second = pl.pallas_call(
        pack_kernel,
        out_shape=(tile_shape(10),) * 2,
        in_specs=in_vmem(1),
        out_specs=tuple(in_vmem(2)),
        compiler_params=params,
    )(field)
    vel = pl.pallas_call(
        velocity_kernel,
        out_shape=tile_shape(2, 3, extent_x),
        in_specs=in_any(1),
        out_specs=in_vmem(1)[0],
        scratch_shapes=[
            pltpu.VMEM((2 * extent_x, 27, 16, 128), jnp.float32),
            pltpu.SemaphoreType.DMA((2 * extent_x,)),
        ],
        compiler_params=params,
    )(saved)
    for step in (1, 0):
        last = step == 0
        own = first
        first = send(own, along_z(0))
        second = send(second, along_z(1))
        others = [send(own, hop_z(hop)) for hop in range(2, count - 1)]
        side = pl.pallas_call(
            side_kernel,
            out_shape=tile_shape(11),
            in_specs=in_vmem(3),
            out_specs=in_vmem(1)[0],
            compiler_params=params,
        )(field, first, second)
        side = send(side, along_x)
        cross = pl.pallas_call(
            lambda *refs: cross_kernel(count, *refs),
            out_shape=tile_shape(11),
            in_specs=in_vmem(2 + count),
            out_specs=in_vmem(1)[0],
            compiler_params=params,
        )(field, own, first, second, *others, info)
        cross = send(cross, along_x_or_flip)
        columns = () if last else (tile_shape(),) * 2
        inner = pl.pallas_call(
            lambda *refs, step=step, last=last: inner_kernel(step, last, *refs),
            out_shape=(tile_shape(27, extent_x), *columns),
            in_specs=in_vmem(5),
            out_specs=tuple(in_any(1) + in_vmem(len(columns))),
            scratch_shapes=[
                pltpu.VMEM((extent_x - 2, 27, 16, 128), jnp.float32),
                pltpu.VMEM((27, 16, 128), jnp.float32),
                pltpu.SemaphoreType.DMA((extent_x - 2,)),
            ],
            compiler_params=params,
        )(field, vel, solid, first, second)
        messages = () if last else (tile_shape(10),) * 2
        outer = pl.pallas_call(
            lambda *refs, step=step, last=last: outer_kernel(step, last, *refs),
            out_shape=(tile_shape(27, extent_x), *messages),
            in_specs=in_vmem(7) + in_any(1) + in_vmem(len(columns)),
            out_specs=tuple(in_any(1) + in_vmem(len(messages))),
            scratch_shapes=[
                pltpu.VMEM((2, 27, 16, 128), jnp.float32),
                pltpu.VMEM((27, 16, 128), jnp.float32),
                pltpu.SemaphoreType.DMA((2,)),
            ],
            input_output_aliases={7: 0},
            compiler_params=params,
        )(field, vel, solid, first, second, side, cross, *inner)
        if last:
            field = outer[0]
        else:
            field, first, second = outer
    return field[None]


def solution(mesh):
    sizes = tuple(mesh.shape[axis] for axis in ("zone", "gx", "yz"))
    in_specs = (
        P("zone", None, "gx", None, "yz"),
        P(None, "zone", None, "gx", None, "yz"),
        P("zone", "gx", None, "yz"),
        P("zone", None, "yz", None),
        P("zone", None, "yz", None),
        P("zone", None, "yz", None),
    )
    out_specs = P("zone", None, "gx", None, "yz")
    return jax.shard_map(
        lambda *args: body(sizes, *args),
        mesh=mesh,
        in_specs=in_specs,
        out_specs=out_specs,
        check_vma=False,
    )
```

time: 60.8 us -> 40.4 us (0.66)
  the two profiles are of different devices: /device:TPU:7 before, /device:TPU:4 now
where the time goes in v3:
time: 40.4 us; the launch traced here: 40.1 us
  starting transfers between devices  19.3 us (48%)
  waiting for transfers between devices  11.2 us (28%)
  Pallas kernels  7.89 us (20%)
  local copies, waits for them, and re-layouts  1.51 us (4%)
    ppermute x11, starting transfers between devices, send(): return lax.ppermute(values, axes, pairs)  19.3 us
    ppermute x11, waiting for transfers between devices, send(): return lax.ppermute(values, axes, pairs)  11.2 us
    pallas_call x2, Pallas kernels, body(): pl.pallas_call(lambda *refs, step=step, last=last: inner_kernel(step, las...  3.99 us
    pallas_call x2, Pallas kernels, body(): pl.pallas_call(lambda *refs, step=step, last=last: outer_kernel(step, las...  1.63 us
    unnamed x15, local copies, waits for them, and re-layouts  1.51 us
    pallas_call x1, Pallas kernels, body(): pl.pallas_call(velocity_kernel, out_shape=tile_shape(2, 3, extent_x), in_...  1.32 us
    pallas_call x1, Pallas kernels, body(): pl.pallas_call(pack_kernel, out_shape=(tile_shape(10),) * 2, in_specs=in_...  0.86 us
  transfers between devices with their start and end apart: 11, of which 5 were waited for; matrix products, arithmetic and copies ran while one was open for 0% of the time, Pallas kernels for 13%

profile of v3, /device:TPU:4, one launch (start us, length us, event | category | flops | bytes accessed | tf_op | source)
XLA Modules:
  0.0 40.1 jit_solution(11034066481168354955)
XLA Ops:
  0.0 1.5 %copy-done = f32[1,27,8,16,128]{4,3,2,1,0:T(8,128)S(1)} copy-done((f32[1,27,8,16,128]{4,3,2,1,0:T(8,128)S(1)}, f32[1,27,8,16,128]{4,3,2,1,0:T(8,128)}, u32[]{:S(2)}) %copy-start) | copy-done | bytes 1769496
  1.5 0.9 %shard_map.65 = (f32[10,16,128]{2,1,0:T(8,128)S(1)}, f32[10,16,128]{2,1,0:T(8,128)S(1)}) custom-call(f32[27,8,16,128]{3,2,1,0:T(8,128)S(1)} %bitcast.11), custom_call_target="tpu_custom_call" | custom-call | tf_op jit(solution)/shard_map/pallas_call | solution.py:399
  2.4 0.7 %collective-permute-start.3 = (f32[10,16,128]{2,1,0:T(8,128)S(1)}, f32[10,16,128]{2,1,0:T(8,128)S(1)}, u32[]{:S(2)}, u32[]{:S(2)}) collective-permute-start(f32[10,16,128]{2,1,0:T(8,128)S(1)} %get-tuple-element.13.refs_1_), channel_id=1, source_target_pairs={{12,14},{13,15},{14,12},{15,13},{28,30},{29,31},{30,28},{31,29}} | collective-permute-start | bytes 245768 | tf_op jit(solution)/shard_map/ppermute | solution.py:372
  3.0 1.6 %collective-permute-start = (f32[10,16,128]{2,1,0:T(8,128)S(1)}, f32[10,16,128]{2,1,0:T(8,128)S(1)}, u32[]{:S(2)}, u32[]{:S(2)}) collective-permute-start(f32[10,16,128]{2,1,0:T(8,128)S(1)} %get-tuple-element.13.refs_1_), channel_id=1, source_target_pairs={{0,1},{1,0},{2,3},{3,2},{4,5},{5,4},{6,7},{7,6},{8,9},{9,8},{10,11... | collective-permute-start | bytes 245768 | tf_op jit(solution)/shard_map/ppermute | solution.py:372
  4.7 2.5 %collective-permute-start.1 = (f32[10,16,128]{2,1,0:T(8,128)S(1)}, f32[10,16,128]{2,1,0:T(8,128)S(1)}, u32[]{:S(2)}, u32[]{:S(2)}) collective-permute-start(f32[10,16,128]{2,1,0:T(8,128)S(1)} %get-tuple-element.14), channel_id=1, source_target_pairs={{0,3},{1,2},{2,1},{3,0},{4,7},{5,6},{6,5},{7,4},{8,11},{9,10},{10,... | collective-permute-start | bytes 245768 | tf_op jit(solution)/shard_map/ppermute | solution.py:372
  7.2 0.0 copy-start.2
  7.2 0.8 %collective-permute-start.4 = (f32[4,16,128]{2,1,0:T(8,128)S(1)}, f32[4,16,128]{2,1,0:T(8,128)S(1)}, u32[]{:S(2)}, u32[]{:S(2)}) collective-permute-start(f32[4,16,128]{2,1,0:T(8,128)S(1)} %pad_maximum_fusion), channel_id=1, source_target_pairs={{12,28},{13,29},{14,30},{15,31},{28,12},{29,13},{30,14},{31,15}} | collective-permute-start | bytes 98312 | tf_op jit(solution)/shard_map/ppermute | solution.py:372
  8.0 3.3 %collective-permute-done.1.second.refs_3_.refs_4_ = f32[10,16,128]{2,1,0:T(8,128)S(1)} collective-permute-done((f32[10,16,128]{2,1,0:T(8,128)S(1)}, f32[10,16,128]{2,1,0:T(8,128)S(1)}, u32[]{:S(2)}, u32[]{:S(2)}) %collective-permute-start.1) | collective-permute-done | bytes 81952 | tf_op jit(solution)/shard_map/ppermute | solution.py:372
  11.3 5.0 %collective-permute-start.2 = (f32[11,16,128]{2,1,0:T(8,128)S(1)}, f32[11,16,128]{2,1,0:T(8,128)S(1)}, u32[]{:S(2)}, u32[]{:S(2)}) collective-permute-start(f32[11,16,128]{2,1,0:T(8,128)S(1)} %shard_map.66), channel_id=1, source_target_pairs={{0,4},{1,5},{2,6},{3,7},{4,0},{5,1},{6,2},{7,3},{8,12},{9,13},{10,... | collective-permute-start | bytes 270344 | tf_op jit(solution)/shard_map/ppermute | solution.py:372
  16.4 2.1 %collective-permute-start.5 = (f32[11,16,128]{2,1,0:T(8,128)S(1)}, f32[11,16,128]{2,1,0:T(8,128)S(1)}, u32[]{:S(2)}, u32[]{:S(2)}) collective-permute-start(f32[11,16,128]{2,1,0:T(8,128)S(1)} %shard_map.67), channel_id=1, source_target_pairs={{4,8},{5,9},{6,10},{7,11},{8,4},{9,5},{10,6},{11,7},{12,28},{13,29... | collective-permute-start | bytes 270344 | tf_op jit(solution)/shard_map/ppermute | solution.py:372
  18.5 1.3 %shard_map.64.refs_1_ = f32[2,3,8,16,128]{4,3,2,1,0:T(8,128)S(1)} custom-call(f32[2,1,27,8,16,128]{5,4,3,2,1,0:T(8,128)S(1)} %copy-done.2), custom_call_target="tpu_custom_call" | custom-call | tf_op jit(solution)/shard_map/pallas_call | solution.py:406
  19.8 2.1 %shard_map.68 = (f32[27,8,16,128]{3,2,1,0:T(8,128)S(1)}, f32[16,128]{1,0:T(8,128)S(1)}, f32[16,128]{1,0:T(8,128)S(1)}) custom-call(f32[27,8,16,128]{3,2,1,0:T(8,128)S(1)} %bitcast.14, f32[2,3,8,16,128]{4,3,2,1,0:T(8,128)S(1)} %shard_map.64.refs_1_, s32[1,8,16,128]{3,2,1,0:T(8,128)S(1)} %copy-done.3, ...), custom_call_target="tpu_custom_call" | custom-call | tf_op jit(solution)/shard_map/pallas_call | solution.py:440
  21.9 1.9 %collective-permute-done.5.refs_6_ = f32[11,16,128]{2,1,0:T(8,128)S(1)} collective-permute-done((f32[11,16,128]{2,1,0:T(8,128)S(1)}, f32[11,16,128]{2,1,0:T(8,128)S(1)}, u32[]{:S(2)}, u32[]{:S(2)}) %collective-permute-start.5) | collective-permute-done | bytes 90144 | tf_op jit(solution)/shard_map/ppermute | solution.py:372
  23.8 0.6 %shard_map.69 = (f32[27,8,16,128]{3,2,1,0:T(8,128)S(1)}, f32[10,16,128]{2,1,0:T(8,128)S(1)}, f32[10,16,128]{2,1,0:T(8,128)S(1)}) custom-call(f32[27,8,16,128]{3,2,1,0:T(8,128)S(1)} %bitcast.15, f32[2,3,8,16,128]{4,3,2,1,0:T(8,128)S(1)} %shard_map.64.refs_1_, s32[1,8,16,128]{3,2,1,0:T(8,128)S(1)} %copy-done.3, ...), custom_call_target="tpu_custom_call", output_to_operand_aliasing={{0}: (7, {})} | custom-call | tf_op jit(solution)/shard_map/pallas_call | solution.py:453
  24.5 2.0 %collective-permute-start.7 = (f32[10,16,128]{2,1,0:T(8,128)S(1)}, f32[10,16,128]{2,1,0:T(8,128)S(1)}, u32[]{:S(2)}, u32[]{:S(2)}) collective-permute-start(f32[10,16,128]{2,1,0:T(8,128)S(1)} %get-tuple-element.20), channel_id=1, source_target_pairs={{0,3},{1,2},{2,1},{3,0},{4,7},{5,6},{6,5},{7,4},{8,11},{9,10},{10,... | collective-permute-start | bytes 245768 | tf_op jit(solution)/shard_map/ppermute | solution.py:372
  26.4 1.1 %collective-permute-start.6 = (f32[10,16,128]{2,1,0:T(8,128)S(1)}, f32[10,16,128]{2,1,0:T(8,128)S(1)}, u32[]{:S(2)}, u32[]{:S(2)}) collective-permute-start(f32[10,16,128]{2,1,0:T(8,128)S(1)} %get-tuple-element.19.refs_1_), channel_id=1, source_target_pairs={{0,1},{1,0},{2,3},{3,2},{4,5},{5,4},{6,7},{7,6},{8,9},{9,8},{10,11... | collective-permute-start | bytes 245768 | tf_op jit(solution)/shard_map/ppermute | solution.py:372
  27.5 0.7 %collective-permute-start.9 = (f32[10,16,128]{2,1,0:T(8,128)S(1)}, f32[10,16,128]{2,1,0:T(8,128)S(1)}, u32[]{:S(2)}, u32[]{:S(2)}) collective-permute-start(f32[10,16,128]{2,1,0:T(8,128)S(1)} %get-tuple-element.19.refs_1_), channel_id=1, source_target_pairs={{12,14},{13,15},{14,12},{15,13},{28,30},{29,31},{30,28},{31,29}} | collective-permute-start | bytes 245768 | tf_op jit(solution)/shard_map/ppermute | solution.py:372
  28.2 2.6 %collective-permute-done.7.second.refs_3_.refs_4_ = f32[10,16,128]{2,1,0:T(8,128)S(1)} collective-permute-done((f32[10,16,128]{2,1,0:T(8,128)S(1)}, f32[10,16,128]{2,1,0:T(8,128)S(1)}, u32[]{:S(2)}, u32[]{:S(2)}) %collective-permute-start.7) | collective-permute-done | bytes 81952 | tf_op jit(solution)/shard_map/ppermute | solution.py:372
  30.8 0.8 %collective-permute-done.6.first.refs_2_.refs_3_ = f32[10,16,128]{2,1,0:T(8,128)S(1)} collective-permute-done((f32[10,16,128]{2,1,0:T(8,128)S(1)}, f32[10,16,128]{2,1,0:T(8,128)S(1)}, u32[]{:S(2)}, u32[]{:S(2)}) %collective-permute-start.6) | collective-permute-done | bytes 81952 | tf_op jit(solution)/shard_map/ppermute | solution.py:372
  31.7 0.1 collective-permute-start.8
  31.8 2.9 %collective-permute-start.10 = (f32[11,16,128]{2,1,0:T(8,128)S(1)}, f32[11,16,128]{2,1,0:T(8,128)S(1)}, u32[]{:S(2)}, u32[]{:S(2)}) collective-permute-start(f32[11,16,128]{2,1,0:T(8,128)S(1)} %shard_map.71), channel_id=1, source_target_pairs={{4,8},{5,9},{6,10},{7,11},{8,4},{9,5},{10,6},{11,7},{12,28},{13,29... | collective-permute-start | bytes 270344 | tf_op jit(solution)/shard_map/ppermute | solution.py:372
  34.7 1.9 %shard_map.72.refs_7_ = f32[27,8,16,128]{3,2,1,0:T(8,128)} custom-call(f32[27,8,16,128]{3,2,1,0:T(8,128)S(1)} %get-tuple-element.18.adj.refs_0_, f32[2,3,8,16,128]{4,3,2,1,0:T(8,128)S(1)} %shard_map.64.refs_1_, s32[1,8,16,128]{3,2,1,0:T(8,128)S(1)} %copy-done.3, f32[10,16,128]{2,1,0:T(8,128)S(1)} %collective-permute-done.6.first.refs_2_.refs_3_, ...), custom_call_target="tpu_custom_call" | custom-call | tf_op jit(solution)/shard_map/pallas_call | solution.py:440
  36.6 2.5 %collective-permute-done.10.refs_6_ = f32[11,16,128]{2,1,0:T(8,128)S(1)} collective-permute-done((f32[11,16,128]{2,1,0:T(8,128)S(1)}, f32[11,16,128]{2,1,0:T(8,128)S(1)}, u32[]{:S(2)}, u32[]{:S(2)}) %collective-permute-start.10) | collective-permute-done | bytes 90144 | tf_op jit(solution)/shard_map/ppermute | solution.py:372
  39.1 1.0 %shard_map.73 = f32[27,8,16,128]{3,2,1,0:T(8,128)} custom-call(f32[27,8,16,128]{3,2,1,0:T(8,128)S(1)} %get-tuple-element.18.adj.refs_0_, f32[2,3,8,16,128]{4,3,2,1,0:T(8,128)S(1)} %shard_map.64.refs_1_, s32[1,8,16,128]{3,2,1,0:T(8,128)S(1)} %copy-done.3, ...), custom_call_target="tpu_custom_call", output_to_operand_aliasing={{}: (7, {})} | custom-call | tf_op jit(solution)/shard_map/pallas_call | solution.py:453
  (25 shorter events, 0.1 us)
Async XLA Ops:
  0.0 1.5 %copy-start = (f32[1,27,8,16,128]{4,3,2,1,0:T(8,128)S(1)}, f32[1,27,8,16,128]{4,3,2,1,0:T(8,128)}, u32[]{:S(2)}) copy-start(f32[1,27,8,16,128]{4,3,2,1,0:T(8,128)} %param.6) | copy-start | bytes 5308420
  1.5 5.7 %copy-start.6 = (f32[1,16,128,2]{2,3,1,0:T(2,128)S(1)}, f32[1,16,128,2]{2,3,1,0:T(2,128)}, u32[]{:S(2)}) copy-start(f32[1,16,128,2]{2,3,1,0:T(2,128)} %param.11) | copy-start | bytes 49156
  1.5 5.7 %copy-start.4 = (s32[1,16,128,2]{2,3,1,0:T(2,128)S(1)}, s32[1,16,128,2]{2,3,1,0:T(2,128)}, u32[]{:S(2)}) copy-start(s32[1,16,128,2]{2,3,1,0:T(2,128)} %param.10) | copy-start | bytes 49156
  1.5 5.7 %copy-start.5 = (s32[1,16,128,2]{2,3,1,0:T(2,128)S(1)}, s32[1,16,128,2]{2,3,1,0:T(2,128)}, u32[]{:S(2)}) copy-start(s32[1,16,128,2]{2,3,1,0:T(2,128)} %param.9) | copy-start | bytes 49156
  2.4 14.0 %collective-permute-start.3 = (f32[10,16,128]{2,1,0:T(8,128)S(1)}, f32[10,16,128]{2,1,0:T(8,128)S(1)}, u32[]{:S(2)}, u32[]{:S(2)}) collective-permute-start(f32[10,16,128]{2,1,0:T(8,128)S(1)} %get-tuple-element.13.refs_1_), channel_id=1, source_target_pairs={{12,14},{13,15},{14,12},{15,13},{28,30},{29,31},{30,28},{31,29}} | collective-permute-start | bytes 245768 | tf_op jit(solution)/shard_map/ppermute | solution.py:372
  3.0 8.3 %collective-permute-start = (f32[10,16,128]{2,1,0:T(8,128)S(1)}, f32[10,16,128]{2,1,0:T(8,128)S(1)}, u32[]{:S(2)}, u32[]{:S(2)}) collective-permute-start(f32[10,16,128]{2,1,0:T(8,128)S(1)} %get-tuple-element.13.refs_1_), channel_id=1, source_target_pairs={{0,1},{1,0},{2,3},{3,2},{4,5},{5,4},{6,7},{7,6},{8,9},{9,8},{10,11... | collective-permute-start | bytes 245768 | tf_op jit(solution)/shard_map/ppermute | solution.py:372
  4.7 6.6 %collective-permute-start.1 = (f32[10,16,128]{2,1,0:T(8,128)S(1)}, f32[10,16,128]{2,1,0:T(8,128)S(1)}, u32[]{:S(2)}, u32[]{:S(2)}) collective-permute-start(f32[10,16,128]{2,1,0:T(8,128)S(1)} %get-tuple-element.14), channel_id=1, source_target_pairs={{0,3},{1,2},{2,1},{3,0},{4,7},{5,6},{6,5},{7,4},{8,11},{9,10},{10,... | collective-permute-start | bytes 245768 | tf_op jit(solution)/shard_map/ppermute | solution.py:372
  7.2 11.3 %copy-start.2 = (f32[2,1,27,8,16,128]{5,4,3,2,1,0:T(8,128)S(1)}, f32[2,1,27,8,16,128]{5,4,3,2,1,0:T(8,128)}, u32[]{:S(2)}) copy-start(f32[2,1,27,8,16,128]{5,4,3,2,1,0:T(8,128)} %saved.1) | copy-start | bytes 10616836
  7.2 9.1 %collective-permute-start.4 = (f32[4,16,128]{2,1,0:T(8,128)S(1)}, f32[4,16,128]{2,1,0:T(8,128)S(1)}, u32[]{:S(2)}, u32[]{:S(2)}) collective-permute-start(f32[4,16,128]{2,1,0:T(8,128)S(1)} %pad_maximum_fusion), channel_id=1, source_target_pairs={{12,28},{13,29},{14,30},{15,31},{28,12},{29,13},{30,14},{31,15}} | collective-permute-start | bytes 98312 | tf_op jit(solution)/shard_map/ppermute | solution.py:372
  11.3 10.5 %collective-permute-start.2 = (f32[11,16,128]{2,1,0:T(8,128)S(1)}, f32[11,16,128]{2,1,0:T(8,128)S(1)}, u32[]{:S(2)}, u32[]{:S(2)}) collective-permute-start(f32[11,16,128]{2,1,0:T(8,128)S(1)} %shard_map.66), channel_id=1, source_target_pairs={{0,4},{1,5},{2,6},{3,7},{4,0},{5,1},{6,2},{7,3},{8,12},{9,13},{10,... | collective-permute-start | bytes 270344 | tf_op jit(solution)/shard_map/ppermute | solution.py:372
  16.4 3.4 %copy-start.1 = (f32[1,27,8,16,128]{4,3,2,1,0:T(8,128)S(1)}, f32[1,27,8,16,128]{4,3,2,1,0:T(8,128)}, u32[]{:S(2)}) copy-start(f32[1,27,8,16,128]{4,3,2,1,0:T(8,128)} %param.6) | copy-start | bytes 5308420
  16.4 3.4 %copy-start.3 = (s32[1,8,16,128]{3,2,1,0:T(8,128)S(1)}, s32[1,8,16,128]{3,2,1,0:T(8,128)}, u32[]{:S(2)}) copy-start(s32[1,8,16,128]{3,2,1,0:T(8,128)} %refs_2_.7) | copy-start | bytes 196612
  16.4 7.5 %collective-permute-start.5 = (f32[11,16,128]{2,1,0:T(8,128)S(1)}, f32[11,16,128]{2,1,0:T(8,128)S(1)}, u32[]{:S(2)}, u32[]{:S(2)}) collective-permute-start(f32[11,16,128]{2,1,0:T(8,128)S(1)} %shard_map.67), channel_id=1, source_target_pairs={{4,8},{5,9},{6,10},{7,11},{8,4},{9,5},{10,6},{11,7},{12,28},{13,29... | collective-permute-start | bytes 270344 | tf_op jit(solution)/shard_map/ppermute | solution.py:372
  24.5 6.4 %collective-permute-start.7 = (f32[10,16,128]{2,1,0:T(8,128)S(1)}, f32[10,16,128]{2,1,0:T(8,128)S(1)}, u32[]{:S(2)}, u32[]{:S(2)}) collective-permute-start(f32[10,16,128]{2,1,0:T(8,128)S(1)} %get-tuple-element.20), channel_id=1, source_target_pairs={{0,3},{1,2},{2,1},{3,0},{4,7},{5,6},{6,5},{7,4},{8,11},{9,10},{10,... | collective-permute-start | bytes 245768 | tf_op jit(solution)/shard_map/ppermute | solution.py:372
  26.4 5.2 %collective-permute-start.6 = (f32[10,16,128]{2,1,0:T(8,128)S(1)}, f32[10,16,128]{2,1,0:T(8,128)S(1)}, u32[]{:S(2)}, u32[]{:S(2)}) collective-permute-start(f32[10,16,128]{2,1,0:T(8,128)S(1)} %get-tuple-element.19.refs_1_), channel_id=1, source_target_pairs={{0,1},{1,0},{2,3},{3,2},{4,5},{5,4},{6,7},{7,6},{8,9},{9,8},{10,11... | collective-permute-start | bytes 245768 | tf_op jit(solution)/shard_map/ppermute | solution.py:372
  27.5 4.2 %collective-permute-start.9 = (f32[10,16,128]{2,1,0:T(8,128)S(1)}, f32[10,16,128]{2,1,0:T(8,128)S(1)}, u32[]{:S(2)}, u32[]{:S(2)}) collective-permute-start(f32[10,16,128]{2,1,0:T(8,128)S(1)} %get-tuple-element.19.refs_1_), channel_id=1, source_target_pairs={{12,14},{13,15},{14,12},{15,13},{28,30},{29,31},{30,28},{31,29}} | collective-permute-start | bytes 245768 | tf_op jit(solution)/shard_map/ppermute | solution.py:372
  31.7 5.0 %collective-permute-start.8 = (f32[11,16,128]{2,1,0:T(8,128)S(1)}, f32[11,16,128]{2,1,0:T(8,128)S(1)}, u32[]{:S(2)}, u32[]{:S(2)}) collective-permute-start(f32[11,16,128]{2,1,0:T(8,128)S(1)} %shard_map.70), channel_id=1, source_target_pairs={{0,4},{1,5},{2,6},{3,7},{4,0},{5,1},{6,2},{7,3},{8,12},{9,13},{10,... | collective-permute-start | bytes 270344 | tf_op jit(solution)/shard_map/ppermute | solution.py:372
  31.8 7.3 %collective-permute-start.10 = (f32[11,16,128]{2,1,0:T(8,128)S(1)}, f32[11,16,128]{2,1,0:T(8,128)S(1)}, u32[]{:S(2)}, u32[]{:S(2)}) collective-permute-start(f32[11,16,128]{2,1,0:T(8,128)S(1)} %shard_map.71), channel_id=1, source_target_pairs={{4,8},{5,9},{6,10},{7,11},{8,4},{9,5},{10,6},{11,7},{12,28},{13,29... | collective-permute-start | bytes 270344 | tf_op jit(solution)/shard_map/ppermute | solution.py:372

commit v4 on v3

--- a/solution.py
+++ b/solution.py
@@ -42,31 +42,32 @@
     return lax.rem(lax.axis_index(axis), 2) == 0
 
 
-def write_messages(top, low, high, first, second):
+def write_edges(low, high, first, second):
     even = is_even("yz")
-    for j in range(9):
-        tile = top(j)
-        first[j] = tile
-        second[j] = tile
-    first[9] = jnp.where(even, high, low)
-    second[9] = jnp.where(even, low, high)
+    first[...] = jnp.where(even, high, low)
+    second[...] = jnp.where(even, low, high)
 
 
 def edges_from(first, second):
     even = is_even("yz")
     me, count = lax.axis_index("yz"), lax.axis_size("yz")
-    low = jnp.where(me == 0, 0.0, jnp.where(even, second[9], first[9]))
-    high = jnp.where(me == count - 1, 0.0, jnp.where(even, first[9], second[9]))
+    low = jnp.where(me == 0, 0.0, jnp.where(even, second[...], first[...]))
+    high = jnp.where(me == count - 1, 0.0, jnp.where(even, first[...], second[...]))
     return low, high
 
 
+def top_kernel(adj, out, sem):
+    copy = pltpu.make_async_copy(adj.at[pl.ds(0, 9), adj.shape[1] - 1], out, sem)
+    copy.start()
+    copy.wait()
+
+
 def pack_kernel(adj, first_out, second_out):
-    extent_x = adj.shape[1]
     zero = jnp.zeros((16, 128), jnp.float32)
     low, high = lax.fori_loop(
-        0, extent_x, lambda x, c: pack_columns(lambda i: adj[i, x], x, *c), (zero, zero)
-    )
-    write_messages(lambda j: adj[j, extent_x - 1], low, high, first_out, second_out)
+        0, adj.shape[1], lambda x, c: pack_columns(lambda i: adj[i, x], x, *c), (zero, zero)
+    )
+    write_edges(low, high, first_out, second_out)
 
 
 def velocity_kernel(saved, out, kept, sems):
@@ -97,12 +98,12 @@
 
 
 def cross_kernel(count, *refs):
-    adj, own, first, second = refs[:4]
-    others = refs[4 : 4 + count - 3]
-    info, out = refs[4 + count - 3 :]
+    adj, low_side, high_side, own = refs[:4]
+    blocks = refs[3 : 3 + count]
+    info, _, out = refs[3 + count :]
     extent_x = adj.shape[1]
     interface = lax.axis_index("gx") == lax.axis_size("gx") - 1
-    out[9], out[10] = edges_from(first, second)
+    out[9], out[10] = edges_from(low_side, high_side)
 
     @pl.when(jnp.logical_not(interface))
     def _():
@@ -130,7 +131,7 @@
             for r in rows:
                 total = jnp.zeros((8, 128), jnp.float32)
                 for k in range(2):
-                    tiles = [ref[j, r : r + 8] for ref in (own, first, second, *others)]
+                    tiles = [ref[j, r : r + 8] for ref in blocks]
                     got = [jnp.take_along_axis(tile, spots[r, k], axis=1) for tile in tiles]
                     picked = got[0]
                     for mask, value in zip(picks[r, k], got[1:]):
@@ -248,7 +249,7 @@
                 pulled[i] = shift_y(tile, cy)
 
 
-def inner_kernel(step, last, adj, vel, solid, first, second, *rest):
+def inner_kernel(step, last, adj, vel, solid, first, second, _, *rest):
     if last:
         out, made, pulled, sems = rest
     else:
@@ -283,60 +284,60 @@
     lax.fori_loop(1, extent_x - 1, lambda x, c: (save(x).wait(), c)[1], 0)
 
 
-def outer_kernel(step, last, adj, vel, solid, first, second, side, cross, *rest):
-    if last:
-        _, out, made, pulled, sems = rest
+def outer_plane(n, x, step, adj, vel, solid, edges, side, cross, out, made, pulled, sems):
+    extent_x = adj.shape[1]
+    even = is_even("gx")
+    if x == 0:
+        ghost, start, raw = -1, extent_x * 9, None
+        beyond = lambda j: jnp.where(even, cross[j], side[j])
     else:
-        _, low_in, high_in, out, first_out, second_out, made, pulled, sems = rest
-    extent_x = adj.shape[1]
-    low_edge, high_edge = edges_from(first, second)
-    even = is_even("gx")
-    interface = lax.axis_index("gx") == lax.axis_size("gx") - 1
-    below = lambda j: jnp.where(even, cross[j], side[j])
-    above = lambda j: jnp.where(even, side[j], cross[j])
-
-    def plane(n, x, tile_of, edges_of, raw):
-        pull_plane(tile_of, edges_of, pulled, raw)
-
-        def store(i, tile):
-            made[n, i] = tile
-
-        velocity = [vel[step, a, x] for a in range(3)]
-        collide(lambda i: pulled[i], velocity, solid[0, x], store)
-        save = pltpu.make_async_copy(made.at[n], out.at[:, x], sems.at[n])
-        save.start()
-        return save
-
-    final = extent_x - 1
+        ghost, start = 1, 9
+        raw = lax.axis_index("gx") == lax.axis_size("gx") - 1
+        beyond = lambda j: jnp.where(even, side[j], cross[j])
+    pull_plane(
+        lambda i, cx: beyond(i % 9) if cx == ghost else adj[i, x + cx],
+        lambda cx: (beyond(9), beyond(10), start) if cx == ghost else (*edges, (x + 1 + cx) * 9),
+        pulled,
+        raw,
+    )
+
+    def store(i, tile):
+        made[n, i] = tile
+
+    velocity = [vel[step, a, x] for a in range(3)]
+    collide(lambda i: pulled[i], velocity, solid[0, x], store)
+    save = pltpu.make_async_copy(made.at[n], out.at[:, x], sems.at[n])
+    save.start()
+    return save
+
+
+def top_plane_kernel(step, adj, vel, solid, first, second, side, cross, low_in, high_in, _, *rest):
+    out, top_out, low_out, high_out, made, pulled, sems = rest
+    final = adj.shape[1] - 1
+    edges = edges_from(first, second)
+    save = outer_plane(0, final, step, adj, vel, solid, edges, side, cross, out, made, pulled, sems)
+    for j in range(9):
+        top_out[j] = made[0, j]
+    low_out[...], high_out[...] = pack_columns(lambda i: made[0, i], final, low_in[...], high_in[...])
+    save.wait()
+
+
+def bottom_plane_kernel(step, adj, vel, solid, first, second, side, cross, low_in, high_in, _, *rest):
+    out, first_out, second_out, made, pulled, sems = rest
+    edges = edges_from(first, second)
+    save = outer_plane(0, 0, step, adj, vel, solid, edges, side, cross, out, made, pulled, sems)
+    low, high = pack_columns(lambda i: made[0, i], 0, low_in[...], high_in[...])
+    write_edges(low, high, first_out, second_out)
+    save.wait()
+
+
+def last_planes_kernel(step, adj, vel, solid, first, second, side, cross, _, *rest):
+    out, made, pulled, sems = rest
+    edges = edges_from(first, second)
     saves = [
-        plane(
-            0,
-            0,
-            lambda i, cx: below(i) if cx == -1 else adj[i, cx],
-            lambda cx: (
-                (below(9), below(10), extent_x * 9)
-                if cx == -1
-                else (low_edge, high_edge, (1 + cx) * 9)
-            ),
-            None,
-        ),
-        plane(
-            1,
-            final,
-            lambda i, cx: above(i - 18) if cx == 1 else adj[i, final + cx],
-            lambda cx: (
-                (above(9), above(10), 9)
-                if cx == 1
-                else (low_edge, high_edge, (final + 1 + cx) * 9)
-            ),
-            interface,
-        ),
+        outer_plane(n, x, step, adj, vel, solid, edges, side, cross, out, made, pulled, sems)
+        for n, x in enumerate((0, adj.shape[1] - 1))
     ]
-    if not last:
-        low, high = low_in[...], high_in[...]
-        low, high = pack_columns(lambda i: made[0, i], 0, low, high)
-        low, high = pack_columns(lambda i: made[1, i], final, low, high)
-        write_messages(lambda j: made[1, j], low, high, first_out, second_out)
     for save in saves:
         save.wait()
 
@@ -377,11 +378,14 @@
     def along_z(shift):
         return lambda zone, gx, yz: (zone, gx, partner_of(yz, shift) % count)
 
+    def at_interface(target):
+        return lambda zone, gx, yz: target(zone, gx, yz) if gx == widths - 1 else None
+
     def hop_z(hop):
-        return lambda zone, gx, yz: (zone, gx, (yz + hop) % count) if gx == widths - 1 else None
+        return lambda zone, gx, yz: (zone, gx, (yz + hop) % count)
 
     def flip(zone, gx, yz):
-        return (1 - zone, gx, yz) if gx == widths - 1 else None
+        return (1 - zone, gx, yz)
 
     def along_x(zone, gx, yz):
         return (zone, partner_of(gx, 0), yz)
@@ -395,10 +399,18 @@
     info = jnp.concatenate(
         [jnp.moveaxis(code.astype(jnp.float32), -1, 0), jnp.moveaxis(band_weight[0], -1, 0)]
     )
-    info = send(info, flip)
+    info = send(info, at_interface(flip))
+    top = pl.pallas_call(
+        top_kernel,
+        out_shape=tile_shape(9),
+        in_specs=[pl.BlockSpec(memory_space=pltpu.HBM)],
+        out_specs=in_vmem(1)[0],
+        scratch_shapes=[pltpu.SemaphoreType.DMA(())],
+        compiler_params=params,
+    )(field)
     first, second = pl.pallas_call(
         pack_kernel,
-        out_shape=(tile_shape(10),) * 2,
+        out_shape=(tile_shape(),) * 2,
         in_specs=in_vmem(1),
         out_specs=tuple(in_vmem(2)),
         compiler_params=params,
@@ -416,57 +428,71 @@
     )(saved)
     for step in (1, 0):
         last = step == 0
-        own = first
-        first = send(own, along_z(0))
+        blocks = [send(top, at_interface(hop_z(hop))) for hop in range(2, count - 1)]
+        blocks = [send(top, at_interface(along_z(shift))) for shift in (0, 1)] + blocks
+        first = send(first, along_z(0))
         second = send(second, along_z(1))
-        others = [send(own, hop_z(hop)) for hop in range(2, count - 1)]
-        side = pl.pallas_call(
+        side_out = pl.pallas_call(
             side_kernel,
             out_shape=tile_shape(11),
             in_specs=in_vmem(3),
             out_specs=in_vmem(1)[0],
             compiler_params=params,
         )(field, first, second)
-        side = send(side, along_x)
-        cross = pl.pallas_call(
-            lambda *refs: cross_kernel(count, *refs),
-            out_shape=tile_shape(11),
-            in_specs=in_vmem(2 + count),
-            out_specs=in_vmem(1)[0],
-            compiler_params=params,
-        )(field, own, first, second, *others, info)
-        cross = send(cross, along_x_or_flip)
-        columns = () if last else (tile_shape(),) * 2
-        inner = pl.pallas_call(
-            lambda *refs, step=step, last=last: inner_kernel(step, last, *refs),
-            out_shape=(tile_shape(27, extent_x), *columns),
-            in_specs=in_vmem(5),
-            out_specs=tuple(in_any(1) + in_vmem(len(columns))),
-            scratch_shapes=[
-                pltpu.VMEM((extent_x - 2, 27, 16, 128), jnp.float32),
-                pltpu.VMEM((27, 16, 128), jnp.float32),
-                pltpu.SemaphoreType.DMA((extent_x - 2,)),
-            ],
-            compiler_params=params,
-        )(field, vel, solid, first, second)
-        messages = () if last else (tile_shape(10),) * 2
-        outer = pl.pallas_call(
-            lambda *refs, step=step, last=last: outer_kernel(step, last, *refs),
-            out_shape=(tile_shape(27, extent_x), *messages),
-            in_specs=in_vmem(7) + in_any(1) + in_vmem(len(columns)),
-            out_specs=tuple(in_any(1) + in_vmem(len(messages))),
-            scratch_shapes=[
-                pltpu.VMEM((2, 27, 16, 128), jnp.float32),
-                pltpu.VMEM((27, 16, 128), jnp.float32),
-                pltpu.SemaphoreType.DMA((2,)),
-            ],
-            input_output_aliases={7: 0},
-            compiler_params=params,
-        )(field, vel, solid, first, second, side, cross, *inner)
+        side = send(side_out, along_x)
+
+        def make_inner(after):
+            columns = () if last else (tile_shape(),) * 2
+            return pl.pallas_call(
+                lambda *refs: inner_kernel(step, last, *refs),
+                out_shape=(tile_shape(27, extent_x), *columns),
+                in_specs=in_vmem(5) + in_any(1),
+                out_specs=tuple(in_any(1) + in_vmem(len(columns))),
+                scratch_shapes=[
+                    pltpu.VMEM((extent_x - 2, 27, 16, 128), jnp.float32),
+                    pltpu.VMEM((27, 16, 128), jnp.float32),
+                    pltpu.SemaphoreType.DMA((extent_x - 2,)),
+                ],
+                compiler_params=params,
+            )(field, vel, solid, first, second, after)
+
+        def make_cross(after):
+            return pl.pallas_call(
+                lambda *refs: cross_kernel(count, *refs),
+                out_shape=tile_shape(11),
+                in_specs=in_vmem(4 + count) + in_any(1),
+                out_specs=in_vmem(1)[0],
+                compiler_params=params,
+            )(field, first, second, top, *blocks, info, after)
+
+        def make_outer(kernel, planes, given, extra):
+            return pl.pallas_call(
+                lambda *refs: kernel(step, *refs),
+                out_shape=(tile_shape(27, extent_x), *extra),
+                in_specs=in_vmem(7 + len(given) - 1) + in_any(1),
+                out_specs=tuple(in_any(1) + in_vmem(len(extra))),
+                scratch_shapes=[
+                    pltpu.VMEM((planes, 27, 16, 128), jnp.float32),
+                    pltpu.VMEM((27, 16, 128), jnp.float32),
+                    pltpu.SemaphoreType.DMA((planes,)),
+                ],
+                input_output_aliases={7 + len(given) - 1: 0},
+                compiler_params=params,
+            )(field, vel, solid, first, second, side, cross, *given)
+
         if last:
-            field = outer[0]
+            cross_out = make_cross(side_out)
+            cross = send(cross_out, along_x_or_flip)
+            (new,) = make_inner(cross_out)
+            (field,) = make_outer(last_planes_kernel, 2, (new,), ())
         else:
-            field, first, second = outer
+            new, low, high = make_inner(side_out)
+            cross = send(make_cross(low), along_x_or_flip)
+            tile = tile_shape()
+            new, top, low, high = make_outer(
+                top_plane_kernel, 1, (low, high, new), (tile_shape(9), tile, tile)
+            )
+            field, first, second = make_outer(bottom_plane_kernel, 1, (low, high, new), (tile, tile))
     return field[None]
 
 

time: 40.4 us -> 58.4 us (1.45)
  starting transfers between devices: 19.3 us -> 32.6 us
  waiting for transfers between devices: 11.2 us -> 14 us
  other arithmetic: 0.01 us -> 0.75 us
  local copies, waits for them, and re-layouts: 1.51 us -> 2.21 us
    ppermute x11 -> x15, starting transfers between devices: 19.3 us -> 32.6 us  [send(): return lax.ppermute(values, axes, pairs)]
    ppermute x11 -> x15, waiting for transfers between devices: 11.2 us -> 14 us  [send(): return lax.ppermute(values, axes, pairs)]
    transpose x1, other arithmetic: 0.01 us -> 0.74 us  [body(): jnp.moveaxis(code.astype(jnp.float32), -1, 0)]
    unnamed x15 -> x9, local copies, waits for them, and re-layouts: 1.51 us -> 2.21 us
    pallas_call x7 -> x9, Pallas kernels: 6.53 us -> 6.64 us  [the longest x2 3.98 us: make_inner(): pl.pallas_call(lambda *refs: inner_kernel(step, last, *refs), out_shape=(...]
  transfers between devices with their start and end apart: 11 -> 15, of which waited for: 5 -> 6; matrix products, arithmetic and copies ran while one was open for 0% -> 3% of each run, Pallas kernels for 13% -> 11%
where the time goes in v4:
time: 58.4 us; the launch traced here: 57.8 us
  starting transfers between devices  32.6 us (56%)
  waiting for transfers between devices  14 us (24%)
  Pallas kernels  7.99 us (14%)
  local copies, waits for them, and re-layouts  2.21 us (4%)
  other arithmetic  0.75 us (1%)
    ppermute x15, starting transfers between devices, send(): return lax.ppermute(values, axes, pairs)  32.6 us
    ppermute x15, waiting for transfers between devices, send(): return lax.ppermute(values, axes, pairs)  14 us
    pallas_call x2, Pallas kernels, make_inner(): pl.pallas_call(lambda *refs: inner_kernel(step, last, *refs), out_shape=(...  3.98 us
    unnamed x9, local copies, waits for them, and re-layouts  2.21 us
    pallas_call x3, Pallas kernels, make_outer(): pl.pallas_call(lambda *refs: kernel(step, *refs), out_shape=(tile_shape(2...  1.72 us
    pallas_call x1, Pallas kernels, body(): pl.pallas_call(velocity_kernel, out_shape=tile_shape(2, 3, extent_x), in_...  1.31 us
  transfers between devices with their start and end apart: 15, of which 6 were waited for; matrix products, arithmetic and copies ran while one was open for 3% of the time, Pallas kernels for 11%

profile of v4, /device:TPU:4, one launch (start us, length us, event | category | flops | bytes accessed | tf_op | source)
XLA Modules:
  0.0 57.8 jit_solution(10309830410639531676)
XLA Ops:
  0.0 1.5 %copy-done = f32[1,27,8,16,128]{4,3,2,1,0:T(8,128)S(1)} copy-done((f32[1,27,8,16,128]{4,3,2,1,0:T(8,128)S(1)}, f32[1,27,8,16,128]{4,3,2,1,0:T(8,128)}, u32[]{:S(2)}) %copy-start) | copy-done | bytes 1769496
  1.5 0.8 %collective-permute-start.5 = (f32[9,16,128]{2,1,0:T(8,128)S(1)}, f32[9,16,128]{2,1,0:T(8,128)S(1)}, u32[]{:S(2)}, u32[]{:S(2)}) collective-permute-start(f32[9,16,128]{2,1,0:T(8,128)S(1)} %shard_map.67.refs_3_), channel_id=1, source_target_pairs={{12,14},{13,15},{14,12},{15,13},{28,30},{29,31},{30,28},{31,29}} | collective-permute-start | bytes 221192 | tf_op jit(solution)/shard_map/ppermute | solution.py:373
  2.3 0.8 %collective-permute-start.4 = (f32[9,16,128]{2,1,0:T(8,128)S(1)}, f32[9,16,128]{2,1,0:T(8,128)S(1)}, u32[]{:S(2)}, u32[]{:S(2)}) collective-permute-start(f32[9,16,128]{2,1,0:T(8,128)S(1)} %shard_map.67.refs_3_), channel_id=1, source_target_pairs={{12,15},{13,14},{14,13},{15,12},{28,31},{29,30},{30,29},{31,28}} | collective-permute-start | bytes 221192 | tf_op jit(solution)/shard_map/ppermute | solution.py:373
  3.1 0.7 %collective-permute-start.3 = (f32[9,16,128]{2,1,0:T(8,128)S(1)}, f32[9,16,128]{2,1,0:T(8,128)S(1)}, u32[]{:S(2)}, u32[]{:S(2)}) collective-permute-start(f32[9,16,128]{2,1,0:T(8,128)S(1)} %shard_map.67.refs_3_), channel_id=1, source_target_pairs={{12,13},{13,12},{14,15},{15,14},{28,29},{29,28},{30,31},{31,30}} | collective-permute-start | bytes 221192 | tf_op jit(solution)/shard_map/ppermute | solution.py:373
  3.8 0.7 %copy.22 = f32[1,16,128,2]{2,1,3,0:T(8,128)S(1)} copy(f32[1,16,128,2]{2,3,1,0:T(2,128)} %param.11) | data formatting | bytes 32768 | tf_op args[5]
  4.5 0.7 %fusion.1 = f32[2,16,128]{2,1,0:T(8,128)S(1)} fusion(s32[1,16,128,2]{2,3,1,0:T(2,128)} %param.10, s32[1,16,128,2]{2,3,1,0:T(2,128)} %param.9), kind=kLoop, calls=%fused_computation.4 | loop fusion | flops 12288 | bytes 49152 | tf_op jit(solution)/shard_map/transpose | solution.py:400
  5.9 0.9 %shard_map.65 = (f32[16,128]{1,0:T(8,128)S(1)}, f32[16,128]{1,0:T(8,128)S(1)}) custom-call(f32[27,8,16,128]{3,2,1,0:T(8,128)S(1)} %bitcast.12), custom_call_target="tpu_custom_call" | custom-call | tf_op jit(solution)/shard_map/pallas_call | solution.py:411
  6.8 1.6 %collective-permute-start = (f32[16,128]{1,0:T(8,128)S(1)}, f32[16,128]{1,0:T(8,128)S(1)}, u32[]{:S(2)}, u32[]{:S(2)}) collective-permute-start(f32[16,128]{1,0:T(8,128)S(1)} %get-tuple-element.17), channel_id=1, source_target_pairs={{0,1},{1,0},{2,3},{3,2},{4,5},{5,4},{6,7},{7,6},{8,9},{9,8},{10,11... | collective-permute-start | bytes 24584 | tf_op jit(solution)/shard_map/ppermute | solution.py:373
  8.4 2.1 %collective-permute-done.first.refs_3_.refs_1_ = f32[16,128]{1,0:T(8,128)S(1)} collective-permute-done((f32[16,128]{1,0:T(8,128)S(1)}, f32[16,128]{1,0:T(8,128)S(1)}, u32[]{:S(2)}, u32[]{:S(2)}) %collective-permute-start) | collective-permute-done | bytes 8224 | tf_op jit(solution)/shard_map/ppermute | solution.py:373
  10.5 3.6 %collective-permute-start.1 = (f32[16,128]{1,0:T(8,128)S(1)}, f32[16,128]{1,0:T(8,128)S(1)}, u32[]{:S(2)}, u32[]{:S(2)}) collective-permute-start(f32[16,128]{1,0:T(8,128)S(1)} %get-tuple-element.18), channel_id=1, source_target_pairs={{0,3},{1,2},{2,1},{3,0},{4,7},{5,6},{6,5},{7,4},{8,11},{9,10},{10,... | collective-permute-start | bytes 24584 | tf_op jit(solution)/shard_map/ppermute | solution.py:373
  14.1 1.3 %shard_map.64.refs_1_ = f32[2,3,8,16,128]{4,3,2,1,0:T(8,128)S(1)} custom-call(f32[2,1,27,8,16,128]{5,4,3,2,1,0:T(8,128)S(1)} %copy-done.2), custom_call_target="tpu_custom_call" | custom-call | tf_op jit(solution)/shard_map/pallas_call | solution.py:418
  16.0 10.7 %collective-permute-start.2 = (f32[11,16,128]{2,1,0:T(8,128)S(1)}, f32[11,16,128]{2,1,0:T(8,128)S(1)}, u32[]{:S(2)}, u32[]{:S(2)}) collective-permute-start(f32[11,16,128]{2,1,0:T(8,128)S(1)} %shard_map.66.refs_5_), channel_id=1, source_target_pairs={{0,4},{1,5},{2,6},{3,7},{4,0},{5,1},{6,2},{7,3},{8,12},{9,13},{10,... | collective-permute-start | bytes 270344 | tf_op jit(solution)/shard_map/ppermute | solution.py:373
  26.7 2.1 %shard_map.68 = (f32[27,8,16,128]{3,2,1,0:T(8,128)S(1)}, f32[16,128]{1,0:T(8,128)S(1)}, f32[16,128]{1,0:T(8,128)S(1)}) custom-call(f32[27,8,16,128]{3,2,1,0:T(8,128)S(1)} %bitcast.14, f32[2,3,8,16,128]{4,3,2,1,0:T(8,128)S(1)} %shard_map.64.refs_1_, s32[1,8,16,128]{3,2,1,0:T(8,128)S(1)} %copy-done.3, ...), custom_call_target="tpu_custom_call" | custom-call | tf_op jit(solution)/shard_map/pallas_call | solution.py:446
  28.9 1.9 %collective-permute-start.7 = (f32[11,16,128]{2,1,0:T(8,128)S(1)}, f32[11,16,128]{2,1,0:T(8,128)S(1)}, u32[]{:S(2)}, u32[]{:S(2)}) collective-permute-start(f32[11,16,128]{2,1,0:T(8,128)S(1)} %shard_map.69), channel_id=1, source_target_pairs={{4,8},{5,9},{6,10},{7,11},{8,4},{9,5},{10,6},{11,7},{12,28},{13,29... | collective-permute-start | bytes 270344 | tf_op jit(solution)/shard_map/ppermute | solution.py:373
  30.8 5.4 %collective-permute-done.7.refs_6_ = f32[11,16,128]{2,1,0:T(8,128)S(1)} collective-permute-done((f32[11,16,128]{2,1,0:T(8,128)S(1)}, f32[11,16,128]{2,1,0:T(8,128)S(1)}, u32[]{:S(2)}, u32[]{:S(2)}) %collective-permute-start.7) | collective-permute-done | bytes 90144 | tf_op jit(solution)/shard_map/ppermute | solution.py:373
  36.5 0.7 %collective-permute-start.13 = (f32[9,16,128]{2,1,0:T(8,128)S(1)}, f32[9,16,128]{2,1,0:T(8,128)S(1)}, u32[]{:S(2)}, u32[]{:S(2)}) collective-permute-start(f32[9,16,128]{2,1,0:T(8,128)S(1)} %get-tuple-element.28.refs_3_), channel_id=1, source_target_pairs={{12,14},{13,15},{14,12},{15,13},{28,30},{29,31},{30,28},{31,29}} | collective-permute-start | bytes 221192 | tf_op jit(solution)/shard_map/ppermute | solution.py:373
  37.2 0.7 %collective-permute-start.12 = (f32[9,16,128]{2,1,0:T(8,128)S(1)}, f32[9,16,128]{2,1,0:T(8,128)S(1)}, u32[]{:S(2)}, u32[]{:S(2)}) collective-permute-start(f32[9,16,128]{2,1,0:T(8,128)S(1)} %get-tuple-element.28.refs_3_), channel_id=1, source_target_pairs={{12,15},{13,14},{14,13},{15,12},{28,31},{29,30},{30,29},{31,28}} | collective-permute-start | bytes 221192 | tf_op jit(solution)/shard_map/ppermute | solution.py:373
  39.0 3.0 %collective-permute-start.9 = (f32[16,128]{1,0:T(8,128)S(1)}, f32[16,128]{1,0:T(8,128)S(1)}, u32[]{:S(2)}, u32[]{:S(2)}) collective-permute-start(f32[16,128]{1,0:T(8,128)S(1)} %get-tuple-element.27), channel_id=1, source_target_pairs={{0,3},{1,2},{2,1},{3,0},{4,7},{5,6},{6,5},{7,4},{8,11},{9,10},{10,... | collective-permute-start | bytes 24584 | tf_op jit(solution)/shard_map/ppermute | solution.py:373
  42.6 1.9 %collective-permute-done.9.second.refs_2_.refs_4_ = f32[16,128]{1,0:T(8,128)S(1)} collective-permute-done((f32[16,128]{1,0:T(8,128)S(1)}, f32[16,128]{1,0:T(8,128)S(1)}, u32[]{:S(2)}, u32[]{:S(2)}) %collective-permute-start.9) | collective-permute-done | bytes 8224 | tf_op jit(solution)/shard_map/ppermute | solution.py:373
  44.5 4.9 %collective-permute-start.10 = (f32[11,16,128]{2,1,0:T(8,128)S(1)}, f32[11,16,128]{2,1,0:T(8,128)S(1)}, u32[]{:S(2)}, u32[]{:S(2)}) collective-permute-start(f32[11,16,128]{2,1,0:T(8,128)S(1)} %shard_map.72.refs_8_), channel_id=1, source_target_pairs={{0,4},{1,5},{2,6},{3,7},{4,0},{5,1},{6,2},{7,3},{8,12},{9,13},{10,... | collective-permute-start | bytes 270344 | tf_op jit(solution)/shard_map/ppermute | solution.py:373
  49.5 1.9 %collective-permute-start.14 = (f32[11,16,128]{2,1,0:T(8,128)S(1)}, f32[11,16,128]{2,1,0:T(8,128)S(1)}, u32[]{:S(2)}, u32[]{:S(2)}) collective-permute-start(f32[11,16,128]{2,1,0:T(8,128)S(1)} %shard_map.73.refs_5_), channel_id=1, source_target_pairs={{4,8},{5,9},{6,10},{7,11},{8,4},{9,5},{10,6},{11,7},{12,28},{13,29... | collective-permute-start | bytes 270344 | tf_op jit(solution)/shard_map/ppermute | solution.py:373
  51.4 1.9 %shard_map.74.refs_7_ = f32[27,8,16,128]{3,2,1,0:T(8,128)} custom-call(f32[27,8,16,128]{3,2,1,0:T(8,128)S(1)} %get-tuple-element.25.adj.refs_0_, f32[2,3,8,16,128]{4,3,2,1,0:T(8,128)S(1)} %shard_map.64.refs_1_, s32[1,8,16,128]{3,2,1,0:T(8,128)S(1)} %copy-done.3, f32[16,128]{1,0:T(8,128)S(1)} %collective-permute-done.8.first.refs_1_.refs_3_, ...), custom_call_target="tpu_custom_call" | custom-call | tf_op jit(solution)/shard_map/pallas_call | solution.py:446
  53.3 3.5 %collective-permute-done.14.refs_6_ = f32[11,16,128]{2,1,0:T(8,128)S(1)} collective-permute-done((f32[11,16,128]{2,1,0:T(8,128)S(1)}, f32[11,16,128]{2,1,0:T(8,128)S(1)}, u32[]{:S(2)}, u32[]{:S(2)}) %collective-permute-start.14) | collective-permute-done | bytes 90144 | tf_op jit(solution)/shard_map/ppermute | solution.py:373
  56.8 1.0 %shard_map.75 = f32[27,8,16,128]{3,2,1,0:T(8,128)} custom-call(f32[27,8,16,128]{3,2,1,0:T(8,128)S(1)} %get-tuple-element.25.adj.refs_0_, f32[2,3,8,16,128]{4,3,2,1,0:T(8,128)S(1)} %shard_map.64.refs_1_, s32[1,8,16,128]{3,2,1,0:T(8,128)S(1)} %copy-done.3, f32[16,128]{1,0:T(8,128)S(1)} %collective-permute-done.8.first.refs_1_.refs_3_, ...), custom_call_target="tpu_custom_call", output_to_operand_aliasing={{}: (7, {})} | custom-call | tf_op jit(solution)/shard_map/pallas_call | solution.py:469
  (29 shorter events, 3.4 us)
Async XLA Ops:
  0.0 1.5 %copy-start = (f32[1,27,8,16,128]{4,3,2,1,0:T(8,128)S(1)}, f32[1,27,8,16,128]{4,3,2,1,0:T(8,128)}, u32[]{:S(2)}) copy-start(f32[1,27,8,16,128]{4,3,2,1,0:T(8,128)} %param.6) | copy-start | bytes 5308420
  1.5 12.6 %copy-start.2 = (f32[2,1,27,8,16,128]{5,4,3,2,1,0:T(8,128)S(1)}, f32[2,1,27,8,16,128]{5,4,3,2,1,0:T(8,128)}, u32[]{:S(2)}) copy-start(f32[2,1,27,8,16,128]{5,4,3,2,1,0:T(8,128)} %saved.1) | copy-start | bytes 10616836
  1.5 27.3 %collective-permute-start.5 = (f32[9,16,128]{2,1,0:T(8,128)S(1)}, f32[9,16,128]{2,1,0:T(8,128)S(1)}, u32[]{:S(2)}, u32[]{:S(2)}) collective-permute-start(f32[9,16,128]{2,1,0:T(8,128)S(1)} %shard_map.67.refs_3_), channel_id=1, source_target_pairs={{12,14},{13,15},{14,12},{15,13},{28,30},{29,31},{30,28},{31,29}} | collective-permute-start | bytes 221192 | tf_op jit(solution)/shard_map/ppermute | solution.py:373
  2.3 26.5 %collective-permute-start.4 = (f32[9,16,128]{2,1,0:T(8,128)S(1)}, f32[9,16,128]{2,1,0:T(8,128)S(1)}, u32[]{:S(2)}, u32[]{:S(2)}) collective-permute-start(f32[9,16,128]{2,1,0:T(8,128)S(1)} %shard_map.67.refs_3_), channel_id=1, source_target_pairs={{12,15},{13,14},{14,13},{15,12},{28,31},{29,30},{30,29},{31,28}} | collective-permute-start | bytes 221192 | tf_op jit(solution)/shard_map/ppermute | solution.py:373
  3.1 25.7 %collective-permute-start.3 = (f32[9,16,128]{2,1,0:T(8,128)S(1)}, f32[9,16,128]{2,1,0:T(8,128)S(1)}, u32[]{:S(2)}, u32[]{:S(2)}) collective-permute-start(f32[9,16,128]{2,1,0:T(8,128)S(1)} %shard_map.67.refs_3_), channel_id=1, source_target_pairs={{12,13},{13,12},{14,15},{15,14},{28,29},{29,28},{30,31},{31,30}} | collective-permute-start | bytes 221192 | tf_op jit(solution)/shard_map/ppermute | solution.py:373
  5.3 23.5 %collective-permute-start.6 = (f32[4,16,128]{2,1,0:T(8,128)S(1)}, f32[4,16,128]{2,1,0:T(8,128)S(1)}, u32[]{:S(2)}, u32[]{:S(2)}) collective-permute-start(f32[4,16,128]{2,1,0:T(8,128)S(1)} %pad_maximum_fusion), channel_id=1, source_target_pairs={{12,28},{13,29},{14,30},{15,31},{28,12},{29,13},{30,14},{31,15}} | collective-permute-start | bytes 98312 | tf_op jit(solution)/shard_map/ppermute | solution.py:373
  6.8 3.7 %collective-permute-start = (f32[16,128]{1,0:T(8,128)S(1)}, f32[16,128]{1,0:T(8,128)S(1)}, u32[]{:S(2)}, u32[]{:S(2)}) collective-permute-start(f32[16,128]{1,0:T(8,128)S(1)} %get-tuple-element.17), channel_id=1, source_target_pairs={{0,1},{1,0},{2,3},{3,2},{4,5},{5,4},{6,7},{7,6},{8,9},{9,8},{10,11... | collective-permute-start | bytes 24584 | tf_op jit(solution)/shard_map/ppermute | solution.py:373
  10.5 5.5 %copy-start.1 = (f32[1,27,8,16,128]{4,3,2,1,0:T(8,128)S(1)}, f32[1,27,8,16,128]{4,3,2,1,0:T(8,128)}, u32[]{:S(2)}) copy-start(f32[1,27,8,16,128]{4,3,2,1,0:T(8,128)} %param.6) | copy-start | bytes 5308420
  10.5 5.4 %collective-permute-start.1 = (f32[16,128]{1,0:T(8,128)S(1)}, f32[16,128]{1,0:T(8,128)S(1)}, u32[]{:S(2)}, u32[]{:S(2)}) collective-permute-start(f32[16,128]{1,0:T(8,128)S(1)} %get-tuple-element.18), channel_id=1, source_target_pairs={{0,3},{1,2},{2,1},{3,0},{4,7},{5,6},{6,5},{7,4},{8,11},{9,10},{10,... | collective-permute-start | bytes 24584 | tf_op jit(solution)/shard_map/ppermute | solution.py:373
  15.4 11.3 %copy-start.3 = (s32[1,8,16,128]{3,2,1,0:T(8,128)S(1)}, s32[1,8,16,128]{3,2,1,0:T(8,128)}, u32[]{:S(2)}) copy-start(s32[1,8,16,128]{3,2,1,0:T(8,128)} %refs_2_.9) | copy-start | bytes 196612
  16.0 14.8 %collective-permute-start.2 = (f32[11,16,128]{2,1,0:T(8,128)S(1)}, f32[11,16,128]{2,1,0:T(8,128)S(1)}, u32[]{:S(2)}, u32[]{:S(2)}) collective-permute-start(f32[11,16,128]{2,1,0:T(8,128)S(1)} %shard_map.66.refs_5_), channel_id=1, source_target_pairs={{0,4},{1,5},{2,6},{3,7},{4,0},{5,1},{6,2},{7,3},{8,12},{9,13},{10,... | collective-permute-start | bytes 270344 | tf_op jit(solution)/shard_map/ppermute | solution.py:373
  28.9 7.3 %collective-permute-start.7 = (f32[11,16,128]{2,1,0:T(8,128)S(1)}, f32[11,16,128]{2,1,0:T(8,128)S(1)}, u32[]{:S(2)}, u32[]{:S(2)}) collective-permute-start(f32[11,16,128]{2,1,0:T(8,128)S(1)} %shard_map.69), channel_id=1, source_target_pairs={{4,8},{5,9},{6,10},{7,11},{8,4},{9,5},{10,6},{11,7},{12,28},{13,29... | collective-permute-start | bytes 270344 | tf_op jit(solution)/shard_map/ppermute | solution.py:373
  36.5 12.9 %collective-permute-start.13 = (f32[9,16,128]{2,1,0:T(8,128)S(1)}, f32[9,16,128]{2,1,0:T(8,128)S(1)}, u32[]{:S(2)}, u32[]{:S(2)}) collective-permute-start(f32[9,16,128]{2,1,0:T(8,128)S(1)} %get-tuple-element.28.refs_3_), channel_id=1, source_target_pairs={{12,14},{13,15},{14,12},{15,13},{28,30},{29,31},{30,28},{31,29}} | collective-permute-start | bytes 221192 | tf_op jit(solution)/shard_map/ppermute | solution.py:373
  37.2 12.2 %collective-permute-start.12 = (f32[9,16,128]{2,1,0:T(8,128)S(1)}, f32[9,16,128]{2,1,0:T(8,128)S(1)}, u32[]{:S(2)}, u32[]{:S(2)}) collective-permute-start(f32[9,16,128]{2,1,0:T(8,128)S(1)} %get-tuple-element.28.refs_3_), channel_id=1, source_target_pairs={{12,15},{13,14},{14,13},{15,12},{28,31},{29,30},{30,29},{31,28}} | collective-permute-start | bytes 221192 | tf_op jit(solution)/shard_map/ppermute | solution.py:373
  37.9 11.6 %collective-permute-start.11 = (f32[9,16,128]{2,1,0:T(8,128)S(1)}, f32[9,16,128]{2,1,0:T(8,128)S(1)}, u32[]{:S(2)}, u32[]{:S(2)}) collective-permute-start(f32[9,16,128]{2,1,0:T(8,128)S(1)} %get-tuple-element.28.refs_3_), channel_id=1, source_target_pairs={{12,13},{13,12},{14,15},{15,14},{28,29},{29,28},{30,31},{31,30}} | collective-permute-start | bytes 221192 | tf_op jit(solution)/shard_map/ppermute | solution.py:373
  38.9 3.7 %collective-permute-start.8 = (f32[16,128]{1,0:T(8,128)S(1)}, f32[16,128]{1,0:T(8,128)S(1)}, u32[]{:S(2)}, u32[]{:S(2)}) collective-permute-start(f32[16,128]{1,0:T(8,128)S(1)} %get-tuple-element.26), channel_id=1, source_target_pairs={{0,1},{1,0},{2,3},{3,2},{4,5},{5,4},{6,7},{7,6},{8,9},{9,8},{10,11... | collective-permute-start | bytes 24584 | tf_op jit(solution)/shard_map/ppermute | solution.py:373
  39.0 5.5 %collective-permute-start.9 = (f32[16,128]{1,0:T(8,128)S(1)}, f32[16,128]{1,0:T(8,128)S(1)}, u32[]{:S(2)}, u32[]{:S(2)}) collective-permute-start(f32[16,128]{1,0:T(8,128)S(1)} %get-tuple-element.27), channel_id=1, source_target_pairs={{0,3},{1,2},{2,1},{3,0},{4,7},{5,6},{6,5},{7,4},{8,11},{9,10},{10,... | collective-permute-start | bytes 24584 | tf_op jit(solution)/shard_map/ppermute | solution.py:373
  44.5 8.8 %collective-permute-start.10 = (f32[11,16,128]{2,1,0:T(8,128)S(1)}, f32[11,16,128]{2,1,0:T(8,128)S(1)}, u32[]{:S(2)}, u32[]{:S(2)}) collective-permute-start(f32[11,16,128]{2,1,0:T(8,128)S(1)} %shard_map.72.refs_8_), channel_id=1, source_target_pairs={{0,4},{1,5},{2,6},{3,7},{4,0},{5,1},{6,2},{7,3},{8,12},{9,13},{10,... | collective-permute-start | bytes 270344 | tf_op jit(solution)/shard_map/ppermute | solution.py:373
  49.5 7.3 %collective-permute-start.14 = (f32[11,16,128]{2,1,0:T(8,128)S(1)}, f32[11,16,128]{2,1,0:T(8,128)S(1)}, u32[]{:S(2)}, u32[]{:S(2)}) collective-permute-start(f32[11,16,128]{2,1,0:T(8,128)S(1)} %shard_map.73.refs_5_), channel_id=1, source_target_pairs={{4,8},{5,9},{6,10},{7,11},{8,4},{9,5},{10,6},{11,7},{12,28},{13,29... | collective-permute-start | bytes 270344 | tf_op jit(solution)/shard_map/ppermute | solution.py:373

commit v5 on v4

--- a/solution.py
+++ b/solution.py
@@ -42,17 +42,21 @@
     return lax.rem(lax.axis_index(axis), 2) == 0
 
 
-def write_edges(low, high, first, second):
+def write_messages(top, low, high, first, second):
     even = is_even("yz")
-    first[...] = jnp.where(even, high, low)
-    second[...] = jnp.where(even, low, high)
+    for j in range(9):
+        tile = top(j)
+        first[j] = tile
+        second[j] = tile
+    first[9] = jnp.where(even, high, low)
+    second[9] = jnp.where(even, low, high)
 
 
 def edges_from(first, second):
     even = is_even("yz")
     me, count = lax.axis_index("yz"), lax.axis_size("yz")
-    low = jnp.where(me == 0, 0.0, jnp.where(even, second[...], first[...]))
-    high = jnp.where(me == count - 1, 0.0, jnp.where(even, first[...], second[...]))
+    low = jnp.where(me == 0, 0.0, jnp.where(even, second[9], first[9]))
+    high = jnp.where(me == count - 1, 0.0, jnp.where(even, first[9], second[9]))
     return low, high
 
 
@@ -67,7 +71,7 @@
     low, high = lax.fori_loop(
         0, adj.shape[1], lambda x, c: pack_columns(lambda i: adj[i, x], x, *c), (zero, zero)
     )
-    write_edges(low, high, first_out, second_out)
+    write_messages(lambda j: adj[j, adj.shape[1] - 1], low, high, first_out, second_out)
 
 
 def velocity_kernel(saved, out, kept, sems):
@@ -98,12 +102,12 @@
 
 
 def cross_kernel(count, *refs):
-    adj, low_side, high_side, own = refs[:4]
-    blocks = refs[3 : 3 + count]
-    info, _, out = refs[3 + count :]
+    adj, own, first, second = refs[:4]
+    blocks = refs[1 : 1 + count]
+    info, out = refs[1 + count :]
     extent_x = adj.shape[1]
     interface = lax.axis_index("gx") == lax.axis_size("gx") - 1
-    out[9], out[10] = edges_from(low_side, high_side)
+    out[9], out[10] = edges_from(first, second)
 
     @pl.when(jnp.logical_not(interface))
     def _():
@@ -249,11 +253,11 @@
                 pulled[i] = shift_y(tile, cy)
 
 
-def inner_kernel(step, last, adj, vel, solid, first, second, _, *rest):
+def inner_kernel(step, last, adj, vel, solid, first, second, *rest):
     if last:
         out, made, pulled, sems = rest
     else:
-        out, low_out, high_out, made, pulled, sems = rest
+        low_in, high_in, _, out, low_out, high_out, made, pulled, sems = rest
     extent_x = adj.shape[1]
     low_edge, high_edge = edges_from(first, second)
 
@@ -277,8 +281,8 @@
             return carry
         return pack_columns(lambda i: made[x - 1, i], x, *carry)
 
-    zero = jnp.zeros((16, 128), jnp.float32)
-    carry = lax.fori_loop(1, extent_x - 1, plane, 0 if last else (zero, zero))
+    carry = 0 if last else (low_in[...], high_in[...])
+    carry = lax.fori_loop(1, extent_x - 1, plane, carry)
     if not last:
         low_out[...], high_out[...] = carry
     lax.fori_loop(1, extent_x - 1, lambda x, c: (save(x).wait(), c)[1], 0)
@@ -311,23 +315,24 @@
     return save
 
 
-def top_plane_kernel(step, adj, vel, solid, first, second, side, cross, low_in, high_in, _, *rest):
+def top_plane_kernel(step, adj, vel, solid, first, second, side, cross, *rest):
     out, top_out, low_out, high_out, made, pulled, sems = rest
     final = adj.shape[1] - 1
     edges = edges_from(first, second)
     save = outer_plane(0, final, step, adj, vel, solid, edges, side, cross, out, made, pulled, sems)
     for j in range(9):
         top_out[j] = made[0, j]
-    low_out[...], high_out[...] = pack_columns(lambda i: made[0, i], final, low_in[...], high_in[...])
+    zero = jnp.zeros((16, 128), jnp.float32)
+    low_out[...], high_out[...] = pack_columns(lambda i: made[0, i], final, zero, zero)
     save.wait()
 
 
-def bottom_plane_kernel(step, adj, vel, solid, first, second, side, cross, low_in, high_in, _, *rest):
-    out, first_out, second_out, made, pulled, sems = rest
+def bottom_plane_kernel(step, adj, vel, solid, first, second, side, cross, *rest):
+    low_in, high_in, top, *_, out, first_out, second_out, made, pulled, sems = rest
     edges = edges_from(first, second)
     save = outer_plane(0, 0, step, adj, vel, solid, edges, side, cross, out, made, pulled, sems)
     low, high = pack_columns(lambda i: made[0, i], 0, low_in[...], high_in[...])
-    write_edges(low, high, first_out, second_out)
+    write_messages(lambda j: top[j], low, high, first_out, second_out)
     save.wait()
 
 
@@ -394,6 +399,9 @@
         if gx == widths - 1:
             return (1 - zone, gx, yz)
         return None if gx == 0 else (zone, partner_of(gx, 1), yz)
+
+    def far_blocks(plane):
+        return [send(plane, at_interface(hop_z(hop))) for hop in range(2, count - 1)]
 
     code = band_device[0] * 128 + band_cell[0]
     info = jnp.concatenate(
@@ -410,7 +418,7 @@
     )(field)
     first, second = pl.pallas_call(
         pack_kernel,
-        out_shape=(tile_shape(),) * 2,
+        out_shape=(tile_shape(10),) * 2,
         in_specs=in_vmem(1),
         out_specs=tuple(in_vmem(2)),
         compiler_params=params,
@@ -426,73 +434,63 @@
         ],
         compiler_params=params,
     )(saved)
+    others = far_blocks(top)
     for step in (1, 0):
         last = step == 0
-        blocks = [send(top, at_interface(hop_z(hop))) for hop in range(2, count - 1)]
-        blocks = [send(top, at_interface(along_z(shift))) for shift in (0, 1)] + blocks
         first = send(first, along_z(0))
         second = send(second, along_z(1))
-        side_out = pl.pallas_call(
+        side = pl.pallas_call(
             side_kernel,
             out_shape=tile_shape(11),
             in_specs=in_vmem(3),
             out_specs=in_vmem(1)[0],
             compiler_params=params,
         )(field, first, second)
-        side = send(side_out, along_x)
-
-        def make_inner(after):
-            columns = () if last else (tile_shape(),) * 2
-            return pl.pallas_call(
-                lambda *refs: inner_kernel(step, last, *refs),
-                out_shape=(tile_shape(27, extent_x), *columns),
-                in_specs=in_vmem(5) + in_any(1),
-                out_specs=tuple(in_any(1) + in_vmem(len(columns))),
-                scratch_shapes=[
-                    pltpu.VMEM((extent_x - 2, 27, 16, 128), jnp.float32),
-                    pltpu.VMEM((27, 16, 128), jnp.float32),
-                    pltpu.SemaphoreType.DMA((extent_x - 2,)),
-                ],
-                compiler_params=params,
-            )(field, vel, solid, first, second, after)
-
-        def make_cross(after):
-            return pl.pallas_call(
-                lambda *refs: cross_kernel(count, *refs),
-                out_shape=tile_shape(11),
-                in_specs=in_vmem(4 + count) + in_any(1),
-                out_specs=in_vmem(1)[0],
-                compiler_params=params,
-            )(field, first, second, top, *blocks, info, after)
-
-        def make_outer(kernel, planes, given, extra):
+        side = send(side, along_x)
+        cross = pl.pallas_call(
+            lambda *refs: cross_kernel(count, *refs),
+            out_shape=tile_shape(11),
+            in_specs=in_vmem(2 + count),
+            out_specs=in_vmem(1)[0],
+            compiler_params=params,
+        )(field, top, first, second, *others, info)
+        cross = send(cross, along_x_or_flip)
+
+        def make_planes(kernel, planes, given, new, extra, after=()):
+            operands = (field, vel, solid, *given)
             return pl.pallas_call(
                 lambda *refs: kernel(step, *refs),
                 out_shape=(tile_shape(27, extent_x), *extra),
-                in_specs=in_vmem(7 + len(given) - 1) + in_any(1),
+                in_specs=in_vmem(len(operands)) + in_any(len(after) + len(new)),
                 out_specs=tuple(in_any(1) + in_vmem(len(extra))),
                 scratch_shapes=[
                     pltpu.VMEM((planes, 27, 16, 128), jnp.float32),
                     pltpu.VMEM((27, 16, 128), jnp.float32),
                     pltpu.SemaphoreType.DMA((planes,)),
                 ],
-                input_output_aliases={7 + len(given) - 1: 0},
+                input_output_aliases={len(operands) + len(after): 0} if new else {},
                 compiler_params=params,
-            )(field, vel, solid, first, second, side, cross, *given)
-
+            )(*operands, *after, *new)
+
+        def inner(step, *refs):
+            inner_kernel(step, last, *refs)
+
+        ghosts = (first, second, side, cross)
+        tile = tile_shape()
         if last:
-            cross_out = make_cross(side_out)
-            cross = send(cross_out, along_x_or_flip)
-            (new,) = make_inner(cross_out)
-            (field,) = make_outer(last_planes_kernel, 2, (new,), ())
+            new = make_planes(inner, extent_x - 2, ghosts[:2], (), ())
+            (field,) = make_planes(last_planes_kernel, 2, ghosts, new, ())
         else:
-            new, low, high = make_inner(side_out)
-            cross = send(make_cross(low), along_x_or_flip)
-            tile = tile_shape()
-            new, top, low, high = make_outer(
-                top_plane_kernel, 1, (low, high, new), (tile_shape(9), tile, tile)
+            pair = (tile, tile)
+            new, top, *columns = make_planes(top_plane_kernel, 1, ghosts, (), (tile_shape(9), *pair))
+            new, *columns = make_planes(
+                inner, extent_x - 2, (*ghosts[:2], *columns), (new,), pair
             )
-            field, first, second = make_outer(bottom_plane_kernel, 1, (low, high, new), (tile, tile))
+            others = far_blocks(top)
+            messages = (tile_shape(10),) * 2
+            field, first, second = make_planes(
+                bottom_plane_kernel, 1, (*ghosts, *columns, top), (new,), messages, others
+            )
     return field[None]
 
 

time: 58.4 us -> 44.4 us (0.76)
  starting transfers between devices: 32.6 us -> 19.8 us
  other arithmetic: 0.75 us -> 0.01 us
  local copies, waits for them, and re-layouts: 2.21 us -> 1.51 us
  waiting for transfers between devices: 14 us -> 14.6 us
    ppermute x15 -> x11, starting transfers between devices: 32.6 us -> 19.8 us  [send(): return lax.ppermute(values, axes, pairs)]
    transpose x1, other arithmetic: 0.74 us -> 0.01 us  [body(): jnp.moveaxis(code.astype(jnp.float32), -1, 0)]
    unnamed x9 -> x15, local copies, waits for them, and re-layouts: 2.21 us -> 1.51 us
    ppermute x15 -> x11, waiting for transfers between devices: 14 us -> 14.6 us  [send(): return lax.ppermute(values, axes, pairs)]
  transfers between devices with their start and end apart: 15 -> 11, of which waited for: 6 -> 5; matrix products, arithmetic and copies ran while one was open for 3% -> 0% of each run, Pallas kernels for 11% -> 14%
where the time goes in v5:
time: 44.4 us; the launch traced here: 44.1 us
  starting transfers between devices  19.8 us (45%)
  waiting for transfers between devices  14.6 us (33%)
  Pallas kernels  7.98 us (18%)
  local copies, waits for them, and re-layouts  1.51 us (3%)
    ppermute x11, starting transfers between devices, send(): return lax.ppermute(values, axes, pairs)  19.8 us
    ppermute x11, waiting for transfers between devices, send(): return lax.ppermute(values, axes, pairs)  14.6 us
    pallas_call x5, Pallas kernels, make_planes(): pl.pallas_call(lambda *refs: kernel(step, *refs), out_shape=(tile_shape(2...  5.7 us
    unnamed x15, local copies, waits for them, and re-layouts  1.51 us
    pallas_call x1, Pallas kernels, body(): pl.pallas_call(velocity_kernel, out_shape=tile_shape(2, 3, extent_x), in_...  1.32 us
  transfers between devices with their start and end apart: 11, of which 5 were waited for; matrix products, arithmetic and copies ran while one was open for 0% of the time, Pallas kernels for 14%

profile of v5, /device:TPU:4, one launch (start us, length us, event | category | flops | bytes accessed | tf_op | source)
XLA Modules:
  0.0 44.1 jit_solution(17932100303572481401)
XLA Ops:
  0.0 1.5 %copy-done = f32[1,27,8,16,128]{4,3,2,1,0:T(8,128)S(1)} copy-done((f32[1,27,8,16,128]{4,3,2,1,0:T(8,128)S(1)}, f32[1,27,8,16,128]{4,3,2,1,0:T(8,128)}, u32[]{:S(2)}) %copy-start) | copy-done | bytes 1769496
  1.5 0.7 %collective-permute-start.3 = (f32[9,16,128]{2,1,0:T(8,128)S(1)}, f32[9,16,128]{2,1,0:T(8,128)S(1)}, u32[]{:S(2)}, u32[]{:S(2)}) collective-permute-start(f32[9,16,128]{2,1,0:T(8,128)S(1)} %shard_map.67.refs_1_), channel_id=1, source_target_pairs={{12,14},{13,15},{14,12},{15,13},{28,30},{29,31},{30,28},{31,29}} | collective-permute-start | bytes 221192 | tf_op jit(solution)/shard_map/ppermute | solution.py:378
  2.2 0.9 %shard_map.65 = (f32[10,16,128]{2,1,0:T(8,128)S(1)}, f32[10,16,128]{2,1,0:T(8,128)S(1)}) custom-call(f32[27,8,16,128]{3,2,1,0:T(8,128)S(1)} %bitcast.12), custom_call_target="tpu_custom_call" | custom-call | tf_op jit(solution)/shard_map/pallas_call | solution.py:419
  3.1 1.6 %collective-permute-start = (f32[10,16,128]{2,1,0:T(8,128)S(1)}, f32[10,16,128]{2,1,0:T(8,128)S(1)}, u32[]{:S(2)}, u32[]{:S(2)}) collective-permute-start(f32[10,16,128]{2,1,0:T(8,128)S(1)} %get-tuple-element.17), channel_id=1, source_target_pairs={{0,1},{1,0},{2,3},{3,2},{4,5},{5,4},{6,7},{7,6},{8,9},{9,8},{10,11... | collective-permute-start | bytes 245768 | tf_op jit(solution)/shard_map/ppermute | solution.py:378
  4.7 2.5 %collective-permute-start.1 = (f32[10,16,128]{2,1,0:T(8,128)S(1)}, f32[10,16,128]{2,1,0:T(8,128)S(1)}, u32[]{:S(2)}, u32[]{:S(2)}) collective-permute-start(f32[10,16,128]{2,1,0:T(8,128)S(1)} %get-tuple-element.18), channel_id=1, source_target_pairs={{0,3},{1,2},{2,1},{3,0},{4,7},{5,6},{6,5},{7,4},{8,11},{9,10},{10,... | collective-permute-start | bytes 245768 | tf_op jit(solution)/shard_map/ppermute | solution.py:378
  7.2 0.8 %collective-permute-start.4 = (f32[4,16,128]{2,1,0:T(8,128)S(1)}, f32[4,16,128]{2,1,0:T(8,128)S(1)}, u32[]{:S(2)}, u32[]{:S(2)}) collective-permute-start(f32[4,16,128]{2,1,0:T(8,128)S(1)} %pad_maximum_fusion), channel_id=1, source_target_pairs={{12,28},{13,29},{14,30},{15,31},{28,12},{29,13},{30,14},{31,15}} | collective-permute-start | bytes 98312 | tf_op jit(solution)/shard_map/ppermute | solution.py:378
  8.0 3.3 %collective-permute-done.1.second.refs_3_.refs_4_ = f32[10,16,128]{2,1,0:T(8,128)S(1)} collective-permute-done((f32[10,16,128]{2,1,0:T(8,128)S(1)}, f32[10,16,128]{2,1,0:T(8,128)S(1)}, u32[]{:S(2)}, u32[]{:S(2)}) %collective-permute-start.1) | collective-permute-done | bytes 81952 | tf_op jit(solution)/shard_map/ppermute | solution.py:378
  11.4 5.0 %collective-permute-start.2 = (f32[11,16,128]{2,1,0:T(8,128)S(1)}, f32[11,16,128]{2,1,0:T(8,128)S(1)}, u32[]{:S(2)}, u32[]{:S(2)}) collective-permute-start(f32[11,16,128]{2,1,0:T(8,128)S(1)} %shard_map.66), channel_id=1, source_target_pairs={{0,4},{1,5},{2,6},{3,7},{4,0},{5,1},{6,2},{7,3},{8,12},{9,13},{10,... | collective-permute-start | bytes 270344 | tf_op jit(solution)/shard_map/ppermute | solution.py:378
  16.4 2.1 %collective-permute-start.5 = (f32[11,16,128]{2,1,0:T(8,128)S(1)}, f32[11,16,128]{2,1,0:T(8,128)S(1)}, u32[]{:S(2)}, u32[]{:S(2)}) collective-permute-start(f32[11,16,128]{2,1,0:T(8,128)S(1)} %shard_map.68), channel_id=1, source_target_pairs={{4,8},{5,9},{6,10},{7,11},{8,4},{9,5},{10,6},{11,7},{12,28},{13,29... | collective-permute-start | bytes 270344 | tf_op jit(solution)/shard_map/ppermute | solution.py:378
  18.5 1.3 %shard_map.64.refs_1_ = f32[2,3,8,16,128]{4,3,2,1,0:T(8,128)S(1)} custom-call(f32[2,1,27,8,16,128]{5,4,3,2,1,0:T(8,128)S(1)} %copy-done.2), custom_call_target="tpu_custom_call" | custom-call | tf_op jit(solution)/shard_map/pallas_call | solution.py:426
  19.8 4.0 %collective-permute-done.5.refs_6_ = f32[11,16,128]{2,1,0:T(8,128)S(1)} collective-permute-done((f32[11,16,128]{2,1,0:T(8,128)S(1)}, f32[11,16,128]{2,1,0:T(8,128)S(1)}, u32[]{:S(2)}, u32[]{:S(2)}) %collective-permute-start.5) | collective-permute-done | bytes 90144 | tf_op jit(solution)/shard_map/ppermute | solution.py:378
  23.9 0.3 shard_map.69
  24.2 0.7 %collective-permute-start.6 = (f32[9,16,128]{2,1,0:T(8,128)S(1)}, f32[9,16,128]{2,1,0:T(8,128)S(1)}, u32[]{:S(2)}, u32[]{:S(2)}) collective-permute-start(f32[9,16,128]{2,1,0:T(8,128)S(1)} %get-tuple-element.24.refs_9_.refs_1_), channel_id=1, source_target_pairs={{12,14},{13,15},{14,12},{15,13},{28,30},{29,31},{30,28},{31,29}} | collective-permute-start | bytes 221192 | tf_op jit(solution)/shard_map/ppermute | solution.py:378
  24.9 2.1 %shard_map.70 = (f32[27,8,16,128]{3,2,1,0:T(8,128)S(1)}, f32[16,128]{1,0:T(8,128)S(1)}, f32[16,128]{1,0:T(8,128)S(1)}) custom-call(f32[27,8,16,128]{3,2,1,0:T(8,128)S(1)} %bitcast.16, f32[2,3,8,16,128]{4,3,2,1,0:T(8,128)S(1)} %shard_map.64.refs_1_, s32[1,8,16,128]{3,2,1,0:T(8,128)S(1)} %copy-done.3, ...), custom_call_target="tpu_custom_call", output_to_operand_aliasing={{0}: (7, {})} | custom-call | tf_op jit(solution)/shard_map/pallas_call | solution.py:461
  27.0 0.4 shard_map.71
  27.4 0.1 collective-permute-start.7
  27.4 2.7 %collective-permute-start.8 = (f32[10,16,128]{2,1,0:T(8,128)S(1)}, f32[10,16,128]{2,1,0:T(8,128)S(1)}, u32[]{:S(2)}, u32[]{:S(2)}) collective-permute-start(f32[10,16,128]{2,1,0:T(8,128)S(1)} %get-tuple-element.28), channel_id=1, source_target_pairs={{0,3},{1,2},{2,1},{3,0},{4,7},{5,6},{6,5},{7,4},{8,11},{9,10},{10,... | collective-permute-start | bytes 245768 | tf_op jit(solution)/shard_map/ppermute | solution.py:378
  30.1 1.8 %collective-permute-done.7.first.refs_2_.refs_3_ = f32[10,16,128]{2,1,0:T(8,128)S(1)} collective-permute-done((f32[10,16,128]{2,1,0:T(8,128)S(1)}, f32[10,16,128]{2,1,0:T(8,128)S(1)}, u32[]{:S(2)}, u32[]{:S(2)}) %collective-permute-start.7) | collective-permute-done | bytes 81952 | tf_op jit(solution)/shard_map/ppermute | solution.py:378
  31.9 2.0 %collective-permute-done.8.second.refs_3_.refs_4_ = f32[10,16,128]{2,1,0:T(8,128)S(1)} collective-permute-done((f32[10,16,128]{2,1,0:T(8,128)S(1)}, f32[10,16,128]{2,1,0:T(8,128)S(1)}, u32[]{:S(2)}, u32[]{:S(2)}) %collective-permute-start.8) | collective-permute-done | bytes 81952 | tf_op jit(solution)/shard_map/ppermute | solution.py:378
  33.9 1.9 %collective-permute-start.9 = (f32[11,16,128]{2,1,0:T(8,128)S(1)}, f32[11,16,128]{2,1,0:T(8,128)S(1)}, u32[]{:S(2)}, u32[]{:S(2)}) collective-permute-start(f32[11,16,128]{2,1,0:T(8,128)S(1)} %shard_map.72), channel_id=1, source_target_pairs={{0,4},{1,5},{2,6},{3,7},{4,0},{5,1},{6,2},{7,3},{8,12},{9,13},{10,... | collective-permute-start | bytes 270344 | tf_op jit(solution)/shard_map/ppermute | solution.py:378
  35.8 1.9 %collective-permute-start.10 = (f32[11,16,128]{2,1,0:T(8,128)S(1)}, f32[11,16,128]{2,1,0:T(8,128)S(1)}, u32[]{:S(2)}, u32[]{:S(2)}) collective-permute-start(f32[11,16,128]{2,1,0:T(8,128)S(1)} %shard_map.73), channel_id=1, source_target_pairs={{4,8},{5,9},{6,10},{7,11},{8,4},{9,5},{10,6},{11,7},{12,28},{13,29... | collective-permute-start | bytes 270344 | tf_op jit(solution)/shard_map/ppermute | solution.py:378
  37.7 1.9 %shard_map.74.refs_7_ = f32[27,8,16,128]{3,2,1,0:T(8,128)} custom-call(f32[27,8,16,128]{3,2,1,0:T(8,128)S(1)} %get-tuple-element.26.adj.refs_0_, f32[2,3,8,16,128]{4,3,2,1,0:T(8,128)S(1)} %shard_map.64.refs_1_, s32[1,8,16,128]{3,2,1,0:T(8,128)S(1)} %copy-done.3, f32[10,16,128]{2,1,0:T(8,128)S(1)} %collective-permute-done.7.first.refs_2_.refs_3_, ...), custom_call_target="tpu_custom_call" | custom-call | tf_op jit(solution)/shard_map/pallas_call | solution.py:461
  39.7 3.5 %collective-permute-done.10.refs_6_ = f32[11,16,128]{2,1,0:T(8,128)S(1)} collective-permute-done((f32[11,16,128]{2,1,0:T(8,128)S(1)}, f32[11,16,128]{2,1,0:T(8,128)S(1)}, u32[]{:S(2)}, u32[]{:S(2)}) %collective-permute-start.10) | collective-permute-done | bytes 90144 | tf_op jit(solution)/shard_map/ppermute | solution.py:378
  43.1 1.0 %shard_map.75 = f32[27,8,16,128]{3,2,1,0:T(8,128)} custom-call(f32[27,8,16,128]{3,2,1,0:T(8,128)S(1)} %get-tuple-element.26.adj.refs_0_, f32[2,3,8,16,128]{4,3,2,1,0:T(8,128)S(1)} %shard_map.64.refs_1_, s32[1,8,16,128]{3,2,1,0:T(8,128)S(1)} %copy-done.3, ...), custom_call_target="tpu_custom_call", output_to_operand_aliasing={{}: (7, {})} | custom-call | tf_op jit(solution)/shard_map/pallas_call | solution.py:461
  (27 shorter events, 0.2 us)
Async XLA Ops:
  0.0 1.5 %copy-start = (f32[1,27,8,16,128]{4,3,2,1,0:T(8,128)S(1)}, f32[1,27,8,16,128]{4,3,2,1,0:T(8,128)}, u32[]{:S(2)}) copy-start(f32[1,27,8,16,128]{4,3,2,1,0:T(8,128)} %param.6) | copy-start | bytes 5308420
  1.5 5.7 %copy-start.6 = (f32[1,16,128,2]{2,3,1,0:T(2,128)S(1)}, f32[1,16,128,2]{2,3,1,0:T(2,128)}, u32[]{:S(2)}) copy-start(f32[1,16,128,2]{2,3,1,0:T(2,128)} %param.11) | copy-start | bytes 49156
  1.5 5.7 %copy-start.4 = (s32[1,16,128,2]{2,3,1,0:T(2,128)S(1)}, s32[1,16,128,2]{2,3,1,0:T(2,128)}, u32[]{:S(2)}) copy-start(s32[1,16,128,2]{2,3,1,0:T(2,128)} %param.10) | copy-start | bytes 49156
  1.5 5.7 %copy-start.5 = (s32[1,16,128,2]{2,3,1,0:T(2,128)S(1)}, s32[1,16,128,2]{2,3,1,0:T(2,128)}, u32[]{:S(2)}) copy-start(s32[1,16,128,2]{2,3,1,0:T(2,128)} %param.9) | copy-start | bytes 49156
  1.5 14.8 %collective-permute-start.3 = (f32[9,16,128]{2,1,0:T(8,128)S(1)}, f32[9,16,128]{2,1,0:T(8,128)S(1)}, u32[]{:S(2)}, u32[]{:S(2)}) collective-permute-start(f32[9,16,128]{2,1,0:T(8,128)S(1)} %shard_map.67.refs_1_), channel_id=1, source_target_pairs={{12,14},{13,15},{14,12},{15,13},{28,30},{29,31},{30,28},{31,29}} | collective-permute-start | bytes 221192 | tf_op jit(solution)/shard_map/ppermute | solution.py:378
  3.1 5.0 %collective-permute-start = (f32[10,16,128]{2,1,0:T(8,128)S(1)}, f32[10,16,128]{2,1,0:T(8,128)S(1)}, u32[]{:S(2)}, u32[]{:S(2)}) collective-permute-start(f32[10,16,128]{2,1,0:T(8,128)S(1)} %get-tuple-element.17), channel_id=1, source_target_pairs={{0,1},{1,0},{2,3},{3,2},{4,5},{5,4},{6,7},{7,6},{8,9},{9,8},{10,11... | collective-permute-start | bytes 245768 | tf_op jit(solution)/shard_map/ppermute | solution.py:378
  4.7 6.6 %collective-permute-start.1 = (f32[10,16,128]{2,1,0:T(8,128)S(1)}, f32[10,16,128]{2,1,0:T(8,128)S(1)}, u32[]{:S(2)}, u32[]{:S(2)}) collective-permute-start(f32[10,16,128]{2,1,0:T(8,128)S(1)} %get-tuple-element.18), channel_id=1, source_target_pairs={{0,3},{1,2},{2,1},{3,0},{4,7},{5,6},{6,5},{7,4},{8,11},{9,10},{10,... | collective-permute-start | bytes 245768 | tf_op jit(solution)/shard_map/ppermute | solution.py:378
  7.2 11.3 %copy-start.2 = (f32[2,1,27,8,16,128]{5,4,3,2,1,0:T(8,128)S(1)}, f32[2,1,27,8,16,128]{5,4,3,2,1,0:T(8,128)}, u32[]{:S(2)}) copy-start(f32[2,1,27,8,16,128]{5,4,3,2,1,0:T(8,128)} %saved.1) | copy-start | bytes 10616836
  7.2 9.1 %collective-permute-start.4 = (f32[4,16,128]{2,1,0:T(8,128)S(1)}, f32[4,16,128]{2,1,0:T(8,128)S(1)}, u32[]{:S(2)}, u32[]{:S(2)}) collective-permute-start(f32[4,16,128]{2,1,0:T(8,128)S(1)} %pad_maximum_fusion), channel_id=1, source_target_pairs={{12,28},{13,29},{14,30},{15,31},{28,12},{29,13},{30,14},{31,15}} | collective-permute-start | bytes 98312 | tf_op jit(solution)/shard_map/ppermute | solution.py:378
  11.4 8.4 %collective-permute-start.2 = (f32[11,16,128]{2,1,0:T(8,128)S(1)}, f32[11,16,128]{2,1,0:T(8,128)S(1)}, u32[]{:S(2)}, u32[]{:S(2)}) collective-permute-start(f32[11,16,128]{2,1,0:T(8,128)S(1)} %shard_map.66), channel_id=1, source_target_pairs={{0,4},{1,5},{2,6},{3,7},{4,0},{5,1},{6,2},{7,3},{8,12},{9,13},{10,... | collective-permute-start | bytes 270344 | tf_op jit(solution)/shard_map/ppermute | solution.py:378
  16.4 7.5 %copy-start.1 = (f32[1,27,8,16,128]{4,3,2,1,0:T(8,128)S(1)}, f32[1,27,8,16,128]{4,3,2,1,0:T(8,128)}, u32[]{:S(2)}) copy-start(f32[1,27,8,16,128]{4,3,2,1,0:T(8,128)} %param.6) | copy-start | bytes 5308420
  16.4 7.5 %copy-start.3 = (s32[1,8,16,128]{3,2,1,0:T(8,128)S(1)}, s32[1,8,16,128]{3,2,1,0:T(8,128)}, u32[]{:S(2)}) copy-start(s32[1,8,16,128]{3,2,1,0:T(8,128)} %refs_2_.9) | copy-start | bytes 196612
  16.4 7.5 %collective-permute-start.5 = (f32[11,16,128]{2,1,0:T(8,128)S(1)}, f32[11,16,128]{2,1,0:T(8,128)S(1)}, u32[]{:S(2)}, u32[]{:S(2)}) collective-permute-start(f32[11,16,128]{2,1,0:T(8,128)S(1)} %shard_map.68), channel_id=1, source_target_pairs={{4,8},{5,9},{6,10},{7,11},{8,4},{9,5},{10,6},{11,7},{12,28},{13,29... | collective-permute-start | bytes 270344 | tf_op jit(solution)/shard_map/ppermute | solution.py:378
  24.2 2.8 %collective-permute-start.6 = (f32[9,16,128]{2,1,0:T(8,128)S(1)}, f32[9,16,128]{2,1,0:T(8,128)S(1)}, u32[]{:S(2)}, u32[]{:S(2)}) collective-permute-start(f32[9,16,128]{2,1,0:T(8,128)S(1)} %get-tuple-element.24.refs_9_.refs_1_), channel_id=1, source_target_pairs={{12,14},{13,15},{14,12},{15,13},{28,30},{29,31},{30,28},{31,29}} | collective-permute-start | bytes 221192 | tf_op jit(solution)/shard_map/ppermute | solution.py:378
  27.4 4.5 %collective-permute-start.7 = (f32[10,16,128]{2,1,0:T(8,128)S(1)}, f32[10,16,128]{2,1,0:T(8,128)S(1)}, u32[]{:S(2)}, u32[]{:S(2)}) collective-permute-start(f32[10,16,128]{2,1,0:T(8,128)S(1)} %get-tuple-element.27), channel_id=1, source_target_pairs={{0,1},{1,0},{2,3},{3,2},{4,5},{5,4},{6,7},{7,6},{8,9},{9,8},{10,11... | collective-permute-start | bytes 245768 | tf_op jit(solution)/shard_map/ppermute | solution.py:378
  27.4 6.4 %collective-permute-start.8 = (f32[10,16,128]{2,1,0:T(8,128)S(1)}, f32[10,16,128]{2,1,0:T(8,128)S(1)}, u32[]{:S(2)}, u32[]{:S(2)}) collective-permute-start(f32[10,16,128]{2,1,0:T(8,128)S(1)} %get-tuple-element.28), channel_id=1, source_target_pairs={{0,3},{1,2},{2,1},{3,0},{4,7},{5,6},{6,5},{7,4},{8,11},{9,10},{10,... | collective-permute-start | bytes 245768 | tf_op jit(solution)/shard_map/ppermute | solution.py:378
  33.9 5.8 %collective-permute-start.9 = (f32[11,16,128]{2,1,0:T(8,128)S(1)}, f32[11,16,128]{2,1,0:T(8,128)S(1)}, u32[]{:S(2)}, u32[]{:S(2)}) collective-permute-start(f32[11,16,128]{2,1,0:T(8,128)S(1)} %shard_map.72), channel_id=1, source_target_pairs={{0,4},{1,5},{2,6},{3,7},{4,0},{5,1},{6,2},{7,3},{8,12},{9,13},{10,... | collective-permute-start | bytes 270344 | tf_op jit(solution)/shard_map/ppermute | solution.py:378
  35.8 7.3 %collective-permute-start.10 = (f32[11,16,128]{2,1,0:T(8,128)S(1)}, f32[11,16,128]{2,1,0:T(8,128)S(1)}, u32[]{:S(2)}, u32[]{:S(2)}) collective-permute-start(f32[11,16,128]{2,1,0:T(8,128)S(1)} %shard_map.73), channel_id=1, source_target_pairs={{4,8},{5,9},{6,10},{7,11},{8,4},{9,5},{10,6},{11,7},{12,28},{13,29... | collective-permute-start | bytes 270344 | tf_op jit(solution)/shard_map/ppermute | solution.py:378

commit v6 on v3

--- a/solution.py
+++ b/solution.py
@@ -88,27 +88,23 @@
     lax.fori_loop(0, total, one, 0)
 
 
-def side_kernel(adj, first, second, out):
+def side_kernel(adj, first, second, one_out, two_out):
     extent_x = adj.shape[1]
     even = is_even("gx")
     for j in range(9):
-        out[j] = jnp.where(even, adj[j, extent_x - 1], adj[18 + j, 0])
-    out[9], out[10] = edges_from(first, second)
+        top, bottom = adj[j, extent_x - 1], adj[18 + j, 0]
+        one_out[j] = jnp.where(even, top, bottom)
+        two_out[j] = jnp.where(even, bottom, top)
+    low, high = edges_from(first, second)
+    one_out[9], one_out[10] = low, high
+    two_out[9], two_out[10] = low, high
 
 
 def cross_kernel(count, *refs):
-    adj, own, first, second = refs[:4]
-    others = refs[4 : 4 + count - 3]
-    info, out = refs[4 + count - 3 :]
-    extent_x = adj.shape[1]
+    own, first, second = refs[:3]
+    blocks = refs[:count]
+    info, _, out = refs[count:]
     interface = lax.axis_index("gx") == lax.axis_size("gx") - 1
-    out[9], out[10] = edges_from(first, second)
-
-    @pl.when(jnp.logical_not(interface))
-    def _():
-        even = is_even("gx")
-        for j in range(9):
-            out[j] = jnp.where(even, adj[18 + j, 0], adj[j, extent_x - 1])
 
     @pl.when(interface)
     def _():
@@ -130,7 +126,7 @@
             for r in rows:
                 total = jnp.zeros((8, 128), jnp.float32)
                 for k in range(2):
-                    tiles = [ref[j, r : r + 8] for ref in (own, first, second, *others)]
+                    tiles = [ref[j, r : r + 8] for ref in blocks]
                     got = [jnp.take_along_axis(tile, spots[r, k], axis=1) for tile in tiles]
                     picked = got[0]
                     for mask, value in zip(picks[r, k], got[1:]):
@@ -249,10 +245,7 @@
 
 
 def inner_kernel(step, last, adj, vel, solid, first, second, *rest):
-    if last:
-        out, made, pulled, sems = rest
-    else:
-        out, low_out, high_out, made, pulled, sems = rest
+    out, low_out, high_out, made, pulled, sems = rest
     extent_x = adj.shape[1]
     low_edge, high_edge = edges_from(first, second)
 
@@ -277,26 +270,34 @@
         return pack_columns(lambda i: made[x - 1, i], x, *carry)
 
     zero = jnp.zeros((16, 128), jnp.float32)
-    carry = lax.fori_loop(1, extent_x - 1, plane, 0 if last else (zero, zero))
-    if not last:
-        low_out[...], high_out[...] = carry
+    low_out[...], high_out[...] = lax.fori_loop(1, extent_x - 1, plane, (zero, zero))
     lax.fori_loop(1, extent_x - 1, lambda x, c: (save(x).wait(), c)[1], 0)
 
 
-def outer_kernel(step, last, adj, vel, solid, first, second, side, cross, *rest):
-    if last:
-        _, out, made, pulled, sems = rest
-    else:
-        _, low_in, high_in, out, first_out, second_out, made, pulled, sems = rest
+def outer_kernel(step, adj, vel, solid, first, second, one, two, cross, *rest):
+    *rest, made, pulled, sems = rest
+    low_in, high_in, _, out, *messages = rest
     extent_x = adj.shape[1]
-    low_edge, high_edge = edges_from(first, second)
+    edges = edges_from(first, second)
     even = is_even("gx")
     interface = lax.axis_index("gx") == lax.axis_size("gx") - 1
-    below = lambda j: jnp.where(even, cross[j], side[j])
-    above = lambda j: jnp.where(even, side[j], cross[j])
-
-    def plane(n, x, tile_of, edges_of, raw):
-        pull_plane(tile_of, edges_of, pulled, raw)
+
+    def below(j):
+        return jnp.where(even, two[j], one[j])
+
+    def above(j):
+        tile = jnp.where(even, one[j], two[j])
+        return jnp.where(interface, cross[j], tile) if j < 9 else tile
+
+    def plane(n, x, ghost, beyond, start, raw):
+        pull_plane(
+            lambda i, cx: beyond(i % 9) if cx == ghost else adj[i, x + cx],
+            lambda cx: (
+                (beyond(9), beyond(10), start) if cx == ghost else (*edges, (x + 1 + cx) * 9)
+            ),
+            pulled,
+            raw,
+        )
 
         def store(i, tile):
             made[n, i] = tile
@@ -308,35 +309,12 @@
         return save
 
     final = extent_x - 1
-    saves = [
-        plane(
-            0,
-            0,
-            lambda i, cx: below(i) if cx == -1 else adj[i, cx],
-            lambda cx: (
-                (below(9), below(10), extent_x * 9)
-                if cx == -1
-                else (low_edge, high_edge, (1 + cx) * 9)
-            ),
-            None,
-        ),
-        plane(
-            1,
-            final,
-            lambda i, cx: above(i - 18) if cx == 1 else adj[i, final + cx],
-            lambda cx: (
-                (above(9), above(10), 9)
-                if cx == 1
-                else (low_edge, high_edge, (final + 1 + cx) * 9)
-            ),
-            interface,
-        ),
-    ]
-    if not last:
+    saves = [plane(0, 0, -1, below, extent_x * 9, None), plane(1, final, 1, above, 9, interface)]
+    if messages:
         low, high = low_in[...], high_in[...]
         low, high = pack_columns(lambda i: made[0, i], 0, low, high)
         low, high = pack_columns(lambda i: made[1, i], final, low, high)
-        write_messages(lambda j: made[1, j], low, high, first_out, second_out)
+        write_messages(lambda j: made[1, j], low, high, *messages)
     for save in saves:
         save.wait()
 
@@ -377,25 +355,27 @@
     def along_z(shift):
         return lambda zone, gx, yz: (zone, gx, partner_of(yz, shift) % count)
 
+    def at_interface(target):
+        return lambda zone, gx, yz: target(zone, gx, yz) if gx == widths - 1 else None
+
     def hop_z(hop):
-        return lambda zone, gx, yz: (zone, gx, (yz + hop) % count) if gx == widths - 1 else None
+        return lambda zone, gx, yz: (zone, gx, (yz + hop) % count)
 
     def flip(zone, gx, yz):
-        return (1 - zone, gx, yz) if gx == widths - 1 else None
-
-    def along_x(zone, gx, yz):
-        return (zone, partner_of(gx, 0), yz)
-
-    def along_x_or_flip(zone, gx, yz):
-        if gx == widths - 1:
-            return (1 - zone, gx, yz)
-        return None if gx == 0 else (zone, partner_of(gx, 1), yz)
+        return (1 - zone, gx, yz)
+
+    def along_x(shift):
+        def target(zone, gx, yz):
+            to = partner_of(gx, shift)
+            return (zone, to, yz) if 0 <= to < widths else None
+
+        return target
 
     code = band_device[0] * 128 + band_cell[0]
     info = jnp.concatenate(
         [jnp.moveaxis(code.astype(jnp.float32), -1, 0), jnp.moveaxis(band_weight[0], -1, 0)]
     )
-    info = send(info, flip)
+    info = send(info, at_interface(flip))
     first, second = pl.pallas_call(
         pack_kernel,
         out_shape=(tile_shape(10),) * 2,
@@ -419,54 +399,50 @@
         own = first
         first = send(own, along_z(0))
         second = send(second, along_z(1))
-        others = [send(own, hop_z(hop)) for hop in range(2, count - 1)]
-        side = pl.pallas_call(
+        others = [send(own, at_interface(hop_z(hop))) for hop in range(2, count - 1)]
+        one, two = pl.pallas_call(
             side_kernel,
-            out_shape=tile_shape(11),
+            out_shape=(tile_shape(11),) * 2,
             in_specs=in_vmem(3),
+            out_specs=tuple(in_vmem(2)),
+            compiler_params=params,
+        )(field, first, second)
+        two = send(two, along_x(1))
+        one = send(one, along_x(0))
+
+        def make_planes(kernel, planes, given, new, extra):
+            operands = (field, vel, solid, first, second, *given)
+            return pl.pallas_call(
+                lambda *refs: kernel(step, *refs),
+                out_shape=(tile_shape(27, extent_x), *extra),
+                in_specs=in_vmem(len(operands)) + in_any(len(new)),
+                out_specs=tuple(in_any(1) + in_vmem(len(extra))),
+                scratch_shapes=[
+                    pltpu.VMEM((planes, 27, 16, 128), jnp.float32),
+                    pltpu.VMEM((27, 16, 128), jnp.float32),
+                    pltpu.SemaphoreType.DMA((planes,)),
+                ],
+                input_output_aliases={len(operands): 0} if new else {},
+                compiler_params=params,
+            )(*operands, *new)
+
+        messages = () if last else (tile_shape(10),) * 2
+        new, *columns = make_planes(
+            lambda step, *refs: inner_kernel(step, last, *refs), extent_x - 2, (), (), (tile_shape(),) * 2
+        )
+        cross = pl.pallas_call(
+            lambda *refs: cross_kernel(count, *refs),
+            out_shape=tile_shape(9),
+            in_specs=in_vmem(count + 1) + in_any(1),
             out_specs=in_vmem(1)[0],
             compiler_params=params,
-        )(field, first, second)
-        side = send(side, along_x)
-        cross = pl.pallas_call(
-            lambda *refs: cross_kernel(count, *refs),
-            out_shape=tile_shape(11),
-            in_specs=in_vmem(2 + count),
-            out_specs=in_vmem(1)[0],
-            compiler_params=params,
-        )(field, own, first, second, *others, info)
-        cross = send(cross, along_x_or_flip)
-        columns = () if last else (tile_shape(),) * 2
-        inner = pl.pallas_call(
-            lambda *refs, step=step, last=last: inner_kernel(step, last, *refs),
-            out_shape=(tile_shape(27, extent_x), *columns),
-            in_specs=in_vmem(5),
-            out_specs=tuple(in_any(1) + in_vmem(len(columns))),
-            scratch_shapes=[
-                pltpu.VMEM((extent_x - 2, 27, 16, 128), jnp.float32),
-                pltpu.VMEM((27, 16, 128), jnp.float32),
-                pltpu.SemaphoreType.DMA((extent_x - 2,)),
-            ],
-            compiler_params=params,
-        )(field, vel, solid, first, second)
-        messages = () if last else (tile_shape(10),) * 2
-        outer = pl.pallas_call(
-            lambda *refs, step=step, last=last: outer_kernel(step, last, *refs),
-            out_shape=(tile_shape(27, extent_x), *messages),
-            in_specs=in_vmem(7) + in_any(1) + in_vmem(len(columns)),
-            out_specs=tuple(in_any(1) + in_vmem(len(messages))),
-            scratch_shapes=[
-                pltpu.VMEM((2, 27, 16, 128), jnp.float32),
-                pltpu.VMEM((27, 16, 128), jnp.float32),
-                pltpu.SemaphoreType.DMA((2,)),
-            ],
-            input_output_aliases={7: 0},
-            compiler_params=params,
-        )(field, vel, solid, first, second, side, cross, *inner)
-        if last:
-            field = outer[0]
-        else:
-            field, first, second = outer
+        )(own, first, second, *others, info, columns[0])
+        cross = send(cross, at_interface(flip))
+        field, *messages = make_planes(
+            outer_kernel, 2, (one, two, cross, *columns), (new,), messages
+        )
+        if not last:
+            first, second = messages
     return field[None]
 
 

time: 40.4 us -> 41.8 us (1.035)
  waiting for transfers between devices: 11.2 us -> 8.88 us
  starting transfers between devices: 19.3 us -> 21.4 us
  other arithmetic: 0.01 us -> 0.75 us
  local copies, waits for them, and re-layouts: 1.51 us -> 2.21 us
    ppermute x11 -> x13, waiting for transfers between devices: 11.2 us -> 8.88 us  [send(): return lax.ppermute(values, axes, pairs)]
    ppermute x11 -> x13, starting transfers between devices: 19.3 us -> 21.4 us  [send(): return lax.ppermute(values, axes, pairs)]
    transpose x1, other arithmetic: 0.01 us -> 0.74 us  [body(): jnp.moveaxis(code.astype(jnp.float32), -1, 0)]
    unnamed x15 -> x9, local copies, waits for them, and re-layouts: 1.51 us -> 2.21 us
  transfers between devices with their start and end apart: 11 -> 13, of which waited for: 5 -> 5; matrix products, arithmetic and copies ran while one was open for 0% -> 4% of each run, Pallas kernels for 13% -> 13%
where the time goes in v6:
time: 41.8 us; the launch traced here: 41.3 us
  starting transfers between devices  21.4 us (51%)
  waiting for transfers between devices  8.88 us (21%)
  Pallas kernels  7.89 us (19%)
  local copies, waits for them, and re-layouts  2.21 us (5%)
  other arithmetic  0.75 us (2%)
    ppermute x13, starting transfers between devices, send(): return lax.ppermute(values, axes, pairs)  21.4 us
    ppermute x13, waiting for transfers between devices, send(): return lax.ppermute(values, axes, pairs)  8.88 us
    pallas_call x4, Pallas kernels, make_planes(): pl.pallas_call(lambda *refs: kernel(step, *refs), out_shape=(tile_shape(2...  5.62 us
    unnamed x9, local copies, waits for them, and re-layouts  2.21 us
    pallas_call x1, Pallas kernels, body(): pl.pallas_call(velocity_kernel, out_shape=tile_shape(2, 3, extent_x), in_...  1.32 us
    pallas_call x1, Pallas kernels, body(): pl.pallas_call(pack_kernel, out_shape=(tile_shape(10),) * 2, in_specs=in_...  0.86 us
  transfers between devices with their start and end apart: 13, of which 5 were waited for; matrix products, arithmetic and copies ran while one was open for 4% of the time, Pallas kernels for 13%

profile of v6, /device:TPU:4, one launch (start us, length us, event | category | flops | bytes accessed | tf_op | source)
XLA Modules:
  0.0 41.3 jit_solution(8831076817176943697)
XLA Ops:
  0.0 1.5 %copy-done = f32[1,27,8,16,128]{4,3,2,1,0:T(8,128)S(1)} copy-done((f32[1,27,8,16,128]{4,3,2,1,0:T(8,128)S(1)}, f32[1,27,8,16,128]{4,3,2,1,0:T(8,128)}, u32[]{:S(2)}) %copy-start) | copy-done | bytes 1769496
  1.5 0.9 %shard_map.65 = (f32[10,16,128]{2,1,0:T(8,128)S(1)}, f32[10,16,128]{2,1,0:T(8,128)S(1)}) custom-call(f32[27,8,16,128]{3,2,1,0:T(8,128)S(1)} %bitcast.11), custom_call_target="tpu_custom_call" | custom-call | tf_op jit(solution)/shard_map/pallas_call | solution.py:379
  2.4 0.8 %collective-permute-start.4 = (f32[10,16,128]{2,1,0:T(8,128)S(1)}, f32[10,16,128]{2,1,0:T(8,128)S(1)}, u32[]{:S(2)}, u32[]{:S(2)}) collective-permute-start(f32[10,16,128]{2,1,0:T(8,128)S(1)} %get-tuple-element.20.refs_0_), channel_id=1, source_target_pairs={{12,14},{13,15},{14,12},{15,13},{28,30},{29,31},{30,28},{31,29}} | collective-permute-start | bytes 245768 | tf_op jit(solution)/shard_map/ppermute | solution.py:350
  3.2 1.6 %collective-permute-start = (f32[10,16,128]{2,1,0:T(8,128)S(1)}, f32[10,16,128]{2,1,0:T(8,128)S(1)}, u32[]{:S(2)}, u32[]{:S(2)}) collective-permute-start(f32[10,16,128]{2,1,0:T(8,128)S(1)} %get-tuple-element.20.refs_0_), channel_id=1, source_target_pairs={{0,1},{1,0},{2,3},{3,2},{4,5},{5,4},{6,7},{7,6},{8,9},{9,8},{10,11... | collective-permute-start | bytes 245768 | tf_op jit(solution)/shard_map/ppermute | solution.py:350
  4.8 2.5 %collective-permute-start.1 = (f32[10,16,128]{2,1,0:T(8,128)S(1)}, f32[10,16,128]{2,1,0:T(8,128)S(1)}, u32[]{:S(2)}, u32[]{:S(2)}) collective-permute-start(f32[10,16,128]{2,1,0:T(8,128)S(1)} %get-tuple-element.21), channel_id=1, source_target_pairs={{0,3},{1,2},{2,1},{3,0},{4,7},{5,6},{6,5},{7,4},{8,11},{9,10},{10,... | collective-permute-start | bytes 245768 | tf_op jit(solution)/shard_map/ppermute | solution.py:350
  7.3 0.7 %copy.21 = f32[1,16,128,2]{2,1,3,0:T(8,128)S(1)} copy(f32[1,16,128,2]{2,3,1,0:T(2,128)} %param.11) | data formatting | bytes 32768 | tf_op args[5]
  8.0 0.7 %fusion.1 = f32[2,16,128]{2,1,0:T(8,128)S(1)} fusion(s32[1,16,128,2]{2,3,1,0:T(2,128)} %param.10, s32[1,16,128,2]{2,3,1,0:T(2,128)} %param.9), kind=kLoop, calls=%fused_computation.4 | loop fusion | flops 12288 | bytes 49152 | tf_op jit(solution)/shard_map/transpose | solution.py:376
  9.4 2.0 %collective-permute-done.1.second.refs_4_.refs_2_ = f32[10,16,128]{2,1,0:T(8,128)S(1)} collective-permute-done((f32[10,16,128]{2,1,0:T(8,128)S(1)}, f32[10,16,128]{2,1,0:T(8,128)S(1)}, u32[]{:S(2)}, u32[]{:S(2)}) %collective-permute-start.1) | collective-permute-done | bytes 81952 | tf_op jit(solution)/shard_map/ppermute | solution.py:350
  11.5 5.0 %collective-permute-start.2 = (f32[11,16,128]{2,1,0:T(8,128)S(1)}, f32[11,16,128]{2,1,0:T(8,128)S(1)}, u32[]{:S(2)}, u32[]{:S(2)}) collective-permute-start(f32[11,16,128]{2,1,0:T(8,128)S(1)} %get-tuple-element.22), channel_id=1, source_target_pairs={{0,4},{1,5},{2,6},{3,7},{4,0},{5,1},{6,2},{7,3},{8,12},{9,13},{10,... | collective-permute-start | bytes 270344 | tf_op jit(solution)/shard_map/ppermute | solution.py:350
  16.5 2.0 %collective-permute-start.3 = (f32[11,16,128]{2,1,0:T(8,128)S(1)}, f32[11,16,128]{2,1,0:T(8,128)S(1)}, u32[]{:S(2)}, u32[]{:S(2)}) collective-permute-start(f32[11,16,128]{2,1,0:T(8,128)S(1)} %get-tuple-element.23), channel_id=1, source_target_pairs={{4,8},{5,9},{6,10},{7,11},{8,4},{9,5},{10,6},{11,7},{20,24},{21,25... | collective-permute-start | bytes 270344 | tf_op jit(solution)/shard_map/ppermute | solution.py:350
  18.5 1.3 %shard_map.64.refs_1_ = f32[2,3,8,16,128]{4,3,2,1,0:T(8,128)S(1)} custom-call(f32[2,1,27,8,16,128]{5,4,3,2,1,0:T(8,128)S(1)} %copy-done.2), custom_call_target="tpu_custom_call" | custom-call | tf_op jit(solution)/shard_map/pallas_call | solution.py:386
  19.9 2.1 %shard_map.67 = (f32[27,8,16,128]{3,2,1,0:T(8,128)S(1)}, f32[16,128]{1,0:T(8,128)S(1)}, f32[16,128]{1,0:T(8,128)S(1)}) custom-call(f32[27,8,16,128]{3,2,1,0:T(8,128)S(1)} %bitcast.13, f32[2,3,8,16,128]{4,3,2,1,0:T(8,128)S(1)} %shard_map.64.refs_1_, s32[1,8,16,128]{3,2,1,0:T(8,128)S(1)} %copy-done.3, ...), custom_call_target="tpu_custom_call" | custom-call | tf_op jit(solution)/shard_map/pallas_call | solution.py:415
  22.0 0.7 %collective-permute-start.6 = (f32[9,16,128]{2,1,0:T(8,128)S(1)}, f32[9,16,128]{2,1,0:T(8,128)S(1)}, u32[]{:S(2)}, u32[]{:S(2)}) collective-permute-start(f32[9,16,128]{2,1,0:T(8,128)S(1)} %shard_map.68), channel_id=1, source_target_pairs={{12,28},{13,29},{14,30},{15,31},{28,12},{29,13},{30,14},{31,15}} | collective-permute-start | bytes 221192 | tf_op jit(solution)/shard_map/ppermute | solution.py:350
  22.7 1.2 %collective-permute-done.3.refs_6_ = f32[11,16,128]{2,1,0:T(8,128)S(1)} collective-permute-done((f32[11,16,128]{2,1,0:T(8,128)S(1)}, f32[11,16,128]{2,1,0:T(8,128)S(1)}, u32[]{:S(2)}, u32[]{:S(2)}) %collective-permute-start.3) | collective-permute-done | bytes 90144 | tf_op jit(solution)/shard_map/ppermute | solution.py:350
  24.5 2.0 %collective-permute-start.8 = (f32[10,16,128]{2,1,0:T(8,128)S(1)}, f32[10,16,128]{2,1,0:T(8,128)S(1)}, u32[]{:S(2)}, u32[]{:S(2)}) collective-permute-start(f32[10,16,128]{2,1,0:T(8,128)S(1)} %get-tuple-element.29), channel_id=1, source_target_pairs={{0,3},{1,2},{2,1},{3,0},{4,7},{5,6},{6,5},{7,4},{8,11},{9,10},{10,... | collective-permute-start | bytes 245768 | tf_op jit(solution)/shard_map/ppermute | solution.py:350
  26.5 1.1 %collective-permute-start.7 = (f32[10,16,128]{2,1,0:T(8,128)S(1)}, f32[10,16,128]{2,1,0:T(8,128)S(1)}, u32[]{:S(2)}, u32[]{:S(2)}) collective-permute-start(f32[10,16,128]{2,1,0:T(8,128)S(1)} %get-tuple-element.28.refs_0_), channel_id=1, source_target_pairs={{0,1},{1,0},{2,3},{3,2},{4,5},{5,4},{6,7},{7,6},{8,9},{9,8},{10,11... | collective-permute-start | bytes 245768 | tf_op jit(solution)/shard_map/ppermute | solution.py:350
  28.3 2.6 %collective-permute-done.8.second.refs_4_.refs_2_ = f32[10,16,128]{2,1,0:T(8,128)S(1)} collective-permute-done((f32[10,16,128]{2,1,0:T(8,128)S(1)}, f32[10,16,128]{2,1,0:T(8,128)S(1)}, u32[]{:S(2)}, u32[]{:S(2)}) %collective-permute-start.8) | collective-permute-done | bytes 81952 | tf_op jit(solution)/shard_map/ppermute | solution.py:350
  30.9 0.8 %collective-permute-done.7.first.refs_3_.refs_1_ = f32[10,16,128]{2,1,0:T(8,128)S(1)} collective-permute-done((f32[10,16,128]{2,1,0:T(8,128)S(1)}, f32[10,16,128]{2,1,0:T(8,128)S(1)}, u32[]{:S(2)}, u32[]{:S(2)}) %collective-permute-start.7) | collective-permute-done | bytes 81952 | tf_op jit(solution)/shard_map/ppermute | solution.py:350
  31.7 1.2 %collective-permute-start.9 = (f32[11,16,128]{2,1,0:T(8,128)S(1)}, f32[11,16,128]{2,1,0:T(8,128)S(1)}, u32[]{:S(2)}, u32[]{:S(2)}) collective-permute-start(f32[11,16,128]{2,1,0:T(8,128)S(1)} %get-tuple-element.30), channel_id=1, source_target_pairs={{0,4},{1,5},{2,6},{3,7},{4,0},{5,1},{6,2},{7,3},{8,12},{9,13},{10,... | collective-permute-start | bytes 270344 | tf_op jit(solution)/shard_map/ppermute | solution.py:350
  33.0 2.5 %collective-permute-start.10 = (f32[11,16,128]{2,1,0:T(8,128)S(1)}, f32[11,16,128]{2,1,0:T(8,128)S(1)}, u32[]{:S(2)}, u32[]{:S(2)}) collective-permute-start(f32[11,16,128]{2,1,0:T(8,128)S(1)} %get-tuple-element.31), channel_id=1, source_target_pairs={{4,8},{5,9},{6,10},{7,11},{8,4},{9,5},{10,6},{11,7},{20,24},{21,25... | collective-permute-start | bytes 270344 | tf_op jit(solution)/shard_map/ppermute | solution.py:350
  35.5 1.9 %shard_map.71 = (f32[27,8,16,128]{3,2,1,0:T(8,128)}, f32[16,128]{1,0:T(8,128)S(1)}, f32[16,128]{1,0:T(8,128)S(1)}) custom-call(f32[27,8,16,128]{3,2,1,0:T(8,128)S(1)} %get-tuple-element.27.adj.refs_0_, f32[2,3,8,16,128]{4,3,2,1,0:T(8,128)S(1)} %shard_map.64.refs_1_, s32[1,8,16,128]{3,2,1,0:T(8,128)S(1)} %copy-done.3, ...), custom_call_target="tpu_custom_call" | custom-call | tf_op jit(solution)/shard_map/pallas_call | solution.py:415
  37.4 0.7 %collective-permute-start.12 = (f32[9,16,128]{2,1,0:T(8,128)S(1)}, f32[9,16,128]{2,1,0:T(8,128)S(1)}, u32[]{:S(2)}, u32[]{:S(2)}) collective-permute-start(f32[9,16,128]{2,1,0:T(8,128)S(1)} %shard_map.72), channel_id=1, source_target_pairs={{12,28},{13,29},{14,30},{15,31},{28,12},{29,13},{30,14},{31,15}} | collective-permute-start | bytes 221192 | tf_op jit(solution)/shard_map/ppermute | solution.py:350
  38.1 2.2 %collective-permute-done.10.refs_6_ = f32[11,16,128]{2,1,0:T(8,128)S(1)} collective-permute-done((f32[11,16,128]{2,1,0:T(8,128)S(1)}, f32[11,16,128]{2,1,0:T(8,128)S(1)}, u32[]{:S(2)}, u32[]{:S(2)}) %collective-permute-start.10) | collective-permute-done | bytes 90144 | tf_op jit(solution)/shard_map/ppermute | solution.py:350
  40.3 1.0 %shard_map.73 = f32[27,8,16,128]{3,2,1,0:T(8,128)} custom-call(f32[27,8,16,128]{3,2,1,0:T(8,128)S(1)} %get-tuple-element.27.adj.refs_0_, f32[2,3,8,16,128]{4,3,2,1,0:T(8,128)S(1)} %shard_map.64.refs_1_, s32[1,8,16,128]{3,2,1,0:T(8,128)S(1)} %copy-done.3, ...), custom_call_target="tpu_custom_call", output_to_operand_aliasing={{}: (10, {})} | custom-call | tf_op jit(solution)/shard_map/pallas_call | solution.py:415
  (23 shorter events, 2.0 us)
Async XLA Ops:
  0.0 1.5 %copy-start = (f32[1,27,8,16,128]{4,3,2,1,0:T(8,128)S(1)}, f32[1,27,8,16,128]{4,3,2,1,0:T(8,128)}, u32[]{:S(2)}) copy-start(f32[1,27,8,16,128]{4,3,2,1,0:T(8,128)} %param.6) | copy-start | bytes 5308420
  1.5 17.0 %copy-start.2 = (f32[2,1,27,8,16,128]{5,4,3,2,1,0:T(8,128)S(1)}, f32[2,1,27,8,16,128]{5,4,3,2,1,0:T(8,128)}, u32[]{:S(2)}) copy-start(f32[2,1,27,8,16,128]{5,4,3,2,1,0:T(8,128)} %saved.1) | copy-start | bytes 10616836
  2.4 19.6 %collective-permute-start.4 = (f32[10,16,128]{2,1,0:T(8,128)S(1)}, f32[10,16,128]{2,1,0:T(8,128)S(1)}, u32[]{:S(2)}, u32[]{:S(2)}) collective-permute-start(f32[10,16,128]{2,1,0:T(8,128)S(1)} %get-tuple-element.20.refs_0_), channel_id=1, source_target_pairs={{12,14},{13,15},{14,12},{15,13},{28,30},{29,31},{30,28},{31,29}} | collective-permute-start | bytes 245768 | tf_op jit(solution)/shard_map/ppermute | solution.py:350
  3.2 8.3 %collective-permute-start = (f32[10,16,128]{2,1,0:T(8,128)S(1)}, f32[10,16,128]{2,1,0:T(8,128)S(1)}, u32[]{:S(2)}, u32[]{:S(2)}) collective-permute-start(f32[10,16,128]{2,1,0:T(8,128)S(1)} %get-tuple-element.20.refs_0_), channel_id=1, source_target_pairs={{0,1},{1,0},{2,3},{3,2},{4,5},{5,4},{6,7},{7,6},{8,9},{9,8},{10,11... | collective-permute-start | bytes 245768 | tf_op jit(solution)/shard_map/ppermute | solution.py:350
  4.8 6.6 %collective-permute-start.1 = (f32[10,16,128]{2,1,0:T(8,128)S(1)}, f32[10,16,128]{2,1,0:T(8,128)S(1)}, u32[]{:S(2)}, u32[]{:S(2)}) collective-permute-start(f32[10,16,128]{2,1,0:T(8,128)S(1)} %get-tuple-element.21), channel_id=1, source_target_pairs={{0,3},{1,2},{2,1},{3,0},{4,7},{5,6},{6,5},{7,4},{8,11},{9,10},{10,... | collective-permute-start | bytes 245768 | tf_op jit(solution)/shard_map/ppermute | solution.py:350
  8.7 13.2 %collective-permute-start.5 = (f32[4,16,128]{2,1,0:T(8,128)S(1)}, f32[4,16,128]{2,1,0:T(8,128)S(1)}, u32[]{:S(2)}, u32[]{:S(2)}) collective-permute-start(f32[4,16,128]{2,1,0:T(8,128)S(1)} %pad_maximum_fusion), channel_id=1, source_target_pairs={{12,28},{13,29},{14,30},{15,31},{28,12},{29,13},{30,14},{31,15}} | collective-permute-start | bytes 98312 | tf_op jit(solution)/shard_map/ppermute | solution.py:350
  11.5 11.2 %collective-permute-start.2 = (f32[11,16,128]{2,1,0:T(8,128)S(1)}, f32[11,16,128]{2,1,0:T(8,128)S(1)}, u32[]{:S(2)}, u32[]{:S(2)}) collective-permute-start(f32[11,16,128]{2,1,0:T(8,128)S(1)} %get-tuple-element.22), channel_id=1, source_target_pairs={{0,4},{1,5},{2,6},{3,7},{4,0},{5,1},{6,2},{7,3},{8,12},{9,13},{10,... | collective-permute-start | bytes 270344 | tf_op jit(solution)/shard_map/ppermute | solution.py:350
  16.5 3.4 %copy-start.1 = (f32[1,27,8,16,128]{4,3,2,1,0:T(8,128)S(1)}, f32[1,27,8,16,128]{4,3,2,1,0:T(8,128)}, u32[]{:S(2)}) copy-start(f32[1,27,8,16,128]{4,3,2,1,0:T(8,128)} %param.6) | copy-start | bytes 5308420
  16.5 3.4 %copy-start.3 = (s32[1,8,16,128]{3,2,1,0:T(8,128)S(1)}, s32[1,8,16,128]{3,2,1,0:T(8,128)}, u32[]{:S(2)}) copy-start(s32[1,8,16,128]{3,2,1,0:T(8,128)} %refs_2_.7) | copy-start | bytes 196612
  16.5 7.4 %collective-permute-start.3 = (f32[11,16,128]{2,1,0:T(8,128)S(1)}, f32[11,16,128]{2,1,0:T(8,128)S(1)}, u32[]{:S(2)}, u32[]{:S(2)}) collective-permute-start(f32[11,16,128]{2,1,0:T(8,128)S(1)} %get-tuple-element.23), channel_id=1, source_target_pairs={{4,8},{5,9},{6,10},{7,11},{8,4},{9,5},{10,6},{11,7},{20,24},{21,25... | collective-permute-start | bytes 270344 | tf_op jit(solution)/shard_map/ppermute | solution.py:350
  22.0 0.7 %collective-permute-start.6 = (f32[9,16,128]{2,1,0:T(8,128)S(1)}, f32[9,16,128]{2,1,0:T(8,128)S(1)}, u32[]{:S(2)}, u32[]{:S(2)}) collective-permute-start(f32[9,16,128]{2,1,0:T(8,128)S(1)} %shard_map.68), channel_id=1, source_target_pairs={{12,28},{13,29},{14,30},{15,31},{28,12},{29,13},{30,14},{31,15}} | collective-permute-start | bytes 221192 | tf_op jit(solution)/shard_map/ppermute | solution.py:350
  24.5 6.4 %collective-permute-start.8 = (f32[10,16,128]{2,1,0:T(8,128)S(1)}, f32[10,16,128]{2,1,0:T(8,128)S(1)}, u32[]{:S(2)}, u32[]{:S(2)}) collective-permute-start(f32[10,16,128]{2,1,0:T(8,128)S(1)} %get-tuple-element.29), channel_id=1, source_target_pairs={{0,3},{1,2},{2,1},{3,0},{4,7},{5,6},{6,5},{7,4},{8,11},{9,10},{10,... | collective-permute-start | bytes 245768 | tf_op jit(solution)/shard_map/ppermute | solution.py:350
  26.5 5.2 %collective-permute-start.7 = (f32[10,16,128]{2,1,0:T(8,128)S(1)}, f32[10,16,128]{2,1,0:T(8,128)S(1)}, u32[]{:S(2)}, u32[]{:S(2)}) collective-permute-start(f32[10,16,128]{2,1,0:T(8,128)S(1)} %get-tuple-element.28.refs_0_), channel_id=1, source_target_pairs={{0,1},{1,0},{2,3},{3,2},{4,5},{5,4},{6,7},{7,6},{8,9},{9,8},{10,11... | collective-permute-start | bytes 245768 | tf_op jit(solution)/shard_map/ppermute | solution.py:350
  27.6 9.8 %collective-permute-start.11 = (f32[10,16,128]{2,1,0:T(8,128)S(1)}, f32[10,16,128]{2,1,0:T(8,128)S(1)}, u32[]{:S(2)}, u32[]{:S(2)}) collective-permute-start(f32[10,16,128]{2,1,0:T(8,128)S(1)} %get-tuple-element.28.refs_0_), channel_id=1, source_target_pairs={{12,14},{13,15},{14,12},{15,13},{28,30},{29,31},{30,28},{31,29}} | collective-permute-start | bytes 245768 | tf_op jit(solution)/shard_map/ppermute | solution.py:350
  31.7 6.4 %collective-permute-start.9 = (f32[11,16,128]{2,1,0:T(8,128)S(1)}, f32[11,16,128]{2,1,0:T(8,128)S(1)}, u32[]{:S(2)}, u32[]{:S(2)}) collective-permute-start(f32[11,16,128]{2,1,0:T(8,128)S(1)} %get-tuple-element.30), channel_id=1, source_target_pairs={{0,4},{1,5},{2,6},{3,7},{4,0},{5,1},{6,2},{7,3},{8,12},{9,13},{10,... | collective-permute-start | bytes 270344 | tf_op jit(solution)/shard_map/ppermute | solution.py:350
  33.0 7.3 %collective-permute-start.10 = (f32[11,16,128]{2,1,0:T(8,128)S(1)}, f32[11,16,128]{2,1,0:T(8,128)S(1)}, u32[]{:S(2)}, u32[]{:S(2)}) collective-permute-start(f32[11,16,128]{2,1,0:T(8,128)S(1)} %get-tuple-element.31), channel_id=1, source_target_pairs={{4,8},{5,9},{6,10},{7,11},{8,4},{9,5},{10,6},{11,7},{20,24},{21,25... | collective-permute-start | bytes 270344 | tf_op jit(solution)/shard_map/ppermute | solution.py:350
  37.4 0.7 %collective-permute-start.12 = (f32[9,16,128]{2,1,0:T(8,128)S(1)}, f32[9,16,128]{2,1,0:T(8,128)S(1)}, u32[]{:S(2)}, u32[]{:S(2)}) collective-permute-start(f32[9,16,128]{2,1,0:T(8,128)S(1)} %shard_map.72), channel_id=1, source_target_pairs={{12,28},{13,29},{14,30},{15,31},{28,12},{29,13},{30,14},{31,15}} | collective-permute-start | bytes 221192 | tf_op jit(solution)/shard_map/ppermute | solution.py:350

commit v7 on v6

--- a/solution.py
+++ b/solution.py
@@ -69,6 +69,12 @@
     write_messages(lambda j: adj[j, extent_x - 1], low, high, first_out, second_out)
 
 
+def info_kernel(device, cell, weight, out):
+    for k in range(2):
+        out[k] = (device[:, k] * 128 + cell[:, k]).astype(jnp.float32)
+        out[2 + k] = weight[:, k]
+
+
 def velocity_kernel(saved, out, kept, sems):
     steps, _, _, extent_x = saved.shape[:4]
 
@@ -88,7 +94,7 @@
     lax.fori_loop(0, total, one, 0)
 
 
-def side_kernel(adj, first, second, one_out, two_out):
+def side_kernel(adj, first, second, _, two_out, one_out):
     extent_x = adj.shape[1]
     even = is_even("gx")
     for j in range(9):
@@ -274,7 +280,7 @@
     lax.fori_loop(1, extent_x - 1, lambda x, c: (save(x).wait(), c)[1], 0)
 
 
-def outer_kernel(step, adj, vel, solid, first, second, one, two, cross, *rest):
+def outer_kernel(step, adj, vel, solid, first, second, two, one, cross, *rest):
     *rest, made, pulled, sems = rest
     low_in, high_in, _, out, *messages = rest
     extent_x = adj.shape[1]
@@ -371,10 +377,13 @@
 
         return target
 
-    code = band_device[0] * 128 + band_cell[0]
-    info = jnp.concatenate(
-        [jnp.moveaxis(code.astype(jnp.float32), -1, 0), jnp.moveaxis(band_weight[0], -1, 0)]
-    )
+    info = pl.pallas_call(
+        info_kernel,
+        out_shape=tile_shape(4),
+        in_specs=in_vmem(3),
+        out_specs=in_vmem(1)[0],
+        compiler_params=params,
+    )(*[jnp.swapaxes(array[0], 1, 2) for array in (band_device, band_cell, band_weight)])
     info = send(info, at_interface(flip))
     first, second = pl.pallas_call(
         pack_kernel,
@@ -400,13 +409,13 @@
         first = send(own, along_z(0))
         second = send(second, along_z(1))
         others = [send(own, at_interface(hop_z(hop))) for hop in range(2, count - 1)]
-        one, two = pl.pallas_call(
+        two, one = pl.pallas_call(
             side_kernel,
             out_shape=(tile_shape(11),) * 2,
-            in_specs=in_vmem(3),
+            in_specs=in_vmem(3) + in_any(1),
             out_specs=tuple(in_vmem(2)),
             compiler_params=params,
-        )(field, first, second)
+        )(field, first, second, vel)
         two = send(two, along_x(1))
         one = send(one, along_x(0))
 
@@ -427,19 +436,28 @@
             )(*operands, *new)
 
         messages = () if last else (tile_shape(10),) * 2
-        new, *columns = make_planes(
-            lambda step, *refs: inner_kernel(step, last, *refs), extent_x - 2, (), (), (tile_shape(),) * 2
-        )
-        cross = pl.pallas_call(
-            lambda *refs: cross_kernel(count, *refs),
-            out_shape=tile_shape(9),
-            in_specs=in_vmem(count + 1) + in_any(1),
-            out_specs=in_vmem(1)[0],
-            compiler_params=params,
-        )(own, first, second, *others, info, columns[0])
+        def make_inner():
+            kernel = lambda step, *refs: inner_kernel(step, last, *refs)
+            return make_planes(kernel, extent_x - 2, (), (), (tile_shape(),) * 2)
+
+        def make_cross(after):
+            return pl.pallas_call(
+                lambda *refs: cross_kernel(count, *refs),
+                out_shape=tile_shape(9),
+                in_specs=in_vmem(count + 1) + in_any(1),
+                out_specs=in_vmem(1)[0],
+                compiler_params=params,
+            )(own, first, second, *others, info, after)
+
+        if last:
+            new, *columns = make_inner()
+            cross = make_cross(columns[0])
+        else:
+            cross = make_cross(vel)
+            new, *columns = make_inner()
         cross = send(cross, at_interface(flip))
         field, *messages = make_planes(
-            outer_kernel, 2, (one, two, cross, *columns), (new,), messages
+            outer_kernel, 2, (two, one, cross, *columns), (new,), messages
         )
         if not last:
             first, second = messages

time: 41.8 us -> 40.2 us (0.962)
  the two profiles are of different devices: /device:TPU:4 before, /device:TPU:0 now
where the time goes in v7:
time: 40.2 us; the launch traced here: 39.9 us
  starting transfers between devices  21.8 us (54%)
  Pallas kernels  7.88 us (20%)
  waiting for transfers between devices  6.47 us (16%)
  local copies, waits for them, and re-layouts  3.5 us (9%)
    ppermute x13, starting transfers between devices, send(): return lax.ppermute(values, axes, pairs)  21.8 us
    ppermute x13, waiting for transfers between devices, send(): return lax.ppermute(values, axes, pairs)  6.47 us
    pallas_call x4, Pallas kernels, make_planes(): pl.pallas_call(lambda *refs: kernel(step, *refs), out_shape=(tile_shape(2...  5.61 us
    unnamed x14, local copies, waits for them, and re-layouts  3.5 us
    pallas_call x1, Pallas kernels, body(): pl.pallas_call(velocity_kernel, out_shape=tile_shape(2, 3, extent_x), in_...  1.31 us
    pallas_call x1, Pallas kernels, body(): pl.pallas_call(pack_kernel, out_shape=(tile_shape(10),) * 2, in_specs=in_...  0.86 us
  transfers between devices with their start and end apart: 13, of which 4 were waited for; matrix products, arithmetic and copies ran while one was open for 0% of the time, Pallas kernels for 14%

profile of v7, /device:TPU:0, one launch (start us, length us, event | category | flops | bytes accessed | tf_op | source)
XLA Modules:
  0.0 39.9 jit_solution(15424072993316197865)
XLA Ops:
  0.0 1.5 %copy-done = f32[1,27,8,16,128]{4,3,2,1,0:T(8,128)S(1)} copy-done((f32[1,27,8,16,128]{4,3,2,1,0:T(8,128)S(1)}, f32[1,27,8,16,128]{4,3,2,1,0:T(8,128)}, u32[]{:S(2)}) %copy-start) | copy-done | bytes 1769496
  1.5 0.9 %shard_map.65 = (f32[10,16,128]{2,1,0:T(8,128)S(1)}, f32[10,16,128]{2,1,0:T(8,128)S(1)}) custom-call(f32[27,8,16,128]{3,2,1,0:T(8,128)S(1)} %bitcast.11), custom_call_target="tpu_custom_call" | custom-call | tf_op jit(solution)/shard_map/pallas_call | solution.py:388
  2.4 5.1 %collective-permute-start.1 = (f32[10,16,128]{2,1,0:T(8,128)S(1)}, f32[10,16,128]{2,1,0:T(8,128)S(1)}, u32[]{:S(2)}, u32[]{:S(2)}) collective-permute-start(f32[10,16,128]{2,1,0:T(8,128)S(1)} %get-tuple-element.21), channel_id=1, source_target_pairs={{0,3},{1,2},{2,1},{3,0},{4,7},{5,6},{6,5},{7,4},{8,11},{9,10},{10,... | collective-permute-start | bytes 245768 | tf_op jit(solution)/shard_map/ppermute | solution.py:356
  7.5 0.7 %collective-permute-start.4 = (f32[10,16,128]{2,1,0:T(8,128)S(1)}, f32[10,16,128]{2,1,0:T(8,128)S(1)}, u32[]{:S(2)}, u32[]{:S(2)}) collective-permute-start(f32[10,16,128]{2,1,0:T(8,128)S(1)} %get-tuple-element.20.refs_0_), channel_id=1, source_target_pairs={{12,14},{13,15},{14,12},{15,13},{28,30},{29,31},{30,28},{31,29}} | collective-permute-start | bytes 245768 | tf_op jit(solution)/shard_map/ppermute | solution.py:356
  8.2 0.8 %collective-permute-start.5 = (f32[4,16,128]{2,1,0:T(8,128)S(1)}, f32[4,16,128]{2,1,0:T(8,128)S(1)}, u32[]{:S(2)}, u32[]{:S(2)}) collective-permute-start(f32[4,16,128]{2,1,0:T(8,128)S(1)} %shard_map.67), channel_id=1, source_target_pairs={{12,28},{13,29},{14,30},{15,31},{28,12},{29,13},{30,14},{31,15}} | collective-permute-start | bytes 98312 | tf_op jit(solution)/shard_map/ppermute | solution.py:356
  9.0 2.0 %copy-done.2 = f32[2,1,27,8,16,128]{5,4,3,2,1,0:T(8,128)S(1)} copy-done((f32[2,1,27,8,16,128]{5,4,3,2,1,0:T(8,128)S(1)}, f32[2,1,27,8,16,128]{5,4,3,2,1,0:T(8,128)}, u32[]{:S(2)}) %copy-start.2) | copy-done | bytes 3538968
  11.0 1.3 %shard_map.64._.refs_5_.refs_1_ = f32[2,3,8,16,128]{4,3,2,1,0:T(8,128)S(1)} custom-call(f32[2,1,27,8,16,128]{5,4,3,2,1,0:T(8,128)S(1)} %copy-done.2), custom_call_target="tpu_custom_call" | custom-call | tf_op jit(solution)/shard_map/pallas_call | solution.py:395
  12.4 0.7 %collective-permute-start.2 = (f32[11,16,128]{2,1,0:T(8,128)S(1)}, f32[11,16,128]{2,1,0:T(8,128)S(1)}, u32[]{:S(2)}, u32[]{:S(2)}) collective-permute-start(f32[11,16,128]{2,1,0:T(8,128)S(1)} %get-tuple-element.22), channel_id=1, source_target_pairs={{4,8},{5,9},{6,10},{7,11},{8,4},{9,5},{10,6},{11,7},{20,24},{21,25... | collective-permute-start | bytes 270344 | tf_op jit(solution)/shard_map/ppermute | solution.py:356
  13.1 4.3 %collective-permute-start.3 = (f32[11,16,128]{2,1,0:T(8,128)S(1)}, f32[11,16,128]{2,1,0:T(8,128)S(1)}, u32[]{:S(2)}, u32[]{:S(2)}) collective-permute-start(f32[11,16,128]{2,1,0:T(8,128)S(1)} %get-tuple-element.23), channel_id=1, source_target_pairs={{0,4},{1,5},{2,6},{3,7},{4,0},{5,1},{6,2},{7,3},{8,12},{9,13},{10,... | collective-permute-start | bytes 270344 | tf_op jit(solution)/shard_map/ppermute | solution.py:356
  17.4 0.7 %collective-permute-start.6 = (f32[9,16,128]{2,1,0:T(8,128)S(1)}, f32[9,16,128]{2,1,0:T(8,128)S(1)}, u32[]{:S(2)}, u32[]{:S(2)}) collective-permute-start(f32[9,16,128]{2,1,0:T(8,128)S(1)} %shard_map.68), channel_id=1, source_target_pairs={{12,28},{13,29},{14,30},{15,31},{28,12},{29,13},{30,14},{31,15}} | collective-permute-start | bytes 221192 | tf_op jit(solution)/shard_map/ppermute | solution.py:356
  18.1 2.1 %shard_map.69 = (f32[27,8,16,128]{3,2,1,0:T(8,128)S(1)}, f32[16,128]{1,0:T(8,128)S(1)}, f32[16,128]{1,0:T(8,128)S(1)}) custom-call(f32[27,8,16,128]{3,2,1,0:T(8,128)S(1)} %bitcast.13, f32[2,3,8,16,128]{4,3,2,1,0:T(8,128)S(1)} %shard_map.64._.refs_5_.refs_1_, s32[1,8,16,128]{3,2,1,0:T(8,128)S(1)} %copy-done.3, ...), custom_call_target="tpu_custom_call" | custom-call | tf_op jit(solution)/shard_map/pallas_call | solution.py:424
  20.2 1.1 %collective-permute-done.3.refs_6_ = f32[11,16,128]{2,1,0:T(8,128)S(1)} collective-permute-done((f32[11,16,128]{2,1,0:T(8,128)S(1)}, f32[11,16,128]{2,1,0:T(8,128)S(1)}, u32[]{:S(2)}, u32[]{:S(2)}) %collective-permute-start.3) | collective-permute-done | bytes 90144 | tf_op jit(solution)/shard_map/ppermute | solution.py:356
  21.3 0.6 %shard_map.70 = (f32[27,8,16,128]{3,2,1,0:T(8,128)S(1)}, f32[10,16,128]{2,1,0:T(8,128)S(1)}, f32[10,16,128]{2,1,0:T(8,128)S(1)}) custom-call(f32[27,8,16,128]{3,2,1,0:T(8,128)S(1)} %bitcast.14, f32[2,3,8,16,128]{4,3,2,1,0:T(8,128)S(1)} %shard_map.64._.refs_5_.refs_1_, s32[1,8,16,128]{3,2,1,0:T(8,128)S(1)} %copy-done.3, ...), custom_call_target="tpu_custom_call", output_to_operand_aliasing={{0}: (10, {})} | custom-call | tf_op jit(solution)/shard_map/pallas_call | solution.py:424
  21.9 1.5 %collective-permute-start.8 = (f32[10,16,128]{2,1,0:T(8,128)S(1)}, f32[10,16,128]{2,1,0:T(8,128)S(1)}, u32[]{:S(2)}, u32[]{:S(2)}) collective-permute-start(f32[10,16,128]{2,1,0:T(8,128)S(1)} %get-tuple-element.29), channel_id=1, source_target_pairs={{0,3},{1,2},{2,1},{3,0},{4,7},{5,6},{6,5},{7,4},{8,11},{9,10},{10,... | collective-permute-start | bytes 245768 | tf_op jit(solution)/shard_map/ppermute | solution.py:356
  23.4 0.4 collective-permute-start.7
  23.8 0.7 %collective-permute-start.11 = (f32[10,16,128]{2,1,0:T(8,128)S(1)}, f32[10,16,128]{2,1,0:T(8,128)S(1)}, u32[]{:S(2)}, u32[]{:S(2)}) collective-permute-start(f32[10,16,128]{2,1,0:T(8,128)S(1)} %get-tuple-element.28.refs_0_), channel_id=1, source_target_pairs={{12,14},{13,15},{14,12},{15,13},{28,30},{29,31},{30,28},{31,29}} | collective-permute-start | bytes 245768 | tf_op jit(solution)/shard_map/ppermute | solution.py:356
  24.5 3.9 %collective-permute-done.8.second.refs_4_.refs_2_ = f32[10,16,128]{2,1,0:T(8,128)S(1)} collective-permute-done((f32[10,16,128]{2,1,0:T(8,128)S(1)}, f32[10,16,128]{2,1,0:T(8,128)S(1)}, u32[]{:S(2)}, u32[]{:S(2)}) %collective-permute-start.8) | collective-permute-done | bytes 81952 | tf_op jit(solution)/shard_map/ppermute | solution.py:356
  28.4 0.4 collective-permute-done.7.first.refs_3_.refs_1_
  28.7 0.7 %collective-permute-start.9 = (f32[11,16,128]{2,1,0:T(8,128)S(1)}, f32[11,16,128]{2,1,0:T(8,128)S(1)}, u32[]{:S(2)}, u32[]{:S(2)}) collective-permute-start(f32[11,16,128]{2,1,0:T(8,128)S(1)} %get-tuple-element.30), channel_id=1, source_target_pairs={{4,8},{5,9},{6,10},{7,11},{8,4},{9,5},{10,6},{11,7},{20,24},{21,25... | collective-permute-start | bytes 270344 | tf_op jit(solution)/shard_map/ppermute | solution.py:356
  29.4 5.7 %collective-permute-start.10 = (f32[11,16,128]{2,1,0:T(8,128)S(1)}, f32[11,16,128]{2,1,0:T(8,128)S(1)}, u32[]{:S(2)}, u32[]{:S(2)}) collective-permute-start(f32[11,16,128]{2,1,0:T(8,128)S(1)} %get-tuple-element.31), channel_id=1, source_target_pairs={{0,4},{1,5},{2,6},{3,7},{4,0},{5,1},{6,2},{7,3},{8,12},{9,13},{10,... | collective-permute-start | bytes 270344 | tf_op jit(solution)/shard_map/ppermute | solution.py:356
  35.1 1.9 %shard_map.72 = (f32[27,8,16,128]{3,2,1,0:T(8,128)}, f32[16,128]{1,0:T(8,128)S(1)}, f32[16,128]{1,0:T(8,128)S(1)}) custom-call(f32[27,8,16,128]{3,2,1,0:T(8,128)S(1)} %get-tuple-element.27.adj.refs_0_, f32[2,3,8,16,128]{4,3,2,1,0:T(8,128)S(1)} %shard_map.64._.refs_5_.refs_1_, s32[1,8,16,128]{3,2,1,0:T(8,128)S(1)} %copy-done.3, ...), custom_call_target="tpu_custom_call" | custom-call | tf_op jit(solution)/shard_map/pallas_call | solution.py:424
  37.1 0.7 %collective-permute-start.12 = (f32[9,16,128]{2,1,0:T(8,128)S(1)}, f32[9,16,128]{2,1,0:T(8,128)S(1)}, u32[]{:S(2)}, u32[]{:S(2)}) collective-permute-start(f32[9,16,128]{2,1,0:T(8,128)S(1)} %shard_map.73), channel_id=1, source_target_pairs={{12,28},{13,29},{14,30},{15,31},{28,12},{29,13},{30,14},{31,15}} | collective-permute-start | bytes 221192 | tf_op jit(solution)/shard_map/ppermute | solution.py:356
  37.8 1.1 %collective-permute-done.10.refs_6_ = f32[11,16,128]{2,1,0:T(8,128)S(1)} collective-permute-done((f32[11,16,128]{2,1,0:T(8,128)S(1)}, f32[11,16,128]{2,1,0:T(8,128)S(1)}, u32[]{:S(2)}, u32[]{:S(2)}) %collective-permute-start.10) | collective-permute-done | bytes 90144 | tf_op jit(solution)/shard_map/ppermute | solution.py:356
  38.8 1.0 %shard_map.74 = f32[27,8,16,128]{3,2,1,0:T(8,128)} custom-call(f32[27,8,16,128]{3,2,1,0:T(8,128)S(1)} %get-tuple-element.27.adj.refs_0_, f32[2,3,8,16,128]{4,3,2,1,0:T(8,128)S(1)} %shard_map.64._.refs_5_.refs_1_, s32[1,8,16,128]{3,2,1,0:T(8,128)S(1)} %copy-done.3, ...), custom_call_target="tpu_custom_call", output_to_operand_aliasing={{}: (10, {})} | custom-call | tf_op jit(solution)/shard_map/pallas_call | solution.py:424
  (27 shorter events, 0.2 us)
Async XLA Ops:
  0.0 1.5 %copy-start = (f32[1,27,8,16,128]{4,3,2,1,0:T(8,128)S(1)}, f32[1,27,8,16,128]{4,3,2,1,0:T(8,128)}, u32[]{:S(2)}) copy-start(f32[1,27,8,16,128]{4,3,2,1,0:T(8,128)} %param.6) | copy-start | bytes 5308420
  1.5 6.7 %copy-start.4 = (s32[1,16,128,2]{2,3,1,0:T(2,128)S(1)}, s32[1,16,128,2]{2,3,1,0:T(2,128)}, u32[]{:S(2)}) copy-start(s32[1,16,128,2]{2,3,1,0:T(2,128)} %param.9) | copy-start | bytes 49156
  1.5 6.7 %copy-start.5 = (s32[1,16,128,2]{2,3,1,0:T(2,128)S(1)}, s32[1,16,128,2]{2,3,1,0:T(2,128)}, u32[]{:S(2)}) copy-start(s32[1,16,128,2]{2,3,1,0:T(2,128)} %param.10) | copy-start | bytes 49156
  1.5 6.7 %copy-start.6 = (f32[1,16,128,2]{2,3,1,0:T(2,128)S(1)}, f32[1,16,128,2]{2,3,1,0:T(2,128)}, u32[]{:S(2)}) copy-start(f32[1,16,128,2]{2,3,1,0:T(2,128)} %param.11) | copy-start | bytes 49156
  2.4 10.0 %collective-permute-start.1 = (f32[10,16,128]{2,1,0:T(8,128)S(1)}, f32[10,16,128]{2,1,0:T(8,128)S(1)}, u32[]{:S(2)}, u32[]{:S(2)}) collective-permute-start(f32[10,16,128]{2,1,0:T(8,128)S(1)} %get-tuple-element.21), channel_id=1, source_target_pairs={{0,3},{1,2},{2,1},{3,0},{4,7},{5,6},{6,5},{7,4},{8,11},{9,10},{10,... | collective-permute-start | bytes 245768 | tf_op jit(solution)/shard_map/ppermute | solution.py:356
  7.5 4.9 %collective-permute-start = (f32[10,16,128]{2,1,0:T(8,128)S(1)}, f32[10,16,128]{2,1,0:T(8,128)S(1)}, u32[]{:S(2)}, u32[]{:S(2)}) collective-permute-start(f32[10,16,128]{2,1,0:T(8,128)S(1)} %get-tuple-element.20.refs_0_), channel_id=1, source_target_pairs={{0,1},{1,0},{2,3},{3,2},{4,5},{5,4},{6,7},{7,6},{8,9},{9,8},{10,11... | collective-permute-start | bytes 245768 | tf_op jit(solution)/shard_map/ppermute | solution.py:356
  7.5 9.9 %collective-permute-start.4 = (f32[10,16,128]{2,1,0:T(8,128)S(1)}, f32[10,16,128]{2,1,0:T(8,128)S(1)}, u32[]{:S(2)}, u32[]{:S(2)}) collective-permute-start(f32[10,16,128]{2,1,0:T(8,128)S(1)} %get-tuple-element.20.refs_0_), channel_id=1, source_target_pairs={{12,14},{13,15},{14,12},{15,13},{28,30},{29,31},{30,28},{31,29}} | collective-permute-start | bytes 245768 | tf_op jit(solution)/shard_map/ppermute | solution.py:356
  8.2 4.2 %copy-start.1 = (f32[1,27,8,16,128]{4,3,2,1,0:T(8,128)S(1)}, f32[1,27,8,16,128]{4,3,2,1,0:T(8,128)}, u32[]{:S(2)}) copy-start(f32[1,27,8,16,128]{4,3,2,1,0:T(8,128)} %param.6) | copy-start | bytes 5308420
  8.2 9.2 %collective-permute-start.5 = (f32[4,16,128]{2,1,0:T(8,128)S(1)}, f32[4,16,128]{2,1,0:T(8,128)S(1)}, u32[]{:S(2)}, u32[]{:S(2)}) collective-permute-start(f32[4,16,128]{2,1,0:T(8,128)S(1)} %shard_map.67), channel_id=1, source_target_pairs={{12,28},{13,29},{14,30},{15,31},{28,12},{29,13},{30,14},{31,15}} | collective-permute-start | bytes 98312 | tf_op jit(solution)/shard_map/ppermute | solution.py:356
  9.0 2.0 %copy-start.2 = (f32[2,1,27,8,16,128]{5,4,3,2,1,0:T(8,128)S(1)}, f32[2,1,27,8,16,128]{5,4,3,2,1,0:T(8,128)}, u32[]{:S(2)}) copy-start(f32[2,1,27,8,16,128]{5,4,3,2,1,0:T(8,128)} %saved.1) | copy-start | bytes 10616836
  12.3 5.7 %copy-start.3 = (s32[1,8,16,128]{3,2,1,0:T(8,128)S(1)}, s32[1,8,16,128]{3,2,1,0:T(8,128)}, u32[]{:S(2)}) copy-start(s32[1,8,16,128]{3,2,1,0:T(8,128)} %refs_2_.7) | copy-start | bytes 196612
  12.4 7.7 %collective-permute-start.2 = (f32[11,16,128]{2,1,0:T(8,128)S(1)}, f32[11,16,128]{2,1,0:T(8,128)S(1)}, u32[]{:S(2)}, u32[]{:S(2)}) collective-permute-start(f32[11,16,128]{2,1,0:T(8,128)S(1)} %get-tuple-element.22), channel_id=1, source_target_pairs={{4,8},{5,9},{6,10},{7,11},{8,4},{9,5},{10,6},{11,7},{20,24},{21,25... | collective-permute-start | bytes 270344 | tf_op jit(solution)/shard_map/ppermute | solution.py:356
  13.1 8.2 %collective-permute-start.3 = (f32[11,16,128]{2,1,0:T(8,128)S(1)}, f32[11,16,128]{2,1,0:T(8,128)S(1)}, u32[]{:S(2)}, u32[]{:S(2)}) collective-permute-start(f32[11,16,128]{2,1,0:T(8,128)S(1)} %get-tuple-element.23), channel_id=1, source_target_pairs={{0,4},{1,5},{2,6},{3,7},{4,0},{5,1},{6,2},{7,3},{8,12},{9,13},{10,... | collective-permute-start | bytes 270344 | tf_op jit(solution)/shard_map/ppermute | solution.py:356
  17.4 2.8 %collective-permute-start.6 = (f32[9,16,128]{2,1,0:T(8,128)S(1)}, f32[9,16,128]{2,1,0:T(8,128)S(1)}, u32[]{:S(2)}, u32[]{:S(2)}) collective-permute-start(f32[9,16,128]{2,1,0:T(8,128)S(1)} %shard_map.68), channel_id=1, source_target_pairs={{12,28},{13,29},{14,30},{15,31},{28,12},{29,13},{30,14},{31,15}} | collective-permute-start | bytes 221192 | tf_op jit(solution)/shard_map/ppermute | solution.py:356
  21.9 6.5 %collective-permute-start.8 = (f32[10,16,128]{2,1,0:T(8,128)S(1)}, f32[10,16,128]{2,1,0:T(8,128)S(1)}, u32[]{:S(2)}, u32[]{:S(2)}) collective-permute-start(f32[10,16,128]{2,1,0:T(8,128)S(1)} %get-tuple-element.29), channel_id=1, source_target_pairs={{0,3},{1,2},{2,1},{3,0},{4,7},{5,6},{6,5},{7,4},{8,11},{9,10},{10,... | collective-permute-start | bytes 245768 | tf_op jit(solution)/shard_map/ppermute | solution.py:356
  23.4 5.3 %collective-permute-start.7 = (f32[10,16,128]{2,1,0:T(8,128)S(1)}, f32[10,16,128]{2,1,0:T(8,128)S(1)}, u32[]{:S(2)}, u32[]{:S(2)}) collective-permute-start(f32[10,16,128]{2,1,0:T(8,128)S(1)} %get-tuple-element.28.refs_0_), channel_id=1, source_target_pairs={{0,1},{1,0},{2,3},{3,2},{4,5},{5,4},{6,7},{7,6},{8,9},{9,8},{10,11... | collective-permute-start | bytes 245768 | tf_op jit(solution)/shard_map/ppermute | solution.py:356
  23.8 13.2 %collective-permute-start.11 = (f32[10,16,128]{2,1,0:T(8,128)S(1)}, f32[10,16,128]{2,1,0:T(8,128)S(1)}, u32[]{:S(2)}, u32[]{:S(2)}) collective-permute-start(f32[10,16,128]{2,1,0:T(8,128)S(1)} %get-tuple-element.28.refs_0_), channel_id=1, source_target_pairs={{12,14},{13,15},{14,12},{15,13},{28,30},{29,31},{30,28},{31,29}} | collective-permute-start | bytes 245768 | tf_op jit(solution)/shard_map/ppermute | solution.py:356
  28.7 9.0 %collective-permute-start.9 = (f32[11,16,128]{2,1,0:T(8,128)S(1)}, f32[11,16,128]{2,1,0:T(8,128)S(1)}, u32[]{:S(2)}, u32[]{:S(2)}) collective-permute-start(f32[11,16,128]{2,1,0:T(8,128)S(1)} %get-tuple-element.30), channel_id=1, source_target_pairs={{4,8},{5,9},{6,10},{7,11},{8,4},{9,5},{10,6},{11,7},{20,24},{21,25... | collective-permute-start | bytes 270344 | tf_op jit(solution)/shard_map/ppermute | solution.py:356
  29.4 9.4 %collective-permute-start.10 = (f32[11,16,128]{2,1,0:T(8,128)S(1)}, f32[11,16,128]{2,1,0:T(8,128)S(1)}, u32[]{:S(2)}, u32[]{:S(2)}) collective-permute-start(f32[11,16,128]{2,1,0:T(8,128)S(1)} %get-tuple-element.31), channel_id=1, source_target_pairs={{0,4},{1,5},{2,6},{3,7},{4,0},{5,1},{6,2},{7,3},{8,12},{9,13},{10,... | collective-permute-start | bytes 270344 | tf_op jit(solution)/shard_map/ppermute | solution.py:356
  37.1 0.7 %collective-permute-start.12 = (f32[9,16,128]{2,1,0:T(8,128)S(1)}, f32[9,16,128]{2,1,0:T(8,128)S(1)}, u32[]{:S(2)}, u32[]{:S(2)}) collective-permute-start(f32[9,16,128]{2,1,0:T(8,128)S(1)} %shard_map.73), channel_id=1, source_target_pairs={{12,28},{13,29},{14,30},{15,31},{28,12},{29,13},{30,14},{31,15}} | collective-permute-start | bytes 221192 | tf_op jit(solution)/shard_map/ppermute | solution.py:356

commit v8 on v7

--- a/solution.py
+++ b/solution.py
@@ -1,3 +1,5 @@
+import itertools
+
 import jax
 import jax.numpy as jnp
 import numpy as np
@@ -60,13 +62,22 @@
     return low, high
 
 
-def pack_kernel(adj, first_out, second_out):
+def pack_kernel(adj, first_out, second_out, kept, sems):
     extent_x = adj.shape[1]
+
+    def load(x):
+        return pltpu.make_async_copy(adj.at[:, x], kept.at[x], sems.at[x])
+
+    for x in range(extent_x):
+        load(x).start()
+
+    def one(x, carry):
+        load(x).wait()
+        return pack_columns(lambda i: kept[x, i], x, *carry)
+
     zero = jnp.zeros((16, 128), jnp.float32)
-    low, high = lax.fori_loop(
-        0, extent_x, lambda x, c: pack_columns(lambda i: adj[i, x], x, *c), (zero, zero)
-    )
-    write_messages(lambda j: adj[j, extent_x - 1], low, high, first_out, second_out)
+    low, high = lax.fori_loop(0, extent_x, one, (zero, zero))
+    write_messages(lambda j: kept[extent_x - 1, j], low, high, first_out, second_out)
 
 
 def info_kernel(device, cell, weight, out):
@@ -75,23 +86,21 @@
         out[2 + k] = weight[:, k]
 
 
-def velocity_kernel(saved, out, kept, sems):
-    steps, _, _, extent_x = saved.shape[:4]
-
-    def load(n):
-        step, x = n // extent_x, lax.rem(n, extent_x)
-        return pltpu.make_async_copy(saved.at[step, 0, :, x], kept.at[n], sems.at[n])
-
-    total = steps * extent_x
-    lax.fori_loop(0, total, lambda n, c: (load(n).start(), c)[1], 0)
-
-    def one(n, carry):
-        load(n).wait()
-        for a, tile in enumerate(velocity_of(lambda i: kept[n, i])):
-            out[n // extent_x, a, lax.rem(n, extent_x)] = tile
+def velocity_kernel(step, saved, out, kept, sems):
+    extent_x = out.shape[1]
+
+    def load(x):
+        return pltpu.make_async_copy(saved.at[step, 0, :, x], kept.at[x], sems.at[x])
+
+    lax.fori_loop(0, extent_x, lambda x, c: (load(x).start(), c)[1], 0)
+
+    def one(x, carry):
+        load(x).wait()
+        for a, tile in enumerate(velocity_of(lambda i: kept[x, i])):
+            out[a, x] = tile
         return carry
 
-    lax.fori_loop(0, total, one, 0)
+    lax.fori_loop(0, extent_x, one, 0)
 
 
 def side_kernel(adj, first, second, _, two_out, one_out):
@@ -268,7 +277,7 @@
         def store(i, tile):
             made[x - 1, i] = tile
 
-        velocity = [vel[step, a, x] for a in range(3)]
+        velocity = [vel[a, x] for a in range(3)]
         collide(lambda i: pulled[i], velocity, solid[0, x], store)
         save(x).start()
         if last:
@@ -288,8 +297,10 @@
     even = is_even("gx")
     interface = lax.axis_index("gx") == lax.axis_size("gx") - 1
 
+    bottom = lax.axis_index("gx") == 0
+
     def below(j):
-        return jnp.where(even, two[j], one[j])
+        return jnp.where(bottom, 0.0, jnp.where(even, two[j], one[j]))
 
     def above(j):
         tile = jnp.where(even, one[j], two[j])
@@ -308,7 +319,7 @@
         def store(i, tile):
             made[n, i] = tile
 
-        velocity = [vel[step, a, x] for a in range(3)]
+        velocity = [vel[a, x] for a in range(3)]
         collide(lambda i: pulled[i], velocity, solid[0, x], store)
         save = pltpu.make_async_copy(made.at[n], out.at[:, x], sems.at[n])
         save.start()
@@ -346,34 +357,36 @@
 
     def send(values, target):
         flat = lambda zone, gx, yz: (zone * widths + gx) * count + yz
-        pairs = []
-        for zone in range(zones):
-            for gx in range(widths):
-                for yz in range(count):
-                    to = target(zone, gx, yz)
-                    if to is not None:
-                        pairs.append((flat(zone, gx, yz), flat(*to)))
-        return lax.ppermute(values, axes, pairs)
+        places = itertools.product(range(zones), range(widths), range(count))
+        return lax.ppermute(values, axes, [(flat(*here), flat(*target(*here))) for here in places])
 
     def partner_of(place, shift):
         return place + 1 if (place + shift) % 2 == 0 else place - 1
 
-    def along_z(shift):
-        return lambda zone, gx, yz: (zone, gx, partner_of(yz, shift) % count)
-
-    def at_interface(target):
-        return lambda zone, gx, yz: target(zone, gx, yz) if gx == widths - 1 else None
-
-    def hop_z(hop):
-        return lambda zone, gx, yz: (zone, gx, (yz + hop) % count)
-
     def flip(zone, gx, yz):
         return (1 - zone, gx, yz)
+
+    def along_z(shift):
+        def target(zone, gx, yz):
+            to = partner_of(yz, shift)
+            if gx == widths - 1 or 0 <= to < count:
+                return (zone, gx, to % count)
+            return flip(zone, gx, yz)
+
+        return target
+
+    def hop_z(hop):
+        def target(zone, gx, yz):
+            if gx == widths - 1:
+                return (zone, gx, (yz + hop) % count)
+            return flip(zone, gx, yz)
+
+        return target
 
     def along_x(shift):
         def target(zone, gx, yz):
             to = partner_of(gx, shift)
-            return (zone, to, yz) if 0 <= to < widths else None
+            return (zone, to, yz) if 0 <= to < widths else flip(zone, gx, yz)
 
         return target
 
@@ -384,31 +397,36 @@
         out_specs=in_vmem(1)[0],
         compiler_params=params,
     )(*[jnp.swapaxes(array[0], 1, 2) for array in (band_device, band_cell, band_weight)])
-    info = send(info, at_interface(flip))
+    info = send(info, flip)
     first, second = pl.pallas_call(
         pack_kernel,
         out_shape=(tile_shape(10),) * 2,
-        in_specs=in_vmem(1),
+        in_specs=[pl.BlockSpec(memory_space=pltpu.HBM)],
         out_specs=tuple(in_vmem(2)),
-        compiler_params=params,
-    )(field)
-    vel = pl.pallas_call(
-        velocity_kernel,
-        out_shape=tile_shape(2, 3, extent_x),
-        in_specs=in_any(1),
-        out_specs=in_vmem(1)[0],
         scratch_shapes=[
-            pltpu.VMEM((2 * extent_x, 27, 16, 128), jnp.float32),
-            pltpu.SemaphoreType.DMA((2 * extent_x,)),
+            pltpu.VMEM((extent_x, 27, 16, 128), jnp.float32),
+            pltpu.SemaphoreType.DMA((extent_x,)),
         ],
         compiler_params=params,
-    )(saved)
+    )(pltpu.with_memory_space_constraint(field, pltpu.HBM))
+    saved = pltpu.with_memory_space_constraint(saved, pltpu.HBM)
     for step in (1, 0):
         last = step == 0
         own = first
         first = send(own, along_z(0))
         second = send(second, along_z(1))
-        others = [send(own, at_interface(hop_z(hop))) for hop in range(2, count - 1)]
+        others = [send(own, hop_z(hop)) for hop in range(2, count - 1)]
+        vel = pl.pallas_call(
+            lambda *refs: velocity_kernel(step, *refs),
+            out_shape=tile_shape(3, extent_x),
+            in_specs=[pl.BlockSpec(memory_space=pltpu.HBM)],
+            out_specs=in_vmem(1)[0],
+            scratch_shapes=[
+                pltpu.VMEM((extent_x, 27, 16, 128), jnp.float32),
+                pltpu.SemaphoreType.DMA((extent_x,)),
+            ],
+            compiler_params=params,
+        )(saved)
         two, one = pl.pallas_call(
             side_kernel,
             out_shape=(tile_shape(11),) * 2,
@@ -455,7 +473,7 @@
         else:
             cross = make_cross(vel)
             new, *columns = make_inner()
-        cross = send(cross, at_interface(flip))
+        cross = send(cross, flip)
         field, *messages = make_planes(
             outer_kernel, 2, (two, one, cross, *columns), (new,), messages
         )

time: 40.2 us -> 32.2 us (0.80)
  starting transfers between devices: 21.8 us -> 14.6 us
  local copies, waits for them, and re-layouts: 3.5 us -> 0.02 us
  Pallas kernels: 7.88 us -> 10.9 us
    ppermute x13, starting transfers between devices: 21.8 us -> 14.6 us  [send(): lax.ppermute(values, axes, [(flat(*here), flat(*target(*here))) for here...]
    unnamed x14 -> x10, local copies, waits for them, and re-layouts: 3.5 us -> 0.02 us
    pallas_call x2 -> x3, Pallas kernels: 2.17 us -> 5.17 us  [the longest x2 3.27 us: body(): pl.pallas_call(lambda *refs: velocity_kernel(step, *refs), out_shape=tile...]
  transfers between devices with their start and end apart: 13 -> 13, of which waited for: 4 -> 5; matrix products, arithmetic and copies ran while one was open for 0% -> 0% of each run, Pallas kernels for 14% -> 23%
where the time goes in v8:
time: 32.2 us; the launch traced here: 32 us
  starting transfers between devices  14.6 us (45%)
  Pallas kernels  10.9 us (34%)
  waiting for transfers between devices  6.33 us (20%)
    ppermute x13, starting transfers between devices, send(): lax.ppermute(values, axes, [(flat(*here), flat(*target(*here))) for here...  14.6 us
    ppermute x13, waiting for transfers between devices, send(): lax.ppermute(values, axes, [(flat(*here), flat(*target(*here))) for here...  6.33 us
    pallas_call x4, Pallas kernels, make_planes(): pl.pallas_call(lambda *refs: kernel(step, *refs), out_shape=(tile_shape(2...  5.61 us
    pallas_call x2, Pallas kernels, body(): pl.pallas_call(lambda *refs: velocity_kernel(step, *refs), out_shape=tile...  3.27 us
    pallas_call x1, Pallas kernels, body(): pl.pallas_call(pack_kernel, out_shape=(tile_shape(10),) * 2, in_specs=[pl...  1.9 us
  transfers between devices with their start and end apart: 13, of which 5 were waited for; matrix products, arithmetic and copies ran while one was open for 0% of the time, Pallas kernels for 23%

profile of v8, /device:TPU:0, one launch (start us, length us, event | category | flops | bytes accessed | tf_op | source)
XLA Modules:
  0.0 32.0 jit_solution(13872491132805380758)
XLA Ops:
  0.0 1.9 %shard_map.65 = (f32[10,16,128]{2,1,0:T(8,128)S(1)}, f32[10,16,128]{2,1,0:T(8,128)S(1)}) custom-call(f32[27,8,16,128]{3,2,1,0:T(8,128)} %bitcast.11), custom_call_target="tpu_custom_call" | custom-call | tf_op jit(solution)/shard_map/pallas_call | solution.py:401
  1.9 0.5 %collective-permute-start.1 = (f32[10,16,128]{2,1,0:T(8,128)S(1)}, f32[10,16,128]{2,1,0:T(8,128)S(1)}, u32[]{:S(2)}, u32[]{:S(2)}) collective-permute-start(f32[10,16,128]{2,1,0:T(8,128)S(1)} %get-tuple-element.21), channel_id=1, source_target_pairs={{0,16},{1,2},{2,1},{3,19},{4,20},{5,6},{6,5},{7,23},{8,24},{9,10},... | collective-permute-start | bytes 245768 | tf_op jit(solution)/shard_map/ppermute | solution.py:361
  2.5 4.1 %collective-permute-start = (f32[10,16,128]{2,1,0:T(8,128)S(1)}, f32[10,16,128]{2,1,0:T(8,128)S(1)}, u32[]{:S(2)}, u32[]{:S(2)}) collective-permute-start(f32[10,16,128]{2,1,0:T(8,128)S(1)} %get-tuple-element.20.refs_0_), channel_id=1, source_target_pairs={{0,1},{1,0},{2,3},{3,2},{4,5},{5,4},{6,7},{7,6},{8,9},{9,8},{10,11... | collective-permute-start | bytes 245768 | tf_op jit(solution)/shard_map/ppermute | solution.py:361
  6.7 0.0 copy-start
  6.7 0.6 %collective-permute-start.5 = (f32[4,16,128]{2,1,0:T(8,128)S(1)}, f32[4,16,128]{2,1,0:T(8,128)S(1)}, u32[]{:S(2)}, u32[]{:S(2)}) collective-permute-start(f32[4,16,128]{2,1,0:T(8,128)S(1)} %shard_map.67), channel_id=1, source_target_pairs={{0,16},{1,17},{2,18},{3,19},{4,20},{5,21},{6,22},{7,23},{8,24},{9,... | collective-permute-start | bytes 98312 | tf_op jit(solution)/shard_map/ppermute | solution.py:361
  7.2 1.6 %shard_map.64._.refs_5_.refs_1_ = f32[3,8,16,128]{3,2,1,0:T(8,128)S(1)} custom-call(f32[2,1,27,8,16,128]{5,4,3,2,1,0:T(8,128)} %refs_0_.3), custom_call_target="tpu_custom_call" | custom-call | tf_op jit(solution)/shard_map/pallas_call | solution.py:419
  8.9 0.0 copy-start.1
  8.9 0.1 collective-permute-done.first.refs_1_.refs_3_
  9.1 0.3 %collective-permute-start.2 = (f32[11,16,128]{2,1,0:T(8,128)S(1)}, f32[11,16,128]{2,1,0:T(8,128)S(1)}, u32[]{:S(2)}, u32[]{:S(2)}) collective-permute-start(f32[11,16,128]{2,1,0:T(8,128)S(1)} %get-tuple-element.22), channel_id=1, source_target_pairs={{0,16},{1,17},{2,18},{3,19},{4,8},{5,9},{6,10},{7,11},{8,4},{9,5},... | collective-permute-start | bytes 270344 | tf_op jit(solution)/shard_map/ppermute | solution.py:361
  9.4 2.7 %collective-permute-start.3 = (f32[11,16,128]{2,1,0:T(8,128)S(1)}, f32[11,16,128]{2,1,0:T(8,128)S(1)}, u32[]{:S(2)}, u32[]{:S(2)}) collective-permute-start(f32[11,16,128]{2,1,0:T(8,128)S(1)} %get-tuple-element.23), channel_id=1, source_target_pairs={{0,4},{1,5},{2,6},{3,7},{4,0},{5,1},{6,2},{7,3},{8,12},{9,13},{10,... | collective-permute-start | bytes 270344 | tf_op jit(solution)/shard_map/ppermute | solution.py:361
  12.1 2.1 %shard_map.69 = (f32[27,8,16,128]{3,2,1,0:T(8,128)S(1)}, f32[16,128]{1,0:T(8,128)S(1)}, f32[16,128]{1,0:T(8,128)S(1)}) custom-call(f32[27,8,16,128]{3,2,1,0:T(8,128)S(1)} %bitcast.13, f32[3,8,16,128]{3,2,1,0:T(8,128)S(1)} %shard_map.64._.refs_5_.refs_1_, s32[1,8,16,128]{3,2,1,0:T(8,128)S(1)} %copy-done.1, ...), custom_call_target="tpu_custom_call" | custom-call | tf_op jit(solution)/shard_map/pallas_call | solution.py:442
  14.2 2.6 %collective-permute-done.3.refs_6_ = f32[11,16,128]{2,1,0:T(8,128)S(1)} collective-permute-done((f32[11,16,128]{2,1,0:T(8,128)S(1)}, f32[11,16,128]{2,1,0:T(8,128)S(1)}, u32[]{:S(2)}, u32[]{:S(2)}) %collective-permute-start.3) | collective-permute-done | bytes 90144 | tf_op jit(solution)/shard_map/ppermute | solution.py:361
  16.8 0.6 %shard_map.70 = (f32[27,8,16,128]{3,2,1,0:T(8,128)S(1)}, f32[10,16,128]{2,1,0:T(8,128)S(1)}, f32[10,16,128]{2,1,0:T(8,128)S(1)}) custom-call(f32[27,8,16,128]{3,2,1,0:T(8,128)S(1)} %bitcast.14, f32[3,8,16,128]{3,2,1,0:T(8,128)S(1)} %shard_map.64._.refs_5_.refs_1_, s32[1,8,16,128]{3,2,1,0:T(8,128)S(1)} %copy-done.1, ...), custom_call_target="tpu_custom_call", output_to_operand_aliasing={{0}: (10, {})} | custom-call | tf_op jit(solution)/shard_map/pallas_call | solution.py:442
  17.4 0.1 collective-permute-start.8
  17.5 1.6 %collective-permute-start.7 = (f32[10,16,128]{2,1,0:T(8,128)S(1)}, f32[10,16,128]{2,1,0:T(8,128)S(1)}, u32[]{:S(2)}, u32[]{:S(2)}) collective-permute-start(f32[10,16,128]{2,1,0:T(8,128)S(1)} %get-tuple-element.28.refs_0_), channel_id=1, source_target_pairs={{0,1},{1,0},{2,3},{3,2},{4,5},{5,4},{6,7},{7,6},{8,9},{9,8},{10,11... | collective-permute-start | bytes 245768 | tf_op jit(solution)/shard_map/ppermute | solution.py:361
  19.2 1.6 %shard_map.71._.refs_1_ = f32[3,8,16,128]{3,2,1,0:T(8,128)S(1)} custom-call(f32[2,1,27,8,16,128]{5,4,3,2,1,0:T(8,128)} %refs_0_.3), custom_call_target="tpu_custom_call" | custom-call | tf_op jit(solution)/shard_map/pallas_call | solution.py:419
  20.8 1.6 %collective-permute-done.7.first.refs_3_.refs_1_ = f32[10,16,128]{2,1,0:T(8,128)S(1)} collective-permute-done((f32[10,16,128]{2,1,0:T(8,128)S(1)}, f32[10,16,128]{2,1,0:T(8,128)S(1)}, u32[]{:S(2)}, u32[]{:S(2)}) %collective-permute-start.7) | collective-permute-done | bytes 81952 | tf_op jit(solution)/shard_map/ppermute | solution.py:361
  22.4 0.1 collective-permute-start.9
  22.5 4.4 %collective-permute-start.10 = (f32[11,16,128]{2,1,0:T(8,128)S(1)}, f32[11,16,128]{2,1,0:T(8,128)S(1)}, u32[]{:S(2)}, u32[]{:S(2)}) collective-permute-start(f32[11,16,128]{2,1,0:T(8,128)S(1)} %get-tuple-element.31), channel_id=1, source_target_pairs={{0,4},{1,5},{2,6},{3,7},{4,0},{5,1},{6,2},{7,3},{8,12},{9,13},{10,... | collective-permute-start | bytes 270344 | tf_op jit(solution)/shard_map/ppermute | solution.py:361
  26.9 1.9 %shard_map.73 = (f32[27,8,16,128]{3,2,1,0:T(8,128)}, f32[16,128]{1,0:T(8,128)S(1)}, f32[16,128]{1,0:T(8,128)S(1)}) custom-call(f32[27,8,16,128]{3,2,1,0:T(8,128)S(1)} %get-tuple-element.27.adj.refs_0_, f32[3,8,16,128]{3,2,1,0:T(8,128)S(1)} %shard_map.71._.refs_1_, s32[1,8,16,128]{3,2,1,0:T(8,128)S(1)} %copy-done.1, ...), custom_call_target="tpu_custom_call" | custom-call | tf_op jit(solution)/shard_map/pallas_call | solution.py:442
  28.9 0.1 collective-permute-start.12
  28.9 1.3 %collective-permute-done.12.refs_7_ = f32[9,16,128]{2,1,0:T(8,128)S(1)} collective-permute-done((f32[9,16,128]{2,1,0:T(8,128)S(1)}, f32[9,16,128]{2,1,0:T(8,128)S(1)}, u32[]{:S(2)}, u32[]{:S(2)}) %collective-permute-start.12) | collective-permute-done | bytes 73760 | tf_op jit(solution)/shard_map/ppermute | solution.py:361
  30.2 0.8 %collective-permute-done.10.refs_6_ = f32[11,16,128]{2,1,0:T(8,128)S(1)} collective-permute-done((f32[11,16,128]{2,1,0:T(8,128)S(1)}, f32[11,16,128]{2,1,0:T(8,128)S(1)}, u32[]{:S(2)}, u32[]{:S(2)}) %collective-permute-start.10) | collective-permute-done | bytes 90144 | tf_op jit(solution)/shard_map/ppermute | solution.py:361
  31.0 1.0 %shard_map.75 = f32[27,8,16,128]{3,2,1,0:T(8,128)} custom-call(f32[27,8,16,128]{3,2,1,0:T(8,128)S(1)} %get-tuple-element.27.adj.refs_0_, f32[3,8,16,128]{3,2,1,0:T(8,128)S(1)} %shard_map.71._.refs_1_, s32[1,8,16,128]{3,2,1,0:T(8,128)S(1)} %copy-done.1, ...), custom_call_target="tpu_custom_call", output_to_operand_aliasing={{}: (10, {})} | custom-call | tf_op jit(solution)/shard_map/pallas_call | solution.py:442
  (24 shorter events, 0.1 us)
Async XLA Ops:
  0.0 6.6 %copy-start.4 = (f32[1,16,128,2]{2,3,1,0:T(2,128)S(1)}, f32[1,16,128,2]{2,3,1,0:T(2,128)}, u32[]{:S(2)}) copy-start(f32[1,16,128,2]{2,3,1,0:T(2,128)} %param.11) | copy-start | bytes 49156
  0.0 6.6 %copy-start.3 = (s32[1,16,128,2]{2,3,1,0:T(2,128)S(1)}, s32[1,16,128,2]{2,3,1,0:T(2,128)}, u32[]{:S(2)}) copy-start(s32[1,16,128,2]{2,3,1,0:T(2,128)} %param.10) | copy-start | bytes 49156
  0.0 6.6 %copy-start.2 = (s32[1,16,128,2]{2,3,1,0:T(2,128)S(1)}, s32[1,16,128,2]{2,3,1,0:T(2,128)}, u32[]{:S(2)}) copy-start(s32[1,16,128,2]{2,3,1,0:T(2,128)} %param.9) | copy-start | bytes 49156
  1.9 7.0 %collective-permute-start.1 = (f32[10,16,128]{2,1,0:T(8,128)S(1)}, f32[10,16,128]{2,1,0:T(8,128)S(1)}, u32[]{:S(2)}, u32[]{:S(2)}) collective-permute-start(f32[10,16,128]{2,1,0:T(8,128)S(1)} %get-tuple-element.21), channel_id=1, source_target_pairs={{0,16},{1,2},{2,1},{3,19},{4,20},{5,6},{6,5},{7,23},{8,24},{9,10},... | collective-permute-start | bytes 245768 | tf_op jit(solution)/shard_map/ppermute | solution.py:361
  2.5 6.6 %collective-permute-start = (f32[10,16,128]{2,1,0:T(8,128)S(1)}, f32[10,16,128]{2,1,0:T(8,128)S(1)}, u32[]{:S(2)}, u32[]{:S(2)}) collective-permute-start(f32[10,16,128]{2,1,0:T(8,128)S(1)} %get-tuple-element.20.refs_0_), channel_id=1, source_target_pairs={{0,1},{1,0},{2,3},{3,2},{4,5},{5,4},{6,7},{7,6},{8,9},{9,8},{10,11... | collective-permute-start | bytes 245768 | tf_op jit(solution)/shard_map/ppermute | solution.py:361
  6.6 5.5 %collective-permute-start.4 = (f32[10,16,128]{2,1,0:T(8,128)S(1)}, f32[10,16,128]{2,1,0:T(8,128)S(1)}, u32[]{:S(2)}, u32[]{:S(2)}) collective-permute-start(f32[10,16,128]{2,1,0:T(8,128)S(1)} %get-tuple-element.20.refs_0_), channel_id=1, source_target_pairs={{0,16},{1,17},{2,18},{3,19},{4,20},{5,21},{6,22},{7,23},{8,24},{9,... | collective-permute-start | bytes 245768 | tf_op jit(solution)/shard_map/ppermute | solution.py:361
  6.7 2.4 %copy-start = (f32[1,27,8,16,128]{4,3,2,1,0:T(8,128)S(1)}, f32[1,27,8,16,128]{4,3,2,1,0:T(8,128)}, u32[]{:S(2)}) copy-start(f32[1,27,8,16,128]{4,3,2,1,0:T(8,128)} %param.6) | copy-start | bytes 5308420
  6.7 5.4 %collective-permute-start.5 = (f32[4,16,128]{2,1,0:T(8,128)S(1)}, f32[4,16,128]{2,1,0:T(8,128)S(1)}, u32[]{:S(2)}, u32[]{:S(2)}) collective-permute-start(f32[4,16,128]{2,1,0:T(8,128)S(1)} %shard_map.67), channel_id=1, source_target_pairs={{0,16},{1,17},{2,18},{3,19},{4,20},{5,21},{6,22},{7,23},{8,24},{9,... | collective-permute-start | bytes 98312 | tf_op jit(solution)/shard_map/ppermute | solution.py:361
  8.9 3.2 %copy-start.1 = (s32[1,8,16,128]{3,2,1,0:T(8,128)S(1)}, s32[1,8,16,128]{3,2,1,0:T(8,128)}, u32[]{:S(2)}) copy-start(s32[1,8,16,128]{3,2,1,0:T(8,128)} %refs_2_.7) | copy-start | bytes 196612
  9.1 5.2 %collective-permute-start.2 = (f32[11,16,128]{2,1,0:T(8,128)S(1)}, f32[11,16,128]{2,1,0:T(8,128)S(1)}, u32[]{:S(2)}, u32[]{:S(2)}) collective-permute-start(f32[11,16,128]{2,1,0:T(8,128)S(1)} %get-tuple-element.22), channel_id=1, source_target_pairs={{0,16},{1,17},{2,18},{3,19},{4,8},{5,9},{6,10},{7,11},{8,4},{9,5},... | collective-permute-start | bytes 270344 | tf_op jit(solution)/shard_map/ppermute | solution.py:361
  9.4 7.4 %collective-permute-start.3 = (f32[11,16,128]{2,1,0:T(8,128)S(1)}, f32[11,16,128]{2,1,0:T(8,128)S(1)}, u32[]{:S(2)}, u32[]{:S(2)}) collective-permute-start(f32[11,16,128]{2,1,0:T(8,128)S(1)} %get-tuple-element.23), channel_id=1, source_target_pairs={{0,4},{1,5},{2,6},{3,7},{4,0},{5,1},{6,2},{7,3},{8,12},{9,13},{10,... | collective-permute-start | bytes 270344 | tf_op jit(solution)/shard_map/ppermute | solution.py:361
  12.1 2.1 %collective-permute-start.6 = (f32[9,16,128]{2,1,0:T(8,128)S(1)}, f32[9,16,128]{2,1,0:T(8,128)S(1)}, u32[]{:S(2)}, u32[]{:S(2)}) collective-permute-start(f32[9,16,128]{2,1,0:T(8,128)S(1)} %shard_map.68), channel_id=1, source_target_pairs={{0,16},{1,17},{2,18},{3,19},{4,20},{5,21},{6,22},{7,23},{8,24},{9,... | collective-permute-start | bytes 221192 | tf_op jit(solution)/shard_map/ppermute | solution.py:361
  17.4 3.4 %collective-permute-start.8 = (f32[10,16,128]{2,1,0:T(8,128)S(1)}, f32[10,16,128]{2,1,0:T(8,128)S(1)}, u32[]{:S(2)}, u32[]{:S(2)}) collective-permute-start(f32[10,16,128]{2,1,0:T(8,128)S(1)} %get-tuple-element.29), channel_id=1, source_target_pairs={{0,16},{1,2},{2,1},{3,19},{4,20},{5,6},{6,5},{7,23},{8,24},{9,10},... | collective-permute-start | bytes 245768 | tf_op jit(solution)/shard_map/ppermute | solution.py:361
  17.5 4.9 %collective-permute-start.7 = (f32[10,16,128]{2,1,0:T(8,128)S(1)}, f32[10,16,128]{2,1,0:T(8,128)S(1)}, u32[]{:S(2)}, u32[]{:S(2)}) collective-permute-start(f32[10,16,128]{2,1,0:T(8,128)S(1)} %get-tuple-element.28.refs_0_), channel_id=1, source_target_pairs={{0,1},{1,0},{2,3},{3,2},{4,5},{5,4},{6,7},{7,6},{8,9},{9,8},{10,11... | collective-permute-start | bytes 245768 | tf_op jit(solution)/shard_map/ppermute | solution.py:361
  19.1 9.7 %collective-permute-start.11 = (f32[10,16,128]{2,1,0:T(8,128)S(1)}, f32[10,16,128]{2,1,0:T(8,128)S(1)}, u32[]{:S(2)}, u32[]{:S(2)}) collective-permute-start(f32[10,16,128]{2,1,0:T(8,128)S(1)} %get-tuple-element.28.refs_0_), channel_id=1, source_target_pairs={{0,16},{1,17},{2,18},{3,19},{4,20},{5,21},{6,22},{7,23},{8,24},{9,... | collective-permute-start | bytes 245768 | tf_op jit(solution)/shard_map/ppermute | solution.py:361
  22.4 7.8 %collective-permute-start.9 = (f32[11,16,128]{2,1,0:T(8,128)S(1)}, f32[11,16,128]{2,1,0:T(8,128)S(1)}, u32[]{:S(2)}, u32[]{:S(2)}) collective-permute-start(f32[11,16,128]{2,1,0:T(8,128)S(1)} %get-tuple-element.30), channel_id=1, source_target_pairs={{0,16},{1,17},{2,18},{3,19},{4,8},{5,9},{6,10},{7,11},{8,4},{9,5},... | collective-permute-start | bytes 270344 | tf_op jit(solution)/shard_map/ppermute | solution.py:361
  22.5 8.5 %collective-permute-start.10 = (f32[11,16,128]{2,1,0:T(8,128)S(1)}, f32[11,16,128]{2,1,0:T(8,128)S(1)}, u32[]{:S(2)}, u32[]{:S(2)}) collective-permute-start(f32[11,16,128]{2,1,0:T(8,128)S(1)} %get-tuple-element.31), channel_id=1, source_target_pairs={{0,4},{1,5},{2,6},{3,7},{4,0},{5,1},{6,2},{7,3},{8,12},{9,13},{10,... | collective-permute-start | bytes 270344 | tf_op jit(solution)/shard_map/ppermute | solution.py:361
  28.9 1.3 %collective-permute-start.12 = (f32[9,16,128]{2,1,0:T(8,128)S(1)}, f32[9,16,128]{2,1,0:T(8,128)S(1)}, u32[]{:S(2)}, u32[]{:S(2)}) collective-permute-start(f32[9,16,128]{2,1,0:T(8,128)S(1)} %shard_map.74), channel_id=1, source_target_pairs={{0,16},{1,17},{2,18},{3,19},{4,20},{5,21},{6,22},{7,23},{8,24},{9,... | collective-permute-start | bytes 221192 | tf_op jit(solution)/shard_map/ppermute | solution.py:361

commit v9 on v8

--- a/solution.py
+++ b/solution.py
@@ -62,22 +62,23 @@
     return low, high
 
 
-def pack_kernel(adj, first_out, second_out, kept, sems):
-    extent_x = adj.shape[1]
-
-    def load(x):
-        return pltpu.make_async_copy(adj.at[:, x], kept.at[x], sems.at[x])
-
+def pack_kernel(adj, first_out, second_out, kept, top, sems):
+    extent_x = adj.shape[2]
+    copies = [
+        pltpu.make_async_copy(adj.at[:, 2 * side, x], kept.at[side, x], sems.at[side, x])
+        for x in range(extent_x)
+        for side in range(2)
+    ]
+    copies.append(pltpu.make_async_copy(adj.at[pl.ds(0, 3), :, extent_x - 1], top, sems.at[2, 0]))
+    for copy in copies:
+        copy.start()
+    edges = jnp.zeros((16, 128), jnp.float32), jnp.zeros((16, 128), jnp.float32)
     for x in range(extent_x):
-        load(x).start()
-
-    def one(x, carry):
-        load(x).wait()
-        return pack_columns(lambda i: kept[x, i], x, *carry)
-
-    zero = jnp.zeros((16, 128), jnp.float32)
-    low, high = lax.fori_loop(0, extent_x, one, (zero, zero))
-    write_messages(lambda j: kept[extent_x - 1, j], low, high, first_out, second_out)
+        for copy in copies[2 * x : 2 * x + 2]:
+            copy.wait()
+        edges = pack_columns(lambda i: kept[(i % 3) // 2, x, i // 3], x, *edges)
+    copies[-1].wait()
+    write_messages(lambda j: top[j // 3, j % 3], *edges, first_out, second_out)
 
 
 def info_kernel(device, cell, weight, out):
@@ -106,25 +107,32 @@
 def side_kernel(adj, first, second, _, two_out, one_out):
     extent_x = adj.shape[1]
     even = is_even("gx")
+    interface = lax.axis_index("gx") == lax.axis_size("gx") - 1
     for j in range(9):
         top, bottom = adj[j, extent_x - 1], adj[18 + j, 0]
         one_out[j] = jnp.where(even, top, bottom)
-        two_out[j] = jnp.where(even, bottom, top)
+        two_out[j] = jnp.where(even | interface, jnp.where(interface, top, bottom), top)
+    lane = lanes()
     low, high = edges_from(first, second)
-    one_out[9], one_out[10] = low, high
-    two_out[9], two_out[10] = low, high
+    top, bottom = [
+        jnp.where(lane < 64, pltpu.roll(low, 128 - start, 1), pltpu.roll(high, 192 - start, 1))
+        for start in (9 * extent_x, 9)
+    ]
+    one_out[9] = jnp.where(even, top, bottom)
+    two_out[9] = jnp.where(even, bottom, top)
 
 
 def cross_kernel(count, *refs):
-    own, first, second = refs[:3]
-    blocks = refs[:count]
-    info, _, out = refs[count:]
+    own, first, second, ends = refs[:4]
+    others = refs[4 : 1 + count]
+    info, _, out = refs[1 + count :]
     interface = lax.axis_index("gx") == lax.axis_size("gx") - 1
 
     @pl.when(interface)
     def _():
         me = lax.axis_index("yz")
         even = is_even("yz")
+        at_end = (me == 0) | (me == count - 1)
         rows = (0, 8)
         spots, picks = {}, {}
         for r in rows:
@@ -141,7 +149,8 @@
             for r in rows:
                 total = jnp.zeros((8, 128), jnp.float32)
                 for k in range(2):
-                    tiles = [ref[j, r : r + 8] for ref in blocks]
+                    tiles = [ref[j, r : r + 8] for ref in (own, first, second, *others)]
+                    tiles[2] = jnp.where(at_end, ends[j, r : r + 8], tiles[2])
                     got = [jnp.take_along_axis(tile, spots[r, k], axis=1) for tile in tiles]
                     picked = got[0]
                     for mask, value in zip(picks[r, k], got[1:]):
@@ -268,24 +277,25 @@
         return pltpu.make_async_copy(made.at[x - 1], out.at[:, x], sems.at[x - 1])
 
     def plane(x, carry):
+        here = pulled.at[lax.rem(x, 2)]
         pull_plane(
             lambda i, cx: adj[i, x + cx],
             lambda cx: (low_edge, high_edge, (x + 1 + cx) * 9),
-            pulled,
+            here,
         )
 
         def store(i, tile):
             made[x - 1, i] = tile
 
         velocity = [vel[a, x] for a in range(3)]
-        collide(lambda i: pulled[i], velocity, solid[0, x], store)
+        collide(lambda i: here[i], velocity, solid[0, x], store)
         save(x).start()
         if last:
             return carry
         return pack_columns(lambda i: made[x - 1, i], x, *carry)
 
     zero = jnp.zeros((16, 128), jnp.float32)
-    low_out[...], high_out[...] = lax.fori_loop(1, extent_x - 1, plane, (zero, zero))
+    low_out[...], high_out[...] = lax.fori_loop(1, extent_x - 1, plane, (zero, zero), unroll=2)
     lax.fori_loop(1, extent_x - 1, lambda x, c: (save(x).wait(), c)[1], 0)
 
 
@@ -306,13 +316,15 @@
         tile = jnp.where(even, one[j], two[j])
         return jnp.where(interface, cross[j], tile) if j < 9 else tile
 
-    def plane(n, x, ghost, beyond, start, raw):
+    def plane(n, x, ghost, beyond, raw):
         pull_plane(
             lambda i, cx: beyond(i % 9) if cx == ghost else adj[i, x + cx],
             lambda cx: (
-                (beyond(9), beyond(10), start) if cx == ghost else (*edges, (x + 1 + cx) * 9)
+                (beyond(9), pltpu.roll(beyond(9), 64, 1), 0)
+                if cx == ghost
+                else (*edges, (x + 1 + cx) * 9)
             ),
-            pulled,
+            pulled.at[n],
             raw,
         )
 
@@ -320,13 +332,13 @@
             made[n, i] = tile
 
         velocity = [vel[a, x] for a in range(3)]
-        collide(lambda i: pulled[i], velocity, solid[0, x], store)
+        collide(lambda i: pulled[n, i], velocity, solid[0, x], store)
         save = pltpu.make_async_copy(made.at[n], out.at[:, x], sems.at[n])
         save.start()
         return save
 
     final = extent_x - 1
-    saves = [plane(0, 0, -1, below, extent_x * 9, None), plane(1, final, 1, above, 9, interface)]
+    saves = [plane(0, 0, -1, below, None), plane(1, final, 1, above, interface)]
     if messages:
         low, high = low_in[...], high_in[...]
         low, high = pack_columns(lambda i: made[0, i], 0, low, high)
@@ -369,9 +381,7 @@
     def along_z(shift):
         def target(zone, gx, yz):
             to = partner_of(yz, shift)
-            if gx == widths - 1 or 0 <= to < count:
-                return (zone, gx, to % count)
-            return flip(zone, gx, yz)
+            return (zone, gx, to) if 0 <= to < count else flip(zone, gx, yz)
 
         return target
 
@@ -386,6 +396,8 @@
     def along_x(shift):
         def target(zone, gx, yz):
             to = partner_of(gx, shift)
+            if gx == widths - 1 and shift == 1 and yz in (0, count - 1):
+                return (zone, gx, count - 1 - yz)
             return (zone, to, yz) if 0 <= to < widths else flip(zone, gx, yz)
 
         return target
@@ -404,11 +416,12 @@
         in_specs=[pl.BlockSpec(memory_space=pltpu.HBM)],
         out_specs=tuple(in_vmem(2)),
         scratch_shapes=[
-            pltpu.VMEM((extent_x, 27, 16, 128), jnp.float32),
-            pltpu.SemaphoreType.DMA((extent_x,)),
+            pltpu.VMEM((2, extent_x, 9, 16, 128), jnp.float32),
+            pltpu.VMEM((3, 3, 16, 128), jnp.float32),
+            pltpu.SemaphoreType.DMA((3, extent_x)),
         ],
         compiler_params=params,
-    )(pltpu.with_memory_space_constraint(field, pltpu.HBM))
+    )(pltpu.with_memory_space_constraint(field.reshape(9, 3, extent_x, 16, 128), pltpu.HBM))
     saved = pltpu.with_memory_space_constraint(saved, pltpu.HBM)
     for step in (1, 0):
         last = step == 0
@@ -429,7 +442,7 @@
         )(saved)
         two, one = pl.pallas_call(
             side_kernel,
-            out_shape=(tile_shape(11),) * 2,
+            out_shape=(tile_shape(10),) * 2,
             in_specs=in_vmem(3) + in_any(1),
             out_specs=tuple(in_vmem(2)),
             compiler_params=params,
@@ -446,7 +459,7 @@
                 out_specs=tuple(in_any(1) + in_vmem(len(extra))),
                 scratch_shapes=[
                     pltpu.VMEM((planes, 27, 16, 128), jnp.float32),
-                    pltpu.VMEM((27, 16, 128), jnp.float32),
+                    pltpu.VMEM((2, 27, 16, 128), jnp.float32),
                     pltpu.SemaphoreType.DMA((planes,)),
                 ],
                 input_output_aliases={len(operands): 0} if new else {},
@@ -454,25 +467,15 @@
             )(*operands, *new)
 
         messages = () if last else (tile_shape(10),) * 2
-        def make_inner():
-            kernel = lambda step, *refs: inner_kernel(step, last, *refs)
-            return make_planes(kernel, extent_x - 2, (), (), (tile_shape(),) * 2)
-
-        def make_cross(after):
-            return pl.pallas_call(
-                lambda *refs: cross_kernel(count, *refs),
-                out_shape=tile_shape(9),
-                in_specs=in_vmem(count + 1) + in_any(1),
-                out_specs=in_vmem(1)[0],
-                compiler_params=params,
-            )(own, first, second, *others, info, after)
-
-        if last:
-            new, *columns = make_inner()
-            cross = make_cross(columns[0])
-        else:
-            cross = make_cross(vel)
-            new, *columns = make_inner()
+        kernel = lambda step, *refs: inner_kernel(step, last, *refs)
+        new, *columns = make_planes(kernel, extent_x - 2, (), (), (tile_shape(),) * 2)
+        cross = pl.pallas_call(
+            lambda *refs: cross_kernel(count, *refs),
+            out_shape=tile_shape(9),
+            in_specs=in_vmem(count + 2) + in_any(1),
+            out_specs=in_vmem(1)[0],
+            compiler_params=params,
+        )(own, first, second, two, *others, info, columns[0])
         cross = send(cross, flip)
         field, *messages = make_planes(
             outer_kernel, 2, (two, one, cross, *columns), (new,), messages

time: 32.2 us -> 32.6 us (1.012)
  the two profiles are of different devices: /device:TPU:0 before, /device:TPU:7 now
where the time goes in v9:
time: 32.6 us; the launch traced here: 32.4 us
  starting transfers between devices  17.1 us (52%)
  Pallas kernels  11.5 us (35%)
  waiting for transfers between devices  3.71 us (11%)
    ppermute x13, starting transfers between devices, send(): lax.ppermute(values, axes, [(flat(*here), flat(*target(*here))) for here...  17.1 us
    pallas_call x4, Pallas kernels, make_planes(): pl.pallas_call(lambda *refs: kernel(step, *refs), out_shape=(tile_shape(2...  5.27 us
    ppermute x13, waiting for transfers between devices, send(): lax.ppermute(values, axes, [(flat(*here), flat(*target(*here))) for here...  3.71 us
    pallas_call x2, Pallas kernels, body(): pl.pallas_call(lambda *refs: velocity_kernel(step, *refs), out_shape=tile...  3.27 us
    pallas_call x1, Pallas kernels, body(): pl.pallas_call(pack_kernel, out_shape=(tile_shape(10),) * 2, in_specs=[pl...  2 us
    pallas_call x2, Pallas kernels, body(): pl.pallas_call(lambda *refs: cross_kernel(count, *refs), out_shape=tile_s...  0.69 us
  transfers between devices with their start and end apart: 13, of which 4 were waited for; matrix products, arithmetic and copies ran while one was open for 0% of the time, Pallas kernels for 24%

profile of v9, /device:TPU:7, one launch (start us, length us, event | category | flops | bytes accessed | tf_op | source)
XLA Modules:
  0.0 32.4 jit_solution(8437064726034491104)
XLA Ops:
  0.0 2.0 %shard_map.65 = (f32[10,16,128]{2,1,0:T(8,128)S(1)}, f32[10,16,128]{2,1,0:T(8,128)S(1)}) custom-call(f32[9,3,8,16,128]{4,3,2,1,0:T(8,128)} %bitcast.12), custom_call_target="tpu_custom_call" | custom-call | tf_op jit(solution)/shard_map/pallas_call | solution.py:413
  2.0 0.7 %collective-permute-start.1 = (f32[10,16,128]{2,1,0:T(8,128)S(1)}, f32[10,16,128]{2,1,0:T(8,128)S(1)}, u32[]{:S(2)}, u32[]{:S(2)}) collective-permute-start(f32[10,16,128]{2,1,0:T(8,128)S(1)} %get-tuple-element.21), channel_id=1, source_target_pairs={{0,16},{1,2},{2,1},{3,19},{4,20},{5,6},{6,5},{7,23},{8,24},{9,10},... | collective-permute-start | bytes 245768 | tf_op jit(solution)/shard_map/ppermute | solution.py:373
  2.8 1.9 %collective-permute-start = (f32[10,16,128]{2,1,0:T(8,128)S(1)}, f32[10,16,128]{2,1,0:T(8,128)S(1)}, u32[]{:S(2)}, u32[]{:S(2)}) collective-permute-start(f32[10,16,128]{2,1,0:T(8,128)S(1)} %get-tuple-element.20.refs_0_), channel_id=1, source_target_pairs={{0,1},{1,0},{2,3},{3,2},{4,5},{5,4},{6,7},{7,6},{8,9},{9,8},{10,11... | collective-permute-start | bytes 245768 | tf_op jit(solution)/shard_map/ppermute | solution.py:373
  4.7 1.7 %collective-permute-start.4 = (f32[10,16,128]{2,1,0:T(8,128)S(1)}, f32[10,16,128]{2,1,0:T(8,128)S(1)}, u32[]{:S(2)}, u32[]{:S(2)}) collective-permute-start(f32[10,16,128]{2,1,0:T(8,128)S(1)} %get-tuple-element.20.refs_0_), channel_id=1, source_target_pairs={{0,16},{1,17},{2,18},{3,19},{4,20},{5,21},{6,22},{7,23},{8,24},{9,... | collective-permute-start | bytes 245768 | tf_op jit(solution)/shard_map/ppermute | solution.py:373
  6.4 1.6 %shard_map.64._.refs_1_ = f32[3,8,16,128]{3,2,1,0:T(8,128)S(1)} custom-call(f32[2,1,27,8,16,128]{5,4,3,2,1,0:T(8,128)} %refs_0_.3), custom_call_target="tpu_custom_call" | custom-call | tf_op jit(solution)/shard_map/pallas_call | solution.py:432
  8.1 0.1 shard_map.66
  8.2 2.9 %collective-permute-start.2 = (f32[10,16,128]{2,1,0:T(8,128)S(1)}, f32[10,16,128]{2,1,0:T(8,128)S(1)}, u32[]{:S(2)}, u32[]{:S(2)}) collective-permute-start(f32[10,16,128]{2,1,0:T(8,128)S(1)} %get-tuple-element.22), channel_id=1, source_target_pairs={{0,16},{1,17},{2,18},{3,19},{4,8},{5,9},{6,10},{7,11},{8,4},{9,5},... | collective-permute-start | bytes 245768 | tf_op jit(solution)/shard_map/ppermute | solution.py:373
  11.1 1.6 %collective-permute-start.5 = (f32[4,16,128]{2,1,0:T(8,128)S(1)}, f32[4,16,128]{2,1,0:T(8,128)S(1)}, u32[]{:S(2)}, u32[]{:S(2)}) collective-permute-start(f32[4,16,128]{2,1,0:T(8,128)S(1)} %shard_map.67), channel_id=1, source_target_pairs={{0,16},{1,17},{2,18},{3,19},{4,20},{5,21},{6,22},{7,23},{8,24},{9,... | collective-permute-start | bytes 98312 | tf_op jit(solution)/shard_map/ppermute | solution.py:373
  12.7 1.8 %shard_map.68 = (f32[27,8,16,128]{3,2,1,0:T(8,128)S(1)}, f32[16,128]{1,0:T(8,128)S(1)}, f32[16,128]{1,0:T(8,128)S(1)}) custom-call(f32[27,8,16,128]{3,2,1,0:T(8,128)S(1)} %bitcast.14, f32[3,8,16,128]{3,2,1,0:T(8,128)S(1)} %shard_map.64._.refs_1_, s32[1,8,16,128]{3,2,1,0:T(8,128)S(1)} %copy-done.1, ...), custom_call_target="tpu_custom_call" | custom-call | tf_op jit(solution)/shard_map/pallas_call | solution.py:455
  14.6 0.4 %shard_map.69 = f32[9,16,128]{2,1,0:T(8,128)S(1)} custom-call(f32[10,16,128]{2,1,0:T(8,128)S(1)} %get-tuple-element.20.refs_0_, f32[10,16,128]{2,1,0:T(8,128)S(1)} %collective-permute-done.first.refs_3_.refs_1_, f32[10,16,128]{2,1,0:T(8,128)S(1)} %collective-permute-done.1.second.refs_4_.refs_2_, f32[10,16,128]{2,1,0:T(8,128)S(1)} %collective-permute-done.2.refs_3_.refs_5_, ...), custom_call_target="tpu_custom_call" | custom-call | tf_op jit(solution)/shard_map/pallas_call | solution.py:472
  15.0 0.5 %collective-permute-start.6 = (f32[9,16,128]{2,1,0:T(8,128)S(1)}, f32[9,16,128]{2,1,0:T(8,128)S(1)}, u32[]{:S(2)}, u32[]{:S(2)}) collective-permute-start(f32[9,16,128]{2,1,0:T(8,128)S(1)} %shard_map.69), channel_id=1, source_target_pairs={{0,16},{1,17},{2,18},{3,19},{4,20},{5,21},{6,22},{7,23},{8,24},{9,... | collective-permute-start | bytes 221192 | tf_op jit(solution)/shard_map/ppermute | solution.py:373
  15.5 1.2 %collective-permute-done.3.refs_6_ = f32[10,16,128]{2,1,0:T(8,128)S(1)} collective-permute-done((f32[10,16,128]{2,1,0:T(8,128)S(1)}, f32[10,16,128]{2,1,0:T(8,128)S(1)}, u32[]{:S(2)}, u32[]{:S(2)}) %collective-permute-start.3) | collective-permute-done | bytes 81952 | tf_op jit(solution)/shard_map/ppermute | solution.py:373
  16.7 0.7 %shard_map.70 = (f32[27,8,16,128]{3,2,1,0:T(8,128)S(1)}, f32[10,16,128]{2,1,0:T(8,128)S(1)}, f32[10,16,128]{2,1,0:T(8,128)S(1)}) custom-call(f32[27,8,16,128]{3,2,1,0:T(8,128)S(1)} %bitcast.15, f32[3,8,16,128]{3,2,1,0:T(8,128)S(1)} %shard_map.64._.refs_1_, s32[1,8,16,128]{3,2,1,0:T(8,128)S(1)} %copy-done.1, ...), custom_call_target="tpu_custom_call", output_to_operand_aliasing={{0}: (10, {})} | custom-call | tf_op jit(solution)/shard_map/pallas_call | solution.py:455
  17.4 0.9 %collective-permute-start.8 = (f32[10,16,128]{2,1,0:T(8,128)S(1)}, f32[10,16,128]{2,1,0:T(8,128)S(1)}, u32[]{:S(2)}, u32[]{:S(2)}) collective-permute-start(f32[10,16,128]{2,1,0:T(8,128)S(1)} %get-tuple-element.29), channel_id=1, source_target_pairs={{0,16},{1,2},{2,1},{3,19},{4,20},{5,6},{6,5},{7,23},{8,24},{9,10},... | collective-permute-start | bytes 245768 | tf_op jit(solution)/shard_map/ppermute | solution.py:373
  18.3 1.6 %shard_map.71._.refs_1_ = f32[3,8,16,128]{3,2,1,0:T(8,128)S(1)} custom-call(f32[2,1,27,8,16,128]{5,4,3,2,1,0:T(8,128)} %refs_0_.3), custom_call_target="tpu_custom_call" | custom-call | tf_op jit(solution)/shard_map/pallas_call | solution.py:432
  20.0 3.0 %collective-permute-start.11 = (f32[10,16,128]{2,1,0:T(8,128)S(1)}, f32[10,16,128]{2,1,0:T(8,128)S(1)}, u32[]{:S(2)}, u32[]{:S(2)}) collective-permute-start(f32[10,16,128]{2,1,0:T(8,128)S(1)} %get-tuple-element.28.refs_0_), channel_id=1, source_target_pairs={{0,16},{1,17},{2,18},{3,19},{4,20},{5,21},{6,22},{7,23},{8,24},{9,... | collective-permute-start | bytes 245768 | tf_op jit(solution)/shard_map/ppermute | solution.py:373
  23.1 1.9 %collective-permute-start.9 = (f32[10,16,128]{2,1,0:T(8,128)S(1)}, f32[10,16,128]{2,1,0:T(8,128)S(1)}, u32[]{:S(2)}, u32[]{:S(2)}) collective-permute-start(f32[10,16,128]{2,1,0:T(8,128)S(1)} %get-tuple-element.30), channel_id=1, source_target_pairs={{0,16},{1,17},{2,18},{3,19},{4,8},{5,9},{6,10},{7,11},{8,4},{9,5},... | collective-permute-start | bytes 245768 | tf_op jit(solution)/shard_map/ppermute | solution.py:373
  25.0 1.7 %shard_map.73 = (f32[27,8,16,128]{3,2,1,0:T(8,128)}, f32[16,128]{1,0:T(8,128)S(1)}, f32[16,128]{1,0:T(8,128)S(1)}) custom-call(f32[27,8,16,128]{3,2,1,0:T(8,128)S(1)} %get-tuple-element.27.adj.refs_0_, f32[3,8,16,128]{3,2,1,0:T(8,128)S(1)} %shard_map.71._.refs_1_, s32[1,8,16,128]{3,2,1,0:T(8,128)S(1)} %copy-done.1, ...), custom_call_target="tpu_custom_call" | custom-call | tf_op jit(solution)/shard_map/pallas_call | solution.py:455
  26.7 0.4 %collective-permute-done.11.refs_4_ = f32[10,16,128]{2,1,0:T(8,128)S(1)} collective-permute-done((f32[10,16,128]{2,1,0:T(8,128)S(1)}, f32[10,16,128]{2,1,0:T(8,128)S(1)}, u32[]{:S(2)}, u32[]{:S(2)}) %collective-permute-start.11) | collective-permute-done | bytes 81952 | tf_op jit(solution)/shard_map/ppermute | solution.py:373
  27.2 1.1 %collective-permute-done.9.refs_3_.refs_5_ = f32[10,16,128]{2,1,0:T(8,128)S(1)} collective-permute-done((f32[10,16,128]{2,1,0:T(8,128)S(1)}, f32[10,16,128]{2,1,0:T(8,128)S(1)}, u32[]{:S(2)}, u32[]{:S(2)}) %collective-permute-start.9) | collective-permute-done | bytes 81952 | tf_op jit(solution)/shard_map/ppermute | solution.py:373
  28.3 0.3 %shard_map.74 = f32[9,16,128]{2,1,0:T(8,128)S(1)} custom-call(f32[10,16,128]{2,1,0:T(8,128)S(1)} %get-tuple-element.28.refs_0_, f32[10,16,128]{2,1,0:T(8,128)S(1)} %collective-permute-done.7.first.refs_3_.refs_1_, f32[10,16,128]{2,1,0:T(8,128)S(1)} %collective-permute-done.8.second.refs_4_.refs_2_, ...), custom_call_target="tpu_custom_call" | custom-call | tf_op jit(solution)/shard_map/pallas_call | solution.py:472
  28.6 1.8 %collective-permute-start.12 = (f32[9,16,128]{2,1,0:T(8,128)S(1)}, f32[9,16,128]{2,1,0:T(8,128)S(1)}, u32[]{:S(2)}, u32[]{:S(2)}) collective-permute-start(f32[9,16,128]{2,1,0:T(8,128)S(1)} %shard_map.74), channel_id=1, source_target_pairs={{0,16},{1,17},{2,18},{3,19},{4,20},{5,21},{6,22},{7,23},{8,24},{9,... | collective-permute-start | bytes 221192 | tf_op jit(solution)/shard_map/ppermute | solution.py:373
  30.5 0.9 %collective-permute-done.12.refs_7_ = f32[9,16,128]{2,1,0:T(8,128)S(1)} collective-permute-done((f32[9,16,128]{2,1,0:T(8,128)S(1)}, f32[9,16,128]{2,1,0:T(8,128)S(1)}, u32[]{:S(2)}, u32[]{:S(2)}) %collective-permute-start.12) | collective-permute-done | bytes 73760 | tf_op jit(solution)/shard_map/ppermute | solution.py:373
  31.4 1.0 %shard_map.75 = f32[27,8,16,128]{3,2,1,0:T(8,128)} custom-call(f32[27,8,16,128]{3,2,1,0:T(8,128)S(1)} %get-tuple-element.27.adj.refs_0_, f32[3,8,16,128]{3,2,1,0:T(8,128)S(1)} %shard_map.71._.refs_1_, s32[1,8,16,128]{3,2,1,0:T(8,128)S(1)} %copy-done.1, ...), custom_call_target="tpu_custom_call", output_to_operand_aliasing={{}: (10, {})} | custom-call | tf_op jit(solution)/shard_map/pallas_call | solution.py:455
  (24 shorter events, 0.2 us)
Async XLA Ops:
  2.0 6.1 %collective-permute-start.1 = (f32[10,16,128]{2,1,0:T(8,128)S(1)}, f32[10,16,128]{2,1,0:T(8,128)S(1)}, u32[]{:S(2)}, u32[]{:S(2)}) collective-permute-start(f32[10,16,128]{2,1,0:T(8,128)S(1)} %get-tuple-element.21), channel_id=1, source_target_pairs={{0,16},{1,2},{2,1},{3,19},{4,20},{5,6},{6,5},{7,23},{8,24},{9,10},... | collective-permute-start | bytes 245768 | tf_op jit(solution)/shard_map/ppermute | solution.py:373
  2.8 5.3 %copy-start = (f32[1,27,8,16,128]{4,3,2,1,0:T(8,128)S(1)}, f32[1,27,8,16,128]{4,3,2,1,0:T(8,128)}, u32[]{:S(2)}) copy-start(f32[1,27,8,16,128]{4,3,2,1,0:T(8,128)} %param.6) | copy-start | bytes 5308420
  2.8 5.3 %collective-permute-start = (f32[10,16,128]{2,1,0:T(8,128)S(1)}, f32[10,16,128]{2,1,0:T(8,128)S(1)}, u32[]{:S(2)}, u32[]{:S(2)}) collective-permute-start(f32[10,16,128]{2,1,0:T(8,128)S(1)} %get-tuple-element.20.refs_0_), channel_id=1, source_target_pairs={{0,1},{1,0},{2,3},{3,2},{4,5},{5,4},{6,7},{7,6},{8,9},{9,8},{10,11... | collective-permute-start | bytes 245768 | tf_op jit(solution)/shard_map/ppermute | solution.py:373
  4.7 9.9 %collective-permute-start.4 = (f32[10,16,128]{2,1,0:T(8,128)S(1)}, f32[10,16,128]{2,1,0:T(8,128)S(1)}, u32[]{:S(2)}, u32[]{:S(2)}) collective-permute-start(f32[10,16,128]{2,1,0:T(8,128)S(1)} %get-tuple-element.20.refs_0_), channel_id=1, source_target_pairs={{0,16},{1,17},{2,18},{3,19},{4,20},{5,21},{6,22},{7,23},{8,24},{9,... | collective-permute-start | bytes 245768 | tf_op jit(solution)/shard_map/ppermute | solution.py:373
  8.0 3.1 %copy-start.2 = (s32[1,16,128,2]{2,3,1,0:T(2,128)S(1)}, s32[1,16,128,2]{2,3,1,0:T(2,128)}, u32[]{:S(2)}) copy-start(s32[1,16,128,2]{2,3,1,0:T(2,128)} %param.9) | copy-start | bytes 49156
  8.0 3.1 %copy-start.3 = (s32[1,16,128,2]{2,3,1,0:T(2,128)S(1)}, s32[1,16,128,2]{2,3,1,0:T(2,128)}, u32[]{:S(2)}) copy-start(s32[1,16,128,2]{2,3,1,0:T(2,128)} %param.10) | copy-start | bytes 49156
  8.0 3.0 %copy-start.4 = (f32[1,16,128,2]{2,3,1,0:T(2,128)S(1)}, f32[1,16,128,2]{2,3,1,0:T(2,128)}, u32[]{:S(2)}) copy-start(f32[1,16,128,2]{2,3,1,0:T(2,128)} %param.11) | copy-start | bytes 49156
  8.1 4.7 %copy-start.1 = (s32[1,8,16,128]{3,2,1,0:T(8,128)S(1)}, s32[1,8,16,128]{3,2,1,0:T(8,128)}, u32[]{:S(2)}) copy-start(s32[1,8,16,128]{3,2,1,0:T(8,128)} %refs_2_.7) | copy-start | bytes 196612
  8.2 6.4 %collective-permute-start.2 = (f32[10,16,128]{2,1,0:T(8,128)S(1)}, f32[10,16,128]{2,1,0:T(8,128)S(1)}, u32[]{:S(2)}, u32[]{:S(2)}) collective-permute-start(f32[10,16,128]{2,1,0:T(8,128)S(1)} %get-tuple-element.22), channel_id=1, source_target_pairs={{0,16},{1,17},{2,18},{3,19},{4,8},{5,9},{6,10},{7,11},{8,4},{9,5},... | collective-permute-start | bytes 245768 | tf_op jit(solution)/shard_map/ppermute | solution.py:373
  11.1 3.5 %collective-permute-start.5 = (f32[4,16,128]{2,1,0:T(8,128)S(1)}, f32[4,16,128]{2,1,0:T(8,128)S(1)}, u32[]{:S(2)}, u32[]{:S(2)}) collective-permute-start(f32[4,16,128]{2,1,0:T(8,128)S(1)} %shard_map.67), channel_id=1, source_target_pairs={{0,16},{1,17},{2,18},{3,19},{4,20},{5,21},{6,22},{7,23},{8,24},{9,... | collective-permute-start | bytes 98312 | tf_op jit(solution)/shard_map/ppermute | solution.py:373
  12.7 4.0 %collective-permute-start.3 = (f32[10,16,128]{2,1,0:T(8,128)S(1)}, f32[10,16,128]{2,1,0:T(8,128)S(1)}, u32[]{:S(2)}, u32[]{:S(2)}) collective-permute-start(f32[10,16,128]{2,1,0:T(8,128)S(1)} %get-tuple-element.23), channel_id=1, source_target_pairs={{0,4},{1,5},{2,6},{3,7},{4,0},{5,1},{6,2},{7,3},{8,12},{9,13},{10,... | collective-permute-start | bytes 245768 | tf_op jit(solution)/shard_map/ppermute | solution.py:373
  15.0 1.8 %collective-permute-start.6 = (f32[9,16,128]{2,1,0:T(8,128)S(1)}, f32[9,16,128]{2,1,0:T(8,128)S(1)}, u32[]{:S(2)}, u32[]{:S(2)}) collective-permute-start(f32[9,16,128]{2,1,0:T(8,128)S(1)} %shard_map.69), channel_id=1, source_target_pairs={{0,16},{1,17},{2,18},{3,19},{4,20},{5,21},{6,22},{7,23},{8,24},{9,... | collective-permute-start | bytes 221192 | tf_op jit(solution)/shard_map/ppermute | solution.py:373
  17.4 5.6 %collective-permute-start.8 = (f32[10,16,128]{2,1,0:T(8,128)S(1)}, f32[10,16,128]{2,1,0:T(8,128)S(1)}, u32[]{:S(2)}, u32[]{:S(2)}) collective-permute-start(f32[10,16,128]{2,1,0:T(8,128)S(1)} %get-tuple-element.29), channel_id=1, source_target_pairs={{0,16},{1,2},{2,1},{3,19},{4,20},{5,6},{6,5},{7,23},{8,24},{9,10},... | collective-permute-start | bytes 245768 | tf_op jit(solution)/shard_map/ppermute | solution.py:373
  18.3 4.6 %collective-permute-start.7 = (f32[10,16,128]{2,1,0:T(8,128)S(1)}, f32[10,16,128]{2,1,0:T(8,128)S(1)}, u32[]{:S(2)}, u32[]{:S(2)}) collective-permute-start(f32[10,16,128]{2,1,0:T(8,128)S(1)} %get-tuple-element.28.refs_0_), channel_id=1, source_target_pairs={{0,1},{1,0},{2,3},{3,2},{4,5},{5,4},{6,7},{7,6},{8,9},{9,8},{10,11... | collective-permute-start | bytes 245768 | tf_op jit(solution)/shard_map/ppermute | solution.py:373
  20.0 7.2 %collective-permute-start.11 = (f32[10,16,128]{2,1,0:T(8,128)S(1)}, f32[10,16,128]{2,1,0:T(8,128)S(1)}, u32[]{:S(2)}, u32[]{:S(2)}) collective-permute-start(f32[10,16,128]{2,1,0:T(8,128)S(1)} %get-tuple-element.28.refs_0_), channel_id=1, source_target_pairs={{0,16},{1,17},{2,18},{3,19},{4,20},{5,21},{6,22},{7,23},{8,24},{9,... | collective-permute-start | bytes 245768 | tf_op jit(solution)/shard_map/ppermute | solution.py:373
  23.1 5.2 %collective-permute-start.9 = (f32[10,16,128]{2,1,0:T(8,128)S(1)}, f32[10,16,128]{2,1,0:T(8,128)S(1)}, u32[]{:S(2)}, u32[]{:S(2)}) collective-permute-start(f32[10,16,128]{2,1,0:T(8,128)S(1)} %get-tuple-element.30), channel_id=1, source_target_pairs={{0,16},{1,17},{2,18},{3,19},{4,8},{5,9},{6,10},{7,11},{8,4},{9,5},... | collective-permute-start | bytes 245768 | tf_op jit(solution)/shard_map/ppermute | solution.py:373
  25.0 5.5 %collective-permute-start.10 = (f32[10,16,128]{2,1,0:T(8,128)S(1)}, f32[10,16,128]{2,1,0:T(8,128)S(1)}, u32[]{:S(2)}, u32[]{:S(2)}) collective-permute-start(f32[10,16,128]{2,1,0:T(8,128)S(1)} %get-tuple-element.31), channel_id=1, source_target_pairs={{0,4},{1,5},{2,6},{3,7},{4,0},{5,1},{6,2},{7,3},{8,12},{9,13},{10,... | collective-permute-start | bytes 245768 | tf_op jit(solution)/shard_map/ppermute | solution.py:373
  28.6 2.7 %collective-permute-start.12 = (f32[9,16,128]{2,1,0:T(8,128)S(1)}, f32[9,16,128]{2,1,0:T(8,128)S(1)}, u32[]{:S(2)}, u32[]{:S(2)}) collective-permute-start(f32[9,16,128]{2,1,0:T(8,128)S(1)} %shard_map.74), channel_id=1, source_target_pairs={{0,16},{1,17},{2,18},{3,19},{4,20},{5,21},{6,22},{7,23},{8,24},{9,... | collective-permute-start | bytes 221192 | tf_op jit(solution)/shard_map/ppermute | solution.py:373

commit v10 on v9

--- a/solution.py
+++ b/solution.py
@@ -107,11 +107,10 @@
 def side_kernel(adj, first, second, _, two_out, one_out):
     extent_x = adj.shape[1]
     even = is_even("gx")
-    interface = lax.axis_index("gx") == lax.axis_size("gx") - 1
     for j in range(9):
         top, bottom = adj[j, extent_x - 1], adj[18 + j, 0]
         one_out[j] = jnp.where(even, top, bottom)
-        two_out[j] = jnp.where(even | interface, jnp.where(interface, top, bottom), top)
+        two_out[j] = jnp.where(even, bottom, top)
     lane = lanes()
     low, high = edges_from(first, second)
     top, bottom = [
@@ -393,11 +392,14 @@
 
         return target
 
+    def ends_z(zone, gx, yz):
+        if gx == widths - 1 and yz in (0, count - 1):
+            return (zone, gx, count - 1 - yz)
+        return flip(zone, gx, yz)
+
     def along_x(shift):
         def target(zone, gx, yz):
             to = partner_of(gx, shift)
-            if gx == widths - 1 and shift == 1 and yz in (0, count - 1):
-                return (zone, gx, count - 1 - yz)
             return (zone, to, yz) if 0 <= to < widths else flip(zone, gx, yz)
 
         return target
@@ -428,7 +430,7 @@
         own = first
         first = send(own, along_z(0))
         second = send(second, along_z(1))
-        others = [send(own, hop_z(hop)) for hop in range(2, count - 1)]
+        others = [send(own, target) for target in (ends_z, *map(hop_z, range(2, count - 1)))]
         vel = pl.pallas_call(
             lambda *refs: velocity_kernel(step, *refs),
             out_shape=tile_shape(3, extent_x),
@@ -475,7 +477,7 @@
             in_specs=in_vmem(count + 2) + in_any(1),
             out_specs=in_vmem(1)[0],
             compiler_params=params,
-        )(own, first, second, two, *others, info, columns[0])
+        )(own, first, second, *others, info, columns[0])
         cross = send(cross, flip)
         field, *messages = make_planes(
             outer_kernel, 2, (two, one, cross, *columns), (new,), messages

time: 32.6 us -> 29.8 us (0.914)
  the two profiles are of different devices: /device:TPU:7 before, /device:TPU:0 now
where the time goes in v10:
time: 29.8 us; the launch traced here: 29.6 us
  starting transfers between devices  13.3 us (45%)
  Pallas kernels  10.9 us (37%)
  waiting for transfers between devices  4.96 us (17%)
    ppermute x15, starting transfers between devices, send(): lax.ppermute(values, axes, [(flat(*here), flat(*target(*here))) for here...  13.3 us
    pallas_call x4, Pallas kernels, make_planes(): pl.pallas_call(lambda *refs: kernel(step, *refs), out_shape=(tile_shape(2...  5.26 us
    ppermute x15, waiting for transfers between devices, send(): lax.ppermute(values, axes, [(flat(*here), flat(*target(*here))) for here...  4.96 us
    pallas_call x2, Pallas kernels, body(): pl.pallas_call(lambda *refs: velocity_kernel(step, *refs), out_shape=tile...  3.38 us
    pallas_call x1, Pallas kernels, body(): pl.pallas_call(pack_kernel, out_shape=(tile_shape(10),) * 2, in_specs=[pl...  2.02 us
  transfers between devices with their start and end apart: 15, of which 5 were waited for; matrix products, arithmetic and copies ran while one was open for 0% of the time, Pallas kernels for 24%

profile of v10, /device:TPU:0, one launch (start us, length us, event | category | flops | bytes accessed | tf_op | source)
XLA Modules:
  0.0 29.6 jit_solution(2169016468130602193)
XLA Ops:
  0.0 2.0 %shard_map.65 = (f32[10,16,128]{2,1,0:T(8,128)S(1)}, f32[10,16,128]{2,1,0:T(8,128)S(1)}) custom-call(f32[9,3,8,16,128]{4,3,2,1,0:T(8,128)} %bitcast.12), custom_call_target="tpu_custom_call" | custom-call | tf_op jit(solution)/shard_map/pallas_call | solution.py:415
  2.0 0.5 %collective-permute-start.1 = (f32[10,16,128]{2,1,0:T(8,128)S(1)}, f32[10,16,128]{2,1,0:T(8,128)S(1)}, u32[]{:S(2)}, u32[]{:S(2)}) collective-permute-start(f32[10,16,128]{2,1,0:T(8,128)S(1)} %get-tuple-element.21), channel_id=1, source_target_pairs={{0,16},{1,2},{2,1},{3,19},{4,20},{5,6},{6,5},{7,23},{8,24},{9,10},... | collective-permute-start | bytes 245768 | tf_op jit(solution)/shard_map/ppermute | solution.py:372
  2.6 4.1 %collective-permute-start = (f32[10,16,128]{2,1,0:T(8,128)S(1)}, f32[10,16,128]{2,1,0:T(8,128)S(1)}, u32[]{:S(2)}, u32[]{:S(2)}) collective-permute-start(f32[10,16,128]{2,1,0:T(8,128)S(1)} %get-tuple-element.20.refs_0_), channel_id=1, source_target_pairs={{0,1},{1,0},{2,3},{3,2},{4,5},{5,4},{6,7},{7,6},{8,9},{9,8},{10,11... | collective-permute-start | bytes 245768 | tf_op jit(solution)/shard_map/ppermute | solution.py:372
  6.7 0.5 %collective-permute-start.4 = (f32[10,16,128]{2,1,0:T(8,128)S(1)}, f32[10,16,128]{2,1,0:T(8,128)S(1)}, u32[]{:S(2)}, u32[]{:S(2)}) collective-permute-start(f32[10,16,128]{2,1,0:T(8,128)S(1)} %get-tuple-element.20.refs_0_), channel_id=1, source_target_pairs={{0,16},{1,17},{2,18},{3,19},{4,20},{5,21},{6,22},{7,23},{8,24},{9,... | collective-permute-start | bytes 245768 | tf_op jit(solution)/shard_map/ppermute | solution.py:372
  7.3 0.1 collective-permute-start.6
  7.4 1.7 %shard_map.64._.refs_1_ = f32[3,8,16,128]{3,2,1,0:T(8,128)S(1)} custom-call(f32[2,1,27,8,16,128]{5,4,3,2,1,0:T(8,128)} %refs_0_.3), custom_call_target="tpu_custom_call" | custom-call | tf_op jit(solution)/shard_map/pallas_call | solution.py:434
  9.2 0.3 copy-done
  9.4 0.1 shard_map.66
  9.5 0.2 collective-permute-start.2
  9.7 2.8 %collective-permute-start.3 = (f32[10,16,128]{2,1,0:T(8,128)S(1)}, f32[10,16,128]{2,1,0:T(8,128)S(1)}, u32[]{:S(2)}, u32[]{:S(2)}) collective-permute-start(f32[10,16,128]{2,1,0:T(8,128)S(1)} %get-tuple-element.23), channel_id=1, source_target_pairs={{0,4},{1,5},{2,6},{3,7},{4,0},{5,1},{6,2},{7,3},{8,12},{9,13},{10,... | collective-permute-start | bytes 245768 | tf_op jit(solution)/shard_map/ppermute | solution.py:372
  12.5 1.8 %shard_map.68 = (f32[27,8,16,128]{3,2,1,0:T(8,128)S(1)}, f32[16,128]{1,0:T(8,128)S(1)}, f32[16,128]{1,0:T(8,128)S(1)}) custom-call(f32[27,8,16,128]{3,2,1,0:T(8,128)S(1)} %bitcast.14, f32[3,8,16,128]{3,2,1,0:T(8,128)S(1)} %shard_map.64._.refs_1_, s32[1,8,16,128]{3,2,1,0:T(8,128)S(1)} %copy-done.1, ...), custom_call_target="tpu_custom_call" | custom-call | tf_op jit(solution)/shard_map/pallas_call | solution.py:457
  14.5 1.3 %collective-permute-done.7.refs_7_ = f32[9,16,128]{2,1,0:T(8,128)S(1)} collective-permute-done((f32[9,16,128]{2,1,0:T(8,128)S(1)}, f32[9,16,128]{2,1,0:T(8,128)S(1)}, u32[]{:S(2)}, u32[]{:S(2)}) %collective-permute-start.7) | collective-permute-done | bytes 73760 | tf_op jit(solution)/shard_map/ppermute | solution.py:372
  15.7 1.0 %collective-permute-done.3.refs_6_ = f32[10,16,128]{2,1,0:T(8,128)S(1)} collective-permute-done((f32[10,16,128]{2,1,0:T(8,128)S(1)}, f32[10,16,128]{2,1,0:T(8,128)S(1)}, u32[]{:S(2)}, u32[]{:S(2)}) %collective-permute-start.3) | collective-permute-done | bytes 81952 | tf_op jit(solution)/shard_map/ppermute | solution.py:372
  16.7 0.7 %shard_map.70 = (f32[27,8,16,128]{3,2,1,0:T(8,128)S(1)}, f32[10,16,128]{2,1,0:T(8,128)S(1)}, f32[10,16,128]{2,1,0:T(8,128)S(1)}) custom-call(f32[27,8,16,128]{3,2,1,0:T(8,128)S(1)} %bitcast.15, f32[3,8,16,128]{3,2,1,0:T(8,128)S(1)} %shard_map.64._.refs_1_, s32[1,8,16,128]{3,2,1,0:T(8,128)S(1)} %copy-done.1, ...), custom_call_target="tpu_custom_call", output_to_operand_aliasing={{0}: (10, {})} | custom-call | tf_op jit(solution)/shard_map/pallas_call | solution.py:457
  17.5 1.7 %collective-permute-start.8 = (f32[10,16,128]{2,1,0:T(8,128)S(1)}, f32[10,16,128]{2,1,0:T(8,128)S(1)}, u32[]{:S(2)}, u32[]{:S(2)}) collective-permute-start(f32[10,16,128]{2,1,0:T(8,128)S(1)} %get-tuple-element.28.refs_0_), channel_id=1, source_target_pairs={{0,1},{1,0},{2,3},{3,2},{4,5},{5,4},{6,7},{7,6},{8,9},{9,8},{10,11... | collective-permute-start | bytes 245768 | tf_op jit(solution)/shard_map/ppermute | solution.py:372
  19.2 0.5 %collective-permute-start.12 = (f32[10,16,128]{2,1,0:T(8,128)S(1)}, f32[10,16,128]{2,1,0:T(8,128)S(1)}, u32[]{:S(2)}, u32[]{:S(2)}) collective-permute-start(f32[10,16,128]{2,1,0:T(8,128)S(1)} %get-tuple-element.28.refs_0_), channel_id=1, source_target_pairs={{0,16},{1,17},{2,18},{3,19},{4,20},{5,21},{6,22},{7,23},{8,24},{9,... | collective-permute-start | bytes 245768 | tf_op jit(solution)/shard_map/ppermute | solution.py:372
  19.7 1.6 %shard_map.71._.refs_1_ = f32[3,8,16,128]{3,2,1,0:T(8,128)S(1)} custom-call(f32[2,1,27,8,16,128]{5,4,3,2,1,0:T(8,128)} %refs_0_.3), custom_call_target="tpu_custom_call" | custom-call | tf_op jit(solution)/shard_map/pallas_call | solution.py:434
  21.4 0.9 %collective-permute-done.8.first.refs_3_.refs_1_ = f32[10,16,128]{2,1,0:T(8,128)S(1)} collective-permute-done((f32[10,16,128]{2,1,0:T(8,128)S(1)}, f32[10,16,128]{2,1,0:T(8,128)S(1)}, u32[]{:S(2)}, u32[]{:S(2)}) %collective-permute-start.8) | collective-permute-done | bytes 81952 | tf_op jit(solution)/shard_map/ppermute | solution.py:372
  22.3 0.1 shard_map.72
  22.4 2.5 %collective-permute-start.11 = (f32[10,16,128]{2,1,0:T(8,128)S(1)}, f32[10,16,128]{2,1,0:T(8,128)S(1)}, u32[]{:S(2)}, u32[]{:S(2)}) collective-permute-start(f32[10,16,128]{2,1,0:T(8,128)S(1)} %get-tuple-element.31), channel_id=1, source_target_pairs={{0,4},{1,5},{2,6},{3,7},{4,0},{5,1},{6,2},{7,3},{8,12},{9,13},{10,... | collective-permute-start | bytes 245768 | tf_op jit(solution)/shard_map/ppermute | solution.py:372
  24.9 1.7 %shard_map.73 = (f32[27,8,16,128]{3,2,1,0:T(8,128)}, f32[16,128]{1,0:T(8,128)S(1)}, f32[16,128]{1,0:T(8,128)S(1)}) custom-call(f32[27,8,16,128]{3,2,1,0:T(8,128)S(1)} %get-tuple-element.27.adj.refs_0_, f32[3,8,16,128]{3,2,1,0:T(8,128)S(1)} %shard_map.71._.refs_1_, s32[1,8,16,128]{3,2,1,0:T(8,128)S(1)} %copy-done.1, ...), custom_call_target="tpu_custom_call" | custom-call | tf_op jit(solution)/shard_map/pallas_call | solution.py:457
  26.8 1.3 %collective-permute-done.14.refs_7_ = f32[9,16,128]{2,1,0:T(8,128)S(1)} collective-permute-done((f32[9,16,128]{2,1,0:T(8,128)S(1)}, f32[9,16,128]{2,1,0:T(8,128)S(1)}, u32[]{:S(2)}, u32[]{:S(2)}) %collective-permute-start.14) | collective-permute-done | bytes 73760 | tf_op jit(solution)/shard_map/ppermute | solution.py:372
  28.1 0.5 %collective-permute-done.11.refs_6_ = f32[10,16,128]{2,1,0:T(8,128)S(1)} collective-permute-done((f32[10,16,128]{2,1,0:T(8,128)S(1)}, f32[10,16,128]{2,1,0:T(8,128)S(1)}, u32[]{:S(2)}, u32[]{:S(2)}) %collective-permute-start.11) | collective-permute-done | bytes 81952 | tf_op jit(solution)/shard_map/ppermute | solution.py:372
  28.6 1.0 %shard_map.75 = f32[27,8,16,128]{3,2,1,0:T(8,128)} custom-call(f32[27,8,16,128]{3,2,1,0:T(8,128)S(1)} %get-tuple-element.27.adj.refs_0_, f32[3,8,16,128]{3,2,1,0:T(8,128)S(1)} %shard_map.71._.refs_1_, s32[1,8,16,128]{3,2,1,0:T(8,128)S(1)} %copy-done.1, ...), custom_call_target="tpu_custom_call", output_to_operand_aliasing={{}: (10, {})} | custom-call | tf_op jit(solution)/shard_map/pallas_call | solution.py:457
  (28 shorter events, 0.4 us)
Async XLA Ops:
  0.0 7.2 %copy-start.4 = (f32[1,16,128,2]{2,3,1,0:T(2,128)S(1)}, f32[1,16,128,2]{2,3,1,0:T(2,128)}, u32[]{:S(2)}) copy-start(f32[1,16,128,2]{2,3,1,0:T(2,128)} %param.11) | copy-start | bytes 49156
  0.0 7.2 %copy-start.3 = (s32[1,16,128,2]{2,3,1,0:T(2,128)S(1)}, s32[1,16,128,2]{2,3,1,0:T(2,128)}, u32[]{:S(2)}) copy-start(s32[1,16,128,2]{2,3,1,0:T(2,128)} %param.10) | copy-start | bytes 49156
  0.0 7.2 %copy-start.2 = (s32[1,16,128,2]{2,3,1,0:T(2,128)S(1)}, s32[1,16,128,2]{2,3,1,0:T(2,128)}, u32[]{:S(2)}) copy-start(s32[1,16,128,2]{2,3,1,0:T(2,128)} %param.9) | copy-start | bytes 49156
  2.0 7.1 %collective-permute-start.1 = (f32[10,16,128]{2,1,0:T(8,128)S(1)}, f32[10,16,128]{2,1,0:T(8,128)S(1)}, u32[]{:S(2)}, u32[]{:S(2)}) collective-permute-start(f32[10,16,128]{2,1,0:T(8,128)S(1)} %get-tuple-element.21), channel_id=1, source_target_pairs={{0,16},{1,2},{2,1},{3,19},{4,20},{5,6},{6,5},{7,23},{8,24},{9,10},... | collective-permute-start | bytes 245768 | tf_op jit(solution)/shard_map/ppermute | solution.py:372
  2.6 6.6 %collective-permute-start = (f32[10,16,128]{2,1,0:T(8,128)S(1)}, f32[10,16,128]{2,1,0:T(8,128)S(1)}, u32[]{:S(2)}, u32[]{:S(2)}) collective-permute-start(f32[10,16,128]{2,1,0:T(8,128)S(1)} %get-tuple-element.20.refs_0_), channel_id=1, source_target_pairs={{0,1},{1,0},{2,3},{3,2},{4,5},{5,4},{6,7},{7,6},{8,9},{9,8},{10,11... | collective-permute-start | bytes 245768 | tf_op jit(solution)/shard_map/ppermute | solution.py:372
  6.7 7.6 %collective-permute-start.5 = (f32[10,16,128]{2,1,0:T(8,128)S(1)}, f32[10,16,128]{2,1,0:T(8,128)S(1)}, u32[]{:S(2)}, u32[]{:S(2)}) collective-permute-start(f32[10,16,128]{2,1,0:T(8,128)S(1)} %get-tuple-element.20.refs_0_), channel_id=1, source_target_pairs={{0,16},{1,17},{2,18},{3,19},{4,20},{5,21},{6,22},{7,23},{8,24},{9,... | collective-permute-start | bytes 245768 | tf_op jit(solution)/shard_map/ppermute | solution.py:372
  6.7 7.6 %collective-permute-start.4 = (f32[10,16,128]{2,1,0:T(8,128)S(1)}, f32[10,16,128]{2,1,0:T(8,128)S(1)}, u32[]{:S(2)}, u32[]{:S(2)}) collective-permute-start(f32[10,16,128]{2,1,0:T(8,128)S(1)} %get-tuple-element.20.refs_0_), channel_id=1, source_target_pairs={{0,16},{1,17},{2,18},{3,19},{4,20},{5,21},{6,22},{7,23},{8,24},{9,... | collective-permute-start | bytes 245768 | tf_op jit(solution)/shard_map/ppermute | solution.py:372
  7.3 2.1 %copy-start = (f32[1,27,8,16,128]{4,3,2,1,0:T(8,128)S(1)}, f32[1,27,8,16,128]{4,3,2,1,0:T(8,128)}, u32[]{:S(2)}) copy-start(f32[1,27,8,16,128]{4,3,2,1,0:T(8,128)} %param.6) | copy-start | bytes 5308420
  7.3 7.1 %collective-permute-start.6 = (f32[4,16,128]{2,1,0:T(8,128)S(1)}, f32[4,16,128]{2,1,0:T(8,128)S(1)}, u32[]{:S(2)}, u32[]{:S(2)}) collective-permute-start(f32[4,16,128]{2,1,0:T(8,128)S(1)} %shard_map.67), channel_id=1, source_target_pairs={{0,16},{1,17},{2,18},{3,19},{4,20},{5,21},{6,22},{7,23},{8,24},{9,... | collective-permute-start | bytes 98312 | tf_op jit(solution)/shard_map/ppermute | solution.py:372
  9.1 3.4 %copy-start.1 = (s32[1,8,16,128]{3,2,1,0:T(8,128)S(1)}, s32[1,8,16,128]{3,2,1,0:T(8,128)}, u32[]{:S(2)}) copy-start(s32[1,8,16,128]{3,2,1,0:T(8,128)} %refs_2_.7) | copy-start | bytes 196612
  9.5 6.2 %collective-permute-start.2 = (f32[10,16,128]{2,1,0:T(8,128)S(1)}, f32[10,16,128]{2,1,0:T(8,128)S(1)}, u32[]{:S(2)}, u32[]{:S(2)}) collective-permute-start(f32[10,16,128]{2,1,0:T(8,128)S(1)} %get-tuple-element.22), channel_id=1, source_target_pairs={{0,16},{1,17},{2,18},{3,19},{4,8},{5,9},{6,10},{7,11},{8,4},{9,5},... | collective-permute-start | bytes 245768 | tf_op jit(solution)/shard_map/ppermute | solution.py:372
  9.7 7.1 %collective-permute-start.3 = (f32[10,16,128]{2,1,0:T(8,128)S(1)}, f32[10,16,128]{2,1,0:T(8,128)S(1)}, u32[]{:S(2)}, u32[]{:S(2)}) collective-permute-start(f32[10,16,128]{2,1,0:T(8,128)S(1)} %get-tuple-element.23), channel_id=1, source_target_pairs={{0,4},{1,5},{2,6},{3,7},{4,0},{5,1},{6,2},{7,3},{8,12},{9,13},{10,... | collective-permute-start | bytes 245768 | tf_op jit(solution)/shard_map/ppermute | solution.py:372
  14.4 1.3 %collective-permute-start.7 = (f32[9,16,128]{2,1,0:T(8,128)S(1)}, f32[9,16,128]{2,1,0:T(8,128)S(1)}, u32[]{:S(2)}, u32[]{:S(2)}) collective-permute-start(f32[9,16,128]{2,1,0:T(8,128)S(1)} %shard_map.69), channel_id=1, source_target_pairs={{0,16},{1,17},{2,18},{3,19},{4,20},{5,21},{6,22},{7,23},{8,24},{9,... | collective-permute-start | bytes 221192 | tf_op jit(solution)/shard_map/ppermute | solution.py:372
  17.4 4.0 %collective-permute-start.9 = (f32[10,16,128]{2,1,0:T(8,128)S(1)}, f32[10,16,128]{2,1,0:T(8,128)S(1)}, u32[]{:S(2)}, u32[]{:S(2)}) collective-permute-start(f32[10,16,128]{2,1,0:T(8,128)S(1)} %get-tuple-element.29), channel_id=1, source_target_pairs={{0,16},{1,2},{2,1},{3,19},{4,20},{5,6},{6,5},{7,23},{8,24},{9,10},... | collective-permute-start | bytes 245768 | tf_op jit(solution)/shard_map/ppermute | solution.py:372
  17.5 4.9 %collective-permute-start.8 = (f32[10,16,128]{2,1,0:T(8,128)S(1)}, f32[10,16,128]{2,1,0:T(8,128)S(1)}, u32[]{:S(2)}, u32[]{:S(2)}) collective-permute-start(f32[10,16,128]{2,1,0:T(8,128)S(1)} %get-tuple-element.28.refs_0_), channel_id=1, source_target_pairs={{0,1},{1,0},{2,3},{3,2},{4,5},{5,4},{6,7},{7,6},{8,9},{9,8},{10,11... | collective-permute-start | bytes 245768 | tf_op jit(solution)/shard_map/ppermute | solution.py:372
  19.2 7.5 %collective-permute-start.13 = (f32[10,16,128]{2,1,0:T(8,128)S(1)}, f32[10,16,128]{2,1,0:T(8,128)S(1)}, u32[]{:S(2)}, u32[]{:S(2)}) collective-permute-start(f32[10,16,128]{2,1,0:T(8,128)S(1)} %get-tuple-element.28.refs_0_), channel_id=1, source_target_pairs={{0,16},{1,17},{2,18},{3,19},{4,20},{5,21},{6,22},{7,23},{8,24},{9,... | collective-permute-start | bytes 245768 | tf_op jit(solution)/shard_map/ppermute | solution.py:372
  19.2 7.5 %collective-permute-start.12 = (f32[10,16,128]{2,1,0:T(8,128)S(1)}, f32[10,16,128]{2,1,0:T(8,128)S(1)}, u32[]{:S(2)}, u32[]{:S(2)}) collective-permute-start(f32[10,16,128]{2,1,0:T(8,128)S(1)} %get-tuple-element.28.refs_0_), channel_id=1, source_target_pairs={{0,16},{1,17},{2,18},{3,19},{4,20},{5,21},{6,22},{7,23},{8,24},{9,... | collective-permute-start | bytes 245768 | tf_op jit(solution)/shard_map/ppermute | solution.py:372
  22.4 5.7 %collective-permute-start.10 = (f32[10,16,128]{2,1,0:T(8,128)S(1)}, f32[10,16,128]{2,1,0:T(8,128)S(1)}, u32[]{:S(2)}, u32[]{:S(2)}) collective-permute-start(f32[10,16,128]{2,1,0:T(8,128)S(1)} %get-tuple-element.30), channel_id=1, source_target_pairs={{0,16},{1,17},{2,18},{3,19},{4,8},{5,9},{6,10},{7,11},{8,4},{9,5},... | collective-permute-start | bytes 245768 | tf_op jit(solution)/shard_map/ppermute | solution.py:372
  22.4 6.1 %collective-permute-start.11 = (f32[10,16,128]{2,1,0:T(8,128)S(1)}, f32[10,16,128]{2,1,0:T(8,128)S(1)}, u32[]{:S(2)}, u32[]{:S(2)}) collective-permute-start(f32[10,16,128]{2,1,0:T(8,128)S(1)} %get-tuple-element.31), channel_id=1, source_target_pairs={{0,4},{1,5},{2,6},{3,7},{4,0},{5,1},{6,2},{7,3},{8,12},{9,13},{10,... | collective-permute-start | bytes 245768 | tf_op jit(solution)/shard_map/ppermute | solution.py:372
  26.7 1.3 %collective-permute-start.14 = (f32[9,16,128]{2,1,0:T(8,128)S(1)}, f32[9,16,128]{2,1,0:T(8,128)S(1)}, u32[]{:S(2)}, u32[]{:S(2)}) collective-permute-start(f32[9,16,128]{2,1,0:T(8,128)S(1)} %shard_map.74), channel_id=1, source_target_pairs={{0,16},{1,17},{2,18},{3,19},{4,20},{5,21},{6,22},{7,23},{8,24},{9,... | collective-permute-start | bytes 221192 | tf_op jit(solution)/shard_map/ppermute | solution.py:372

commit v11 on v10

--- a/solution.py
+++ b/solution.py
@@ -62,23 +62,20 @@
     return low, high
 
 
-def pack_kernel(adj, first_out, second_out, kept, top, sems):
-    extent_x = adj.shape[2]
-    copies = [
-        pltpu.make_async_copy(adj.at[:, 2 * side, x], kept.at[side, x], sems.at[side, x])
-        for x in range(extent_x)
-        for side in range(2)
-    ]
-    copies.append(pltpu.make_async_copy(adj.at[pl.ds(0, 3), :, extent_x - 1], top, sems.at[2, 0]))
+def pack_kernel(adj, top_out, first_out, second_out, kept, sems):
+    extent_x = adj.shape[1]
+    sides = [i for i in range(27) if i % 3 != 1]
+    pairs = [(adj.at[i], kept.at[n]) for n, i in enumerate(sides)]
+    pairs.append((adj.at[pl.ds(0, 9), extent_x - 1], top_out))
+    copies = [pltpu.make_async_copy(*pair, sems.at[n]) for n, pair in enumerate(pairs)]
     for copy in copies:
         copy.start()
+    for copy in copies:
+        copy.wait()
     edges = jnp.zeros((16, 128), jnp.float32), jnp.zeros((16, 128), jnp.float32)
     for x in range(extent_x):
-        for copy in copies[2 * x : 2 * x + 2]:
-            copy.wait()
-        edges = pack_columns(lambda i: kept[(i % 3) // 2, x, i // 3], x, *edges)
-    copies[-1].wait()
-    write_messages(lambda j: top[j // 3, j % 3], *edges, first_out, second_out)
+        edges = pack_columns(lambda i: kept[sides.index(i), x], x, *edges)
+    write_messages(lambda j: top_out[j], *edges, first_out, second_out)
 
 
 def info_kernel(device, cell, weight, out):
@@ -104,7 +101,7 @@
     lax.fori_loop(0, extent_x, one, 0)
 
 
-def side_kernel(adj, first, second, _, two_out, one_out):
+def side_kernel(adj, second, first, _, two_out, one_out):
     extent_x = adj.shape[1]
     even = is_even("gx")
     for j in range(9):
@@ -298,9 +295,11 @@
     lax.fori_loop(1, extent_x - 1, lambda x, c: (save(x).wait(), c)[1], 0)
 
 
-def outer_kernel(step, adj, vel, solid, first, second, two, one, cross, *rest):
-    *rest, made, pulled, sems = rest
-    low_in, high_in, _, out, *messages = rest
+def outer_kernel(x, step, adj, vel, solid, first, second, two, one, *rest):
+    if x == 0:
+        low_in, high_in, _, out, low_out, high_out, made, pulled, sems = rest
+    else:
+        cross, low_in, high_in, _, out, *messages, made, pulled, sems = rest
     extent_x = adj.shape[1]
     edges = edges_from(first, second)
     even = is_even("gx")
@@ -315,36 +314,36 @@
         tile = jnp.where(even, one[j], two[j])
         return jnp.where(interface, cross[j], tile) if j < 9 else tile
 
-    def plane(n, x, ghost, beyond, raw):
-        pull_plane(
-            lambda i, cx: beyond(i % 9) if cx == ghost else adj[i, x + cx],
-            lambda cx: (
-                (beyond(9), pltpu.roll(beyond(9), 64, 1), 0)
-                if cx == ghost
-                else (*edges, (x + 1 + cx) * 9)
-            ),
-            pulled.at[n],
-            raw,
+    ghost, beyond, raw = (-1, below, None) if x == 0 else (1, above, interface)
+    pull_plane(
+        lambda i, cx: beyond(i % 9) if cx == ghost else adj[i, x + cx],
+        lambda cx: (
+            (beyond(9), pltpu.roll(beyond(9), 64, 1), 0)
+            if cx == ghost
+            else (*edges, (x + 1 + cx) * 9)
+        ),
+        pulled.at[0],
+        raw,
+    )
+
+    def store(i, tile):
+        made[0, i] = tile
+
+    velocity = [vel[a, x] for a in range(3)]
+    collide(lambda i: pulled[0, i], velocity, solid[0, x], store)
+    save = pltpu.make_async_copy(made.at[0], out.at[:, x], sems.at[0])
+    save.start()
+    if x == 0:
+        low_out[...], high_out[...] = pack_columns(
+            lambda i: made[0, i], x, low_in[...], high_in[...]
         )
-
-        def store(i, tile):
-            made[n, i] = tile
-
-        velocity = [vel[a, x] for a in range(3)]
-        collide(lambda i: pulled[n, i], velocity, solid[0, x], store)
-        save = pltpu.make_async_copy(made.at[n], out.at[:, x], sems.at[n])
-        save.start()
-        return save
-
-    final = extent_x - 1
-    saves = [plane(0, 0, -1, below, None), plane(1, final, 1, above, interface)]
-    if messages:
-        low, high = low_in[...], high_in[...]
-        low, high = pack_columns(lambda i: made[0, i], 0, low, high)
-        low, high = pack_columns(lambda i: made[1, i], final, low, high)
-        write_messages(lambda j: made[1, j], low, high, *messages)
-    for save in saves:
-        save.wait()
+    elif messages:
+        low, high = pack_columns(lambda i: made[0, i], x, low_in[...], high_in[...])
+        top_out, *messages = messages
+        write_messages(lambda j: made[0, j], low, high, *messages)
+        for j in range(9):
+            top_out[j] = made[0, j]
+    save.wait()
 
 
 def tile_shape(*lead):
@@ -412,25 +411,25 @@
         compiler_params=params,
     )(*[jnp.swapaxes(array[0], 1, 2) for array in (band_device, band_cell, band_weight)])
     info = send(info, flip)
-    first, second = pl.pallas_call(
+    resident = pltpu.with_memory_space_constraint(field, pltpu.HBM)
+    messages = (tile_shape(9), tile_shape(10), tile_shape(10))
+    own, first, second = pl.pallas_call(
         pack_kernel,
-        out_shape=(tile_shape(10),) * 2,
+        out_shape=messages,
         in_specs=[pl.BlockSpec(memory_space=pltpu.HBM)],
-        out_specs=tuple(in_vmem(2)),
+        out_specs=tuple(in_vmem(3)),
         scratch_shapes=[
-            pltpu.VMEM((2, extent_x, 9, 16, 128), jnp.float32),
-            pltpu.VMEM((3, 3, 16, 128), jnp.float32),
-            pltpu.SemaphoreType.DMA((3, extent_x)),
+            pltpu.VMEM((18, extent_x, 16, 128), jnp.float32),
+            pltpu.SemaphoreType.DMA((19,)),
         ],
         compiler_params=params,
-    )(pltpu.with_memory_space_constraint(field.reshape(9, 3, extent_x, 16, 128), pltpu.HBM))
+    )(resident)
     saved = pltpu.with_memory_space_constraint(saved, pltpu.HBM)
     for step in (1, 0):
         last = step == 0
-        own = first
-        first = send(own, along_z(0))
+        others = [send(own, target) for target in (ends_z, *map(hop_z, range(2, count - 1)))]
+        first = send(first, along_z(0))
         second = send(second, along_z(1))
-        others = [send(own, target) for target in (ends_z, *map(hop_z, range(2, count - 1)))]
         vel = pl.pallas_call(
             lambda *refs: velocity_kernel(step, *refs),
             out_shape=tile_shape(3, extent_x),
@@ -448,7 +447,7 @@
             in_specs=in_vmem(3) + in_any(1),
             out_specs=tuple(in_vmem(2)),
             compiler_params=params,
-        )(field, first, second, vel)
+        )(field, second, first, vel)
         two = send(two, along_x(1))
         one = send(one, along_x(0))
 
@@ -468,7 +467,6 @@
                 compiler_params=params,
             )(*operands, *new)
 
-        messages = () if last else (tile_shape(10),) * 2
         kernel = lambda step, *refs: inner_kernel(step, last, *refs)
         new, *columns = make_planes(kernel, extent_x - 2, (), (), (tile_shape(),) * 2)
         cross = pl.pallas_call(
@@ -479,11 +477,19 @@
             compiler_params=params,
         )(own, first, second, *others, info, columns[0])
         cross = send(cross, flip)
-        field, *messages = make_planes(
-            outer_kernel, 2, (two, one, cross, *columns), (new,), messages
+        ghosts = (two, one)
+        new, *columns = make_planes(
+            lambda *refs: outer_kernel(0, *refs), 1, (*ghosts, *columns), (new,), (tile_shape(),) * 2
+        )
+        field, *results = make_planes(
+            lambda *refs: outer_kernel(extent_x - 1, *refs),
+            1,
+            (*ghosts, cross, *columns),
+            (new,),
+            () if last else messages,
         )
         if not last:
-            first, second = messages
+            own, first, second = results
     return field[None]
 
 

time: 29.8 us -> 31.9 us (1.070)
  starting transfers between devices: 13.3 us -> 15 us
  Pallas kernels: 10.9 us -> 11.6 us
    ppermute x15, starting transfers between devices: 13.3 us -> 15 us  [send(): lax.ppermute(values, axes, [(flat(*here), flat(*target(*here))) for here...]
    pallas_call x4 -> x6, Pallas kernels: 5.26 us -> 6.16 us  [make_planes(): pl.pallas_call(lambda *refs: kernel(step, *refs), out_shape=(tile_shape(2...]
  transfers between devices with their start and end apart: 15 -> 15, of which waited for: 5 -> 3; matrix products, arithmetic and copies ran while one was open for 0% -> 0% of each run, Pallas kernels for 24% -> 26%
where the time goes in v11:
time: 31.9 us; the launch traced here: 31.7 us
  starting transfers between devices  15 us (47%)
  Pallas kernels  11.6 us (36%)
  waiting for transfers between devices  4.85 us (15%)
    ppermute x15, starting transfers between devices, send(): lax.ppermute(values, axes, [(flat(*here), flat(*target(*here))) for here...  15 us
    pallas_call x6, Pallas kernels, make_planes(): pl.pallas_call(lambda *refs: kernel(step, *refs), out_shape=(tile_shape(2...  6.16 us
    ppermute x15, waiting for transfers between devices, send(): lax.ppermute(values, axes, [(flat(*here), flat(*target(*here))) for here...  4.85 us
    pallas_call x2, Pallas kernels, body(): pl.pallas_call(lambda *refs: velocity_kernel(step, *refs), out_shape=tile...  3.27 us
    pallas_call x1, Pallas kernels, body(): pl.pallas_call(pack_kernel, out_shape=messages, in_specs=[pl.BlockSpec(me...  1.91 us
  transfers between devices with their start and end apart: 15, of which 3 were waited for; matrix products, arithmetic and copies ran while one was open for 0% of the time, Pallas kernels for 26%

profile of v11, /device:TPU:0, one launch (start us, length us, event | category | flops | bytes accessed | tf_op | source)
XLA Modules:
  0.0 31.7 jit_solution(11379032890629716110)
XLA Ops:
  0.0 1.9 %shard_map.65 = (f32[9,16,128]{2,1,0:T(8,128)S(1)}, f32[10,16,128]{2,1,0:T(8,128)S(1)}, f32[10,16,128]{2,1,0:T(8,128)S(1)}) custom-call(f32[27,8,16,128]{3,2,1,0:T(8,128)} %bitcast.11), custom_call_target="tpu_custom_call" | custom-call | tf_op jit(solution)/shard_map/pallas_call | solution.py:416
  1.9 3.1 %collective-permute-start = (f32[10,16,128]{2,1,0:T(8,128)S(1)}, f32[10,16,128]{2,1,0:T(8,128)S(1)}, u32[]{:S(2)}, u32[]{:S(2)}) collective-permute-start(f32[10,16,128]{2,1,0:T(8,128)S(1)} %get-tuple-element.28), channel_id=1, source_target_pairs={{0,1},{1,0},{2,3},{3,2},{4,5},{5,4},{6,7},{7,6},{8,9},{9,8},{10,11... | collective-permute-start | bytes 245768 | tf_op jit(solution)/shard_map/ppermute | solution.py:371
  5.0 0.5 %collective-permute-start.5 = (f32[9,16,128]{2,1,0:T(8,128)S(1)}, f32[9,16,128]{2,1,0:T(8,128)S(1)}, u32[]{:S(2)}, u32[]{:S(2)}) collective-permute-start(f32[9,16,128]{2,1,0:T(8,128)S(1)} %get-tuple-element.32.refs_0_), channel_id=1, source_target_pairs={{0,16},{1,17},{2,18},{3,19},{4,20},{5,21},{6,22},{7,23},{8,24},{9,... | collective-permute-start | bytes 221192 | tf_op jit(solution)/shard_map/ppermute | solution.py:371
  5.6 0.6 %collective-permute-start.6 = (f32[4,16,128]{2,1,0:T(8,128)S(1)}, f32[4,16,128]{2,1,0:T(8,128)S(1)}, u32[]{:S(2)}, u32[]{:S(2)}) collective-permute-start(f32[4,16,128]{2,1,0:T(8,128)S(1)} %shard_map.67), channel_id=1, source_target_pairs={{0,16},{1,17},{2,18},{3,19},{4,20},{5,21},{6,22},{7,23},{8,24},{9,... | collective-permute-start | bytes 98312 | tf_op jit(solution)/shard_map/ppermute | solution.py:371
  6.2 1.6 %shard_map.64._.refs_1_ = f32[3,8,16,128]{3,2,1,0:T(8,128)S(1)} custom-call(f32[2,1,27,8,16,128]{5,4,3,2,1,0:T(8,128)} %refs_0_.3), custom_call_target="tpu_custom_call" | custom-call | tf_op jit(solution)/shard_map/pallas_call | solution.py:433
  7.9 0.1 shard_map.66
  8.0 0.4 %collective-permute-start.2 = (f32[10,16,128]{2,1,0:T(8,128)S(1)}, f32[10,16,128]{2,1,0:T(8,128)S(1)}, u32[]{:S(2)}, u32[]{:S(2)}) collective-permute-start(f32[10,16,128]{2,1,0:T(8,128)S(1)} %get-tuple-element.30), channel_id=1, source_target_pairs={{0,16},{1,17},{2,18},{3,19},{4,8},{5,9},{6,10},{7,11},{8,4},{9,5},... | collective-permute-start | bytes 245768 | tf_op jit(solution)/shard_map/ppermute | solution.py:371
  8.3 2.6 %collective-permute-start.3 = (f32[10,16,128]{2,1,0:T(8,128)S(1)}, f32[10,16,128]{2,1,0:T(8,128)S(1)}, u32[]{:S(2)}, u32[]{:S(2)}) collective-permute-start(f32[10,16,128]{2,1,0:T(8,128)S(1)} %get-tuple-element.31), channel_id=1, source_target_pairs={{0,4},{1,5},{2,6},{3,7},{4,0},{5,1},{6,2},{7,3},{8,12},{9,13},{10,... | collective-permute-start | bytes 245768 | tf_op jit(solution)/shard_map/ppermute | solution.py:371
  11.0 1.8 %shard_map.68 = (f32[27,8,16,128]{3,2,1,0:T(8,128)S(1)}, f32[16,128]{1,0:T(8,128)S(1)}, f32[16,128]{1,0:T(8,128)S(1)}) custom-call(f32[27,8,16,128]{3,2,1,0:T(8,128)S(1)} %bitcast.13, f32[3,8,16,128]{3,2,1,0:T(8,128)S(1)} %shard_map.64._.refs_1_, s32[1,8,16,128]{3,2,1,0:T(8,128)S(1)} %copy-done.1, ...), custom_call_target="tpu_custom_call" | custom-call | tf_op jit(solution)/shard_map/pallas_call | solution.py:456
  12.9 0.1 collective-permute-start.7
  13.0 2.4 %collective-permute-done.3.refs_6_ = f32[10,16,128]{2,1,0:T(8,128)S(1)} collective-permute-done((f32[10,16,128]{2,1,0:T(8,128)S(1)}, f32[10,16,128]{2,1,0:T(8,128)S(1)}, u32[]{:S(2)}, u32[]{:S(2)}) %collective-permute-start.3) | collective-permute-done | bytes 81952 | tf_op jit(solution)/shard_map/ppermute | solution.py:371
  15.4 0.4 %shard_map.70 = (f32[27,8,16,128]{3,2,1,0:T(8,128)S(1)}, f32[16,128]{1,0:T(8,128)S(1)}, f32[16,128]{1,0:T(8,128)S(1)}) custom-call(f32[27,8,16,128]{3,2,1,0:T(8,128)S(1)} %bitcast.14, f32[3,8,16,128]{3,2,1,0:T(8,128)S(1)} %shard_map.64._.refs_1_, s32[1,8,16,128]{3,2,1,0:T(8,128)S(1)} %copy-done.1, ...), custom_call_target="tpu_custom_call", output_to_operand_aliasing={{0}: (9, {})} | custom-call | tf_op jit(solution)/shard_map/pallas_call | solution.py:456
  15.8 0.4 %shard_map.71 = (f32[27,8,16,128]{3,2,1,0:T(8,128)S(1)}, f32[9,16,128]{2,1,0:T(8,128)S(1)}, f32[10,16,128]{2,1,0:T(8,128)S(1)}, f32[10,16,128]{2,1,0:T(8,128)S(1)}) custom-call(f32[27,8,16,128]{3,2,1,0:T(8,128)S(1)} %bitcast.15, f32[3,8,16,128]{3,2,1,0:T(8,128)S(1)} %shard_map.64._.refs_1_, ...), custom_call_target="tpu_custom_call", output_to_operand_aliasing={{0}: (10, {})} | custom-call | tf_op jit(solution)/shard_map/pallas_call | solution.py:456
  16.2 2.9 %collective-permute-start.8 = (f32[10,16,128]{2,1,0:T(8,128)S(1)}, f32[10,16,128]{2,1,0:T(8,128)S(1)}, u32[]{:S(2)}, u32[]{:S(2)}) collective-permute-start(f32[10,16,128]{2,1,0:T(8,128)S(1)} %get-tuple-element.40), channel_id=1, source_target_pairs={{0,1},{1,0},{2,3},{3,2},{4,5},{5,4},{6,7},{7,6},{8,9},{9,8},{10,11... | collective-permute-start | bytes 245768 | tf_op jit(solution)/shard_map/ppermute | solution.py:371
  19.0 0.5 %collective-permute-start.13 = (f32[9,16,128]{2,1,0:T(8,128)S(1)}, f32[9,16,128]{2,1,0:T(8,128)S(1)}, u32[]{:S(2)}, u32[]{:S(2)}) collective-permute-start(f32[9,16,128]{2,1,0:T(8,128)S(1)} %get-tuple-element.44.refs_0_), channel_id=1, source_target_pairs={{0,16},{1,17},{2,18},{3,19},{4,20},{5,21},{6,22},{7,23},{8,24},{9,... | collective-permute-start | bytes 221192 | tf_op jit(solution)/shard_map/ppermute | solution.py:371
  19.5 1.6 %shard_map.72._.refs_1_ = f32[3,8,16,128]{3,2,1,0:T(8,128)S(1)} custom-call(f32[2,1,27,8,16,128]{5,4,3,2,1,0:T(8,128)} %refs_0_.3), custom_call_target="tpu_custom_call" | custom-call | tf_op jit(solution)/shard_map/pallas_call | solution.py:433
  21.2 0.3 collective-permute-done.8.first.refs_3_.refs_1_
  21.4 0.1 shard_map.73
  21.5 0.3 collective-permute-start.10
  21.8 4.0 %collective-permute-start.11 = (f32[10,16,128]{2,1,0:T(8,128)S(1)}, f32[10,16,128]{2,1,0:T(8,128)S(1)}, u32[]{:S(2)}, u32[]{:S(2)}) collective-permute-start(f32[10,16,128]{2,1,0:T(8,128)S(1)} %get-tuple-element.43), channel_id=1, source_target_pairs={{0,4},{1,5},{2,6},{3,7},{4,0},{5,1},{6,2},{7,3},{8,12},{9,13},{10,... | collective-permute-start | bytes 245768 | tf_op jit(solution)/shard_map/ppermute | solution.py:371
  25.8 1.7 %shard_map.74 = (f32[27,8,16,128]{3,2,1,0:T(8,128)}, f32[16,128]{1,0:T(8,128)S(1)}, f32[16,128]{1,0:T(8,128)S(1)}) custom-call(f32[27,8,16,128]{3,2,1,0:T(8,128)S(1)} %get-tuple-element.39.adj.refs_0_, f32[3,8,16,128]{3,2,1,0:T(8,128)S(1)} %shard_map.72._.refs_1_, s32[1,8,16,128]{3,2,1,0:T(8,128)S(1)} %copy-done.1, ...), custom_call_target="tpu_custom_call" | custom-call | tf_op jit(solution)/shard_map/pallas_call | solution.py:456
  27.7 2.1 %collective-permute-done.11.refs_6_ = f32[10,16,128]{2,1,0:T(8,128)S(1)} collective-permute-done((f32[10,16,128]{2,1,0:T(8,128)S(1)}, f32[10,16,128]{2,1,0:T(8,128)S(1)}, u32[]{:S(2)}, u32[]{:S(2)}) %collective-permute-start.11) | collective-permute-done | bytes 81952 | tf_op jit(solution)/shard_map/ppermute | solution.py:371
  29.8 0.9 %shard_map.76 = (f32[27,8,16,128]{3,2,1,0:T(8,128)}, f32[16,128]{1,0:T(8,128)S(1)}, f32[16,128]{1,0:T(8,128)S(1)}) custom-call(f32[27,8,16,128]{3,2,1,0:T(8,128)S(1)} %get-tuple-element.39.adj.refs_0_, f32[3,8,16,128]{3,2,1,0:T(8,128)S(1)} %shard_map.72._.refs_1_, s32[1,8,16,128]{3,2,1,0:T(8,128)S(1)} %copy-done.1, ...), custom_call_target="tpu_custom_call", output_to_operand_aliasing={{0}: (9, {})} | custom-call | tf_op jit(solution)/shard_map/pallas_call | solution.py:456
  30.8 0.9 %shard_map.77 = f32[27,8,16,128]{3,2,1,0:T(8,128)} custom-call(f32[27,8,16,128]{3,2,1,0:T(8,128)S(1)} %get-tuple-element.39.adj.refs_0_, f32[3,8,16,128]{3,2,1,0:T(8,128)S(1)} %shard_map.72._.refs_1_, s32[1,8,16,128]{3,2,1,0:T(8,128)S(1)} %copy-done.1, ...), custom_call_target="tpu_custom_call", output_to_operand_aliasing={{}: (10, {})} | custom-call | tf_op jit(solution)/shard_map/pallas_call | solution.py:456
  (30 shorter events, 0.2 us)
Async XLA Ops:
  0.0 5.5 %copy-start.4 = (f32[1,16,128,2]{2,3,1,0:T(2,128)S(1)}, f32[1,16,128,2]{2,3,1,0:T(2,128)}, u32[]{:S(2)}) copy-start(f32[1,16,128,2]{2,3,1,0:T(2,128)} %param.11) | copy-start | bytes 49156
  0.0 5.5 %copy-start.3 = (s32[1,16,128,2]{2,3,1,0:T(2,128)S(1)}, s32[1,16,128,2]{2,3,1,0:T(2,128)}, u32[]{:S(2)}) copy-start(s32[1,16,128,2]{2,3,1,0:T(2,128)} %param.10) | copy-start | bytes 49156
  0.0 5.5 %copy-start.2 = (s32[1,16,128,2]{2,3,1,0:T(2,128)S(1)}, s32[1,16,128,2]{2,3,1,0:T(2,128)}, u32[]{:S(2)}) copy-start(s32[1,16,128,2]{2,3,1,0:T(2,128)} %param.9) | copy-start | bytes 49156
  1.9 5.9 %collective-permute-start = (f32[10,16,128]{2,1,0:T(8,128)S(1)}, f32[10,16,128]{2,1,0:T(8,128)S(1)}, u32[]{:S(2)}, u32[]{:S(2)}) collective-permute-start(f32[10,16,128]{2,1,0:T(8,128)S(1)} %get-tuple-element.28), channel_id=1, source_target_pairs={{0,1},{1,0},{2,3},{3,2},{4,5},{5,4},{6,7},{7,6},{8,9},{9,8},{10,11... | collective-permute-start | bytes 245768 | tf_op jit(solution)/shard_map/ppermute | solution.py:371
  5.0 2.8 %collective-permute-start.1 = (f32[10,16,128]{2,1,0:T(8,128)S(1)}, f32[10,16,128]{2,1,0:T(8,128)S(1)}, u32[]{:S(2)}, u32[]{:S(2)}) collective-permute-start(f32[10,16,128]{2,1,0:T(8,128)S(1)} %get-tuple-element.29), channel_id=1, source_target_pairs={{0,16},{1,2},{2,1},{3,19},{4,20},{5,6},{6,5},{7,23},{8,24},{9,10},... | collective-permute-start | bytes 245768 | tf_op jit(solution)/shard_map/ppermute | solution.py:371
  5.0 7.8 %collective-permute-start.5 = (f32[9,16,128]{2,1,0:T(8,128)S(1)}, f32[9,16,128]{2,1,0:T(8,128)S(1)}, u32[]{:S(2)}, u32[]{:S(2)}) collective-permute-start(f32[9,16,128]{2,1,0:T(8,128)S(1)} %get-tuple-element.32.refs_0_), channel_id=1, source_target_pairs={{0,16},{1,17},{2,18},{3,19},{4,20},{5,21},{6,22},{7,23},{8,24},{9,... | collective-permute-start | bytes 221192 | tf_op jit(solution)/shard_map/ppermute | solution.py:371
  5.5 7.3 %collective-permute-start.4 = (f32[9,16,128]{2,1,0:T(8,128)S(1)}, f32[9,16,128]{2,1,0:T(8,128)S(1)}, u32[]{:S(2)}, u32[]{:S(2)}) collective-permute-start(f32[9,16,128]{2,1,0:T(8,128)S(1)} %get-tuple-element.32.refs_0_), channel_id=1, source_target_pairs={{0,16},{1,17},{2,18},{3,19},{4,20},{5,21},{6,22},{7,23},{8,24},{9,... | collective-permute-start | bytes 221192 | tf_op jit(solution)/shard_map/ppermute | solution.py:371
  5.6 2.2 %copy-start = (f32[1,27,8,16,128]{4,3,2,1,0:T(8,128)S(1)}, f32[1,27,8,16,128]{4,3,2,1,0:T(8,128)}, u32[]{:S(2)}) copy-start(f32[1,27,8,16,128]{4,3,2,1,0:T(8,128)} %param.6) | copy-start | bytes 5308420
  5.6 7.2 %collective-permute-start.6 = (f32[4,16,128]{2,1,0:T(8,128)S(1)}, f32[4,16,128]{2,1,0:T(8,128)S(1)}, u32[]{:S(2)}, u32[]{:S(2)}) collective-permute-start(f32[4,16,128]{2,1,0:T(8,128)S(1)} %shard_map.67), channel_id=1, source_target_pairs={{0,16},{1,17},{2,18},{3,19},{4,20},{5,21},{6,22},{7,23},{8,24},{9,... | collective-permute-start | bytes 98312 | tf_op jit(solution)/shard_map/ppermute | solution.py:371
  7.8 3.2 %copy-start.1 = (s32[1,8,16,128]{3,2,1,0:T(8,128)S(1)}, s32[1,8,16,128]{3,2,1,0:T(8,128)}, u32[]{:S(2)}) copy-start(s32[1,8,16,128]{3,2,1,0:T(8,128)} %refs_2_.11) | copy-start | bytes 196612
  8.0 5.0 %collective-permute-start.2 = (f32[10,16,128]{2,1,0:T(8,128)S(1)}, f32[10,16,128]{2,1,0:T(8,128)S(1)}, u32[]{:S(2)}, u32[]{:S(2)}) collective-permute-start(f32[10,16,128]{2,1,0:T(8,128)S(1)} %get-tuple-element.30), channel_id=1, source_target_pairs={{0,16},{1,17},{2,18},{3,19},{4,8},{5,9},{6,10},{7,11},{8,4},{9,5},... | collective-permute-start | bytes 245768 | tf_op jit(solution)/shard_map/ppermute | solution.py:371
  8.3 7.1 %collective-permute-start.3 = (f32[10,16,128]{2,1,0:T(8,128)S(1)}, f32[10,16,128]{2,1,0:T(8,128)S(1)}, u32[]{:S(2)}, u32[]{:S(2)}) collective-permute-start(f32[10,16,128]{2,1,0:T(8,128)S(1)} %get-tuple-element.31), channel_id=1, source_target_pairs={{0,4},{1,5},{2,6},{3,7},{4,0},{5,1},{6,2},{7,3},{8,12},{9,13},{10,... | collective-permute-start | bytes 245768 | tf_op jit(solution)/shard_map/ppermute | solution.py:371
  12.9 2.9 %collective-permute-start.7 = (f32[9,16,128]{2,1,0:T(8,128)S(1)}, f32[9,16,128]{2,1,0:T(8,128)S(1)}, u32[]{:S(2)}, u32[]{:S(2)}) collective-permute-start(f32[9,16,128]{2,1,0:T(8,128)S(1)} %shard_map.69), channel_id=1, source_target_pairs={{0,16},{1,17},{2,18},{3,19},{4,20},{5,21},{6,22},{7,23},{8,24},{9,... | collective-permute-start | bytes 221192 | tf_op jit(solution)/shard_map/ppermute | solution.py:371
  16.2 5.3 %collective-permute-start.8 = (f32[10,16,128]{2,1,0:T(8,128)S(1)}, f32[10,16,128]{2,1,0:T(8,128)S(1)}, u32[]{:S(2)}, u32[]{:S(2)}) collective-permute-start(f32[10,16,128]{2,1,0:T(8,128)S(1)} %get-tuple-element.40), channel_id=1, source_target_pairs={{0,1},{1,0},{2,3},{3,2},{4,5},{5,4},{6,7},{7,6},{8,9},{9,8},{10,11... | collective-permute-start | bytes 245768 | tf_op jit(solution)/shard_map/ppermute | solution.py:371
  19.0 2.4 %collective-permute-start.9 = (f32[10,16,128]{2,1,0:T(8,128)S(1)}, f32[10,16,128]{2,1,0:T(8,128)S(1)}, u32[]{:S(2)}, u32[]{:S(2)}) collective-permute-start(f32[10,16,128]{2,1,0:T(8,128)S(1)} %get-tuple-element.41), channel_id=1, source_target_pairs={{0,16},{1,2},{2,1},{3,19},{4,20},{5,6},{6,5},{7,23},{8,24},{9,10},... | collective-permute-start | bytes 245768 | tf_op jit(solution)/shard_map/ppermute | solution.py:371
  19.0 8.5 %collective-permute-start.13 = (f32[9,16,128]{2,1,0:T(8,128)S(1)}, f32[9,16,128]{2,1,0:T(8,128)S(1)}, u32[]{:S(2)}, u32[]{:S(2)}) collective-permute-start(f32[9,16,128]{2,1,0:T(8,128)S(1)} %get-tuple-element.44.refs_0_), channel_id=1, source_target_pairs={{0,16},{1,17},{2,18},{3,19},{4,20},{5,21},{6,22},{7,23},{8,24},{9,... | collective-permute-start | bytes 221192 | tf_op jit(solution)/shard_map/ppermute | solution.py:371
  19.5 8.0 %collective-permute-start.12 = (f32[9,16,128]{2,1,0:T(8,128)S(1)}, f32[9,16,128]{2,1,0:T(8,128)S(1)}, u32[]{:S(2)}, u32[]{:S(2)}) collective-permute-start(f32[9,16,128]{2,1,0:T(8,128)S(1)} %get-tuple-element.44.refs_0_), channel_id=1, source_target_pairs={{0,16},{1,17},{2,18},{3,19},{4,20},{5,21},{6,22},{7,23},{8,24},{9,... | collective-permute-start | bytes 221192 | tf_op jit(solution)/shard_map/ppermute | solution.py:371
  21.5 6.1 %collective-permute-start.10 = (f32[10,16,128]{2,1,0:T(8,128)S(1)}, f32[10,16,128]{2,1,0:T(8,128)S(1)}, u32[]{:S(2)}, u32[]{:S(2)}) collective-permute-start(f32[10,16,128]{2,1,0:T(8,128)S(1)} %get-tuple-element.42), channel_id=1, source_target_pairs={{0,16},{1,17},{2,18},{3,19},{4,8},{5,9},{6,10},{7,11},{8,4},{9,5},... | collective-permute-start | bytes 245768 | tf_op jit(solution)/shard_map/ppermute | solution.py:371
  21.8 8.0 %collective-permute-start.11 = (f32[10,16,128]{2,1,0:T(8,128)S(1)}, f32[10,16,128]{2,1,0:T(8,128)S(1)}, u32[]{:S(2)}, u32[]{:S(2)}) collective-permute-start(f32[10,16,128]{2,1,0:T(8,128)S(1)} %get-tuple-element.43), channel_id=1, source_target_pairs={{0,4},{1,5},{2,6},{3,7},{4,0},{5,1},{6,2},{7,3},{8,12},{9,13},{10,... | collective-permute-start | bytes 245768 | tf_op jit(solution)/shard_map/ppermute | solution.py:371
  27.6 3.2 %collective-permute-start.14 = (f32[9,16,128]{2,1,0:T(8,128)S(1)}, f32[9,16,128]{2,1,0:T(8,128)S(1)}, u32[]{:S(2)}, u32[]{:S(2)}) collective-permute-start(f32[9,16,128]{2,1,0:T(8,128)S(1)} %shard_map.75), channel_id=1, source_target_pairs={{0,16},{1,17},{2,18},{3,19},{4,20},{5,21},{6,22},{7,23},{8,24},{9,... | collective-permute-start | bytes 221192 | tf_op jit(solution)/shard_map/ppermute | solution.py:371

commit v12 on v10

--- a/solution.py
+++ b/solution.py
@@ -44,25 +44,26 @@
     return lax.rem(lax.axis_index(axis), 2) == 0
 
 
-def write_messages(top, low, high, first, second):
+def write_messages(top, low, high, own, first, second):
     even = is_even("yz")
     for j in range(9):
         tile = top(j)
+        own[j] = tile
         first[j] = tile
         second[j] = tile
-    first[9] = jnp.where(even, high, low)
-    second[9] = jnp.where(even, low, high)
+    first[9] = jnp.where(even, low, high)
+    second[9] = jnp.where(even, high, low)
 
 
 def edges_from(first, second):
     even = is_even("yz")
     me, count = lax.axis_index("yz"), lax.axis_size("yz")
-    low = jnp.where(me == 0, 0.0, jnp.where(even, second[9], first[9]))
-    high = jnp.where(me == count - 1, 0.0, jnp.where(even, first[9], second[9]))
+    low = jnp.where(me == 0, 0.0, jnp.where(even, first[9], second[9]))
+    high = jnp.where(me == count - 1, 0.0, jnp.where(even, second[9], first[9]))
     return low, high
 
 
-def pack_kernel(adj, first_out, second_out, kept, top, sems):
+def pack_kernel(adj, own_out, first_out, second_out, kept, top, sems):
     extent_x = adj.shape[2]
     copies = [
         pltpu.make_async_copy(adj.at[:, 2 * side, x], kept.at[side, x], sems.at[side, x])
@@ -78,7 +79,7 @@
             copy.wait()
         edges = pack_columns(lambda i: kept[(i % 3) // 2, x, i // 3], x, *edges)
     copies[-1].wait()
-    write_messages(lambda j: top[j // 3, j % 3], *edges, first_out, second_out)
+    write_messages(lambda j: top[j // 3, j % 3], *edges, own_out, first_out, second_out)
 
 
 def info_kernel(device, cell, weight, out):
@@ -139,7 +140,7 @@
                 code = info[k, r : r + 8].astype(jnp.int32)
                 ahead = lax.rem(code // 128 - me + count, count)
                 spots[r, k] = lax.rem(code, 128)
-                turned = jnp.where(even, ahead, lax.rem(count - ahead, count))
+                turned = jnp.where(even, lax.rem(count - ahead, count), ahead)
                 masks = [turned == 1, turned == count - 1]
                 masks += [ahead == count - hop for hop in range(2, count - 1)]
                 picks[r, k] = masks
@@ -149,7 +150,7 @@
                 total = jnp.zeros((8, 128), jnp.float32)
                 for k in range(2):
                     tiles = [ref[j, r : r + 8] for ref in (own, first, second, *others)]
-                    tiles[2] = jnp.where(at_end, ends[j, r : r + 8], tiles[2])
+                    tiles[1] = jnp.where(at_end, ends[j, r : r + 8], tiles[1])
                     got = [jnp.take_along_axis(tile, spots[r, k], axis=1) for tile in tiles]
                     picked = got[0]
                     for mask, value in zip(picks[r, k], got[1:]):
@@ -412,11 +413,12 @@
         compiler_params=params,
     )(*[jnp.swapaxes(array[0], 1, 2) for array in (band_device, band_cell, band_weight)])
     info = send(info, flip)
-    first, second = pl.pallas_call(
+    messages = (tile_shape(9), tile_shape(10), tile_shape(10))
+    own, first, second = pl.pallas_call(
         pack_kernel,
-        out_shape=(tile_shape(10),) * 2,
+        out_shape=messages,
         in_specs=[pl.BlockSpec(memory_space=pltpu.HBM)],
-        out_specs=tuple(in_vmem(2)),
+        out_specs=tuple(in_vmem(3)),
         scratch_shapes=[
             pltpu.VMEM((2, extent_x, 9, 16, 128), jnp.float32),
             pltpu.VMEM((3, 3, 16, 128), jnp.float32),
@@ -427,9 +429,8 @@
     saved = pltpu.with_memory_space_constraint(saved, pltpu.HBM)
     for step in (1, 0):
         last = step == 0
-        own = first
-        first = send(own, along_z(0))
-        second = send(second, along_z(1))
+        first = send(first, along_z(1))
+        second = send(second, along_z(0))
         others = [send(own, target) for target in (ends_z, *map(hop_z, range(2, count - 1)))]
         vel = pl.pallas_call(
             lambda *refs: velocity_kernel(step, *refs),
@@ -468,7 +469,6 @@
                 compiler_params=params,
             )(*operands, *new)
 
-        messages = () if last else (tile_shape(10),) * 2
         kernel = lambda step, *refs: inner_kernel(step, last, *refs)
         new, *columns = make_planes(kernel, extent_x - 2, (), (), (tile_shape(),) * 2)
         cross = pl.pallas_call(
@@ -479,11 +479,11 @@
             compiler_params=params,
         )(own, first, second, *others, info, columns[0])
         cross = send(cross, flip)
-        field, *messages = make_planes(
-            outer_kernel, 2, (two, one, cross, *columns), (new,), messages
+        field, *results = make_planes(
+            outer_kernel, 2, (two, one, cross, *columns), (new,), () if last else messages
         )
         if not last:
-            first, second = messages
+            own, first, second = results
     return field[None]
 
 

time: 29.8 us -> 29.8 us (level)
  no operation moved by 1% of the time
where the time goes in v12:
time: 29.8 us; the launch traced here: 29.6 us
  starting transfers between devices  13.3 us (45%)
  Pallas kernels  10.9 us (37%)
  waiting for transfers between devices  4.96 us (17%)
    ppermute x15, starting transfers between devices, send(): lax.ppermute(values, axes, [(flat(*here), flat(*target(*here))) for here...  13.3 us
    pallas_call x4, Pallas kernels, make_planes(): pl.pallas_call(lambda *refs: kernel(step, *refs), out_shape=(tile_shape(2...  5.26 us
    ppermute x15, waiting for transfers between devices, send(): lax.ppermute(values, axes, [(flat(*here), flat(*target(*here))) for here...  4.96 us
    pallas_call x2, Pallas kernels, body(): pl.pallas_call(lambda *refs: velocity_kernel(step, *refs), out_shape=tile...  3.38 us
    pallas_call x1, Pallas kernels, body(): pl.pallas_call(pack_kernel, out_shape=messages, in_specs=[pl.BlockSpec(me...  2.03 us
  transfers between devices with their start and end apart: 15, of which 5 were waited for; matrix products, arithmetic and copies ran while one was open for 0% of the time, Pallas kernels for 24%

profile of v12, /device:TPU:0, one launch (start us, length us, event | category | flops | bytes accessed | tf_op | source)
XLA Modules:
  0.0 29.6 jit_solution(11855788922997980283)
XLA Ops:
  0.0 2.0 %shard_map.65 = (f32[9,16,128]{2,1,0:T(8,128)S(1)}, f32[10,16,128]{2,1,0:T(8,128)S(1)}, f32[10,16,128]{2,1,0:T(8,128)S(1)}) custom-call(f32[9,3,8,16,128]{4,3,2,1,0:T(8,128)} %bitcast.12), custom_call_target="tpu_custom_call" | custom-call | tf_op jit(solution)/shard_map/pallas_call | solution.py:417
  2.0 0.5 %collective-permute-start = (f32[10,16,128]{2,1,0:T(8,128)S(1)}, f32[10,16,128]{2,1,0:T(8,128)S(1)}, u32[]{:S(2)}, u32[]{:S(2)}) collective-permute-start(f32[10,16,128]{2,1,0:T(8,128)S(1)} %get-tuple-element.22), channel_id=1, source_target_pairs={{0,16},{1,2},{2,1},{3,19},{4,20},{5,6},{6,5},{7,23},{8,24},{9,10},... | collective-permute-start | bytes 245768 | tf_op jit(solution)/shard_map/ppermute | solution.py:373
  2.6 4.1 %collective-permute-start.1 = (f32[10,16,128]{2,1,0:T(8,128)S(1)}, f32[10,16,128]{2,1,0:T(8,128)S(1)}, u32[]{:S(2)}, u32[]{:S(2)}) collective-permute-start(f32[10,16,128]{2,1,0:T(8,128)S(1)} %get-tuple-element.23), channel_id=1, source_target_pairs={{0,1},{1,0},{2,3},{3,2},{4,5},{5,4},{6,7},{7,6},{8,9},{9,8},{10,11... | collective-permute-start | bytes 245768 | tf_op jit(solution)/shard_map/ppermute | solution.py:373
  6.7 0.5 %collective-permute-start.4 = (f32[9,16,128]{2,1,0:T(8,128)S(1)}, f32[9,16,128]{2,1,0:T(8,128)S(1)}, u32[]{:S(2)}, u32[]{:S(2)}) collective-permute-start(f32[9,16,128]{2,1,0:T(8,128)S(1)} %get-tuple-element.26.refs_0_), channel_id=1, source_target_pairs={{0,16},{1,17},{2,18},{3,19},{4,20},{5,21},{6,22},{7,23},{8,24},{9,... | collective-permute-start | bytes 221192 | tf_op jit(solution)/shard_map/ppermute | solution.py:373
  7.3 0.1 collective-permute-start.6
  7.4 1.7 %shard_map.64._.refs_1_ = f32[3,8,16,128]{3,2,1,0:T(8,128)S(1)} custom-call(f32[2,1,27,8,16,128]{5,4,3,2,1,0:T(8,128)} %refs_0_.3), custom_call_target="tpu_custom_call" | custom-call | tf_op jit(solution)/shard_map/pallas_call | solution.py:435
  9.2 0.3 copy-done
  9.4 0.1 shard_map.66
  9.5 0.2 collective-permute-start.2
  9.7 2.8 %collective-permute-start.3 = (f32[10,16,128]{2,1,0:T(8,128)S(1)}, f32[10,16,128]{2,1,0:T(8,128)S(1)}, u32[]{:S(2)}, u32[]{:S(2)}) collective-permute-start(f32[10,16,128]{2,1,0:T(8,128)S(1)} %get-tuple-element.25), channel_id=1, source_target_pairs={{0,4},{1,5},{2,6},{3,7},{4,0},{5,1},{6,2},{7,3},{8,12},{9,13},{10,... | collective-permute-start | bytes 245768 | tf_op jit(solution)/shard_map/ppermute | solution.py:373
  12.5 1.8 %shard_map.68 = (f32[27,8,16,128]{3,2,1,0:T(8,128)S(1)}, f32[16,128]{1,0:T(8,128)S(1)}, f32[16,128]{1,0:T(8,128)S(1)}) custom-call(f32[27,8,16,128]{3,2,1,0:T(8,128)S(1)} %bitcast.14, f32[3,8,16,128]{3,2,1,0:T(8,128)S(1)} %shard_map.64._.refs_1_, s32[1,8,16,128]{3,2,1,0:T(8,128)S(1)} %copy-done.1, ...), custom_call_target="tpu_custom_call" | custom-call | tf_op jit(solution)/shard_map/pallas_call | solution.py:458
  14.5 1.3 %collective-permute-done.7.refs_7_ = f32[9,16,128]{2,1,0:T(8,128)S(1)} collective-permute-done((f32[9,16,128]{2,1,0:T(8,128)S(1)}, f32[9,16,128]{2,1,0:T(8,128)S(1)}, u32[]{:S(2)}, u32[]{:S(2)}) %collective-permute-start.7) | collective-permute-done | bytes 73760 | tf_op jit(solution)/shard_map/ppermute | solution.py:373
  15.8 1.0 %collective-permute-done.3.refs_6_ = f32[10,16,128]{2,1,0:T(8,128)S(1)} collective-permute-done((f32[10,16,128]{2,1,0:T(8,128)S(1)}, f32[10,16,128]{2,1,0:T(8,128)S(1)}, u32[]{:S(2)}, u32[]{:S(2)}) %collective-permute-start.3) | collective-permute-done | bytes 81952 | tf_op jit(solution)/shard_map/ppermute | solution.py:373
  16.7 0.7 %shard_map.70 = (f32[27,8,16,128]{3,2,1,0:T(8,128)S(1)}, f32[9,16,128]{2,1,0:T(8,128)S(1)}, f32[10,16,128]{2,1,0:T(8,128)S(1)}, f32[10,16,128]{2,1,0:T(8,128)S(1)}) custom-call(f32[27,8,16,128]{3,2,1,0:T(8,128)S(1)} %bitcast.15, f32[3,8,16,128]{3,2,1,0:T(8,128)S(1)} %shard_map.64._.refs_1_, ...), custom_call_target="tpu_custom_call", output_to_operand_aliasing={{0}: (10, {})} | custom-call | tf_op jit(solution)/shard_map/pallas_call | solution.py:458
  17.5 1.7 %collective-permute-start.9 = (f32[10,16,128]{2,1,0:T(8,128)S(1)}, f32[10,16,128]{2,1,0:T(8,128)S(1)}, u32[]{:S(2)}, u32[]{:S(2)}) collective-permute-start(f32[10,16,128]{2,1,0:T(8,128)S(1)} %get-tuple-element.32), channel_id=1, source_target_pairs={{0,1},{1,0},{2,3},{3,2},{4,5},{5,4},{6,7},{7,6},{8,9},{9,8},{10,11... | collective-permute-start | bytes 245768 | tf_op jit(solution)/shard_map/ppermute | solution.py:373
  19.2 0.5 %collective-permute-start.12 = (f32[9,16,128]{2,1,0:T(8,128)S(1)}, f32[9,16,128]{2,1,0:T(8,128)S(1)}, u32[]{:S(2)}, u32[]{:S(2)}) collective-permute-start(f32[9,16,128]{2,1,0:T(8,128)S(1)} %get-tuple-element.35.refs_0_), channel_id=1, source_target_pairs={{0,16},{1,17},{2,18},{3,19},{4,20},{5,21},{6,22},{7,23},{8,24},{9,... | collective-permute-start | bytes 221192 | tf_op jit(solution)/shard_map/ppermute | solution.py:373
  19.7 1.6 %shard_map.71._.refs_1_ = f32[3,8,16,128]{3,2,1,0:T(8,128)S(1)} custom-call(f32[2,1,27,8,16,128]{5,4,3,2,1,0:T(8,128)} %refs_0_.3), custom_call_target="tpu_custom_call" | custom-call | tf_op jit(solution)/shard_map/pallas_call | solution.py:435
  21.4 0.9 %collective-permute-done.9.second.refs_4_.refs_2_ = f32[10,16,128]{2,1,0:T(8,128)S(1)} collective-permute-done((f32[10,16,128]{2,1,0:T(8,128)S(1)}, f32[10,16,128]{2,1,0:T(8,128)S(1)}, u32[]{:S(2)}, u32[]{:S(2)}) %collective-permute-start.9) | collective-permute-done | bytes 81952 | tf_op jit(solution)/shard_map/ppermute | solution.py:373
  22.3 0.1 shard_map.72
  22.4 2.5 %collective-permute-start.11 = (f32[10,16,128]{2,1,0:T(8,128)S(1)}, f32[10,16,128]{2,1,0:T(8,128)S(1)}, u32[]{:S(2)}, u32[]{:S(2)}) collective-permute-start(f32[10,16,128]{2,1,0:T(8,128)S(1)} %get-tuple-element.34), channel_id=1, source_target_pairs={{0,4},{1,5},{2,6},{3,7},{4,0},{5,1},{6,2},{7,3},{8,12},{9,13},{10,... | collective-permute-start | bytes 245768 | tf_op jit(solution)/shard_map/ppermute | solution.py:373
  24.9 1.7 %shard_map.73 = (f32[27,8,16,128]{3,2,1,0:T(8,128)}, f32[16,128]{1,0:T(8,128)S(1)}, f32[16,128]{1,0:T(8,128)S(1)}) custom-call(f32[27,8,16,128]{3,2,1,0:T(8,128)S(1)} %get-tuple-element.30.adj.refs_0_, f32[3,8,16,128]{3,2,1,0:T(8,128)S(1)} %shard_map.71._.refs_1_, s32[1,8,16,128]{3,2,1,0:T(8,128)S(1)} %copy-done.1, ...), custom_call_target="tpu_custom_call" | custom-call | tf_op jit(solution)/shard_map/pallas_call | solution.py:458
  26.8 1.3 %collective-permute-done.14.refs_7_ = f32[9,16,128]{2,1,0:T(8,128)S(1)} collective-permute-done((f32[9,16,128]{2,1,0:T(8,128)S(1)}, f32[9,16,128]{2,1,0:T(8,128)S(1)}, u32[]{:S(2)}, u32[]{:S(2)}) %collective-permute-start.14) | collective-permute-done | bytes 73760 | tf_op jit(solution)/shard_map/ppermute | solution.py:373
  28.1 0.5 %collective-permute-done.11.refs_6_ = f32[10,16,128]{2,1,0:T(8,128)S(1)} collective-permute-done((f32[10,16,128]{2,1,0:T(8,128)S(1)}, f32[10,16,128]{2,1,0:T(8,128)S(1)}, u32[]{:S(2)}, u32[]{:S(2)}) %collective-permute-start.11) | collective-permute-done | bytes 81952 | tf_op jit(solution)/shard_map/ppermute | solution.py:373
  28.6 1.0 %shard_map.75 = f32[27,8,16,128]{3,2,1,0:T(8,128)} custom-call(f32[27,8,16,128]{3,2,1,0:T(8,128)S(1)} %get-tuple-element.30.adj.refs_0_, f32[3,8,16,128]{3,2,1,0:T(8,128)S(1)} %shard_map.71._.refs_1_, s32[1,8,16,128]{3,2,1,0:T(8,128)S(1)} %copy-done.1, ...), custom_call_target="tpu_custom_call", output_to_operand_aliasing={{}: (10, {})} | custom-call | tf_op jit(solution)/shard_map/pallas_call | solution.py:458
  (28 shorter events, 0.4 us)
Async XLA Ops:
  0.0 7.2 %copy-start.4 = (f32[1,16,128,2]{2,3,1,0:T(2,128)S(1)}, f32[1,16,128,2]{2,3,1,0:T(2,128)}, u32[]{:S(2)}) copy-start(f32[1,16,128,2]{2,3,1,0:T(2,128)} %param.11) | copy-start | bytes 49156
  0.0 7.2 %copy-start.3 = (s32[1,16,128,2]{2,3,1,0:T(2,128)S(1)}, s32[1,16,128,2]{2,3,1,0:T(2,128)}, u32[]{:S(2)}) copy-start(s32[1,16,128,2]{2,3,1,0:T(2,128)} %param.10) | copy-start | bytes 49156
  0.0 7.2 %copy-start.2 = (s32[1,16,128,2]{2,3,1,0:T(2,128)S(1)}, s32[1,16,128,2]{2,3,1,0:T(2,128)}, u32[]{:S(2)}) copy-start(s32[1,16,128,2]{2,3,1,0:T(2,128)} %param.9) | copy-start | bytes 49156
  2.0 7.1 %collective-permute-start = (f32[10,16,128]{2,1,0:T(8,128)S(1)}, f32[10,16,128]{2,1,0:T(8,128)S(1)}, u32[]{:S(2)}, u32[]{:S(2)}) collective-permute-start(f32[10,16,128]{2,1,0:T(8,128)S(1)} %get-tuple-element.22), channel_id=1, source_target_pairs={{0,16},{1,2},{2,1},{3,19},{4,20},{5,6},{6,5},{7,23},{8,24},{9,10},... | collective-permute-start | bytes 245768 | tf_op jit(solution)/shard_map/ppermute | solution.py:373
  2.6 6.6 %collective-permute-start.1 = (f32[10,16,128]{2,1,0:T(8,128)S(1)}, f32[10,16,128]{2,1,0:T(8,128)S(1)}, u32[]{:S(2)}, u32[]{:S(2)}) collective-permute-start(f32[10,16,128]{2,1,0:T(8,128)S(1)} %get-tuple-element.23), channel_id=1, source_target_pairs={{0,1},{1,0},{2,3},{3,2},{4,5},{5,4},{6,7},{7,6},{8,9},{9,8},{10,11... | collective-permute-start | bytes 245768 | tf_op jit(solution)/shard_map/ppermute | solution.py:373
  6.7 7.6 %collective-permute-start.5 = (f32[9,16,128]{2,1,0:T(8,128)S(1)}, f32[9,16,128]{2,1,0:T(8,128)S(1)}, u32[]{:S(2)}, u32[]{:S(2)}) collective-permute-start(f32[9,16,128]{2,1,0:T(8,128)S(1)} %get-tuple-element.26.refs_0_), channel_id=1, source_target_pairs={{0,16},{1,17},{2,18},{3,19},{4,20},{5,21},{6,22},{7,23},{8,24},{9,... | collective-permute-start | bytes 221192 | tf_op jit(solution)/shard_map/ppermute | solution.py:373
  6.7 7.7 %collective-permute-start.4 = (f32[9,16,128]{2,1,0:T(8,128)S(1)}, f32[9,16,128]{2,1,0:T(8,128)S(1)}, u32[]{:S(2)}, u32[]{:S(2)}) collective-permute-start(f32[9,16,128]{2,1,0:T(8,128)S(1)} %get-tuple-element.26.refs_0_), channel_id=1, source_target_pairs={{0,16},{1,17},{2,18},{3,19},{4,20},{5,21},{6,22},{7,23},{8,24},{9,... | collective-permute-start | bytes 221192 | tf_op jit(solution)/shard_map/ppermute | solution.py:373
  7.3 2.1 %copy-start = (f32[1,27,8,16,128]{4,3,2,1,0:T(8,128)S(1)}, f32[1,27,8,16,128]{4,3,2,1,0:T(8,128)}, u32[]{:S(2)}) copy-start(f32[1,27,8,16,128]{4,3,2,1,0:T(8,128)} %param.6) | copy-start | bytes 5308420
  7.3 7.1 %collective-permute-start.6 = (f32[4,16,128]{2,1,0:T(8,128)S(1)}, f32[4,16,128]{2,1,0:T(8,128)S(1)}, u32[]{:S(2)}, u32[]{:S(2)}) collective-permute-start(f32[4,16,128]{2,1,0:T(8,128)S(1)} %shard_map.67), channel_id=1, source_target_pairs={{0,16},{1,17},{2,18},{3,19},{4,20},{5,21},{6,22},{7,23},{8,24},{9,... | collective-permute-start | bytes 98312 | tf_op jit(solution)/shard_map/ppermute | solution.py:373
  9.1 3.4 %copy-start.1 = (s32[1,8,16,128]{3,2,1,0:T(8,128)S(1)}, s32[1,8,16,128]{3,2,1,0:T(8,128)}, u32[]{:S(2)}) copy-start(s32[1,8,16,128]{3,2,1,0:T(8,128)} %refs_2_.7) | copy-start | bytes 196612
  9.5 6.2 %collective-permute-start.2 = (f32[10,16,128]{2,1,0:T(8,128)S(1)}, f32[10,16,128]{2,1,0:T(8,128)S(1)}, u32[]{:S(2)}, u32[]{:S(2)}) collective-permute-start(f32[10,16,128]{2,1,0:T(8,128)S(1)} %get-tuple-element.24), channel_id=1, source_target_pairs={{0,16},{1,17},{2,18},{3,19},{4,8},{5,9},{6,10},{7,11},{8,4},{9,5},... | collective-permute-start | bytes 245768 | tf_op jit(solution)/shard_map/ppermute | solution.py:373
  9.7 7.1 %collective-permute-start.3 = (f32[10,16,128]{2,1,0:T(8,128)S(1)}, f32[10,16,128]{2,1,0:T(8,128)S(1)}, u32[]{:S(2)}, u32[]{:S(2)}) collective-permute-start(f32[10,16,128]{2,1,0:T(8,128)S(1)} %get-tuple-element.25), channel_id=1, source_target_pairs={{0,4},{1,5},{2,6},{3,7},{4,0},{5,1},{6,2},{7,3},{8,12},{9,13},{10,... | collective-permute-start | bytes 245768 | tf_op jit(solution)/shard_map/ppermute | solution.py:373
  14.4 1.3 %collective-permute-start.7 = (f32[9,16,128]{2,1,0:T(8,128)S(1)}, f32[9,16,128]{2,1,0:T(8,128)S(1)}, u32[]{:S(2)}, u32[]{:S(2)}) collective-permute-start(f32[9,16,128]{2,1,0:T(8,128)S(1)} %shard_map.69), channel_id=1, source_target_pairs={{0,16},{1,17},{2,18},{3,19},{4,20},{5,21},{6,22},{7,23},{8,24},{9,... | collective-permute-start | bytes 221192 | tf_op jit(solution)/shard_map/ppermute | solution.py:373
  17.4 4.0 %collective-permute-start.8 = (f32[10,16,128]{2,1,0:T(8,128)S(1)}, f32[10,16,128]{2,1,0:T(8,128)S(1)}, u32[]{:S(2)}, u32[]{:S(2)}) collective-permute-start(f32[10,16,128]{2,1,0:T(8,128)S(1)} %get-tuple-element.31), channel_id=1, source_target_pairs={{0,16},{1,2},{2,1},{3,19},{4,20},{5,6},{6,5},{7,23},{8,24},{9,10},... | collective-permute-start | bytes 245768 | tf_op jit(solution)/shard_map/ppermute | solution.py:373
  17.5 4.9 %collective-permute-start.9 = (f32[10,16,128]{2,1,0:T(8,128)S(1)}, f32[10,16,128]{2,1,0:T(8,128)S(1)}, u32[]{:S(2)}, u32[]{:S(2)}) collective-permute-start(f32[10,16,128]{2,1,0:T(8,128)S(1)} %get-tuple-element.32), channel_id=1, source_target_pairs={{0,1},{1,0},{2,3},{3,2},{4,5},{5,4},{6,7},{7,6},{8,9},{9,8},{10,11... | collective-permute-start | bytes 245768 | tf_op jit(solution)/shard_map/ppermute | solution.py:373
  19.2 7.5 %collective-permute-start.13 = (f32[9,16,128]{2,1,0:T(8,128)S(1)}, f32[9,16,128]{2,1,0:T(8,128)S(1)}, u32[]{:S(2)}, u32[]{:S(2)}) collective-permute-start(f32[9,16,128]{2,1,0:T(8,128)S(1)} %get-tuple-element.35.refs_0_), channel_id=1, source_target_pairs={{0,16},{1,17},{2,18},{3,19},{4,20},{5,21},{6,22},{7,23},{8,24},{9,... | collective-permute-start | bytes 221192 | tf_op jit(solution)/shard_map/ppermute | solution.py:373
  19.2 7.5 %collective-permute-start.12 = (f32[9,16,128]{2,1,0:T(8,128)S(1)}, f32[9,16,128]{2,1,0:T(8,128)S(1)}, u32[]{:S(2)}, u32[]{:S(2)}) collective-permute-start(f32[9,16,128]{2,1,0:T(8,128)S(1)} %get-tuple-element.35.refs_0_), channel_id=1, source_target_pairs={{0,16},{1,17},{2,18},{3,19},{4,20},{5,21},{6,22},{7,23},{8,24},{9,... | collective-permute-start | bytes 221192 | tf_op jit(solution)/shard_map/ppermute | solution.py:373
  22.4 5.7 %collective-permute-start.10 = (f32[10,16,128]{2,1,0:T(8,128)S(1)}, f32[10,16,128]{2,1,0:T(8,128)S(1)}, u32[]{:S(2)}, u32[]{:S(2)}) collective-permute-start(f32[10,16,128]{2,1,0:T(8,128)S(1)} %get-tuple-element.33), channel_id=1, source_target_pairs={{0,16},{1,17},{2,18},{3,19},{4,8},{5,9},{6,10},{7,11},{8,4},{9,5},... | collective-permute-start | bytes 245768 | tf_op jit(solution)/shard_map/ppermute | solution.py:373
  22.4 6.1 %collective-permute-start.11 = (f32[10,16,128]{2,1,0:T(8,128)S(1)}, f32[10,16,128]{2,1,0:T(8,128)S(1)}, u32[]{:S(2)}, u32[]{:S(2)}) collective-permute-start(f32[10,16,128]{2,1,0:T(8,128)S(1)} %get-tuple-element.34), channel_id=1, source_target_pairs={{0,4},{1,5},{2,6},{3,7},{4,0},{5,1},{6,2},{7,3},{8,12},{9,13},{10,... | collective-permute-start | bytes 245768 | tf_op jit(solution)/shard_map/ppermute | solution.py:373
  26.7 1.3 %collective-permute-start.14 = (f32[9,16,128]{2,1,0:T(8,128)S(1)}, f32[9,16,128]{2,1,0:T(8,128)S(1)}, u32[]{:S(2)}, u32[]{:S(2)}) collective-permute-start(f32[9,16,128]{2,1,0:T(8,128)S(1)} %shard_map.74), channel_id=1, source_target_pairs={{0,16},{1,17},{2,18},{3,19},{4,20},{5,21},{6,22},{7,23},{8,24},{9,... | collective-permute-start | bytes 221192 | tf_op jit(solution)/shard_map/ppermute | solution.py:373

commit v13 on v12

--- a/solution.py
+++ b/solution.py
@@ -63,23 +63,20 @@
     return low, high
 
 
-def pack_kernel(adj, own_out, first_out, second_out, kept, top, sems):
-    extent_x = adj.shape[2]
+def pack_kernel(adj, field_out, own_out, first_out, second_out, sems):
+    extent_x = adj.shape[1]
     copies = [
-        pltpu.make_async_copy(adj.at[:, 2 * side, x], kept.at[side, x], sems.at[side, x])
-        for x in range(extent_x)
-        for side in range(2)
+        pltpu.make_async_copy(adj.at[:, x], field_out.at[:, x], sems.at[x]) for x in range(extent_x)
     ]
-    copies.append(pltpu.make_async_copy(adj.at[pl.ds(0, 3), :, extent_x - 1], top, sems.at[2, 0]))
     for copy in copies:
         copy.start()
     edges = jnp.zeros((16, 128), jnp.float32), jnp.zeros((16, 128), jnp.float32)
     for x in range(extent_x):
-        for copy in copies[2 * x : 2 * x + 2]:
-            copy.wait()
-        edges = pack_columns(lambda i: kept[(i % 3) // 2, x, i // 3], x, *edges)
-    copies[-1].wait()
-    write_messages(lambda j: top[j // 3, j % 3], *edges, own_out, first_out, second_out)
+        copies[x].wait()
+        edges = pack_columns(lambda i: field_out[i, x], x, *edges)
+    write_messages(
+        lambda j: field_out[j, extent_x - 1], *edges, own_out, first_out, second_out
+    )
 
 
 def info_kernel(device, cell, weight, out):
@@ -88,8 +85,13 @@
         out[2 + k] = weight[:, k]
 
 
-def velocity_kernel(step, saved, out, kept, sems):
+def velocity_kernel(step, saved, *rest):
+    *carried, out, kept, sems = rest
     extent_x = out.shape[1]
+    copies = []
+    if carried:
+        copies.append(pltpu.make_async_copy(carried[0], carried[1], sems.at[extent_x]))
+        copies[0].start()
 
     def load(x):
         return pltpu.make_async_copy(saved.at[step, 0, :, x], kept.at[x], sems.at[x])
@@ -103,6 +105,8 @@
         return carry
 
     lax.fori_loop(0, extent_x, one, 0)
+    for copy in copies:
+        copy.wait()
 
 
 def side_kernel(adj, first, second, _, two_out, one_out):
@@ -274,7 +278,7 @@
     low_edge, high_edge = edges_from(first, second)
 
     def save(x):
-        return pltpu.make_async_copy(made.at[x - 1], out.at[:, x], sems.at[x - 1])
+        return pltpu.make_async_copy(made.at[x - 1], out.at[:, x], sems.at[x - 1, 0])
 
     def plane(x, carry):
         here = pulled.at[lax.rem(x, 2)]
@@ -330,12 +334,16 @@
 
         def store(i, tile):
             made[n, i] = tile
+            if i % 9 == 8:
+                save(i // 9).start()
+
+        def save(third):
+            rows = pl.ds(9 * third, 9)
+            return pltpu.make_async_copy(made.at[n, rows], out.at[rows, x], sems.at[n, third])
 
         velocity = [vel[a, x] for a in range(3)]
         collide(lambda i: pulled[n, i], velocity, solid[0, x], store)
-        save = pltpu.make_async_copy(made.at[n], out.at[:, x], sems.at[n])
-        save.start()
-        return save
+        return [save(third) for third in range(3)]
 
     final = extent_x - 1
     saves = [plane(0, 0, -1, below, None), plane(1, final, 1, above, interface)]
@@ -344,7 +352,7 @@
         low, high = pack_columns(lambda i: made[0, i], 0, low, high)
         low, high = pack_columns(lambda i: made[1, i], final, low, high)
         write_messages(lambda j: made[1, j], low, high, *messages)
-    for save in saves:
+    for save in itertools.chain(*saves):
         save.wait()
 
 
@@ -412,37 +420,38 @@
         out_specs=in_vmem(1)[0],
         compiler_params=params,
     )(*[jnp.swapaxes(array[0], 1, 2) for array in (band_device, band_cell, band_weight)])
+    messages = (tile_shape(9), tile_shape(10), tile_shape(10))
+    field, own, first, second = pl.pallas_call(
+        pack_kernel,
+        out_shape=(tile_shape(27, extent_x), *messages),
+        in_specs=[pl.BlockSpec(memory_space=pltpu.HBM)],
+        out_specs=tuple(in_vmem(4)),
+        scratch_shapes=[pltpu.SemaphoreType.DMA((extent_x,))],
+        compiler_params=params,
+    )(pltpu.with_memory_space_constraint(field, pltpu.HBM))
+    saved = pltpu.with_memory_space_constraint(saved, pltpu.HBM)
     info = send(info, flip)
-    messages = (tile_shape(9), tile_shape(10), tile_shape(10))
-    own, first, second = pl.pallas_call(
-        pack_kernel,
-        out_shape=messages,
-        in_specs=[pl.BlockSpec(memory_space=pltpu.HBM)],
-        out_specs=tuple(in_vmem(3)),
-        scratch_shapes=[
-            pltpu.VMEM((2, extent_x, 9, 16, 128), jnp.float32),
-            pltpu.VMEM((3, 3, 16, 128), jnp.float32),
-            pltpu.SemaphoreType.DMA((3, extent_x)),
-        ],
-        compiler_params=params,
-    )(pltpu.with_memory_space_constraint(field.reshape(9, 3, extent_x, 16, 128), pltpu.HBM))
-    saved = pltpu.with_memory_space_constraint(saved, pltpu.HBM)
     for step in (1, 0):
         last = step == 0
         first = send(first, along_z(1))
         second = send(second, along_z(0))
         others = [send(own, target) for target in (ends_z, *map(hop_z, range(2, count - 1)))]
-        vel = pl.pallas_call(
+        carried = () if last else (pltpu.with_memory_space_constraint(solid, pltpu.HBM),)
+        *copied, vel = pl.pallas_call(
             lambda *refs: velocity_kernel(step, *refs),
-            out_shape=tile_shape(3, extent_x),
-            in_specs=[pl.BlockSpec(memory_space=pltpu.HBM)],
-            out_specs=in_vmem(1)[0],
+            out_shape=(
+                *(jax.ShapeDtypeStruct(array.shape, array.dtype) for array in carried),
+                tile_shape(3, extent_x),
+            ),
+            in_specs=[pl.BlockSpec(memory_space=pltpu.HBM)] * (1 + len(carried)),
+            out_specs=tuple(in_vmem(1 + len(carried))),
             scratch_shapes=[
                 pltpu.VMEM((extent_x, 27, 16, 128), jnp.float32),
-                pltpu.SemaphoreType.DMA((extent_x,)),
+                pltpu.SemaphoreType.DMA((extent_x + 1,)),
             ],
             compiler_params=params,
-        )(saved)
+        )(saved, *carried)
+        solid = copied[0] if copied else solid
         two, one = pl.pallas_call(
             side_kernel,
             out_shape=(tile_shape(10),) * 2,
@@ -463,7 +472,7 @@
                 scratch_shapes=[
                     pltpu.VMEM((planes, 27, 16, 128), jnp.float32),
                     pltpu.VMEM((2, 27, 16, 128), jnp.float32),
-                    pltpu.SemaphoreType.DMA((planes,)),
+                    pltpu.SemaphoreType.DMA((planes, 3)),
                 ],
                 input_output_aliases={len(operands): 0} if new else {},
                 compiler_params=params,

time: 29.8 us -> 30.1 us (1.010)
  waiting for transfers between devices: 4.96 us -> 5.39 us
    ppermute x15, waiting for transfers between devices: 4.96 us -> 5.39 us  [send(): lax.ppermute(values, axes, [(flat(*here), flat(*target(*here))) for here...]
    pallas_call x4, Pallas kernels: 5.26 us -> 5.56 us  [make_planes(): pl.pallas_call(lambda *refs: kernel(step, *refs), out_shape=(tile_shape(2...]
  transfers between devices with their start and end apart: 15 -> 15, of which waited for: 5 -> 6; matrix products, arithmetic and copies ran while one was open for 0% -> 0% of each run, Pallas kernels for 24% -> 25%
where the time goes in v13:
time: 30.1 us; the launch traced here: 29.9 us
  starting transfers between devices  13.3 us (44%)
  Pallas kernels  11 us (37%)
  waiting for transfers between devices  5.39 us (18%)
    ppermute x15, starting transfers between devices, send(): lax.ppermute(values, axes, [(flat(*here), flat(*target(*here))) for here...  13.3 us
    pallas_call x4, Pallas kernels, make_planes(): pl.pallas_call(lambda *refs: kernel(step, *refs), out_shape=(tile_shape(2...  5.56 us
    ppermute x15, waiting for transfers between devices, send(): lax.ppermute(values, axes, [(flat(*here), flat(*target(*here))) for here...  5.39 us
    pallas_call x2, Pallas kernels, body(): pl.pallas_call(lambda *refs: velocity_kernel(step, *refs), out_shape=(*(j...  3.34 us
    pallas_call x1, Pallas kernels, body(): pl.pallas_call(pack_kernel, out_shape=(tile_shape(27, extent_x), *message...  1.89 us
  transfers between devices with their start and end apart: 15, of which 6 were waited for; matrix products, arithmetic and copies ran while one was open for 0% of the time, Pallas kernels for 25%

profile of v13, /device:TPU:0, one launch (start us, length us, event | category | flops | bytes accessed | tf_op | source)
XLA Modules:
  0.0 29.9 jit_solution(14797657078153306255)
XLA Ops:
  0.0 1.9 %shard_map.64 = (f32[27,8,16,128]{3,2,1,0:T(8,128)S(1)}, f32[9,16,128]{2,1,0:T(8,128)S(1)}, f32[10,16,128]{2,1,0:T(8,128)S(1)}, f32[10,16,128]{2,1,0:T(8,128)S(1)}) custom-call(f32[27,8,16,128]{3,2,1,0:T(8,128)} %bitcast.14), custom_call_target="tpu_custom_call" | custom-call | tf_op jit(solution)/shard_map/pallas_call | solution.py:424
  1.9 0.5 %collective-permute-start = (f32[10,16,128]{2,1,0:T(8,128)S(1)}, f32[10,16,128]{2,1,0:T(8,128)S(1)}, u32[]{:S(2)}, u32[]{:S(2)}) collective-permute-start(f32[10,16,128]{2,1,0:T(8,128)S(1)} %get-tuple-element.28), channel_id=1, source_target_pairs={{0,16},{1,2},{2,1},{3,19},{4,20},{5,6},{6,5},{7,23},{8,24},{9,10},... | collective-permute-start | bytes 245768 | tf_op jit(solution)/shard_map/ppermute | solution.py:381
  2.4 4.1 %collective-permute-start.1 = (f32[10,16,128]{2,1,0:T(8,128)S(1)}, f32[10,16,128]{2,1,0:T(8,128)S(1)}, u32[]{:S(2)}, u32[]{:S(2)}) collective-permute-start(f32[10,16,128]{2,1,0:T(8,128)S(1)} %get-tuple-element.29), channel_id=1, source_target_pairs={{0,1},{1,0},{2,3},{3,2},{4,5},{5,4},{6,7},{7,6},{8,9},{9,8},{10,11... | collective-permute-start | bytes 245768 | tf_op jit(solution)/shard_map/ppermute | solution.py:381
  6.6 0.5 %collective-permute-start.5 = (f32[9,16,128]{2,1,0:T(8,128)S(1)}, f32[9,16,128]{2,1,0:T(8,128)S(1)}, u32[]{:S(2)}, u32[]{:S(2)}) collective-permute-start(f32[9,16,128]{2,1,0:T(8,128)S(1)} %get-tuple-element.32.refs_0_), channel_id=1, source_target_pairs={{0,16},{1,17},{2,18},{3,19},{4,20},{5,21},{6,22},{7,23},{8,24},{9,... | collective-permute-start | bytes 221192 | tf_op jit(solution)/shard_map/ppermute | solution.py:381
  7.1 0.1 collective-permute-start.6
  7.2 1.7 %shard_map.65 = (s32[1,8,16,128]{3,2,1,0:T(8,128)S(1)}, f32[3,8,16,128]{3,2,1,0:T(8,128)S(1)}) custom-call(f32[2,1,27,8,16,128]{5,4,3,2,1,0:T(8,128)} %refs_0_.3, s32[1,8,16,128]{3,2,1,0:T(8,128)} %refs_1_.1), custom_call_target="tpu_custom_call" | custom-call | tf_op jit(solution)/shard_map/pallas_call | solution.py:440
  9.0 0.1 shard_map.66
  9.1 0.4 %collective-permute-start.2 = (f32[10,16,128]{2,1,0:T(8,128)S(1)}, f32[10,16,128]{2,1,0:T(8,128)S(1)}, u32[]{:S(2)}, u32[]{:S(2)}) collective-permute-start(f32[10,16,128]{2,1,0:T(8,128)S(1)} %get-tuple-element.30), channel_id=1, source_target_pairs={{0,16},{1,17},{2,18},{3,19},{4,8},{5,9},{6,10},{7,11},{8,4},{9,5},... | collective-permute-start | bytes 245768 | tf_op jit(solution)/shard_map/ppermute | solution.py:381
  9.5 2.5 %collective-permute-start.3 = (f32[10,16,128]{2,1,0:T(8,128)S(1)}, f32[10,16,128]{2,1,0:T(8,128)S(1)}, u32[]{:S(2)}, u32[]{:S(2)}) collective-permute-start(f32[10,16,128]{2,1,0:T(8,128)S(1)} %get-tuple-element.31), channel_id=1, source_target_pairs={{0,4},{1,5},{2,6},{3,7},{4,0},{5,1},{6,2},{7,3},{8,12},{9,13},{10,... | collective-permute-start | bytes 245768 | tf_op jit(solution)/shard_map/ppermute | solution.py:381
  12.1 2.0 %shard_map.68 = (f32[27,8,16,128]{3,2,1,0:T(8,128)S(1)}, f32[16,128]{1,0:T(8,128)S(1)}, f32[16,128]{1,0:T(8,128)S(1)}) custom-call(f32[27,8,16,128]{3,2,1,0:T(8,128)S(1)} %get-tuple-element.25.adj.refs_0_, f32[3,8,16,128]{3,2,1,0:T(8,128)S(1)} %get-tuple-element.26._.refs_1_, s32[1,8,16,128]{3,2,1,0:T(8,128)S(1)} %get-tuple-element.27.refs_2_, ...), custom_call_target="tpu_custom_call" | custom-call | tf_op jit(solution)/shard_map/pallas_call | solution.py:467
  14.1 0.1 collective-permute-start.7
  14.2 1.3 %collective-permute-done.7.refs_7_ = f32[9,16,128]{2,1,0:T(8,128)S(1)} collective-permute-done((f32[9,16,128]{2,1,0:T(8,128)S(1)}, f32[9,16,128]{2,1,0:T(8,128)S(1)}, u32[]{:S(2)}, u32[]{:S(2)}) %collective-permute-start.7) | collective-permute-done | bytes 73760 | tf_op jit(solution)/shard_map/ppermute | solution.py:381
  15.4 1.2 %collective-permute-done.3.refs_6_ = f32[10,16,128]{2,1,0:T(8,128)S(1)} collective-permute-done((f32[10,16,128]{2,1,0:T(8,128)S(1)}, f32[10,16,128]{2,1,0:T(8,128)S(1)}, u32[]{:S(2)}, u32[]{:S(2)}) %collective-permute-start.3) | collective-permute-done | bytes 81952 | tf_op jit(solution)/shard_map/ppermute | solution.py:381
  16.6 0.7 %shard_map.70 = (f32[27,8,16,128]{3,2,1,0:T(8,128)S(1)}, f32[9,16,128]{2,1,0:T(8,128)S(1)}, f32[10,16,128]{2,1,0:T(8,128)S(1)}, f32[10,16,128]{2,1,0:T(8,128)S(1)}) custom-call(f32[27,8,16,128]{3,2,1,0:T(8,128)S(1)} %get-tuple-element.25.adj.refs_0_, f32[3,8,16,128]{3,2,1,0:T(8,128)S(1)} %get-tuple-element.26._.refs_1_, ...), custom_call_target="tpu_custom_call", output_to_operand_aliasing={{0}: (10, {})} | custom-call | tf_op jit(solution)/shard_map/pallas_call | solution.py:467
  17.4 1.6 %collective-permute-start.9 = (f32[10,16,128]{2,1,0:T(8,128)S(1)}, f32[10,16,128]{2,1,0:T(8,128)S(1)}, u32[]{:S(2)}, u32[]{:S(2)}) collective-permute-start(f32[10,16,128]{2,1,0:T(8,128)S(1)} %get-tuple-element.38), channel_id=1, source_target_pairs={{0,1},{1,0},{2,3},{3,2},{4,5},{5,4},{6,7},{7,6},{8,9},{9,8},{10,11... | collective-permute-start | bytes 245768 | tf_op jit(solution)/shard_map/ppermute | solution.py:381
  19.0 0.5 %collective-permute-start.13 = (f32[9,16,128]{2,1,0:T(8,128)S(1)}, f32[9,16,128]{2,1,0:T(8,128)S(1)}, u32[]{:S(2)}, u32[]{:S(2)}) collective-permute-start(f32[9,16,128]{2,1,0:T(8,128)S(1)} %get-tuple-element.41.refs_0_), channel_id=1, source_target_pairs={{0,16},{1,17},{2,18},{3,19},{4,20},{5,21},{6,22},{7,23},{8,24},{9,... | collective-permute-start | bytes 221192 | tf_op jit(solution)/shard_map/ppermute | solution.py:381
  19.6 1.6 %shard_map.71._.refs_1_ = f32[3,8,16,128]{3,2,1,0:T(8,128)S(1)} custom-call(f32[2,1,27,8,16,128]{5,4,3,2,1,0:T(8,128)} %refs_0_.3), custom_call_target="tpu_custom_call" | custom-call | tf_op jit(solution)/shard_map/pallas_call | solution.py:440
  21.2 1.1 %collective-permute-done.9.second.refs_4_.refs_2_ = f32[10,16,128]{2,1,0:T(8,128)S(1)} collective-permute-done((f32[10,16,128]{2,1,0:T(8,128)S(1)}, f32[10,16,128]{2,1,0:T(8,128)S(1)}, u32[]{:S(2)}, u32[]{:S(2)}) %collective-permute-start.9) | collective-permute-done | bytes 81952 | tf_op jit(solution)/shard_map/ppermute | solution.py:381
  22.3 0.1 shard_map.72
  22.4 2.7 %collective-permute-start.11 = (f32[10,16,128]{2,1,0:T(8,128)S(1)}, f32[10,16,128]{2,1,0:T(8,128)S(1)}, u32[]{:S(2)}, u32[]{:S(2)}) collective-permute-start(f32[10,16,128]{2,1,0:T(8,128)S(1)} %get-tuple-element.40), channel_id=1, source_target_pairs={{0,4},{1,5},{2,6},{3,7},{4,0},{5,1},{6,2},{7,3},{8,12},{9,13},{10,... | collective-permute-start | bytes 245768 | tf_op jit(solution)/shard_map/ppermute | solution.py:381
  25.1 1.8 %shard_map.73 = (f32[27,8,16,128]{3,2,1,0:T(8,128)}, f32[16,128]{1,0:T(8,128)S(1)}, f32[16,128]{1,0:T(8,128)S(1)}) custom-call(f32[27,8,16,128]{3,2,1,0:T(8,128)S(1)} %get-tuple-element.36.adj.refs_0_, f32[3,8,16,128]{3,2,1,0:T(8,128)S(1)} %shard_map.71._.refs_1_, s32[1,8,16,128]{3,2,1,0:T(8,128)S(1)} %get-tuple-element.27.refs_2_, ...), custom_call_target="tpu_custom_call" | custom-call | tf_op jit(solution)/shard_map/pallas_call | solution.py:467
  27.0 1.3 %collective-permute-done.14.refs_7_ = f32[9,16,128]{2,1,0:T(8,128)S(1)} collective-permute-done((f32[9,16,128]{2,1,0:T(8,128)S(1)}, f32[9,16,128]{2,1,0:T(8,128)S(1)}, u32[]{:S(2)}, u32[]{:S(2)}) %collective-permute-start.14) | collective-permute-done | bytes 73760 | tf_op jit(solution)/shard_map/ppermute | solution.py:381
  28.3 0.6 %collective-permute-done.11.refs_6_ = f32[10,16,128]{2,1,0:T(8,128)S(1)} collective-permute-done((f32[10,16,128]{2,1,0:T(8,128)S(1)}, f32[10,16,128]{2,1,0:T(8,128)S(1)}, u32[]{:S(2)}, u32[]{:S(2)}) %collective-permute-start.11) | collective-permute-done | bytes 81952 | tf_op jit(solution)/shard_map/ppermute | solution.py:381
  28.9 1.0 %shard_map.75 = f32[27,8,16,128]{3,2,1,0:T(8,128)} custom-call(f32[27,8,16,128]{3,2,1,0:T(8,128)S(1)} %get-tuple-element.36.adj.refs_0_, f32[3,8,16,128]{3,2,1,0:T(8,128)S(1)} %shard_map.71._.refs_1_, s32[1,8,16,128]{3,2,1,0:T(8,128)S(1)} %get-tuple-element.27.refs_2_, ...), custom_call_target="tpu_custom_call", output_to_operand_aliasing={{}: (10, {})} | custom-call | tf_op jit(solution)/shard_map/pallas_call | solution.py:467
  (24 shorter events, 0.3 us)
Async XLA Ops:
  0.0 7.1 %copy-start = (s32[1,16,128,2]{2,3,1,0:T(2,128)S(1)}, s32[1,16,128,2]{2,3,1,0:T(2,128)}, u32[]{:S(2)}) copy-start(s32[1,16,128,2]{2,3,1,0:T(2,128)} %param.9) | copy-start | bytes 49156
  0.0 7.1 %copy-start.1 = (s32[1,16,128,2]{2,3,1,0:T(2,128)S(1)}, s32[1,16,128,2]{2,3,1,0:T(2,128)}, u32[]{:S(2)}) copy-start(s32[1,16,128,2]{2,3,1,0:T(2,128)} %param.10) | copy-start | bytes 49156
  0.0 7.1 %copy-start.2 = (f32[1,16,128,2]{2,3,1,0:T(2,128)S(1)}, f32[1,16,128,2]{2,3,1,0:T(2,128)}, u32[]{:S(2)}) copy-start(f32[1,16,128,2]{2,3,1,0:T(2,128)} %param.11) | copy-start | bytes 49156
  1.9 7.0 %collective-permute-start = (f32[10,16,128]{2,1,0:T(8,128)S(1)}, f32[10,16,128]{2,1,0:T(8,128)S(1)}, u32[]{:S(2)}, u32[]{:S(2)}) collective-permute-start(f32[10,16,128]{2,1,0:T(8,128)S(1)} %get-tuple-element.28), channel_id=1, source_target_pairs={{0,16},{1,2},{2,1},{3,19},{4,20},{5,6},{6,5},{7,23},{8,24},{9,10},... | collective-permute-start | bytes 245768 | tf_op jit(solution)/shard_map/ppermute | solution.py:381
  2.4 6.6 %collective-permute-start.1 = (f32[10,16,128]{2,1,0:T(8,128)S(1)}, f32[10,16,128]{2,1,0:T(8,128)S(1)}, u32[]{:S(2)}, u32[]{:S(2)}) collective-permute-start(f32[10,16,128]{2,1,0:T(8,128)S(1)} %get-tuple-element.29), channel_id=1, source_target_pairs={{0,1},{1,0},{2,3},{3,2},{4,5},{5,4},{6,7},{7,6},{8,9},{9,8},{10,11... | collective-permute-start | bytes 245768 | tf_op jit(solution)/shard_map/ppermute | solution.py:381
  6.6 7.5 %collective-permute-start.4 = (f32[9,16,128]{2,1,0:T(8,128)S(1)}, f32[9,16,128]{2,1,0:T(8,128)S(1)}, u32[]{:S(2)}, u32[]{:S(2)}) collective-permute-start(f32[9,16,128]{2,1,0:T(8,128)S(1)} %get-tuple-element.32.refs_0_), channel_id=1, source_target_pairs={{0,16},{1,17},{2,18},{3,19},{4,20},{5,21},{6,22},{7,23},{8,24},{9,... | collective-permute-start | bytes 221192 | tf_op jit(solution)/shard_map/ppermute | solution.py:381
  6.6 7.5 %collective-permute-start.5 = (f32[9,16,128]{2,1,0:T(8,128)S(1)}, f32[9,16,128]{2,1,0:T(8,128)S(1)}, u32[]{:S(2)}, u32[]{:S(2)}) collective-permute-start(f32[9,16,128]{2,1,0:T(8,128)S(1)} %get-tuple-element.32.refs_0_), channel_id=1, source_target_pairs={{0,16},{1,17},{2,18},{3,19},{4,20},{5,21},{6,22},{7,23},{8,24},{9,... | collective-permute-start | bytes 221192 | tf_op jit(solution)/shard_map/ppermute | solution.py:381
  7.1 6.9 %collective-permute-start.6 = (f32[4,16,128]{2,1,0:T(8,128)S(1)}, f32[4,16,128]{2,1,0:T(8,128)S(1)}, u32[]{:S(2)}, u32[]{:S(2)}) collective-permute-start(f32[4,16,128]{2,1,0:T(8,128)S(1)} %shard_map.67), channel_id=1, source_target_pairs={{0,16},{1,17},{2,18},{3,19},{4,20},{5,21},{6,22},{7,23},{8,24},{9,... | collective-permute-start | bytes 98312 | tf_op jit(solution)/shard_map/ppermute | solution.py:381
  9.1 6.3 %collective-permute-start.2 = (f32[10,16,128]{2,1,0:T(8,128)S(1)}, f32[10,16,128]{2,1,0:T(8,128)S(1)}, u32[]{:S(2)}, u32[]{:S(2)}) collective-permute-start(f32[10,16,128]{2,1,0:T(8,128)S(1)} %get-tuple-element.30), channel_id=1, source_target_pairs={{0,16},{1,17},{2,18},{3,19},{4,8},{5,9},{6,10},{7,11},{8,4},{9,5},... | collective-permute-start | bytes 245768 | tf_op jit(solution)/shard_map/ppermute | solution.py:381
  9.5 7.1 %collective-permute-start.3 = (f32[10,16,128]{2,1,0:T(8,128)S(1)}, f32[10,16,128]{2,1,0:T(8,128)S(1)}, u32[]{:S(2)}, u32[]{:S(2)}) collective-permute-start(f32[10,16,128]{2,1,0:T(8,128)S(1)} %get-tuple-element.31), channel_id=1, source_target_pairs={{0,4},{1,5},{2,6},{3,7},{4,0},{5,1},{6,2},{7,3},{8,12},{9,13},{10,... | collective-permute-start | bytes 245768 | tf_op jit(solution)/shard_map/ppermute | solution.py:381
  14.1 1.3 %collective-permute-start.7 = (f32[9,16,128]{2,1,0:T(8,128)S(1)}, f32[9,16,128]{2,1,0:T(8,128)S(1)}, u32[]{:S(2)}, u32[]{:S(2)}) collective-permute-start(f32[9,16,128]{2,1,0:T(8,128)S(1)} %shard_map.69), channel_id=1, source_target_pairs={{0,16},{1,17},{2,18},{3,19},{4,20},{5,21},{6,22},{7,23},{8,24},{9,... | collective-permute-start | bytes 221192 | tf_op jit(solution)/shard_map/ppermute | solution.py:381
  17.3 3.9 %collective-permute-start.8 = (f32[10,16,128]{2,1,0:T(8,128)S(1)}, f32[10,16,128]{2,1,0:T(8,128)S(1)}, u32[]{:S(2)}, u32[]{:S(2)}) collective-permute-start(f32[10,16,128]{2,1,0:T(8,128)S(1)} %get-tuple-element.37), channel_id=1, source_target_pairs={{0,16},{1,2},{2,1},{3,19},{4,20},{5,6},{6,5},{7,23},{8,24},{9,10},... | collective-permute-start | bytes 245768 | tf_op jit(solution)/shard_map/ppermute | solution.py:381
  17.4 4.9 %collective-permute-start.9 = (f32[10,16,128]{2,1,0:T(8,128)S(1)}, f32[10,16,128]{2,1,0:T(8,128)S(1)}, u32[]{:S(2)}, u32[]{:S(2)}) collective-permute-start(f32[10,16,128]{2,1,0:T(8,128)S(1)} %get-tuple-element.38), channel_id=1, source_target_pairs={{0,1},{1,0},{2,3},{3,2},{4,5},{5,4},{6,7},{7,6},{8,9},{9,8},{10,11... | collective-permute-start | bytes 245768 | tf_op jit(solution)/shard_map/ppermute | solution.py:381
  19.0 7.9 %collective-permute-start.12 = (f32[9,16,128]{2,1,0:T(8,128)S(1)}, f32[9,16,128]{2,1,0:T(8,128)S(1)}, u32[]{:S(2)}, u32[]{:S(2)}) collective-permute-start(f32[9,16,128]{2,1,0:T(8,128)S(1)} %get-tuple-element.41.refs_0_), channel_id=1, source_target_pairs={{0,16},{1,17},{2,18},{3,19},{4,20},{5,21},{6,22},{7,23},{8,24},{9,... | collective-permute-start | bytes 221192 | tf_op jit(solution)/shard_map/ppermute | solution.py:381
  19.0 7.9 %collective-permute-start.13 = (f32[9,16,128]{2,1,0:T(8,128)S(1)}, f32[9,16,128]{2,1,0:T(8,128)S(1)}, u32[]{:S(2)}, u32[]{:S(2)}) collective-permute-start(f32[9,16,128]{2,1,0:T(8,128)S(1)} %get-tuple-element.41.refs_0_), channel_id=1, source_target_pairs={{0,16},{1,17},{2,18},{3,19},{4,20},{5,21},{6,22},{7,23},{8,24},{9,... | collective-permute-start | bytes 221192 | tf_op jit(solution)/shard_map/ppermute | solution.py:381
  22.4 5.9 %collective-permute-start.10 = (f32[10,16,128]{2,1,0:T(8,128)S(1)}, f32[10,16,128]{2,1,0:T(8,128)S(1)}, u32[]{:S(2)}, u32[]{:S(2)}) collective-permute-start(f32[10,16,128]{2,1,0:T(8,128)S(1)} %get-tuple-element.39), channel_id=1, source_target_pairs={{0,16},{1,17},{2,18},{3,19},{4,8},{5,9},{6,10},{7,11},{8,4},{9,5},... | collective-permute-start | bytes 245768 | tf_op jit(solution)/shard_map/ppermute | solution.py:381
  22.4 6.5 %collective-permute-start.11 = (f32[10,16,128]{2,1,0:T(8,128)S(1)}, f32[10,16,128]{2,1,0:T(8,128)S(1)}, u32[]{:S(2)}, u32[]{:S(2)}) collective-permute-start(f32[10,16,128]{2,1,0:T(8,128)S(1)} %get-tuple-element.40), channel_id=1, source_target_pairs={{0,4},{1,5},{2,6},{3,7},{4,0},{5,1},{6,2},{7,3},{8,12},{9,13},{10,... | collective-permute-start | bytes 245768 | tf_op jit(solution)/shard_map/ppermute | solution.py:381
  27.0 1.3 %collective-permute-start.14 = (f32[9,16,128]{2,1,0:T(8,128)S(1)}, f32[9,16,128]{2,1,0:T(8,128)S(1)}, u32[]{:S(2)}, u32[]{:S(2)}) collective-permute-start(f32[9,16,128]{2,1,0:T(8,128)S(1)} %shard_map.74), channel_id=1, source_target_pairs={{0,16},{1,17},{2,18},{3,19},{4,20},{5,21},{6,22},{7,23},{8,24},{9,... | collective-permute-start | bytes 221192 | tf_op jit(solution)/shard_map/ppermute | solution.py:381

commit v14 on v13

--- a/solution.py
+++ b/solution.py
@@ -127,8 +127,8 @@
 
 
 def cross_kernel(count, *refs):
-    own, first, second, ends = refs[:4]
-    others = refs[4 : 1 + count]
+    own, first, second = refs[:3]
+    *others, ends = refs[3 : 1 + count]
     info, _, out = refs[1 + count :]
     interface = lax.axis_index("gx") == lax.axis_size("gx") - 1
 
@@ -278,7 +278,7 @@
     low_edge, high_edge = edges_from(first, second)
 
     def save(x):
-        return pltpu.make_async_copy(made.at[x - 1], out.at[:, x], sems.at[x - 1, 0])
+        return pltpu.make_async_copy(made.at[x - 1], out.at[:, x], sems.at[x - 1])
 
     def plane(x, carry):
         here = pulled.at[lax.rem(x, 2)]
@@ -334,16 +334,12 @@
 
         def store(i, tile):
             made[n, i] = tile
-            if i % 9 == 8:
-                save(i // 9).start()
-
-        def save(third):
-            rows = pl.ds(9 * third, 9)
-            return pltpu.make_async_copy(made.at[n, rows], out.at[rows, x], sems.at[n, third])
 
         velocity = [vel[a, x] for a in range(3)]
         collide(lambda i: pulled[n, i], velocity, solid[0, x], store)
-        return [save(third) for third in range(3)]
+        save = pltpu.make_async_copy(made.at[n], out.at[:, x], sems.at[n])
+        save.start()
+        return save
 
     final = extent_x - 1
     saves = [plane(0, 0, -1, below, None), plane(1, final, 1, above, interface)]
@@ -352,7 +348,7 @@
         low, high = pack_columns(lambda i: made[0, i], 0, low, high)
         low, high = pack_columns(lambda i: made[1, i], final, low, high)
         write_messages(lambda j: made[1, j], low, high, *messages)
-    for save in itertools.chain(*saves):
+    for save in saves:
         save.wait()
 
 
@@ -435,7 +431,7 @@
         last = step == 0
         first = send(first, along_z(1))
         second = send(second, along_z(0))
-        others = [send(own, target) for target in (ends_z, *map(hop_z, range(2, count - 1)))]
+        others = [send(own, target) for target in (*map(hop_z, range(2, count - 1)), ends_z)]
         carried = () if last else (pltpu.with_memory_space_constraint(solid, pltpu.HBM),)
         *copied, vel = pl.pallas_call(
             lambda *refs: velocity_kernel(step, *refs),
@@ -472,7 +468,7 @@
                 scratch_shapes=[
                     pltpu.VMEM((planes, 27, 16, 128), jnp.float32),
                     pltpu.VMEM((2, 27, 16, 128), jnp.float32),
-                    pltpu.SemaphoreType.DMA((planes, 3)),
+                    pltpu.SemaphoreType.DMA((planes,)),
                 ],
                 input_output_aliases={len(operands): 0} if new else {},
                 compiler_params=params,

time: 30.1 us -> 29.6 us (0.983)
    pallas_call x4, Pallas kernels: 5.56 us -> 5.26 us  [make_planes(): pl.pallas_call(lambda *refs: kernel(step, *refs), out_shape=(tile_shape(2...]
  transfers between devices with their start and end apart: 15 -> 15, of which waited for: 6 -> 6; matrix products, arithmetic and copies ran while one was open for 0% -> 0% of each run, Pallas kernels for 25% -> 24%
where the time goes in v14:
time: 29.6 us; the launch traced here: 29.4 us
  starting transfers between devices  13.1 us (44%)
  Pallas kernels  10.7 us (36%)
  waiting for transfers between devices  5.44 us (18%)
    ppermute x15, starting transfers between devices, send(): lax.ppermute(values, axes, [(flat(*here), flat(*target(*here))) for here...  13.1 us
    ppermute x15, waiting for transfers between devices, send(): lax.ppermute(values, axes, [(flat(*here), flat(*target(*here))) for here...  5.44 us
    pallas_call x4, Pallas kernels, make_planes(): pl.pallas_call(lambda *refs: kernel(step, *refs), out_shape=(tile_shape(2...  5.26 us
    pallas_call x2, Pallas kernels, body(): pl.pallas_call(lambda *refs: velocity_kernel(step, *refs), out_shape=(*(j...  3.34 us
    pallas_call x1, Pallas kernels, body(): pl.pallas_call(pack_kernel, out_shape=(tile_shape(27, extent_x), *message...  1.89 us
  transfers between devices with their start and end apart: 15, of which 6 were waited for; matrix products, arithmetic and copies ran while one was open for 0% of the time, Pallas kernels for 24%

profile of v14, /device:TPU:0, one launch (start us, length us, event | category | flops | bytes accessed | tf_op | source)
XLA Modules:
  0.0 29.4 jit_solution(13955245132382100837)
XLA Ops:
  0.0 1.9 %shard_map.64 = (f32[27,8,16,128]{3,2,1,0:T(8,128)S(1)}, f32[9,16,128]{2,1,0:T(8,128)S(1)}, f32[10,16,128]{2,1,0:T(8,128)S(1)}, f32[10,16,128]{2,1,0:T(8,128)S(1)}) custom-call(f32[27,8,16,128]{3,2,1,0:T(8,128)} %bitcast.14), custom_call_target="tpu_custom_call" | custom-call | tf_op jit(solution)/shard_map/pallas_call | solution.py:420
  1.9 0.5 %collective-permute-start = (f32[10,16,128]{2,1,0:T(8,128)S(1)}, f32[10,16,128]{2,1,0:T(8,128)S(1)}, u32[]{:S(2)}, u32[]{:S(2)}) collective-permute-start(f32[10,16,128]{2,1,0:T(8,128)S(1)} %get-tuple-element.28), channel_id=1, source_target_pairs={{0,16},{1,2},{2,1},{3,19},{4,20},{5,6},{6,5},{7,23},{8,24},{9,10},... | collective-permute-start | bytes 245768 | tf_op jit(solution)/shard_map/ppermute | solution.py:377
  2.4 4.1 %collective-permute-start.1 = (f32[10,16,128]{2,1,0:T(8,128)S(1)}, f32[10,16,128]{2,1,0:T(8,128)S(1)}, u32[]{:S(2)}, u32[]{:S(2)}) collective-permute-start(f32[10,16,128]{2,1,0:T(8,128)S(1)} %get-tuple-element.29), channel_id=1, source_target_pairs={{0,1},{1,0},{2,3},{3,2},{4,5},{5,4},{6,7},{7,6},{8,9},{9,8},{10,11... | collective-permute-start | bytes 245768 | tf_op jit(solution)/shard_map/ppermute | solution.py:377
  6.6 0.5 %collective-permute-start.5 = (f32[9,16,128]{2,1,0:T(8,128)S(1)}, f32[9,16,128]{2,1,0:T(8,128)S(1)}, u32[]{:S(2)}, u32[]{:S(2)}) collective-permute-start(f32[9,16,128]{2,1,0:T(8,128)S(1)} %get-tuple-element.32.refs_0_), channel_id=1, source_target_pairs={{0,16},{1,17},{2,18},{3,19},{4,20},{5,21},{6,22},{7,23},{8,24},{9,... | collective-permute-start | bytes 221192 | tf_op jit(solution)/shard_map/ppermute | solution.py:377
  7.1 0.1 collective-permute-start.6
  7.2 1.7 %shard_map.65 = (s32[1,8,16,128]{3,2,1,0:T(8,128)S(1)}, f32[3,8,16,128]{3,2,1,0:T(8,128)S(1)}) custom-call(f32[2,1,27,8,16,128]{5,4,3,2,1,0:T(8,128)} %refs_0_.3, s32[1,8,16,128]{3,2,1,0:T(8,128)} %refs_1_.1), custom_call_target="tpu_custom_call" | custom-call | tf_op jit(solution)/shard_map/pallas_call | solution.py:436
  9.0 0.1 shard_map.66
  9.1 0.4 %collective-permute-start.2 = (f32[10,16,128]{2,1,0:T(8,128)S(1)}, f32[10,16,128]{2,1,0:T(8,128)S(1)}, u32[]{:S(2)}, u32[]{:S(2)}) collective-permute-start(f32[10,16,128]{2,1,0:T(8,128)S(1)} %get-tuple-element.30), channel_id=1, source_target_pairs={{0,16},{1,17},{2,18},{3,19},{4,8},{5,9},{6,10},{7,11},{8,4},{9,5},... | collective-permute-start | bytes 245768 | tf_op jit(solution)/shard_map/ppermute | solution.py:377
  9.5 2.5 %collective-permute-start.3 = (f32[10,16,128]{2,1,0:T(8,128)S(1)}, f32[10,16,128]{2,1,0:T(8,128)S(1)}, u32[]{:S(2)}, u32[]{:S(2)}) collective-permute-start(f32[10,16,128]{2,1,0:T(8,128)S(1)} %get-tuple-element.31), channel_id=1, source_target_pairs={{0,4},{1,5},{2,6},{3,7},{4,0},{5,1},{6,2},{7,3},{8,12},{9,13},{10,... | collective-permute-start | bytes 245768 | tf_op jit(solution)/shard_map/ppermute | solution.py:377
  12.1 1.8 %shard_map.68 = (f32[27,8,16,128]{3,2,1,0:T(8,128)S(1)}, f32[16,128]{1,0:T(8,128)S(1)}, f32[16,128]{1,0:T(8,128)S(1)}) custom-call(f32[27,8,16,128]{3,2,1,0:T(8,128)S(1)} %get-tuple-element.25.adj.refs_0_, f32[3,8,16,128]{3,2,1,0:T(8,128)S(1)} %get-tuple-element.26._.refs_1_, s32[1,8,16,128]{3,2,1,0:T(8,128)S(1)} %get-tuple-element.27.refs_2_, ...), custom_call_target="tpu_custom_call" | custom-call | tf_op jit(solution)/shard_map/pallas_call | solution.py:463
  14.1 1.3 %collective-permute-done.7.refs_7_ = f32[9,16,128]{2,1,0:T(8,128)S(1)} collective-permute-done((f32[9,16,128]{2,1,0:T(8,128)S(1)}, f32[9,16,128]{2,1,0:T(8,128)S(1)}, u32[]{:S(2)}, u32[]{:S(2)}) %collective-permute-start.7) | collective-permute-done | bytes 73760 | tf_op jit(solution)/shard_map/ppermute | solution.py:377
  15.3 1.3 %collective-permute-done.3.refs_6_ = f32[10,16,128]{2,1,0:T(8,128)S(1)} collective-permute-done((f32[10,16,128]{2,1,0:T(8,128)S(1)}, f32[10,16,128]{2,1,0:T(8,128)S(1)}, u32[]{:S(2)}, u32[]{:S(2)}) %collective-permute-start.3) | collective-permute-done | bytes 81952 | tf_op jit(solution)/shard_map/ppermute | solution.py:377
  16.6 0.7 %shard_map.70 = (f32[27,8,16,128]{3,2,1,0:T(8,128)S(1)}, f32[9,16,128]{2,1,0:T(8,128)S(1)}, f32[10,16,128]{2,1,0:T(8,128)S(1)}, f32[10,16,128]{2,1,0:T(8,128)S(1)}) custom-call(f32[27,8,16,128]{3,2,1,0:T(8,128)S(1)} %get-tuple-element.25.adj.refs_0_, f32[3,8,16,128]{3,2,1,0:T(8,128)S(1)} %get-tuple-element.26._.refs_1_, ...), custom_call_target="tpu_custom_call", output_to_operand_aliasing={{0}: (10, {})} | custom-call | tf_op jit(solution)/shard_map/pallas_call | solution.py:463
  17.3 0.1 collective-permute-start.8
  17.4 1.6 %collective-permute-start.9 = (f32[10,16,128]{2,1,0:T(8,128)S(1)}, f32[10,16,128]{2,1,0:T(8,128)S(1)}, u32[]{:S(2)}, u32[]{:S(2)}) collective-permute-start(f32[10,16,128]{2,1,0:T(8,128)S(1)} %get-tuple-element.38), channel_id=1, source_target_pairs={{0,1},{1,0},{2,3},{3,2},{4,5},{5,4},{6,7},{7,6},{8,9},{9,8},{10,11... | collective-permute-start | bytes 245768 | tf_op jit(solution)/shard_map/ppermute | solution.py:377
  19.0 0.5 %collective-permute-start.13 = (f32[9,16,128]{2,1,0:T(8,128)S(1)}, f32[9,16,128]{2,1,0:T(8,128)S(1)}, u32[]{:S(2)}, u32[]{:S(2)}) collective-permute-start(f32[9,16,128]{2,1,0:T(8,128)S(1)} %get-tuple-element.41.refs_0_), channel_id=1, source_target_pairs={{0,16},{1,17},{2,18},{3,19},{4,20},{5,21},{6,22},{7,23},{8,24},{9,... | collective-permute-start | bytes 221192 | tf_op jit(solution)/shard_map/ppermute | solution.py:377
  19.5 1.6 %shard_map.71._.refs_1_ = f32[3,8,16,128]{3,2,1,0:T(8,128)S(1)} custom-call(f32[2,1,27,8,16,128]{5,4,3,2,1,0:T(8,128)} %refs_0_.3), custom_call_target="tpu_custom_call" | custom-call | tf_op jit(solution)/shard_map/pallas_call | solution.py:436
  21.2 1.1 %collective-permute-done.9.second.refs_4_.refs_2_ = f32[10,16,128]{2,1,0:T(8,128)S(1)} collective-permute-done((f32[10,16,128]{2,1,0:T(8,128)S(1)}, f32[10,16,128]{2,1,0:T(8,128)S(1)}, u32[]{:S(2)}, u32[]{:S(2)}) %collective-permute-start.9) | collective-permute-done | bytes 81952 | tf_op jit(solution)/shard_map/ppermute | solution.py:377
  22.2 0.1 shard_map.72
  22.3 2.5 %collective-permute-start.11 = (f32[10,16,128]{2,1,0:T(8,128)S(1)}, f32[10,16,128]{2,1,0:T(8,128)S(1)}, u32[]{:S(2)}, u32[]{:S(2)}) collective-permute-start(f32[10,16,128]{2,1,0:T(8,128)S(1)} %get-tuple-element.40), channel_id=1, source_target_pairs={{0,4},{1,5},{2,6},{3,7},{4,0},{5,1},{6,2},{7,3},{8,12},{9,13},{10,... | collective-permute-start | bytes 245768 | tf_op jit(solution)/shard_map/ppermute | solution.py:377
  24.8 1.7 %shard_map.73 = (f32[27,8,16,128]{3,2,1,0:T(8,128)}, f32[16,128]{1,0:T(8,128)S(1)}, f32[16,128]{1,0:T(8,128)S(1)}) custom-call(f32[27,8,16,128]{3,2,1,0:T(8,128)S(1)} %get-tuple-element.36.adj.refs_0_, f32[3,8,16,128]{3,2,1,0:T(8,128)S(1)} %shard_map.71._.refs_1_, s32[1,8,16,128]{3,2,1,0:T(8,128)S(1)} %get-tuple-element.27.refs_2_, ...), custom_call_target="tpu_custom_call" | custom-call | tf_op jit(solution)/shard_map/pallas_call | solution.py:463
  26.7 1.3 %collective-permute-done.14.refs_7_ = f32[9,16,128]{2,1,0:T(8,128)S(1)} collective-permute-done((f32[9,16,128]{2,1,0:T(8,128)S(1)}, f32[9,16,128]{2,1,0:T(8,128)S(1)}, u32[]{:S(2)}, u32[]{:S(2)}) %collective-permute-start.14) | collective-permute-done | bytes 73760 | tf_op jit(solution)/shard_map/ppermute | solution.py:377
  27.9 0.5 %collective-permute-done.11.refs_6_ = f32[10,16,128]{2,1,0:T(8,128)S(1)} collective-permute-done((f32[10,16,128]{2,1,0:T(8,128)S(1)}, f32[10,16,128]{2,1,0:T(8,128)S(1)}, u32[]{:S(2)}, u32[]{:S(2)}) %collective-permute-start.11) | collective-permute-done | bytes 81952 | tf_op jit(solution)/shard_map/ppermute | solution.py:377
  28.4 1.0 %shard_map.75 = f32[27,8,16,128]{3,2,1,0:T(8,128)} custom-call(f32[27,8,16,128]{3,2,1,0:T(8,128)S(1)} %get-tuple-element.36.adj.refs_0_, f32[3,8,16,128]{3,2,1,0:T(8,128)S(1)} %shard_map.71._.refs_1_, s32[1,8,16,128]{3,2,1,0:T(8,128)S(1)} %get-tuple-element.27.refs_2_, ...), custom_call_target="tpu_custom_call", output_to_operand_aliasing={{}: (10, {})} | custom-call | tf_op jit(solution)/shard_map/pallas_call | solution.py:463
  (24 shorter events, 0.3 us)
Async XLA Ops:
  0.0 7.1 %copy-start = (s32[1,16,128,2]{2,3,1,0:T(2,128)S(1)}, s32[1,16,128,2]{2,3,1,0:T(2,128)}, u32[]{:S(2)}) copy-start(s32[1,16,128,2]{2,3,1,0:T(2,128)} %param.9) | copy-start | bytes 49156
  0.0 7.1 %copy-start.1 = (s32[1,16,128,2]{2,3,1,0:T(2,128)S(1)}, s32[1,16,128,2]{2,3,1,0:T(2,128)}, u32[]{:S(2)}) copy-start(s32[1,16,128,2]{2,3,1,0:T(2,128)} %param.10) | copy-start | bytes 49156
  0.0 7.1 %copy-start.2 = (f32[1,16,128,2]{2,3,1,0:T(2,128)S(1)}, f32[1,16,128,2]{2,3,1,0:T(2,128)}, u32[]{:S(2)}) copy-start(f32[1,16,128,2]{2,3,1,0:T(2,128)} %param.11) | copy-start | bytes 49156
  1.9 7.0 %collective-permute-start = (f32[10,16,128]{2,1,0:T(8,128)S(1)}, f32[10,16,128]{2,1,0:T(8,128)S(1)}, u32[]{:S(2)}, u32[]{:S(2)}) collective-permute-start(f32[10,16,128]{2,1,0:T(8,128)S(1)} %get-tuple-element.28), channel_id=1, source_target_pairs={{0,16},{1,2},{2,1},{3,19},{4,20},{5,6},{6,5},{7,23},{8,24},{9,10},... | collective-permute-start | bytes 245768 | tf_op jit(solution)/shard_map/ppermute | solution.py:377
  2.4 6.6 %collective-permute-start.1 = (f32[10,16,128]{2,1,0:T(8,128)S(1)}, f32[10,16,128]{2,1,0:T(8,128)S(1)}, u32[]{:S(2)}, u32[]{:S(2)}) collective-permute-start(f32[10,16,128]{2,1,0:T(8,128)S(1)} %get-tuple-element.29), channel_id=1, source_target_pairs={{0,1},{1,0},{2,3},{3,2},{4,5},{5,4},{6,7},{7,6},{8,9},{9,8},{10,11... | collective-permute-start | bytes 245768 | tf_op jit(solution)/shard_map/ppermute | solution.py:377
  6.6 7.4 %collective-permute-start.4 = (f32[9,16,128]{2,1,0:T(8,128)S(1)}, f32[9,16,128]{2,1,0:T(8,128)S(1)}, u32[]{:S(2)}, u32[]{:S(2)}) collective-permute-start(f32[9,16,128]{2,1,0:T(8,128)S(1)} %get-tuple-element.32.refs_0_), channel_id=1, source_target_pairs={{0,16},{1,17},{2,18},{3,19},{4,20},{5,21},{6,22},{7,23},{8,24},{9,... | collective-permute-start | bytes 221192 | tf_op jit(solution)/shard_map/ppermute | solution.py:377
  6.6 7.4 %collective-permute-start.5 = (f32[9,16,128]{2,1,0:T(8,128)S(1)}, f32[9,16,128]{2,1,0:T(8,128)S(1)}, u32[]{:S(2)}, u32[]{:S(2)}) collective-permute-start(f32[9,16,128]{2,1,0:T(8,128)S(1)} %get-tuple-element.32.refs_0_), channel_id=1, source_target_pairs={{0,16},{1,17},{2,18},{3,19},{4,20},{5,21},{6,22},{7,23},{8,24},{9,... | collective-permute-start | bytes 221192 | tf_op jit(solution)/shard_map/ppermute | solution.py:377
  7.1 6.8 %collective-permute-start.6 = (f32[4,16,128]{2,1,0:T(8,128)S(1)}, f32[4,16,128]{2,1,0:T(8,128)S(1)}, u32[]{:S(2)}, u32[]{:S(2)}) collective-permute-start(f32[4,16,128]{2,1,0:T(8,128)S(1)} %shard_map.67), channel_id=1, source_target_pairs={{0,16},{1,17},{2,18},{3,19},{4,20},{5,21},{6,22},{7,23},{8,24},{9,... | collective-permute-start | bytes 98312 | tf_op jit(solution)/shard_map/ppermute | solution.py:377
  9.1 6.2 %collective-permute-start.2 = (f32[10,16,128]{2,1,0:T(8,128)S(1)}, f32[10,16,128]{2,1,0:T(8,128)S(1)}, u32[]{:S(2)}, u32[]{:S(2)}) collective-permute-start(f32[10,16,128]{2,1,0:T(8,128)S(1)} %get-tuple-element.30), channel_id=1, source_target_pairs={{0,16},{1,17},{2,18},{3,19},{4,8},{5,9},{6,10},{7,11},{8,4},{9,5},... | collective-permute-start | bytes 245768 | tf_op jit(solution)/shard_map/ppermute | solution.py:377
  9.5 7.1 %collective-permute-start.3 = (f32[10,16,128]{2,1,0:T(8,128)S(1)}, f32[10,16,128]{2,1,0:T(8,128)S(1)}, u32[]{:S(2)}, u32[]{:S(2)}) collective-permute-start(f32[10,16,128]{2,1,0:T(8,128)S(1)} %get-tuple-element.31), channel_id=1, source_target_pairs={{0,4},{1,5},{2,6},{3,7},{4,0},{5,1},{6,2},{7,3},{8,12},{9,13},{10,... | collective-permute-start | bytes 245768 | tf_op jit(solution)/shard_map/ppermute | solution.py:377
  14.0 1.3 %collective-permute-start.7 = (f32[9,16,128]{2,1,0:T(8,128)S(1)}, f32[9,16,128]{2,1,0:T(8,128)S(1)}, u32[]{:S(2)}, u32[]{:S(2)}) collective-permute-start(f32[9,16,128]{2,1,0:T(8,128)S(1)} %shard_map.69), channel_id=1, source_target_pairs={{0,16},{1,17},{2,18},{3,19},{4,20},{5,21},{6,22},{7,23},{8,24},{9,... | collective-permute-start | bytes 221192 | tf_op jit(solution)/shard_map/ppermute | solution.py:377
  17.3 3.9 %collective-permute-start.8 = (f32[10,16,128]{2,1,0:T(8,128)S(1)}, f32[10,16,128]{2,1,0:T(8,128)S(1)}, u32[]{:S(2)}, u32[]{:S(2)}) collective-permute-start(f32[10,16,128]{2,1,0:T(8,128)S(1)} %get-tuple-element.37), channel_id=1, source_target_pairs={{0,16},{1,2},{2,1},{3,19},{4,20},{5,6},{6,5},{7,23},{8,24},{9,10},... | collective-permute-start | bytes 245768 | tf_op jit(solution)/shard_map/ppermute | solution.py:377
  17.4 4.9 %collective-permute-start.9 = (f32[10,16,128]{2,1,0:T(8,128)S(1)}, f32[10,16,128]{2,1,0:T(8,128)S(1)}, u32[]{:S(2)}, u32[]{:S(2)}) collective-permute-start(f32[10,16,128]{2,1,0:T(8,128)S(1)} %get-tuple-element.38), channel_id=1, source_target_pairs={{0,1},{1,0},{2,3},{3,2},{4,5},{5,4},{6,7},{7,6},{8,9},{9,8},{10,11... | collective-permute-start | bytes 245768 | tf_op jit(solution)/shard_map/ppermute | solution.py:377
  19.0 7.6 %collective-permute-start.12 = (f32[9,16,128]{2,1,0:T(8,128)S(1)}, f32[9,16,128]{2,1,0:T(8,128)S(1)}, u32[]{:S(2)}, u32[]{:S(2)}) collective-permute-start(f32[9,16,128]{2,1,0:T(8,128)S(1)} %get-tuple-element.41.refs_0_), channel_id=1, source_target_pairs={{0,16},{1,17},{2,18},{3,19},{4,20},{5,21},{6,22},{7,23},{8,24},{9,... | collective-permute-start | bytes 221192 | tf_op jit(solution)/shard_map/ppermute | solution.py:377
  19.0 7.6 %collective-permute-start.13 = (f32[9,16,128]{2,1,0:T(8,128)S(1)}, f32[9,16,128]{2,1,0:T(8,128)S(1)}, u32[]{:S(2)}, u32[]{:S(2)}) collective-permute-start(f32[9,16,128]{2,1,0:T(8,128)S(1)} %get-tuple-element.41.refs_0_), channel_id=1, source_target_pairs={{0,16},{1,17},{2,18},{3,19},{4,20},{5,21},{6,22},{7,23},{8,24},{9,... | collective-permute-start | bytes 221192 | tf_op jit(solution)/shard_map/ppermute | solution.py:377
  22.3 5.6 %collective-permute-start.10 = (f32[10,16,128]{2,1,0:T(8,128)S(1)}, f32[10,16,128]{2,1,0:T(8,128)S(1)}, u32[]{:S(2)}, u32[]{:S(2)}) collective-permute-start(f32[10,16,128]{2,1,0:T(8,128)S(1)} %get-tuple-element.39), channel_id=1, source_target_pairs={{0,16},{1,17},{2,18},{3,19},{4,8},{5,9},{6,10},{7,11},{8,4},{9,5},... | collective-permute-start | bytes 245768 | tf_op jit(solution)/shard_map/ppermute | solution.py:377
  22.3 6.1 %collective-permute-start.11 = (f32[10,16,128]{2,1,0:T(8,128)S(1)}, f32[10,16,128]{2,1,0:T(8,128)S(1)}, u32[]{:S(2)}, u32[]{:S(2)}) collective-permute-start(f32[10,16,128]{2,1,0:T(8,128)S(1)} %get-tuple-element.40), channel_id=1, source_target_pairs={{0,4},{1,5},{2,6},{3,7},{4,0},{5,1},{6,2},{7,3},{8,12},{9,13},{10,... | collective-permute-start | bytes 245768 | tf_op jit(solution)/shard_map/ppermute | solution.py:377
  26.6 1.3 %collective-permute-start.14 = (f32[9,16,128]{2,1,0:T(8,128)S(1)}, f32[9,16,128]{2,1,0:T(8,128)S(1)}, u32[]{:S(2)}, u32[]{:S(2)}) collective-permute-start(f32[9,16,128]{2,1,0:T(8,128)S(1)} %shard_map.74), channel_id=1, source_target_pairs={{0,16},{1,17},{2,18},{3,19},{4,20},{5,21},{6,22},{7,23},{8,24},{9,... | collective-permute-start | bytes 221192 | tf_op jit(solution)/shard_map/ppermute | solution.py:377

commit v15 on v14

--- a/solution.py
+++ b/solution.py
@@ -303,9 +303,10 @@
     lax.fori_loop(1, extent_x - 1, lambda x, c: (save(x).wait(), c)[1], 0)
 
 
-def outer_kernel(step, adj, vel, solid, first, second, two, one, cross, *rest):
+def outer_kernel(swapped, step, adj, vel, solid, first, second, two, one, cross, *rest):
     *rest, made, pulled, sems = rest
     low_in, high_in, _, out, *messages = rest
+    two, one = (one, two) if swapped else (two, one)
     extent_x = adj.shape[1]
     edges = edges_from(first, second)
     even = is_even("gx")
@@ -484,8 +485,10 @@
             compiler_params=params,
         )(own, first, second, *others, info, columns[0])
         cross = send(cross, flip)
+        ghosts = (one, two) if last else (two, one)
+        kernel = lambda step, *refs: outer_kernel(last, step, *refs)
         field, *results = make_planes(
-            outer_kernel, 2, (two, one, cross, *columns), (new,), () if last else messages
+            kernel, 2, (*ghosts, cross, *columns), (new,), () if last else messages
         )
         if not last:
             own, first, second = results

time: 29.6 us -> 29.5 us (level)
  the two profiles are of different devices: /device:TPU:0 before, /device:TPU:4 now
where the time goes in v15:
time: 29.5 us; the launch traced here: 29.3 us
  starting transfers between devices  12.2 us (41%)
  Pallas kernels  10.7 us (36%)
  waiting for transfers between devices  6.17 us (21%)
    ppermute x15, starting transfers between devices, send(): lax.ppermute(values, axes, [(flat(*here), flat(*target(*here))) for here...  12.2 us
    ppermute x15, waiting for transfers between devices, send(): lax.ppermute(values, axes, [(flat(*here), flat(*target(*here))) for here...  6.17 us
    pallas_call x4, Pallas kernels, make_planes(): pl.pallas_call(lambda *refs: kernel(step, *refs), out_shape=(tile_shape(2...  5.26 us
    pallas_call x2, Pallas kernels, body(): pl.pallas_call(lambda *refs: velocity_kernel(step, *refs), out_shape=(*(j...  3.34 us
    pallas_call x1, Pallas kernels, body(): pl.pallas_call(pack_kernel, out_shape=(tile_shape(27, extent_x), *message...  1.9 us
  transfers between devices with their start and end apart: 15, of which 5 were waited for; matrix products, arithmetic and copies ran while one was open for 0% of the time, Pallas kernels for 24%

profile of v15, /device:TPU:4, one launch (start us, length us, event | category | flops | bytes accessed | tf_op | source)
XLA Modules:
  0.0 29.3 jit_solution(10332113736266078247)
XLA Ops:
  0.0 1.9 %shard_map.64 = (f32[27,8,16,128]{3,2,1,0:T(8,128)S(1)}, f32[9,16,128]{2,1,0:T(8,128)S(1)}, f32[10,16,128]{2,1,0:T(8,128)S(1)}, f32[10,16,128]{2,1,0:T(8,128)S(1)}) custom-call(f32[27,8,16,128]{3,2,1,0:T(8,128)} %bitcast.14), custom_call_target="tpu_custom_call" | custom-call | tf_op jit(solution)/shard_map/pallas_call | solution.py:421
  1.9 0.1 collective-permute-start
  2.0 3.1 %collective-permute-start.1 = (f32[10,16,128]{2,1,0:T(8,128)S(1)}, f32[10,16,128]{2,1,0:T(8,128)S(1)}, u32[]{:S(2)}, u32[]{:S(2)}) collective-permute-start(f32[10,16,128]{2,1,0:T(8,128)S(1)} %get-tuple-element.29), channel_id=1, source_target_pairs={{0,1},{1,0},{2,3},{3,2},{4,5},{5,4},{6,7},{7,6},{8,9},{9,8},{10,11... | collective-permute-start | bytes 245768 | tf_op jit(solution)/shard_map/ppermute | solution.py:378
  5.1 0.5 %collective-permute-start.5 = (f32[9,16,128]{2,1,0:T(8,128)S(1)}, f32[9,16,128]{2,1,0:T(8,128)S(1)}, u32[]{:S(2)}, u32[]{:S(2)}) collective-permute-start(f32[9,16,128]{2,1,0:T(8,128)S(1)} %get-tuple-element.32.refs_0_), channel_id=1, source_target_pairs={{0,16},{1,17},{2,18},{3,19},{4,20},{5,21},{6,22},{7,23},{8,24},{9,... | collective-permute-start | bytes 221192 | tf_op jit(solution)/shard_map/ppermute | solution.py:378
  5.7 0.1 collective-permute-start.6
  5.8 1.7 %shard_map.65 = (s32[1,8,16,128]{3,2,1,0:T(8,128)S(1)}, f32[3,8,16,128]{3,2,1,0:T(8,128)S(1)}) custom-call(f32[2,1,27,8,16,128]{5,4,3,2,1,0:T(8,128)} %refs_0_.3, s32[1,8,16,128]{3,2,1,0:T(8,128)} %refs_1_.1), custom_call_target="tpu_custom_call" | custom-call | tf_op jit(solution)/shard_map/pallas_call | solution.py:437
  7.6 0.1 shard_map.66
  7.6 1.4 %collective-permute-start.2 = (f32[10,16,128]{2,1,0:T(8,128)S(1)}, f32[10,16,128]{2,1,0:T(8,128)S(1)}, u32[]{:S(2)}, u32[]{:S(2)}) collective-permute-start(f32[10,16,128]{2,1,0:T(8,128)S(1)} %get-tuple-element.30), channel_id=1, source_target_pairs={{0,16},{1,17},{2,18},{3,19},{4,8},{5,9},{6,10},{7,11},{8,4},{9,5},... | collective-permute-start | bytes 245768 | tf_op jit(solution)/shard_map/ppermute | solution.py:378
  9.1 2.3 %collective-permute-start.3 = (f32[10,16,128]{2,1,0:T(8,128)S(1)}, f32[10,16,128]{2,1,0:T(8,128)S(1)}, u32[]{:S(2)}, u32[]{:S(2)}) collective-permute-start(f32[10,16,128]{2,1,0:T(8,128)S(1)} %get-tuple-element.31), channel_id=1, source_target_pairs={{0,4},{1,5},{2,6},{3,7},{4,0},{5,1},{6,2},{7,3},{8,12},{9,13},{10,... | collective-permute-start | bytes 245768 | tf_op jit(solution)/shard_map/ppermute | solution.py:378
  11.4 1.8 %shard_map.68 = (f32[27,8,16,128]{3,2,1,0:T(8,128)S(1)}, f32[16,128]{1,0:T(8,128)S(1)}, f32[16,128]{1,0:T(8,128)S(1)}) custom-call(f32[27,8,16,128]{3,2,1,0:T(8,128)S(1)} %get-tuple-element.25.adj.refs_0_, f32[3,8,16,128]{3,2,1,0:T(8,128)S(1)} %get-tuple-element.26._.refs_1_, s32[1,8,16,128]{3,2,1,0:T(8,128)S(1)} %get-tuple-element.27.refs_2_, ...), custom_call_target="tpu_custom_call" | custom-call | tf_op jit(solution)/shard_map/pallas_call | solution.py:464
  13.3 0.1 collective-permute-start.7
  13.4 1.3 %collective-permute-done.7.refs_7_ = f32[9,16,128]{2,1,0:T(8,128)S(1)} collective-permute-done((f32[9,16,128]{2,1,0:T(8,128)S(1)}, f32[9,16,128]{2,1,0:T(8,128)S(1)}, u32[]{:S(2)}, u32[]{:S(2)}) %collective-permute-start.7) | collective-permute-done | bytes 73760 | tf_op jit(solution)/shard_map/ppermute | solution.py:378
  14.7 0.7 %shard_map.70 = (f32[27,8,16,128]{3,2,1,0:T(8,128)S(1)}, f32[9,16,128]{2,1,0:T(8,128)S(1)}, f32[10,16,128]{2,1,0:T(8,128)S(1)}, f32[10,16,128]{2,1,0:T(8,128)S(1)}) custom-call(f32[27,8,16,128]{3,2,1,0:T(8,128)S(1)} %get-tuple-element.25.adj.refs_0_, f32[3,8,16,128]{3,2,1,0:T(8,128)S(1)} %get-tuple-element.26._.refs_1_, ...), custom_call_target="tpu_custom_call", output_to_operand_aliasing={{0}: (10, {})} | custom-call | tf_op jit(solution)/shard_map/pallas_call | solution.py:464
  15.3 0.2 collective-permute-start.8
  15.6 1.2 %collective-permute-start.9 = (f32[10,16,128]{2,1,0:T(8,128)S(1)}, f32[10,16,128]{2,1,0:T(8,128)S(1)}, u32[]{:S(2)}, u32[]{:S(2)}) collective-permute-start(f32[10,16,128]{2,1,0:T(8,128)S(1)} %get-tuple-element.38), channel_id=1, source_target_pairs={{0,1},{1,0},{2,3},{3,2},{4,5},{5,4},{6,7},{7,6},{8,9},{9,8},{10,11... | collective-permute-start | bytes 245768 | tf_op jit(solution)/shard_map/ppermute | solution.py:378
  16.7 0.5 %collective-permute-start.13 = (f32[9,16,128]{2,1,0:T(8,128)S(1)}, f32[9,16,128]{2,1,0:T(8,128)S(1)}, u32[]{:S(2)}, u32[]{:S(2)}) collective-permute-start(f32[9,16,128]{2,1,0:T(8,128)S(1)} %get-tuple-element.41.refs_0_), channel_id=1, source_target_pairs={{0,16},{1,17},{2,18},{3,19},{4,20},{5,21},{6,22},{7,23},{8,24},{9,... | collective-permute-start | bytes 221192 | tf_op jit(solution)/shard_map/ppermute | solution.py:378
  17.2 1.6 %shard_map.71._.refs_1_ = f32[3,8,16,128]{3,2,1,0:T(8,128)S(1)} custom-call(f32[2,1,27,8,16,128]{5,4,3,2,1,0:T(8,128)} %refs_0_.3), custom_call_target="tpu_custom_call" | custom-call | tf_op jit(solution)/shard_map/pallas_call | solution.py:437
  18.9 1.4 %collective-permute-done.9.second.refs_4_.refs_2_ = f32[10,16,128]{2,1,0:T(8,128)S(1)} collective-permute-done((f32[10,16,128]{2,1,0:T(8,128)S(1)}, f32[10,16,128]{2,1,0:T(8,128)S(1)}, u32[]{:S(2)}, u32[]{:S(2)}) %collective-permute-start.9) | collective-permute-done | bytes 81952 | tf_op jit(solution)/shard_map/ppermute | solution.py:378
  20.3 0.1 shard_map.72
  20.3 2.6 %collective-permute-start.10 = (f32[10,16,128]{2,1,0:T(8,128)S(1)}, f32[10,16,128]{2,1,0:T(8,128)S(1)}, u32[]{:S(2)}, u32[]{:S(2)}) collective-permute-start(f32[10,16,128]{2,1,0:T(8,128)S(1)} %get-tuple-element.39), channel_id=1, source_target_pairs={{0,4},{1,5},{2,6},{3,7},{4,0},{5,1},{6,2},{7,3},{8,12},{9,13},{10,... | collective-permute-start | bytes 245768 | tf_op jit(solution)/shard_map/ppermute | solution.py:378
  22.9 1.7 %shard_map.73 = (f32[27,8,16,128]{3,2,1,0:T(8,128)}, f32[16,128]{1,0:T(8,128)S(1)}, f32[16,128]{1,0:T(8,128)S(1)}) custom-call(f32[27,8,16,128]{3,2,1,0:T(8,128)S(1)} %get-tuple-element.36.adj.refs_0_, f32[3,8,16,128]{3,2,1,0:T(8,128)S(1)} %shard_map.71._.refs_1_, s32[1,8,16,128]{3,2,1,0:T(8,128)S(1)} %get-tuple-element.27.refs_2_, ...), custom_call_target="tpu_custom_call" | custom-call | tf_op jit(solution)/shard_map/pallas_call | solution.py:464
  24.8 1.3 %collective-permute-done.14.refs_7_ = f32[9,16,128]{2,1,0:T(8,128)S(1)} collective-permute-done((f32[9,16,128]{2,1,0:T(8,128)S(1)}, f32[9,16,128]{2,1,0:T(8,128)S(1)}, u32[]{:S(2)}, u32[]{:S(2)}) %collective-permute-start.14) | collective-permute-done | bytes 73760 | tf_op jit(solution)/shard_map/ppermute | solution.py:378
  26.1 2.2 %collective-permute-done.11.refs_6_ = f32[10,16,128]{2,1,0:T(8,128)S(1)} collective-permute-done((f32[10,16,128]{2,1,0:T(8,128)S(1)}, f32[10,16,128]{2,1,0:T(8,128)S(1)}, u32[]{:S(2)}, u32[]{:S(2)}) %collective-permute-start.11) | collective-permute-done | bytes 81952 | tf_op jit(solution)/shard_map/ppermute | solution.py:378
  28.3 1.0 %shard_map.75 = f32[27,8,16,128]{3,2,1,0:T(8,128)} custom-call(f32[27,8,16,128]{3,2,1,0:T(8,128)S(1)} %get-tuple-element.36.adj.refs_0_, f32[3,8,16,128]{3,2,1,0:T(8,128)S(1)} %shard_map.71._.refs_1_, s32[1,8,16,128]{3,2,1,0:T(8,128)S(1)} %get-tuple-element.27.refs_2_, ...), custom_call_target="tpu_custom_call", output_to_operand_aliasing={{}: (10, {})} | custom-call | tf_op jit(solution)/shard_map/pallas_call | solution.py:464
  (24 shorter events, 0.3 us)
Async XLA Ops:
  0.0 5.7 %copy-start = (s32[1,16,128,2]{2,3,1,0:T(2,128)S(1)}, s32[1,16,128,2]{2,3,1,0:T(2,128)}, u32[]{:S(2)}) copy-start(s32[1,16,128,2]{2,3,1,0:T(2,128)} %param.9) | copy-start | bytes 49156
  0.0 5.7 %copy-start.1 = (s32[1,16,128,2]{2,3,1,0:T(2,128)S(1)}, s32[1,16,128,2]{2,3,1,0:T(2,128)}, u32[]{:S(2)}) copy-start(s32[1,16,128,2]{2,3,1,0:T(2,128)} %param.10) | copy-start | bytes 49156
  0.0 5.7 %copy-start.2 = (f32[1,16,128,2]{2,3,1,0:T(2,128)S(1)}, f32[1,16,128,2]{2,3,1,0:T(2,128)}, u32[]{:S(2)}) copy-start(f32[1,16,128,2]{2,3,1,0:T(2,128)} %param.11) | copy-start | bytes 49156
  1.9 5.6 %collective-permute-start = (f32[10,16,128]{2,1,0:T(8,128)S(1)}, f32[10,16,128]{2,1,0:T(8,128)S(1)}, u32[]{:S(2)}, u32[]{:S(2)}) collective-permute-start(f32[10,16,128]{2,1,0:T(8,128)S(1)} %get-tuple-element.28), channel_id=1, source_target_pairs={{0,16},{1,2},{2,1},{3,19},{4,20},{5,6},{6,5},{7,23},{8,24},{9,10},... | collective-permute-start | bytes 245768 | tf_op jit(solution)/shard_map/ppermute | solution.py:378
  2.0 5.6 %collective-permute-start.1 = (f32[10,16,128]{2,1,0:T(8,128)S(1)}, f32[10,16,128]{2,1,0:T(8,128)S(1)}, u32[]{:S(2)}, u32[]{:S(2)}) collective-permute-start(f32[10,16,128]{2,1,0:T(8,128)S(1)} %get-tuple-element.29), channel_id=1, source_target_pairs={{0,1},{1,0},{2,3},{3,2},{4,5},{5,4},{6,7},{7,6},{8,9},{9,8},{10,11... | collective-permute-start | bytes 245768 | tf_op jit(solution)/shard_map/ppermute | solution.py:378
  5.1 8.2 %collective-permute-start.4 = (f32[9,16,128]{2,1,0:T(8,128)S(1)}, f32[9,16,128]{2,1,0:T(8,128)S(1)}, u32[]{:S(2)}, u32[]{:S(2)}) collective-permute-start(f32[9,16,128]{2,1,0:T(8,128)S(1)} %get-tuple-element.32.refs_0_), channel_id=1, source_target_pairs={{0,16},{1,17},{2,18},{3,19},{4,20},{5,21},{6,22},{7,23},{8,24},{9,... | collective-permute-start | bytes 221192 | tf_op jit(solution)/shard_map/ppermute | solution.py:378
  5.1 8.2 %collective-permute-start.5 = (f32[9,16,128]{2,1,0:T(8,128)S(1)}, f32[9,16,128]{2,1,0:T(8,128)S(1)}, u32[]{:S(2)}, u32[]{:S(2)}) collective-permute-start(f32[9,16,128]{2,1,0:T(8,128)S(1)} %get-tuple-element.32.refs_0_), channel_id=1, source_target_pairs={{0,16},{1,17},{2,18},{3,19},{4,20},{5,21},{6,22},{7,23},{8,24},{9,... | collective-permute-start | bytes 221192 | tf_op jit(solution)/shard_map/ppermute | solution.py:378
  5.7 7.6 %collective-permute-start.6 = (f32[4,16,128]{2,1,0:T(8,128)S(1)}, f32[4,16,128]{2,1,0:T(8,128)S(1)}, u32[]{:S(2)}, u32[]{:S(2)}) collective-permute-start(f32[4,16,128]{2,1,0:T(8,128)S(1)} %shard_map.67), channel_id=1, source_target_pairs={{0,16},{1,17},{2,18},{3,19},{4,20},{5,21},{6,22},{7,23},{8,24},{9,... | collective-permute-start | bytes 98312 | tf_op jit(solution)/shard_map/ppermute | solution.py:378
  7.6 7.0 %collective-permute-start.2 = (f32[10,16,128]{2,1,0:T(8,128)S(1)}, f32[10,16,128]{2,1,0:T(8,128)S(1)}, u32[]{:S(2)}, u32[]{:S(2)}) collective-permute-start(f32[10,16,128]{2,1,0:T(8,128)S(1)} %get-tuple-element.30), channel_id=1, source_target_pairs={{0,16},{1,17},{2,18},{3,19},{4,8},{5,9},{6,10},{7,11},{8,4},{9,5},... | collective-permute-start | bytes 245768 | tf_op jit(solution)/shard_map/ppermute | solution.py:378
  9.1 5.6 %collective-permute-start.3 = (f32[10,16,128]{2,1,0:T(8,128)S(1)}, f32[10,16,128]{2,1,0:T(8,128)S(1)}, u32[]{:S(2)}, u32[]{:S(2)}) collective-permute-start(f32[10,16,128]{2,1,0:T(8,128)S(1)} %get-tuple-element.31), channel_id=1, source_target_pairs={{0,4},{1,5},{2,6},{3,7},{4,0},{5,1},{6,2},{7,3},{8,12},{9,13},{10,... | collective-permute-start | bytes 245768 | tf_op jit(solution)/shard_map/ppermute | solution.py:378
  13.3 1.3 %collective-permute-start.7 = (f32[9,16,128]{2,1,0:T(8,128)S(1)}, f32[9,16,128]{2,1,0:T(8,128)S(1)}, u32[]{:S(2)}, u32[]{:S(2)}) collective-permute-start(f32[9,16,128]{2,1,0:T(8,128)S(1)} %shard_map.69), channel_id=1, source_target_pairs={{0,16},{1,17},{2,18},{3,19},{4,20},{5,21},{6,22},{7,23},{8,24},{9,... | collective-permute-start | bytes 221192 | tf_op jit(solution)/shard_map/ppermute | solution.py:378
  15.3 3.6 %collective-permute-start.8 = (f32[10,16,128]{2,1,0:T(8,128)S(1)}, f32[10,16,128]{2,1,0:T(8,128)S(1)}, u32[]{:S(2)}, u32[]{:S(2)}) collective-permute-start(f32[10,16,128]{2,1,0:T(8,128)S(1)} %get-tuple-element.37), channel_id=1, source_target_pairs={{0,16},{1,2},{2,1},{3,19},{4,20},{5,6},{6,5},{7,23},{8,24},{9,10},... | collective-permute-start | bytes 245768 | tf_op jit(solution)/shard_map/ppermute | solution.py:378
  15.6 4.7 %collective-permute-start.9 = (f32[10,16,128]{2,1,0:T(8,128)S(1)}, f32[10,16,128]{2,1,0:T(8,128)S(1)}, u32[]{:S(2)}, u32[]{:S(2)}) collective-permute-start(f32[10,16,128]{2,1,0:T(8,128)S(1)} %get-tuple-element.38), channel_id=1, source_target_pairs={{0,1},{1,0},{2,3},{3,2},{4,5},{5,4},{6,7},{7,6},{8,9},{9,8},{10,11... | collective-permute-start | bytes 245768 | tf_op jit(solution)/shard_map/ppermute | solution.py:378
  16.7 7.9 %collective-permute-start.12 = (f32[9,16,128]{2,1,0:T(8,128)S(1)}, f32[9,16,128]{2,1,0:T(8,128)S(1)}, u32[]{:S(2)}, u32[]{:S(2)}) collective-permute-start(f32[9,16,128]{2,1,0:T(8,128)S(1)} %get-tuple-element.41.refs_0_), channel_id=1, source_target_pairs={{0,16},{1,17},{2,18},{3,19},{4,20},{5,21},{6,22},{7,23},{8,24},{9,... | collective-permute-start | bytes 221192 | tf_op jit(solution)/shard_map/ppermute | solution.py:378
  16.7 8.0 %collective-permute-start.13 = (f32[9,16,128]{2,1,0:T(8,128)S(1)}, f32[9,16,128]{2,1,0:T(8,128)S(1)}, u32[]{:S(2)}, u32[]{:S(2)}) collective-permute-start(f32[9,16,128]{2,1,0:T(8,128)S(1)} %get-tuple-element.41.refs_0_), channel_id=1, source_target_pairs={{0,16},{1,17},{2,18},{3,19},{4,20},{5,21},{6,22},{7,23},{8,24},{9,... | collective-permute-start | bytes 221192 | tf_op jit(solution)/shard_map/ppermute | solution.py:378
  20.3 5.7 %collective-permute-start.10 = (f32[10,16,128]{2,1,0:T(8,128)S(1)}, f32[10,16,128]{2,1,0:T(8,128)S(1)}, u32[]{:S(2)}, u32[]{:S(2)}) collective-permute-start(f32[10,16,128]{2,1,0:T(8,128)S(1)} %get-tuple-element.39), channel_id=1, source_target_pairs={{0,4},{1,5},{2,6},{3,7},{4,0},{5,1},{6,2},{7,3},{8,12},{9,13},{10,... | collective-permute-start | bytes 245768 | tf_op jit(solution)/shard_map/ppermute | solution.py:378
  22.9 5.3 %collective-permute-start.11 = (f32[10,16,128]{2,1,0:T(8,128)S(1)}, f32[10,16,128]{2,1,0:T(8,128)S(1)}, u32[]{:S(2)}, u32[]{:S(2)}) collective-permute-start(f32[10,16,128]{2,1,0:T(8,128)S(1)} %get-tuple-element.40), channel_id=1, source_target_pairs={{0,16},{1,17},{2,18},{3,19},{4,8},{5,9},{6,10},{7,11},{8,4},{9,5},... | collective-permute-start | bytes 245768 | tf_op jit(solution)/shard_map/ppermute | solution.py:378
  24.7 1.3 %collective-permute-start.14 = (f32[9,16,128]{2,1,0:T(8,128)S(1)}, f32[9,16,128]{2,1,0:T(8,128)S(1)}, u32[]{:S(2)}, u32[]{:S(2)}) collective-permute-start(f32[9,16,128]{2,1,0:T(8,128)S(1)} %shard_map.74), channel_id=1, source_target_pairs={{0,16},{1,17},{2,18},{3,19},{4,20},{5,21},{6,22},{7,23},{8,24},{9,... | collective-permute-start | bytes 221192 | tf_op jit(solution)/shard_map/ppermute | solution.py:378

commit v16 on v14

--- a/solution.py
+++ b/solution.py
@@ -303,21 +303,26 @@
     lax.fori_loop(1, extent_x - 1, lambda x, c: (save(x).wait(), c)[1], 0)
 
 
-def outer_kernel(step, adj, vel, solid, first, second, two, one, cross, *rest):
+def outer_kernel(last, step, adj, vel, solid, first, second, near, two, far, cross, *rest):
     *rest, made, pulled, sems = rest
     low_in, high_in, _, out, *messages = rest
+    near, two = (near, two) if last else (two, near)
     extent_x = adj.shape[1]
     edges = edges_from(first, second)
     even = is_even("gx")
     interface = lax.axis_index("gx") == lax.axis_size("gx") - 1
 
     bottom = lax.axis_index("gx") == 0
+    inside = lax.axis_index("gx") < lax.axis_size("gx") - 2
+
+    def one(j):
+        return jnp.where(inside, near[j], far[j])
 
     def below(j):
-        return jnp.where(bottom, 0.0, jnp.where(even, two[j], one[j]))
+        return jnp.where(bottom, 0.0, jnp.where(even, two[j], one(j)))
 
     def above(j):
-        tile = jnp.where(even, one[j], two[j])
+        tile = jnp.where(even, one(j), two[j])
         return jnp.where(interface, cross[j], tile) if j < 9 else tile
 
     def plane(n, x, ghost, beyond, raw):
@@ -402,10 +407,10 @@
             return (zone, gx, count - 1 - yz)
         return flip(zone, gx, yz)
 
-    def along_x(shift):
+    def along_x(shift, taken):
         def target(zone, gx, yz):
             to = partner_of(gx, shift)
-            return (zone, to, yz) if 0 <= to < widths else flip(zone, gx, yz)
+            return (zone, to, yz) if 0 <= to < widths and taken(gx) else flip(zone, gx, yz)
 
         return target
 
@@ -455,8 +460,13 @@
             out_specs=tuple(in_vmem(2)),
             compiler_params=params,
         )(field, first, second, vel)
-        two = send(two, along_x(1))
-        one = send(one, along_x(0))
+        everywhere = lambda gx: True
+        two = send(two, along_x(1, everywhere))
+        if last:
+            near = send(one, along_x(0, lambda gx: gx < widths - 2))
+            one = send(one, along_x(0, lambda gx: gx >= widths - 2))
+        else:
+            near = one = send(one, along_x(0, everywhere))
 
         def make_planes(kernel, planes, given, new, extra):
             operands = (field, vel, solid, first, second, *given)
@@ -484,8 +494,9 @@
             compiler_params=params,
         )(own, first, second, *others, info, columns[0])
         cross = send(cross, flip)
+        ghosts = (near, two, one) if last else (two, near, one)
         field, *results = make_planes(
-            outer_kernel, 2, (two, one, cross, *columns), (new,), () if last else messages
+            lambda *refs: outer_kernel(last, *refs), 2, (*ghosts, cross, *columns), (new,), () if last else messages
         )
         if not last:
             own, first, second = results

time: 29.6 us -> 28.9 us (0.976)
  starting transfers between devices: 13.1 us -> 11.3 us
  waiting for transfers between devices: 5.44 us -> 6.47 us
    ppermute x15 -> x16, starting transfers between devices: 13.1 us -> 11.3 us  [send(): lax.ppermute(values, axes, [(flat(*here), flat(*target(*here))) for here...]
    ppermute x15 -> x16, waiting for transfers between devices: 5.44 us -> 6.47 us  [send(): lax.ppermute(values, axes, [(flat(*here), flat(*target(*here))) for here...]
  transfers between devices with their start and end apart: 15 -> 16, of which waited for: 6 -> 6; matrix products, arithmetic and copies ran while one was open for 0% -> 0% of each run, Pallas kernels for 24% -> 25%
where the time goes in v16:
time: 28.9 us; the launch traced here: 28.7 us
  starting transfers between devices  11.3 us (39%)
  Pallas kernels  10.7 us (37%)
  waiting for transfers between devices  6.47 us (22%)
    ppermute x16, starting transfers between devices, send(): lax.ppermute(values, axes, [(flat(*here), flat(*target(*here))) for here...  11.3 us
    ppermute x16, waiting for transfers between devices, send(): lax.ppermute(values, axes, [(flat(*here), flat(*target(*here))) for here...  6.47 us
    pallas_call x4, Pallas kernels, make_planes(): pl.pallas_call(lambda *refs: kernel(step, *refs), out_shape=(tile_shape(2...  5.27 us
    pallas_call x2, Pallas kernels, body(): pl.pallas_call(lambda *refs: velocity_kernel(step, *refs), out_shape=(*(j...  3.34 us
    pallas_call x1, Pallas kernels, body(): pl.pallas_call(pack_kernel, out_shape=(tile_shape(27, extent_x), *message...  1.89 us
  transfers between devices with their start and end apart: 16, of which 6 were waited for; matrix products, arithmetic and copies ran while one was open for 0% of the time, Pallas kernels for 25%

profile of v16, /device:TPU:0, one launch (start us, length us, event | category | flops | bytes accessed | tf_op | source)
XLA Modules:
  0.0 28.7 jit_solution(12222130431748862040)
XLA Ops:
  0.0 1.9 %shard_map.64 = (f32[27,8,16,128]{3,2,1,0:T(8,128)S(1)}, f32[9,16,128]{2,1,0:T(8,128)S(1)}, f32[10,16,128]{2,1,0:T(8,128)S(1)}, f32[10,16,128]{2,1,0:T(8,128)S(1)}) custom-call(f32[27,8,16,128]{3,2,1,0:T(8,128)} %bitcast.14), custom_call_target="tpu_custom_call" | custom-call | tf_op jit(solution)/shard_map/pallas_call | solution.py:425
  1.9 0.5 %collective-permute-start = (f32[10,16,128]{2,1,0:T(8,128)S(1)}, f32[10,16,128]{2,1,0:T(8,128)S(1)}, u32[]{:S(2)}, u32[]{:S(2)}) collective-permute-start(f32[10,16,128]{2,1,0:T(8,128)S(1)} %get-tuple-element.28), channel_id=1, source_target_pairs={{0,16},{1,2},{2,1},{3,19},{4,20},{5,6},{6,5},{7,23},{8,24},{9,10},... | collective-permute-start | bytes 245768 | tf_op jit(solution)/shard_map/ppermute | solution.py:382
  2.4 4.1 %collective-permute-start.1 = (f32[10,16,128]{2,1,0:T(8,128)S(1)}, f32[10,16,128]{2,1,0:T(8,128)S(1)}, u32[]{:S(2)}, u32[]{:S(2)}) collective-permute-start(f32[10,16,128]{2,1,0:T(8,128)S(1)} %get-tuple-element.29), channel_id=1, source_target_pairs={{0,1},{1,0},{2,3},{3,2},{4,5},{5,4},{6,7},{7,6},{8,9},{9,8},{10,11... | collective-permute-start | bytes 245768 | tf_op jit(solution)/shard_map/ppermute | solution.py:382
  6.6 0.5 %collective-permute-start.5 = (f32[9,16,128]{2,1,0:T(8,128)S(1)}, f32[9,16,128]{2,1,0:T(8,128)S(1)}, u32[]{:S(2)}, u32[]{:S(2)}) collective-permute-start(f32[9,16,128]{2,1,0:T(8,128)S(1)} %get-tuple-element.32.refs_0_), channel_id=1, source_target_pairs={{0,16},{1,17},{2,18},{3,19},{4,20},{5,21},{6,22},{7,23},{8,24},{9,... | collective-permute-start | bytes 221192 | tf_op jit(solution)/shard_map/ppermute | solution.py:382
  7.1 0.1 collective-permute-start.6
  7.2 1.7 %shard_map.65 = (s32[1,8,16,128]{3,2,1,0:T(8,128)S(1)}, f32[3,8,16,128]{3,2,1,0:T(8,128)S(1)}) custom-call(f32[2,1,27,8,16,128]{5,4,3,2,1,0:T(8,128)} %refs_0_.3, s32[1,8,16,128]{3,2,1,0:T(8,128)} %refs_1_.1), custom_call_target="tpu_custom_call" | custom-call | tf_op jit(solution)/shard_map/pallas_call | solution.py:441
  9.0 0.1 shard_map.66
  9.1 0.4 %collective-permute-start.2 = (f32[10,16,128]{2,1,0:T(8,128)S(1)}, f32[10,16,128]{2,1,0:T(8,128)S(1)}, u32[]{:S(2)}, u32[]{:S(2)}) collective-permute-start(f32[10,16,128]{2,1,0:T(8,128)S(1)} %get-tuple-element.30), channel_id=1, source_target_pairs={{0,16},{1,17},{2,18},{3,19},{4,8},{5,9},{6,10},{7,11},{8,4},{9,5},... | collective-permute-start | bytes 245768 | tf_op jit(solution)/shard_map/ppermute | solution.py:382
  9.5 2.5 %collective-permute-start.3 = (f32[10,16,128]{2,1,0:T(8,128)S(1)}, f32[10,16,128]{2,1,0:T(8,128)S(1)}, u32[]{:S(2)}, u32[]{:S(2)}) collective-permute-start(f32[10,16,128]{2,1,0:T(8,128)S(1)} %get-tuple-element.31), channel_id=1, source_target_pairs={{0,4},{1,5},{2,6},{3,7},{4,0},{5,1},{6,2},{7,3},{8,12},{9,13},{10,... | collective-permute-start | bytes 245768 | tf_op jit(solution)/shard_map/ppermute | solution.py:382
  12.1 1.8 %shard_map.68 = (f32[27,8,16,128]{3,2,1,0:T(8,128)S(1)}, f32[16,128]{1,0:T(8,128)S(1)}, f32[16,128]{1,0:T(8,128)S(1)}) custom-call(f32[27,8,16,128]{3,2,1,0:T(8,128)S(1)} %get-tuple-element.25.adj.refs_0_, f32[3,8,16,128]{3,2,1,0:T(8,128)S(1)} %get-tuple-element.26._.refs_1_, s32[1,8,16,128]{3,2,1,0:T(8,128)S(1)} %get-tuple-element.27.refs_2_, ...), custom_call_target="tpu_custom_call" | custom-call | tf_op jit(solution)/shard_map/pallas_call | solution.py:473
  14.1 1.3 %collective-permute-done.7.refs_8_ = f32[9,16,128]{2,1,0:T(8,128)S(1)} collective-permute-done((f32[9,16,128]{2,1,0:T(8,128)S(1)}, f32[9,16,128]{2,1,0:T(8,128)S(1)}, u32[]{:S(2)}, u32[]{:S(2)}) %collective-permute-start.7) | collective-permute-done | bytes 73760 | tf_op jit(solution)/shard_map/ppermute | solution.py:382
  15.3 1.3 %collective-permute-done.3.refs_6_.refs_7_ = f32[10,16,128]{2,1,0:T(8,128)S(1)} collective-permute-done((f32[10,16,128]{2,1,0:T(8,128)S(1)}, f32[10,16,128]{2,1,0:T(8,128)S(1)}, u32[]{:S(2)}, u32[]{:S(2)}) %collective-permute-start.3) | collective-permute-done | bytes 81952 | tf_op jit(solution)/shard_map/ppermute | solution.py:382
  16.6 0.7 %shard_map.70 = (f32[27,8,16,128]{3,2,1,0:T(8,128)S(1)}, f32[9,16,128]{2,1,0:T(8,128)S(1)}, f32[10,16,128]{2,1,0:T(8,128)S(1)}, f32[10,16,128]{2,1,0:T(8,128)S(1)}) custom-call(f32[27,8,16,128]{3,2,1,0:T(8,128)S(1)} %get-tuple-element.25.adj.refs_0_, f32[3,8,16,128]{3,2,1,0:T(8,128)S(1)} %get-tuple-element.26._.refs_1_, ...), custom_call_target="tpu_custom_call", output_to_operand_aliasing={{0}: (11, {})} | custom-call | tf_op jit(solution)/shard_map/pallas_call | solution.py:473
  17.4 1.6 %collective-permute-start.9 = (f32[10,16,128]{2,1,0:T(8,128)S(1)}, f32[10,16,128]{2,1,0:T(8,128)S(1)}, u32[]{:S(2)}, u32[]{:S(2)}) collective-permute-start(f32[10,16,128]{2,1,0:T(8,128)S(1)} %get-tuple-element.38), channel_id=1, source_target_pairs={{0,1},{1,0},{2,3},{3,2},{4,5},{5,4},{6,7},{7,6},{8,9},{9,8},{10,11... | collective-permute-start | bytes 245768 | tf_op jit(solution)/shard_map/ppermute | solution.py:382
  19.0 0.5 %collective-permute-start.14 = (f32[9,16,128]{2,1,0:T(8,128)S(1)}, f32[9,16,128]{2,1,0:T(8,128)S(1)}, u32[]{:S(2)}, u32[]{:S(2)}) collective-permute-start(f32[9,16,128]{2,1,0:T(8,128)S(1)} %get-tuple-element.41.refs_0_), channel_id=1, source_target_pairs={{0,16},{1,17},{2,18},{3,19},{4,20},{5,21},{6,22},{7,23},{8,24},{9,... | collective-permute-start | bytes 221192 | tf_op jit(solution)/shard_map/ppermute | solution.py:382
  19.5 1.6 %shard_map.71._.refs_1_ = f32[3,8,16,128]{3,2,1,0:T(8,128)S(1)} custom-call(f32[2,1,27,8,16,128]{5,4,3,2,1,0:T(8,128)} %refs_0_.3), custom_call_target="tpu_custom_call" | custom-call | tf_op jit(solution)/shard_map/pallas_call | solution.py:441
  21.2 1.1 %collective-permute-done.9.second.refs_4_.refs_2_ = f32[10,16,128]{2,1,0:T(8,128)S(1)} collective-permute-done((f32[10,16,128]{2,1,0:T(8,128)S(1)}, f32[10,16,128]{2,1,0:T(8,128)S(1)}, u32[]{:S(2)}, u32[]{:S(2)}) %collective-permute-start.9) | collective-permute-done | bytes 81952 | tf_op jit(solution)/shard_map/ppermute | solution.py:382
  22.2 0.1 shard_map.72
  22.4 0.5 %collective-permute-start.12 = (f32[10,16,128]{2,1,0:T(8,128)S(1)}, f32[10,16,128]{2,1,0:T(8,128)S(1)}, u32[]{:S(2)}, u32[]{:S(2)}) collective-permute-start(f32[10,16,128]{2,1,0:T(8,128)S(1)} %get-tuple-element.39), channel_id=1, source_target_pairs={{0,16},{1,17},{2,18},{3,19},{4,20},{5,21},{6,22},{7,23},{8,12},{9,... | collective-permute-start | bytes 245768 | tf_op jit(solution)/shard_map/ppermute | solution.py:382
  22.9 1.7 %shard_map.73 = (f32[27,8,16,128]{3,2,1,0:T(8,128)}, f32[16,128]{1,0:T(8,128)S(1)}, f32[16,128]{1,0:T(8,128)S(1)}) custom-call(f32[27,8,16,128]{3,2,1,0:T(8,128)S(1)} %get-tuple-element.36.adj.refs_0_, f32[3,8,16,128]{3,2,1,0:T(8,128)S(1)} %shard_map.71._.refs_1_, s32[1,8,16,128]{3,2,1,0:T(8,128)S(1)} %get-tuple-element.27.refs_2_, ...), custom_call_target="tpu_custom_call" | custom-call | tf_op jit(solution)/shard_map/pallas_call | solution.py:473
  24.7 0.1 collective-permute-start.15
  24.8 1.2 %collective-permute-done.15.refs_8_ = f32[9,16,128]{2,1,0:T(8,128)S(1)} collective-permute-done((f32[9,16,128]{2,1,0:T(8,128)S(1)}, f32[9,16,128]{2,1,0:T(8,128)S(1)}, u32[]{:S(2)}, u32[]{:S(2)}) %collective-permute-start.15) | collective-permute-done | bytes 73760 | tf_op jit(solution)/shard_map/ppermute | solution.py:382
  26.0 1.6 %collective-permute-done.10.refs_5_ = f32[10,16,128]{2,1,0:T(8,128)S(1)} collective-permute-done((f32[10,16,128]{2,1,0:T(8,128)S(1)}, f32[10,16,128]{2,1,0:T(8,128)S(1)}, u32[]{:S(2)}, u32[]{:S(2)}) %collective-permute-start.10) | collective-permute-done | bytes 81952 | tf_op jit(solution)/shard_map/ppermute | solution.py:382
  27.6 1.0 %shard_map.75 = f32[27,8,16,128]{3,2,1,0:T(8,128)} custom-call(f32[27,8,16,128]{3,2,1,0:T(8,128)S(1)} %get-tuple-element.36.adj.refs_0_, f32[3,8,16,128]{3,2,1,0:T(8,128)S(1)} %shard_map.71._.refs_1_, s32[1,8,16,128]{3,2,1,0:T(8,128)S(1)} %get-tuple-element.27.refs_2_, ...), custom_call_target="tpu_custom_call", output_to_operand_aliasing={{}: (11, {})} | custom-call | tf_op jit(solution)/shard_map/pallas_call | solution.py:473
  (26 shorter events, 0.4 us)
Async XLA Ops:
  0.0 7.1 %copy-start = (s32[1,16,128,2]{2,3,1,0:T(2,128)S(1)}, s32[1,16,128,2]{2,3,1,0:T(2,128)}, u32[]{:S(2)}) copy-start(s32[1,16,128,2]{2,3,1,0:T(2,128)} %param.9) | copy-start | bytes 49156
  0.0 7.1 %copy-start.1 = (s32[1,16,128,2]{2,3,1,0:T(2,128)S(1)}, s32[1,16,128,2]{2,3,1,0:T(2,128)}, u32[]{:S(2)}) copy-start(s32[1,16,128,2]{2,3,1,0:T(2,128)} %param.10) | copy-start | bytes 49156
  0.0 7.1 %copy-start.2 = (f32[1,16,128,2]{2,3,1,0:T(2,128)S(1)}, f32[1,16,128,2]{2,3,1,0:T(2,128)}, u32[]{:S(2)}) copy-start(f32[1,16,128,2]{2,3,1,0:T(2,128)} %param.11) | copy-start | bytes 49156
  1.9 7.0 %collective-permute-start = (f32[10,16,128]{2,1,0:T(8,128)S(1)}, f32[10,16,128]{2,1,0:T(8,128)S(1)}, u32[]{:S(2)}, u32[]{:S(2)}) collective-permute-start(f32[10,16,128]{2,1,0:T(8,128)S(1)} %get-tuple-element.28), channel_id=1, source_target_pairs={{0,16},{1,2},{2,1},{3,19},{4,20},{5,6},{6,5},{7,23},{8,24},{9,10},... | collective-permute-start | bytes 245768 | tf_op jit(solution)/shard_map/ppermute | solution.py:382
  2.4 6.6 %collective-permute-start.1 = (f32[10,16,128]{2,1,0:T(8,128)S(1)}, f32[10,16,128]{2,1,0:T(8,128)S(1)}, u32[]{:S(2)}, u32[]{:S(2)}) collective-permute-start(f32[10,16,128]{2,1,0:T(8,128)S(1)} %get-tuple-element.29), channel_id=1, source_target_pairs={{0,1},{1,0},{2,3},{3,2},{4,5},{5,4},{6,7},{7,6},{8,9},{9,8},{10,11... | collective-permute-start | bytes 245768 | tf_op jit(solution)/shard_map/ppermute | solution.py:382
  6.6 7.4 %collective-permute-start.4 = (f32[9,16,128]{2,1,0:T(8,128)S(1)}, f32[9,16,128]{2,1,0:T(8,128)S(1)}, u32[]{:S(2)}, u32[]{:S(2)}) collective-permute-start(f32[9,16,128]{2,1,0:T(8,128)S(1)} %get-tuple-element.32.refs_0_), channel_id=1, source_target_pairs={{0,16},{1,17},{2,18},{3,19},{4,20},{5,21},{6,22},{7,23},{8,24},{9,... | collective-permute-start | bytes 221192 | tf_op jit(solution)/shard_map/ppermute | solution.py:382
  6.6 7.4 %collective-permute-start.5 = (f32[9,16,128]{2,1,0:T(8,128)S(1)}, f32[9,16,128]{2,1,0:T(8,128)S(1)}, u32[]{:S(2)}, u32[]{:S(2)}) collective-permute-start(f32[9,16,128]{2,1,0:T(8,128)S(1)} %get-tuple-element.32.refs_0_), channel_id=1, source_target_pairs={{0,16},{1,17},{2,18},{3,19},{4,20},{5,21},{6,22},{7,23},{8,24},{9,... | collective-permute-start | bytes 221192 | tf_op jit(solution)/shard_map/ppermute | solution.py:382
  7.1 6.8 %collective-permute-start.6 = (f32[4,16,128]{2,1,0:T(8,128)S(1)}, f32[4,16,128]{2,1,0:T(8,128)S(1)}, u32[]{:S(2)}, u32[]{:S(2)}) collective-permute-start(f32[4,16,128]{2,1,0:T(8,128)S(1)} %shard_map.67), channel_id=1, source_target_pairs={{0,16},{1,17},{2,18},{3,19},{4,20},{5,21},{6,22},{7,23},{8,24},{9,... | collective-permute-start | bytes 98312 | tf_op jit(solution)/shard_map/ppermute | solution.py:382
  9.1 6.2 %collective-permute-start.2 = (f32[10,16,128]{2,1,0:T(8,128)S(1)}, f32[10,16,128]{2,1,0:T(8,128)S(1)}, u32[]{:S(2)}, u32[]{:S(2)}) collective-permute-start(f32[10,16,128]{2,1,0:T(8,128)S(1)} %get-tuple-element.30), channel_id=1, source_target_pairs={{0,16},{1,17},{2,18},{3,19},{4,8},{5,9},{6,10},{7,11},{8,4},{9,5},... | collective-permute-start | bytes 245768 | tf_op jit(solution)/shard_map/ppermute | solution.py:382
  9.5 7.1 %collective-permute-start.3 = (f32[10,16,128]{2,1,0:T(8,128)S(1)}, f32[10,16,128]{2,1,0:T(8,128)S(1)}, u32[]{:S(2)}, u32[]{:S(2)}) collective-permute-start(f32[10,16,128]{2,1,0:T(8,128)S(1)} %get-tuple-element.31), channel_id=1, source_target_pairs={{0,4},{1,5},{2,6},{3,7},{4,0},{5,1},{6,2},{7,3},{8,12},{9,13},{10,... | collective-permute-start | bytes 245768 | tf_op jit(solution)/shard_map/ppermute | solution.py:382
  14.0 1.3 %collective-permute-start.7 = (f32[9,16,128]{2,1,0:T(8,128)S(1)}, f32[9,16,128]{2,1,0:T(8,128)S(1)}, u32[]{:S(2)}, u32[]{:S(2)}) collective-permute-start(f32[9,16,128]{2,1,0:T(8,128)S(1)} %shard_map.69), channel_id=1, source_target_pairs={{0,16},{1,17},{2,18},{3,19},{4,20},{5,21},{6,22},{7,23},{8,24},{9,... | collective-permute-start | bytes 221192 | tf_op jit(solution)/shard_map/ppermute | solution.py:382
  17.3 3.9 %collective-permute-start.8 = (f32[10,16,128]{2,1,0:T(8,128)S(1)}, f32[10,16,128]{2,1,0:T(8,128)S(1)}, u32[]{:S(2)}, u32[]{:S(2)}) collective-permute-start(f32[10,16,128]{2,1,0:T(8,128)S(1)} %get-tuple-element.37), channel_id=1, source_target_pairs={{0,16},{1,2},{2,1},{3,19},{4,20},{5,6},{6,5},{7,23},{8,24},{9,10},... | collective-permute-start | bytes 245768 | tf_op jit(solution)/shard_map/ppermute | solution.py:382
  17.4 4.9 %collective-permute-start.9 = (f32[10,16,128]{2,1,0:T(8,128)S(1)}, f32[10,16,128]{2,1,0:T(8,128)S(1)}, u32[]{:S(2)}, u32[]{:S(2)}) collective-permute-start(f32[10,16,128]{2,1,0:T(8,128)S(1)} %get-tuple-element.38), channel_id=1, source_target_pairs={{0,1},{1,0},{2,3},{3,2},{4,5},{5,4},{6,7},{7,6},{8,9},{9,8},{10,11... | collective-permute-start | bytes 245768 | tf_op jit(solution)/shard_map/ppermute | solution.py:382
  19.0 5.7 %collective-permute-start.13 = (f32[9,16,128]{2,1,0:T(8,128)S(1)}, f32[9,16,128]{2,1,0:T(8,128)S(1)}, u32[]{:S(2)}, u32[]{:S(2)}) collective-permute-start(f32[9,16,128]{2,1,0:T(8,128)S(1)} %get-tuple-element.41.refs_0_), channel_id=1, source_target_pairs={{0,16},{1,17},{2,18},{3,19},{4,20},{5,21},{6,22},{7,23},{8,24},{9,... | collective-permute-start | bytes 221192 | tf_op jit(solution)/shard_map/ppermute | solution.py:382
  19.0 5.7 %collective-permute-start.14 = (f32[9,16,128]{2,1,0:T(8,128)S(1)}, f32[9,16,128]{2,1,0:T(8,128)S(1)}, u32[]{:S(2)}, u32[]{:S(2)}) collective-permute-start(f32[9,16,128]{2,1,0:T(8,128)S(1)} %get-tuple-element.41.refs_0_), channel_id=1, source_target_pairs={{0,16},{1,17},{2,18},{3,19},{4,20},{5,21},{6,22},{7,23},{8,24},{9,... | collective-permute-start | bytes 221192 | tf_op jit(solution)/shard_map/ppermute | solution.py:382
  22.3 5.3 %collective-permute-start.10 = (f32[10,16,128]{2,1,0:T(8,128)S(1)}, f32[10,16,128]{2,1,0:T(8,128)S(1)}, u32[]{:S(2)}, u32[]{:S(2)}) collective-permute-start(f32[10,16,128]{2,1,0:T(8,128)S(1)} %get-tuple-element.39), channel_id=1, source_target_pairs={{0,4},{1,5},{2,6},{3,7},{4,0},{5,1},{6,2},{7,3},{8,24},{9,25},{10,... | collective-permute-start | bytes 245768 | tf_op jit(solution)/shard_map/ppermute | solution.py:382
  22.3 5.3 %collective-permute-start.11 = (f32[10,16,128]{2,1,0:T(8,128)S(1)}, f32[10,16,128]{2,1,0:T(8,128)S(1)}, u32[]{:S(2)}, u32[]{:S(2)}) collective-permute-start(f32[10,16,128]{2,1,0:T(8,128)S(1)} %get-tuple-element.40), channel_id=1, source_target_pairs={{0,16},{1,17},{2,18},{3,19},{4,8},{5,9},{6,10},{7,11},{8,4},{9,5},... | collective-permute-start | bytes 245768 | tf_op jit(solution)/shard_map/ppermute | solution.py:382
  22.4 5.2 %collective-permute-start.12 = (f32[10,16,128]{2,1,0:T(8,128)S(1)}, f32[10,16,128]{2,1,0:T(8,128)S(1)}, u32[]{:S(2)}, u32[]{:S(2)}) collective-permute-start(f32[10,16,128]{2,1,0:T(8,128)S(1)} %get-tuple-element.39), channel_id=1, source_target_pairs={{0,16},{1,17},{2,18},{3,19},{4,20},{5,21},{6,22},{7,23},{8,12},{9,... | collective-permute-start | bytes 245768 | tf_op jit(solution)/shard_map/ppermute | solution.py:382
  24.7 1.3 %collective-permute-start.15 = (f32[9,16,128]{2,1,0:T(8,128)S(1)}, f32[9,16,128]{2,1,0:T(8,128)S(1)}, u32[]{:S(2)}, u32[]{:S(2)}) collective-permute-start(f32[9,16,128]{2,1,0:T(8,128)S(1)} %shard_map.74), channel_id=1, source_target_pairs={{0,16},{1,17},{2,18},{3,19},{4,20},{5,21},{6,22},{7,23},{8,24},{9,... | collective-permute-start | bytes 221192 | tf_op jit(solution)/shard_map/ppermute | solution.py:382

commit v17 on v16

--- a/solution.py
+++ b/solution.py
@@ -109,12 +109,13 @@
         copy.wait()
 
 
-def side_kernel(adj, first, second, _, two_out, one_out):
+def side_kernel(adj, first, second, *rest):
+    *_, near_out, two_out, far_out = rest
     extent_x = adj.shape[1]
     even = is_even("gx")
     for j in range(9):
         top, bottom = adj[j, extent_x - 1], adj[18 + j, 0]
-        one_out[j] = jnp.where(even, top, bottom)
+        near_out[j] = far_out[j] = jnp.where(even, top, bottom)
         two_out[j] = jnp.where(even, bottom, top)
     lane = lanes()
     low, high = edges_from(first, second)
@@ -122,7 +123,7 @@
         jnp.where(lane < 64, pltpu.roll(low, 128 - start, 1), pltpu.roll(high, 192 - start, 1))
         for start in (9 * extent_x, 9)
     ]
-    one_out[9] = jnp.where(even, top, bottom)
+    near_out[9] = far_out[9] = jnp.where(even, top, bottom)
     two_out[9] = jnp.where(even, bottom, top)
 
 
@@ -303,10 +304,9 @@
     lax.fori_loop(1, extent_x - 1, lambda x, c: (save(x).wait(), c)[1], 0)
 
 
-def outer_kernel(last, step, adj, vel, solid, first, second, near, two, far, cross, *rest):
+def outer_kernel(step, adj, vel, solid, first, second, near, two, far, cross, *rest):
     *rest, made, pulled, sems = rest
     low_in, high_in, _, out, *messages = rest
-    near, two = (near, two) if last else (two, near)
     extent_x = adj.shape[1]
     edges = edges_from(first, second)
     even = is_even("gx")
@@ -434,6 +434,7 @@
     info = send(info, flip)
     for step in (1, 0):
         last = step == 0
+        swap = last
         first = send(first, along_z(1))
         second = send(second, along_z(0))
         others = [send(own, target) for target in (*map(hop_z, range(2, count - 1)), ends_z)]
@@ -453,25 +454,26 @@
             compiler_params=params,
         )(saved, *carried)
         solid = copied[0] if copied else solid
-        two, one = pl.pallas_call(
+        near, two, far = pl.pallas_call(
             side_kernel,
-            out_shape=(tile_shape(10),) * 2,
-            in_specs=in_vmem(3) + in_any(1),
-            out_specs=tuple(in_vmem(2)),
+            out_shape=(tile_shape(10),) * 3,
+            in_specs=in_vmem(3) + in_any(2),
+            out_specs=tuple(in_vmem(3)),
             compiler_params=params,
-        )(field, first, second, vel)
-        everywhere = lambda gx: True
-        two = send(two, along_x(1, everywhere))
-        if last:
-            near = send(one, along_x(0, lambda gx: gx < widths - 2))
-            one = send(one, along_x(0, lambda gx: gx >= widths - 2))
-        else:
-            near = one = send(one, along_x(0, everywhere))
+        )(field, first, second, vel, info)
+        near = send(near, along_x(0, lambda gx: gx < widths - 2))
+        two = send(two, along_x(1, lambda gx: True))
+        far = send(far, along_x(0, lambda gx: gx >= widths - 2))
 
         def make_planes(kernel, planes, given, new, extra):
-            operands = (field, vel, solid, first, second, *given)
+            pair = (second, first) if swap else (first, second)
+            operands = (field, vel, solid, *pair, *given)
+
+            def run(adj, vel, solid, *refs):
+                kernel(step, adj, vel, solid, *(refs[1::-1] if swap else refs[:2]), *refs[2:])
+
             return pl.pallas_call(
-                lambda *refs: kernel(step, *refs),
+                run,
                 out_shape=(tile_shape(27, extent_x), *extra),
                 in_specs=in_vmem(len(operands)) + in_any(len(new)),
                 out_specs=tuple(in_any(1) + in_vmem(len(extra))),
@@ -494,9 +496,9 @@
             compiler_params=params,
         )(own, first, second, *others, info, columns[0])
         cross = send(cross, flip)
-        ghosts = (near, two, one) if last else (two, near, one)
+        ghosts = (near, two, far)
         field, *results = make_planes(
-            lambda *refs: outer_kernel(last, *refs), 2, (*ghosts, cross, *columns), (new,), () if last else messages
+            outer_kernel, 2, (*ghosts, cross, *columns), (new,), () if last else messages
         )
         if not last:
             own, first, second = results

time: 28.9 us -> 28.7 us (level)
  the two profiles are of different devices: /device:TPU:0 before, /device:TPU:7 now
where the time goes in v17:
time: 28.7 us; the launch traced here: 28.5 us
  starting transfers between devices  15 us (52%)
  Pallas kernels  11.4 us (40%)
  waiting for transfers between devices  1.86 us (6%)
    ppermute x17, starting transfers between devices, send(): lax.ppermute(values, axes, [(flat(*here), flat(*target(*here))) for here...  15 us
    pallas_call x4, Pallas kernels, make_planes(): pl.pallas_call(run, out_shape=(tile_shape(27, extent_x), *extra), in_spec...  5.28 us
    pallas_call x2, Pallas kernels, body(): pl.pallas_call(lambda *refs: velocity_kernel(step, *refs), out_shape=(*(j...  3.32 us
    pallas_call x1, Pallas kernels, body(): pl.pallas_call(pack_kernel, out_shape=(tile_shape(27, extent_x), *message...  1.9 us
    ppermute x17, waiting for transfers between devices, send(): lax.ppermute(values, axes, [(flat(*here), flat(*target(*here))) for here...  1.86 us
    pallas_call x2, Pallas kernels, body(): pl.pallas_call(lambda *refs: cross_kernel(count, *refs), out_shape=tile_s...  0.71 us
  transfers between devices with their start and end apart: 17, of which 2 were waited for; matrix products, arithmetic and copies ran while one was open for 0% of the time, Pallas kernels for 27%

profile of v17, /device:TPU:7, one launch (start us, length us, event | category | flops | bytes accessed | tf_op | source)
XLA Modules:
  0.0 28.5 jit_solution(5531320600434900100)
XLA Ops:
  0.0 1.9 %shard_map.64 = (f32[27,8,16,128]{3,2,1,0:T(8,128)S(1)}, f32[9,16,128]{2,1,0:T(8,128)S(1)}, f32[10,16,128]{2,1,0:T(8,128)S(1)}, f32[10,16,128]{2,1,0:T(8,128)S(1)}) custom-call(f32[27,8,16,128]{3,2,1,0:T(8,128)} %bitcast.14), custom_call_target="tpu_custom_call" | custom-call | tf_op jit(solution)/shard_map/pallas_call | solution.py:425
  1.9 0.7 %collective-permute-start = (f32[10,16,128]{2,1,0:T(8,128)S(1)}, f32[10,16,128]{2,1,0:T(8,128)S(1)}, u32[]{:S(2)}, u32[]{:S(2)}) collective-permute-start(f32[10,16,128]{2,1,0:T(8,128)S(1)} %get-tuple-element.30), channel_id=1, source_target_pairs={{0,16},{1,2},{2,1},{3,19},{4,20},{5,6},{6,5},{7,23},{8,24},{9,10},... | collective-permute-start | bytes 245768 | tf_op jit(solution)/shard_map/ppermute | solution.py:382
  2.7 1.9 %collective-permute-start.1 = (f32[10,16,128]{2,1,0:T(8,128)S(1)}, f32[10,16,128]{2,1,0:T(8,128)S(1)}, u32[]{:S(2)}, u32[]{:S(2)}) collective-permute-start(f32[10,16,128]{2,1,0:T(8,128)S(1)} %get-tuple-element.31), channel_id=1, source_target_pairs={{0,1},{1,0},{2,3},{3,2},{4,5},{5,4},{6,7},{7,6},{8,9},{9,8},{10,11... | collective-permute-start | bytes 245768 | tf_op jit(solution)/shard_map/ppermute | solution.py:382
  4.6 1.7 %collective-permute-start.6 = (f32[9,16,128]{2,1,0:T(8,128)S(1)}, f32[9,16,128]{2,1,0:T(8,128)S(1)}, u32[]{:S(2)}, u32[]{:S(2)}) collective-permute-start(f32[9,16,128]{2,1,0:T(8,128)S(1)} %get-tuple-element.35.refs_0_), channel_id=1, source_target_pairs={{0,16},{1,17},{2,18},{3,19},{4,20},{5,21},{6,22},{7,23},{8,24},{9,... | collective-permute-start | bytes 221192 | tf_op jit(solution)/shard_map/ppermute | solution.py:382
  6.3 0.4 %collective-permute-start.7 = (f32[9,16,128]{2,1,0:T(8,128)S(1)}, f32[9,16,128]{2,1,0:T(8,128)S(1)}, u32[]{:S(2)}, u32[]{:S(2)}) collective-permute-start(f32[9,16,128]{2,1,0:T(8,128)S(1)} %get-tuple-element.35.refs_0_), channel_id=1, source_target_pairs={{0,16},{1,17},{2,18},{3,19},{4,20},{5,21},{6,22},{7,23},{8,24},{9,... | collective-permute-start | bytes 221192 | tf_op jit(solution)/shard_map/ppermute | solution.py:382
  6.7 1.6 %collective-permute-start.2 = (f32[4,16,128]{2,1,0:T(8,128)S(1)}, f32[4,16,128]{2,1,0:T(8,128)S(1)}, u32[]{:S(2)}, u32[]{:S(2)}) collective-permute-start(f32[4,16,128]{2,1,0:T(8,128)S(1)} %shard_map.66), channel_id=1, source_target_pairs={{0,16},{1,17},{2,18},{3,19},{4,20},{5,21},{6,22},{7,23},{8,24},{9,... | collective-permute-start | bytes 98312 | tf_op jit(solution)/shard_map/ppermute | solution.py:382
  8.3 1.7 %shard_map.65 = (s32[1,8,16,128]{3,2,1,0:T(8,128)S(1)}, f32[3,8,16,128]{3,2,1,0:T(8,128)S(1)}) custom-call(f32[2,1,27,8,16,128]{5,4,3,2,1,0:T(8,128)} %refs_0_.3, s32[1,8,16,128]{3,2,1,0:T(8,128)} %refs_1_.1), custom_call_target="tpu_custom_call" | custom-call | tf_op jit(solution)/shard_map/pallas_call | solution.py:442
  10.2 0.5 %collective-permute-start.4 = (f32[10,16,128]{2,1,0:T(8,128)S(1)}, f32[10,16,128]{2,1,0:T(8,128)S(1)}, u32[]{:S(2)}, u32[]{:S(2)}) collective-permute-start(f32[10,16,128]{2,1,0:T(8,128)S(1)} %get-tuple-element.33), channel_id=1, source_target_pairs={{0,16},{1,17},{2,18},{3,19},{4,8},{5,9},{6,10},{7,11},{8,4},{9,5},... | collective-permute-start | bytes 245768 | tf_op jit(solution)/shard_map/ppermute | solution.py:382
  10.6 1.8 %shard_map.68 = (f32[27,8,16,128]{3,2,1,0:T(8,128)S(1)}, f32[16,128]{1,0:T(8,128)S(1)}, f32[16,128]{1,0:T(8,128)S(1)}) custom-call(f32[27,8,16,128]{3,2,1,0:T(8,128)S(1)} %get-tuple-element.27.adj, f32[3,8,16,128]{3,2,1,0:T(8,128)S(1)} %get-tuple-element.28.rest_0_.vel, s32[1,8,16,128]{3,2,1,0:T(8,128)S(1)} %get-tuple-element.29.solid, ...), custom_call_target="tpu_custom_call" | custom-call | tf_op jit(solution)/shard_map/pallas_call | solution.py:475
  12.5 0.4 %shard_map.69 = f32[9,16,128]{2,1,0:T(8,128)S(1)} custom-call(f32[9,16,128]{2,1,0:T(8,128)S(1)} %get-tuple-element.35.refs_0_, f32[10,16,128]{2,1,0:T(8,128)S(1)} %collective-permute-done.first.refs_0_.refs_1_, f32[10,16,128]{2,1,0:T(8,128)S(1)} %collective-permute-done.1.second.refs_1_.refs_2_, f32[9,16,128]{2,1,0:T(8,128)S(1)} %collective-permute-done.6.refs_3_, ...), custom_call_target="tpu_custom_call" | custom-call | tf_op jit(solution)/shard_map/pallas_call | solution.py:491
  12.9 0.9 %collective-permute-start.8 = (f32[9,16,128]{2,1,0:T(8,128)S(1)}, f32[9,16,128]{2,1,0:T(8,128)S(1)}, u32[]{:S(2)}, u32[]{:S(2)}) collective-permute-start(f32[9,16,128]{2,1,0:T(8,128)S(1)} %shard_map.69), channel_id=1, source_target_pairs={{0,16},{1,17},{2,18},{3,19},{4,20},{5,21},{6,22},{7,23},{8,24},{9,... | collective-permute-start | bytes 221192 | tf_op jit(solution)/shard_map/ppermute | solution.py:382
  13.7 0.9 %collective-permute-done.8.refs_5_ = f32[9,16,128]{2,1,0:T(8,128)S(1)} collective-permute-done((f32[9,16,128]{2,1,0:T(8,128)S(1)}, f32[9,16,128]{2,1,0:T(8,128)S(1)}, u32[]{:S(2)}, u32[]{:S(2)}) %collective-permute-start.8) | collective-permute-done | bytes 73760 | tf_op jit(solution)/shard_map/ppermute | solution.py:382
  14.7 0.7 %shard_map.70 = (f32[27,8,16,128]{3,2,1,0:T(8,128)S(1)}, f32[9,16,128]{2,1,0:T(8,128)S(1)}, f32[10,16,128]{2,1,0:T(8,128)S(1)}, f32[10,16,128]{2,1,0:T(8,128)S(1)}) custom-call(f32[27,8,16,128]{3,2,1,0:T(8,128)S(1)} %get-tuple-element.27.adj, f32[3,8,16,128]{3,2,1,0:T(8,128)S(1)} %get-tuple-element.28.rest_0_.vel, ...), custom_call_target="tpu_custom_call", output_to_operand_aliasing={{0}: (11, {})} | custom-call | tf_op jit(solution)/shard_map/pallas_call | solution.py:475
  15.3 0.9 %collective-permute-start.10 = (f32[10,16,128]{2,1,0:T(8,128)S(1)}, f32[10,16,128]{2,1,0:T(8,128)S(1)}, u32[]{:S(2)}, u32[]{:S(2)}) collective-permute-start(f32[10,16,128]{2,1,0:T(8,128)S(1)} %get-tuple-element.41), channel_id=1, source_target_pairs={{0,16},{1,2},{2,1},{3,19},{4,20},{5,6},{6,5},{7,23},{8,24},{9,10},... | collective-permute-start | bytes 245768 | tf_op jit(solution)/shard_map/ppermute | solution.py:382
  16.2 0.5 %collective-permute-start.9 = (f32[10,16,128]{2,1,0:T(8,128)S(1)}, f32[10,16,128]{2,1,0:T(8,128)S(1)}, u32[]{:S(2)}, u32[]{:S(2)}) collective-permute-start(f32[10,16,128]{2,1,0:T(8,128)S(1)} %get-tuple-element.40), channel_id=1, source_target_pairs={{0,1},{1,0},{2,3},{3,2},{4,5},{5,4},{6,7},{7,6},{8,9},{9,8},{10,11... | collective-permute-start | bytes 245768 | tf_op jit(solution)/shard_map/ppermute | solution.py:382
  16.7 2.1 %collective-permute-start.14 = (f32[9,16,128]{2,1,0:T(8,128)S(1)}, f32[9,16,128]{2,1,0:T(8,128)S(1)}, u32[]{:S(2)}, u32[]{:S(2)}) collective-permute-start(f32[9,16,128]{2,1,0:T(8,128)S(1)} %get-tuple-element.45.refs_0_), channel_id=1, source_target_pairs={{0,16},{1,17},{2,18},{3,19},{4,20},{5,21},{6,22},{7,23},{8,24},{9,... | collective-permute-start | bytes 221192 | tf_op jit(solution)/shard_map/ppermute | solution.py:382
  18.8 1.0 %collective-permute-start.15 = (f32[9,16,128]{2,1,0:T(8,128)S(1)}, f32[9,16,128]{2,1,0:T(8,128)S(1)}, u32[]{:S(2)}, u32[]{:S(2)}) collective-permute-start(f32[9,16,128]{2,1,0:T(8,128)S(1)} %get-tuple-element.45.refs_0_), channel_id=1, source_target_pairs={{0,16},{1,17},{2,18},{3,19},{4,20},{5,21},{6,22},{7,23},{8,24},{9,... | collective-permute-start | bytes 221192 | tf_op jit(solution)/shard_map/ppermute | solution.py:382
  19.8 1.6 %shard_map.71.rest_0_.vel = f32[3,8,16,128]{3,2,1,0:T(8,128)S(1)} custom-call(f32[2,1,27,8,16,128]{5,4,3,2,1,0:T(8,128)} %refs_0_.3), custom_call_target="tpu_custom_call" | custom-call | tf_op jit(solution)/shard_map/pallas_call | solution.py:442
  21.6 0.9 %collective-permute-start.11 = (f32[10,16,128]{2,1,0:T(8,128)S(1)}, f32[10,16,128]{2,1,0:T(8,128)S(1)}, u32[]{:S(2)}, u32[]{:S(2)}) collective-permute-start(f32[10,16,128]{2,1,0:T(8,128)S(1)} %get-tuple-element.42), channel_id=1, source_target_pairs={{0,4},{1,5},{2,6},{3,7},{4,0},{5,1},{6,2},{7,3},{8,24},{9,25},{10,... | collective-permute-start | bytes 245768 | tf_op jit(solution)/shard_map/ppermute | solution.py:382
  22.6 1.7 %shard_map.73 = (f32[27,8,16,128]{3,2,1,0:T(8,128)}, f32[16,128]{1,0:T(8,128)S(1)}, f32[16,128]{1,0:T(8,128)S(1)}) custom-call(f32[27,8,16,128]{3,2,1,0:T(8,128)S(1)} %get-tuple-element.39.adj, f32[3,8,16,128]{3,2,1,0:T(8,128)S(1)} %shard_map.71.rest_0_.vel, s32[1,8,16,128]{3,2,1,0:T(8,128)S(1)} %get-tuple-element.29.solid, ...), custom_call_target="tpu_custom_call" | custom-call | tf_op jit(solution)/shard_map/pallas_call | solution.py:475
  24.3 0.4 %shard_map.74 = f32[9,16,128]{2,1,0:T(8,128)S(1)} custom-call(f32[9,16,128]{2,1,0:T(8,128)S(1)} %get-tuple-element.45.refs_0_, f32[10,16,128]{2,1,0:T(8,128)S(1)} %collective-permute-done.10.first.refs_1_, f32[10,16,128]{2,1,0:T(8,128)S(1)} %collective-permute-done.9.second.refs_0_.refs_2_, f32[9,16,128]{2,1,0:T(8,128)S(1)} %collective-permute-done.14.refs_3_, ...), custom_call_target="tpu_custom_call" | custom-call | tf_op jit(solution)/shard_map/pallas_call | solution.py:491
  24.7 1.8 %collective-permute-start.16 = (f32[9,16,128]{2,1,0:T(8,128)S(1)}, f32[9,16,128]{2,1,0:T(8,128)S(1)}, u32[]{:S(2)}, u32[]{:S(2)}) collective-permute-start(f32[9,16,128]{2,1,0:T(8,128)S(1)} %shard_map.74), channel_id=1, source_target_pairs={{0,16},{1,17},{2,18},{3,19},{4,20},{5,21},{6,22},{7,23},{8,24},{9,... | collective-permute-start | bytes 221192 | tf_op jit(solution)/shard_map/ppermute | solution.py:382
  26.5 0.9 %collective-permute-done.16.refs_5_ = f32[9,16,128]{2,1,0:T(8,128)S(1)} collective-permute-done((f32[9,16,128]{2,1,0:T(8,128)S(1)}, f32[9,16,128]{2,1,0:T(8,128)S(1)}, u32[]{:S(2)}, u32[]{:S(2)}) %collective-permute-start.16) | collective-permute-done | bytes 73760 | tf_op jit(solution)/shard_map/ppermute | solution.py:382
  27.5 1.0 %shard_map.75 = f32[27,8,16,128]{3,2,1,0:T(8,128)} custom-call(f32[27,8,16,128]{3,2,1,0:T(8,128)S(1)} %get-tuple-element.39.adj, f32[3,8,16,128]{3,2,1,0:T(8,128)S(1)} %shard_map.71.rest_0_.vel, s32[1,8,16,128]{3,2,1,0:T(8,128)S(1)} %get-tuple-element.29.solid, ...), custom_call_target="tpu_custom_call", output_to_operand_aliasing={{}: (11, {})} | custom-call | tf_op jit(solution)/shard_map/pallas_call | solution.py:475
  (28 shorter events, 0.4 us)
Async XLA Ops:
  0.0 6.7 %copy-start = (s32[1,16,128,2]{2,3,1,0:T(2,128)S(1)}, s32[1,16,128,2]{2,3,1,0:T(2,128)}, u32[]{:S(2)}) copy-start(s32[1,16,128,2]{2,3,1,0:T(2,128)} %param.9) | copy-start | bytes 49156
  0.0 6.7 %copy-start.1 = (s32[1,16,128,2]{2,3,1,0:T(2,128)S(1)}, s32[1,16,128,2]{2,3,1,0:T(2,128)}, u32[]{:S(2)}) copy-start(s32[1,16,128,2]{2,3,1,0:T(2,128)} %param.10) | copy-start | bytes 49156
  0.0 6.7 %copy-start.2 = (f32[1,16,128,2]{2,3,1,0:T(2,128)S(1)}, f32[1,16,128,2]{2,3,1,0:T(2,128)}, u32[]{:S(2)}) copy-start(f32[1,16,128,2]{2,3,1,0:T(2,128)} %param.11) | copy-start | bytes 49156
  1.9 8.1 %collective-permute-start = (f32[10,16,128]{2,1,0:T(8,128)S(1)}, f32[10,16,128]{2,1,0:T(8,128)S(1)}, u32[]{:S(2)}, u32[]{:S(2)}) collective-permute-start(f32[10,16,128]{2,1,0:T(8,128)S(1)} %get-tuple-element.30), channel_id=1, source_target_pairs={{0,16},{1,2},{2,1},{3,19},{4,20},{5,6},{6,5},{7,23},{8,24},{9,10},... | collective-permute-start | bytes 245768 | tf_op jit(solution)/shard_map/ppermute | solution.py:382
  2.7 7.3 %collective-permute-start.1 = (f32[10,16,128]{2,1,0:T(8,128)S(1)}, f32[10,16,128]{2,1,0:T(8,128)S(1)}, u32[]{:S(2)}, u32[]{:S(2)}) collective-permute-start(f32[10,16,128]{2,1,0:T(8,128)S(1)} %get-tuple-element.31), channel_id=1, source_target_pairs={{0,1},{1,0},{2,3},{3,2},{4,5},{5,4},{6,7},{7,6},{8,9},{9,8},{10,11... | collective-permute-start | bytes 245768 | tf_op jit(solution)/shard_map/ppermute | solution.py:382
  4.6 7.9 %collective-permute-start.6 = (f32[9,16,128]{2,1,0:T(8,128)S(1)}, f32[9,16,128]{2,1,0:T(8,128)S(1)}, u32[]{:S(2)}, u32[]{:S(2)}) collective-permute-start(f32[9,16,128]{2,1,0:T(8,128)S(1)} %get-tuple-element.35.refs_0_), channel_id=1, source_target_pairs={{0,16},{1,17},{2,18},{3,19},{4,20},{5,21},{6,22},{7,23},{8,24},{9,... | collective-permute-start | bytes 221192 | tf_op jit(solution)/shard_map/ppermute | solution.py:382
  6.3 6.2 %collective-permute-start.7 = (f32[9,16,128]{2,1,0:T(8,128)S(1)}, f32[9,16,128]{2,1,0:T(8,128)S(1)}, u32[]{:S(2)}, u32[]{:S(2)}) collective-permute-start(f32[9,16,128]{2,1,0:T(8,128)S(1)} %get-tuple-element.35.refs_0_), channel_id=1, source_target_pairs={{0,16},{1,17},{2,18},{3,19},{4,20},{5,21},{6,22},{7,23},{8,24},{9,... | collective-permute-start | bytes 221192 | tf_op jit(solution)/shard_map/ppermute | solution.py:382
  6.7 3.3 %collective-permute-start.2 = (f32[4,16,128]{2,1,0:T(8,128)S(1)}, f32[4,16,128]{2,1,0:T(8,128)S(1)}, u32[]{:S(2)}, u32[]{:S(2)}) collective-permute-start(f32[4,16,128]{2,1,0:T(8,128)S(1)} %shard_map.66), channel_id=1, source_target_pairs={{0,16},{1,17},{2,18},{3,19},{4,20},{5,21},{6,22},{7,23},{8,24},{9,... | collective-permute-start | bytes 98312 | tf_op jit(solution)/shard_map/ppermute | solution.py:382
  10.1 4.6 %collective-permute-start.3 = (f32[10,16,128]{2,1,0:T(8,128)S(1)}, f32[10,16,128]{2,1,0:T(8,128)S(1)}, u32[]{:S(2)}, u32[]{:S(2)}) collective-permute-start(f32[10,16,128]{2,1,0:T(8,128)S(1)} %get-tuple-element.32), channel_id=1, source_target_pairs={{0,4},{1,5},{2,6},{3,7},{4,0},{5,1},{6,2},{7,3},{8,24},{9,25},{10,... | collective-permute-start | bytes 245768 | tf_op jit(solution)/shard_map/ppermute | solution.py:382
  10.2 4.5 %collective-permute-start.4 = (f32[10,16,128]{2,1,0:T(8,128)S(1)}, f32[10,16,128]{2,1,0:T(8,128)S(1)}, u32[]{:S(2)}, u32[]{:S(2)}) collective-permute-start(f32[10,16,128]{2,1,0:T(8,128)S(1)} %get-tuple-element.33), channel_id=1, source_target_pairs={{0,16},{1,17},{2,18},{3,19},{4,8},{5,9},{6,10},{7,11},{8,4},{9,5},... | collective-permute-start | bytes 245768 | tf_op jit(solution)/shard_map/ppermute | solution.py:382
  10.6 4.0 %collective-permute-start.5 = (f32[10,16,128]{2,1,0:T(8,128)S(1)}, f32[10,16,128]{2,1,0:T(8,128)S(1)}, u32[]{:S(2)}, u32[]{:S(2)}) collective-permute-start(f32[10,16,128]{2,1,0:T(8,128)S(1)} %get-tuple-element.34), channel_id=1, source_target_pairs={{0,16},{1,17},{2,18},{3,19},{4,20},{5,21},{6,22},{7,23},{8,12},{9,... | collective-permute-start | bytes 245768 | tf_op jit(solution)/shard_map/ppermute | solution.py:382
  12.9 1.8 %collective-permute-start.8 = (f32[9,16,128]{2,1,0:T(8,128)S(1)}, f32[9,16,128]{2,1,0:T(8,128)S(1)}, u32[]{:S(2)}, u32[]{:S(2)}) collective-permute-start(f32[9,16,128]{2,1,0:T(8,128)S(1)} %shard_map.69), channel_id=1, source_target_pairs={{0,16},{1,17},{2,18},{3,19},{4,20},{5,21},{6,22},{7,23},{8,24},{9,... | collective-permute-start | bytes 221192 | tf_op jit(solution)/shard_map/ppermute | solution.py:382
  15.3 6.1 %collective-permute-start.10 = (f32[10,16,128]{2,1,0:T(8,128)S(1)}, f32[10,16,128]{2,1,0:T(8,128)S(1)}, u32[]{:S(2)}, u32[]{:S(2)}) collective-permute-start(f32[10,16,128]{2,1,0:T(8,128)S(1)} %get-tuple-element.41), channel_id=1, source_target_pairs={{0,16},{1,2},{2,1},{3,19},{4,20},{5,6},{6,5},{7,23},{8,24},{9,10},... | collective-permute-start | bytes 245768 | tf_op jit(solution)/shard_map/ppermute | solution.py:382
  16.2 5.2 %collective-permute-start.9 = (f32[10,16,128]{2,1,0:T(8,128)S(1)}, f32[10,16,128]{2,1,0:T(8,128)S(1)}, u32[]{:S(2)}, u32[]{:S(2)}) collective-permute-start(f32[10,16,128]{2,1,0:T(8,128)S(1)} %get-tuple-element.40), channel_id=1, source_target_pairs={{0,1},{1,0},{2,3},{3,2},{4,5},{5,4},{6,7},{7,6},{8,9},{9,8},{10,11... | collective-permute-start | bytes 245768 | tf_op jit(solution)/shard_map/ppermute | solution.py:382
  16.7 7.6 %collective-permute-start.14 = (f32[9,16,128]{2,1,0:T(8,128)S(1)}, f32[9,16,128]{2,1,0:T(8,128)S(1)}, u32[]{:S(2)}, u32[]{:S(2)}) collective-permute-start(f32[9,16,128]{2,1,0:T(8,128)S(1)} %get-tuple-element.45.refs_0_), channel_id=1, source_target_pairs={{0,16},{1,17},{2,18},{3,19},{4,20},{5,21},{6,22},{7,23},{8,24},{9,... | collective-permute-start | bytes 221192 | tf_op jit(solution)/shard_map/ppermute | solution.py:382
  18.8 5.5 %collective-permute-start.15 = (f32[9,16,128]{2,1,0:T(8,128)S(1)}, f32[9,16,128]{2,1,0:T(8,128)S(1)}, u32[]{:S(2)}, u32[]{:S(2)}) collective-permute-start(f32[9,16,128]{2,1,0:T(8,128)S(1)} %get-tuple-element.45.refs_0_), channel_id=1, source_target_pairs={{0,16},{1,17},{2,18},{3,19},{4,20},{5,21},{6,22},{7,23},{8,24},{9,... | collective-permute-start | bytes 221192 | tf_op jit(solution)/shard_map/ppermute | solution.py:382
  21.6 5.9 %collective-permute-start.11 = (f32[10,16,128]{2,1,0:T(8,128)S(1)}, f32[10,16,128]{2,1,0:T(8,128)S(1)}, u32[]{:S(2)}, u32[]{:S(2)}) collective-permute-start(f32[10,16,128]{2,1,0:T(8,128)S(1)} %get-tuple-element.42), channel_id=1, source_target_pairs={{0,4},{1,5},{2,6},{3,7},{4,0},{5,1},{6,2},{7,3},{8,24},{9,25},{10,... | collective-permute-start | bytes 245768 | tf_op jit(solution)/shard_map/ppermute | solution.py:382
  22.5 5.0 %collective-permute-start.12 = (f32[10,16,128]{2,1,0:T(8,128)S(1)}, f32[10,16,128]{2,1,0:T(8,128)S(1)}, u32[]{:S(2)}, u32[]{:S(2)}) collective-permute-start(f32[10,16,128]{2,1,0:T(8,128)S(1)} %get-tuple-element.43), channel_id=1, source_target_pairs={{0,16},{1,17},{2,18},{3,19},{4,8},{5,9},{6,10},{7,11},{8,4},{9,5},... | collective-permute-start | bytes 245768 | tf_op jit(solution)/shard_map/ppermute | solution.py:382
  22.6 4.9 %collective-permute-start.13 = (f32[10,16,128]{2,1,0:T(8,128)S(1)}, f32[10,16,128]{2,1,0:T(8,128)S(1)}, u32[]{:S(2)}, u32[]{:S(2)}) collective-permute-start(f32[10,16,128]{2,1,0:T(8,128)S(1)} %get-tuple-element.44), channel_id=1, source_target_pairs={{0,16},{1,17},{2,18},{3,19},{4,20},{5,21},{6,22},{7,23},{8,12},{9,... | collective-permute-start | bytes 245768 | tf_op jit(solution)/shard_map/ppermute | solution.py:382
  24.7 2.7 %collective-permute-start.16 = (f32[9,16,128]{2,1,0:T(8,128)S(1)}, f32[9,16,128]{2,1,0:T(8,128)S(1)}, u32[]{:S(2)}, u32[]{:S(2)}) collective-permute-start(f32[9,16,128]{2,1,0:T(8,128)S(1)} %shard_map.74), channel_id=1, source_target_pairs={{0,16},{1,17},{2,18},{3,19},{4,20},{5,21},{6,22},{7,23},{8,24},{9,... | collective-permute-start | bytes 221192 | tf_op jit(solution)/shard_map/ppermute | solution.py:382

commit v18 on v17

--- a/solution.py
+++ b/solution.py
@@ -110,12 +110,12 @@
 
 
 def side_kernel(adj, first, second, *rest):
-    *_, near_out, two_out, far_out = rest
+    *_, two_out, one_out = rest
     extent_x = adj.shape[1]
     even = is_even("gx")
     for j in range(9):
         top, bottom = adj[j, extent_x - 1], adj[18 + j, 0]
-        near_out[j] = far_out[j] = jnp.where(even, top, bottom)
+        one_out[j] = jnp.where(even, top, bottom)
         two_out[j] = jnp.where(even, bottom, top)
     lane = lanes()
     low, high = edges_from(first, second)
@@ -123,7 +123,7 @@
         jnp.where(lane < 64, pltpu.roll(low, 128 - start, 1), pltpu.roll(high, 192 - start, 1))
         for start in (9 * extent_x, 9)
     ]
-    near_out[9] = far_out[9] = jnp.where(even, top, bottom)
+    one_out[9] = jnp.where(even, top, bottom)
     two_out[9] = jnp.where(even, bottom, top)
 
 
@@ -304,7 +304,7 @@
     lax.fori_loop(1, extent_x - 1, lambda x, c: (save(x).wait(), c)[1], 0)
 
 
-def outer_kernel(step, adj, vel, solid, first, second, near, two, far, cross, *rest):
+def outer_kernel(step, adj, vel, solid, first, second, near, far, two, cross, *rest):
     *rest, made, pulled, sems = rest
     low_in, high_in, _, out, *messages = rest
     extent_x = adj.shape[1]
@@ -454,16 +454,16 @@
             compiler_params=params,
         )(saved, *carried)
         solid = copied[0] if copied else solid
-        near, two, far = pl.pallas_call(
+        two, one = pl.pallas_call(
             side_kernel,
-            out_shape=(tile_shape(10),) * 3,
+            out_shape=(tile_shape(10),) * 2,
             in_specs=in_vmem(3) + in_any(2),
-            out_specs=tuple(in_vmem(3)),
+            out_specs=tuple(in_vmem(2)),
             compiler_params=params,
         )(field, first, second, vel, info)
-        near = send(near, along_x(0, lambda gx: gx < widths - 2))
+        near = send(one, along_x(0, lambda gx: gx < widths - 2))
         two = send(two, along_x(1, lambda gx: True))
-        far = send(far, along_x(0, lambda gx: gx >= widths - 2))
+        one = send(one, along_x(0, lambda gx: gx >= widths - 2))
 
         def make_planes(kernel, planes, given, new, extra):
             pair = (second, first) if swap else (first, second)
@@ -496,7 +496,7 @@
             compiler_params=params,
         )(own, first, second, *others, info, columns[0])
         cross = send(cross, flip)
-        ghosts = (near, two, far)
+        ghosts = (near, one, two)
         field, *results = make_planes(
             outer_kernel, 2, (*ghosts, cross, *columns), (new,), () if last else messages
         )

time: 28.7 us -> 31 us (1.080)
  the two profiles are of different devices: /device:TPU:7 before, /device:TPU:2 now
where the time goes in v18:
time: 31 us; the launch traced here: 30.9 us
  starting transfers between devices  13.9 us (45%)
  Pallas kernels  10.7 us (35%)
  waiting for transfers between devices  6.04 us (19%)
    ppermute x17, starting transfers between devices, send(): lax.ppermute(values, axes, [(flat(*here), flat(*target(*here))) for here...  13.9 us
    ppermute x17, waiting for transfers between devices, send(): lax.ppermute(values, axes, [(flat(*here), flat(*target(*here))) for here...  6.04 us
    pallas_call x4, Pallas kernels, make_planes(): pl.pallas_call(run, out_shape=(tile_shape(27, extent_x), *extra), in_spec...  5.26 us
    pallas_call x2, Pallas kernels, body(): pl.pallas_call(lambda *refs: velocity_kernel(step, *refs), out_shape=(*(j...  3.34 us
    pallas_call x1, Pallas kernels, body(): pl.pallas_call(pack_kernel, out_shape=(tile_shape(27, extent_x), *message...  1.9 us
  transfers between devices with their start and end apart: 17, of which 6 were waited for; matrix products, arithmetic and copies ran while one was open for 0% of the time, Pallas kernels for 23%

profile of v18, /device:TPU:2, one launch (start us, length us, event | category | flops | bytes accessed | tf_op | source)
XLA Modules:
  0.0 30.9 jit_solution(9501849090476106548)
XLA Ops:
  0.0 1.9 %shard_map.64 = (f32[27,8,16,128]{3,2,1,0:T(8,128)S(1)}, f32[9,16,128]{2,1,0:T(8,128)S(1)}, f32[10,16,128]{2,1,0:T(8,128)S(1)}, f32[10,16,128]{2,1,0:T(8,128)S(1)}) custom-call(f32[27,8,16,128]{3,2,1,0:T(8,128)} %bitcast.14), custom_call_target="tpu_custom_call" | custom-call | tf_op jit(solution)/shard_map/pallas_call | solution.py:425
  1.9 0.1 collective-permute-start
  2.0 3.1 %collective-permute-start.1 = (f32[10,16,128]{2,1,0:T(8,128)S(1)}, f32[10,16,128]{2,1,0:T(8,128)S(1)}, u32[]{:S(2)}, u32[]{:S(2)}) collective-permute-start(f32[10,16,128]{2,1,0:T(8,128)S(1)} %get-tuple-element.29), channel_id=1, source_target_pairs={{0,1},{1,0},{2,3},{3,2},{4,5},{5,4},{6,7},{7,6},{8,9},{9,8},{10,11... | collective-permute-start | bytes 245768 | tf_op jit(solution)/shard_map/ppermute | solution.py:382
  5.1 0.5 %collective-permute-start.7 = (f32[9,16,128]{2,1,0:T(8,128)S(1)}, f32[9,16,128]{2,1,0:T(8,128)S(1)}, u32[]{:S(2)}, u32[]{:S(2)}) collective-permute-start(f32[9,16,128]{2,1,0:T(8,128)S(1)} %get-tuple-element.32.refs_0_), channel_id=1, source_target_pairs={{0,16},{1,17},{2,18},{3,19},{4,20},{5,21},{6,22},{7,23},{8,24},{9,... | collective-permute-start | bytes 221192 | tf_op jit(solution)/shard_map/ppermute | solution.py:382
  5.7 0.1 collective-permute-start.2
  5.8 1.7 %shard_map.65 = (s32[1,8,16,128]{3,2,1,0:T(8,128)S(1)}, f32[3,8,16,128]{3,2,1,0:T(8,128)S(1)}) custom-call(f32[2,1,27,8,16,128]{5,4,3,2,1,0:T(8,128)} %refs_0_.3, s32[1,8,16,128]{3,2,1,0:T(8,128)} %refs_1_.1), custom_call_target="tpu_custom_call" | custom-call | tf_op jit(solution)/shard_map/pallas_call | solution.py:442
  7.6 0.1 shard_map.67
  7.6 0.5 %collective-permute-start.3 = (f32[10,16,128]{2,1,0:T(8,128)S(1)}, f32[10,16,128]{2,1,0:T(8,128)S(1)}, u32[]{:S(2)}, u32[]{:S(2)}) collective-permute-start(f32[10,16,128]{2,1,0:T(8,128)S(1)} %get-tuple-element.30), channel_id=1, source_target_pairs={{0,4},{1,5},{2,6},{3,7},{4,0},{5,1},{6,2},{7,3},{8,24},{9,25},{10,... | collective-permute-start | bytes 245768 | tf_op jit(solution)/shard_map/ppermute | solution.py:382
  8.2 0.2 collective-permute-start.4
  8.4 4.6 %collective-permute-start.5 = (f32[10,16,128]{2,1,0:T(8,128)S(1)}, f32[10,16,128]{2,1,0:T(8,128)S(1)}, u32[]{:S(2)}, u32[]{:S(2)}) collective-permute-start(f32[10,16,128]{2,1,0:T(8,128)S(1)} %get-tuple-element.31), channel_id=1, source_target_pairs={{0,16},{1,17},{2,18},{3,19},{4,8},{5,9},{6,10},{7,11},{8,4},{9,5},... | collective-permute-start | bytes 245768 | tf_op jit(solution)/shard_map/ppermute | solution.py:382
  12.9 1.8 %shard_map.68 = (f32[27,8,16,128]{3,2,1,0:T(8,128)S(1)}, f32[16,128]{1,0:T(8,128)S(1)}, f32[16,128]{1,0:T(8,128)S(1)}) custom-call(f32[27,8,16,128]{3,2,1,0:T(8,128)S(1)} %get-tuple-element.25.adj, f32[3,8,16,128]{3,2,1,0:T(8,128)S(1)} %get-tuple-element.26.rest_0_.vel, s32[1,8,16,128]{3,2,1,0:T(8,128)S(1)} %get-tuple-element.27.solid, ...), custom_call_target="tpu_custom_call" | custom-call | tf_op jit(solution)/shard_map/pallas_call | solution.py:475
  14.9 1.3 %collective-permute-done.8.refs_5_ = f32[9,16,128]{2,1,0:T(8,128)S(1)} collective-permute-done((f32[9,16,128]{2,1,0:T(8,128)S(1)}, f32[9,16,128]{2,1,0:T(8,128)S(1)}, u32[]{:S(2)}, u32[]{:S(2)}) %collective-permute-start.8) | collective-permute-done | bytes 73760 | tf_op jit(solution)/shard_map/ppermute | solution.py:382
  16.2 0.9 %collective-permute-done.5.refs_4_ = f32[10,16,128]{2,1,0:T(8,128)S(1)} collective-permute-done((f32[10,16,128]{2,1,0:T(8,128)S(1)}, f32[10,16,128]{2,1,0:T(8,128)S(1)}, u32[]{:S(2)}, u32[]{:S(2)}) %collective-permute-start.5) | collective-permute-done | bytes 81952 | tf_op jit(solution)/shard_map/ppermute | solution.py:382
  17.1 0.7 %shard_map.70 = (f32[27,8,16,128]{3,2,1,0:T(8,128)S(1)}, f32[9,16,128]{2,1,0:T(8,128)S(1)}, f32[10,16,128]{2,1,0:T(8,128)S(1)}, f32[10,16,128]{2,1,0:T(8,128)S(1)}) custom-call(f32[27,8,16,128]{3,2,1,0:T(8,128)S(1)} %get-tuple-element.25.adj, f32[3,8,16,128]{3,2,1,0:T(8,128)S(1)} %get-tuple-element.26.rest_0_.vel, ...), custom_call_target="tpu_custom_call", output_to_operand_aliasing={{0}: (11, {})} | custom-call | tf_op jit(solution)/shard_map/pallas_call | solution.py:475
  17.8 1.6 %collective-permute-start.9 = (f32[10,16,128]{2,1,0:T(8,128)S(1)}, f32[10,16,128]{2,1,0:T(8,128)S(1)}, u32[]{:S(2)}, u32[]{:S(2)}) collective-permute-start(f32[10,16,128]{2,1,0:T(8,128)S(1)} %get-tuple-element.37), channel_id=1, source_target_pairs={{0,1},{1,0},{2,3},{3,2},{4,5},{5,4},{6,7},{7,6},{8,9},{9,8},{10,11... | collective-permute-start | bytes 245768 | tf_op jit(solution)/shard_map/ppermute | solution.py:382
  19.4 0.5 %collective-permute-start.15 = (f32[9,16,128]{2,1,0:T(8,128)S(1)}, f32[9,16,128]{2,1,0:T(8,128)S(1)}, u32[]{:S(2)}, u32[]{:S(2)}) collective-permute-start(f32[9,16,128]{2,1,0:T(8,128)S(1)} %get-tuple-element.41.refs_0_), channel_id=1, source_target_pairs={{0,16},{1,17},{2,18},{3,19},{4,20},{5,21},{6,22},{7,23},{8,24},{9,... | collective-permute-start | bytes 221192 | tf_op jit(solution)/shard_map/ppermute | solution.py:382
  19.9 1.6 %shard_map.71.rest_0_.vel = f32[3,8,16,128]{3,2,1,0:T(8,128)S(1)} custom-call(f32[2,1,27,8,16,128]{5,4,3,2,1,0:T(8,128)} %refs_0_.3), custom_call_target="tpu_custom_call" | custom-call | tf_op jit(solution)/shard_map/pallas_call | solution.py:442
  21.6 1.1 %collective-permute-done.9.second.refs_0_.refs_2_ = f32[10,16,128]{2,1,0:T(8,128)S(1)} collective-permute-done((f32[10,16,128]{2,1,0:T(8,128)S(1)}, f32[10,16,128]{2,1,0:T(8,128)S(1)}, u32[]{:S(2)}, u32[]{:S(2)}) %collective-permute-start.9) | collective-permute-done | bytes 81952 | tf_op jit(solution)/shard_map/ppermute | solution.py:382
  22.7 0.1 shard_map.72
  22.9 2.4 %collective-permute-start.13 = (f32[10,16,128]{2,1,0:T(8,128)S(1)}, f32[10,16,128]{2,1,0:T(8,128)S(1)}, u32[]{:S(2)}, u32[]{:S(2)}) collective-permute-start(f32[10,16,128]{2,1,0:T(8,128)S(1)} %get-tuple-element.40), channel_id=1, source_target_pairs={{0,16},{1,17},{2,18},{3,19},{4,8},{5,9},{6,10},{7,11},{8,4},{9,5},... | collective-permute-start | bytes 245768 | tf_op jit(solution)/shard_map/ppermute | solution.py:382
  25.3 1.7 %shard_map.73 = (f32[27,8,16,128]{3,2,1,0:T(8,128)}, f32[16,128]{1,0:T(8,128)S(1)}, f32[16,128]{1,0:T(8,128)S(1)}) custom-call(f32[27,8,16,128]{3,2,1,0:T(8,128)S(1)} %get-tuple-element.36.adj, f32[3,8,16,128]{3,2,1,0:T(8,128)S(1)} %shard_map.71.rest_0_.vel, s32[1,8,16,128]{3,2,1,0:T(8,128)S(1)} %get-tuple-element.27.solid, ...), custom_call_target="tpu_custom_call" | custom-call | tf_op jit(solution)/shard_map/pallas_call | solution.py:475
  27.2 1.3 %collective-permute-done.16.refs_5_ = f32[9,16,128]{2,1,0:T(8,128)S(1)} collective-permute-done((f32[9,16,128]{2,1,0:T(8,128)S(1)}, f32[9,16,128]{2,1,0:T(8,128)S(1)}, u32[]{:S(2)}, u32[]{:S(2)}) %collective-permute-start.16) | collective-permute-done | bytes 73760 | tf_op jit(solution)/shard_map/ppermute | solution.py:382
  28.4 1.4 %collective-permute-done.13.refs_4_ = f32[10,16,128]{2,1,0:T(8,128)S(1)} collective-permute-done((f32[10,16,128]{2,1,0:T(8,128)S(1)}, f32[10,16,128]{2,1,0:T(8,128)S(1)}, u32[]{:S(2)}, u32[]{:S(2)}) %collective-permute-start.13) | collective-permute-done | bytes 81952 | tf_op jit(solution)/shard_map/ppermute | solution.py:382
  29.8 1.0 %shard_map.75 = f32[27,8,16,128]{3,2,1,0:T(8,128)} custom-call(f32[27,8,16,128]{3,2,1,0:T(8,128)S(1)} %get-tuple-element.36.adj, f32[3,8,16,128]{3,2,1,0:T(8,128)S(1)} %shard_map.71.rest_0_.vel, s32[1,8,16,128]{3,2,1,0:T(8,128)S(1)} %get-tuple-element.27.solid, ...), custom_call_target="tpu_custom_call", output_to_operand_aliasing={{}: (11, {})} | custom-call | tf_op jit(solution)/shard_map/pallas_call | solution.py:475
  (28 shorter events, 0.5 us)
Async XLA Ops:
  0.0 5.7 %copy-start = (s32[1,16,128,2]{2,3,1,0:T(2,128)S(1)}, s32[1,16,128,2]{2,3,1,0:T(2,128)}, u32[]{:S(2)}) copy-start(s32[1,16,128,2]{2,3,1,0:T(2,128)} %param.9) | copy-start | bytes 49156
  0.0 5.7 %copy-start.1 = (s32[1,16,128,2]{2,3,1,0:T(2,128)S(1)}, s32[1,16,128,2]{2,3,1,0:T(2,128)}, u32[]{:S(2)}) copy-start(s32[1,16,128,2]{2,3,1,0:T(2,128)} %param.10) | copy-start | bytes 49156
  0.0 5.7 %copy-start.2 = (f32[1,16,128,2]{2,3,1,0:T(2,128)S(1)}, f32[1,16,128,2]{2,3,1,0:T(2,128)}, u32[]{:S(2)}) copy-start(f32[1,16,128,2]{2,3,1,0:T(2,128)} %param.11) | copy-start | bytes 49156
  1.9 5.6 %collective-permute-start = (f32[10,16,128]{2,1,0:T(8,128)S(1)}, f32[10,16,128]{2,1,0:T(8,128)S(1)}, u32[]{:S(2)}, u32[]{:S(2)}) collective-permute-start(f32[10,16,128]{2,1,0:T(8,128)S(1)} %get-tuple-element.28), channel_id=1, source_target_pairs={{0,16},{1,2},{2,1},{3,19},{4,20},{5,6},{6,5},{7,23},{8,24},{9,10},... | collective-permute-start | bytes 245768 | tf_op jit(solution)/shard_map/ppermute | solution.py:382
  2.0 5.6 %collective-permute-start.1 = (f32[10,16,128]{2,1,0:T(8,128)S(1)}, f32[10,16,128]{2,1,0:T(8,128)S(1)}, u32[]{:S(2)}, u32[]{:S(2)}) collective-permute-start(f32[10,16,128]{2,1,0:T(8,128)S(1)} %get-tuple-element.29), channel_id=1, source_target_pairs={{0,1},{1,0},{2,3},{3,2},{4,5},{5,4},{6,7},{7,6},{8,9},{9,8},{10,11... | collective-permute-start | bytes 245768 | tf_op jit(solution)/shard_map/ppermute | solution.py:382
  5.1 9.6 %collective-permute-start.6 = (f32[9,16,128]{2,1,0:T(8,128)S(1)}, f32[9,16,128]{2,1,0:T(8,128)S(1)}, u32[]{:S(2)}, u32[]{:S(2)}) collective-permute-start(f32[9,16,128]{2,1,0:T(8,128)S(1)} %get-tuple-element.32.refs_0_), channel_id=1, source_target_pairs={{0,16},{1,17},{2,18},{3,19},{4,20},{5,21},{6,22},{7,23},{8,24},{9,... | collective-permute-start | bytes 221192 | tf_op jit(solution)/shard_map/ppermute | solution.py:382
  5.1 9.7 %collective-permute-start.7 = (f32[9,16,128]{2,1,0:T(8,128)S(1)}, f32[9,16,128]{2,1,0:T(8,128)S(1)}, u32[]{:S(2)}, u32[]{:S(2)}) collective-permute-start(f32[9,16,128]{2,1,0:T(8,128)S(1)} %get-tuple-element.32.refs_0_), channel_id=1, source_target_pairs={{0,16},{1,17},{2,18},{3,19},{4,20},{5,21},{6,22},{7,23},{8,24},{9,... | collective-permute-start | bytes 221192 | tf_op jit(solution)/shard_map/ppermute | solution.py:382
  5.7 1.8 %collective-permute-start.2 = (f32[4,16,128]{2,1,0:T(8,128)S(1)}, f32[4,16,128]{2,1,0:T(8,128)S(1)}, u32[]{:S(2)}, u32[]{:S(2)}) collective-permute-start(f32[4,16,128]{2,1,0:T(8,128)S(1)} %shard_map.66), channel_id=1, source_target_pairs={{0,16},{1,17},{2,18},{3,19},{4,20},{5,21},{6,22},{7,23},{8,24},{9,... | collective-permute-start | bytes 98312 | tf_op jit(solution)/shard_map/ppermute | solution.py:382
  7.6 8.5 %collective-permute-start.3 = (f32[10,16,128]{2,1,0:T(8,128)S(1)}, f32[10,16,128]{2,1,0:T(8,128)S(1)}, u32[]{:S(2)}, u32[]{:S(2)}) collective-permute-start(f32[10,16,128]{2,1,0:T(8,128)S(1)} %get-tuple-element.30), channel_id=1, source_target_pairs={{0,4},{1,5},{2,6},{3,7},{4,0},{5,1},{6,2},{7,3},{8,24},{9,25},{10,... | collective-permute-start | bytes 245768 | tf_op jit(solution)/shard_map/ppermute | solution.py:382
  8.2 8.0 %collective-permute-start.4 = (f32[10,16,128]{2,1,0:T(8,128)S(1)}, f32[10,16,128]{2,1,0:T(8,128)S(1)}, u32[]{:S(2)}, u32[]{:S(2)}) collective-permute-start(f32[10,16,128]{2,1,0:T(8,128)S(1)} %get-tuple-element.30), channel_id=1, source_target_pairs={{0,16},{1,17},{2,18},{3,19},{4,20},{5,21},{6,22},{7,23},{8,12},{9,... | collective-permute-start | bytes 245768 | tf_op jit(solution)/shard_map/ppermute | solution.py:382
  8.4 8.7 %collective-permute-start.5 = (f32[10,16,128]{2,1,0:T(8,128)S(1)}, f32[10,16,128]{2,1,0:T(8,128)S(1)}, u32[]{:S(2)}, u32[]{:S(2)}) collective-permute-start(f32[10,16,128]{2,1,0:T(8,128)S(1)} %get-tuple-element.31), channel_id=1, source_target_pairs={{0,16},{1,17},{2,18},{3,19},{4,8},{5,9},{6,10},{7,11},{8,4},{9,5},... | collective-permute-start | bytes 245768 | tf_op jit(solution)/shard_map/ppermute | solution.py:382
  14.8 1.3 %collective-permute-start.8 = (f32[9,16,128]{2,1,0:T(8,128)S(1)}, f32[9,16,128]{2,1,0:T(8,128)S(1)}, u32[]{:S(2)}, u32[]{:S(2)}) collective-permute-start(f32[9,16,128]{2,1,0:T(8,128)S(1)} %shard_map.69), channel_id=1, source_target_pairs={{0,16},{1,17},{2,18},{3,19},{4,20},{5,21},{6,22},{7,23},{8,24},{9,... | collective-permute-start | bytes 221192 | tf_op jit(solution)/shard_map/ppermute | solution.py:382
  17.8 3.8 %collective-permute-start.10 = (f32[10,16,128]{2,1,0:T(8,128)S(1)}, f32[10,16,128]{2,1,0:T(8,128)S(1)}, u32[]{:S(2)}, u32[]{:S(2)}) collective-permute-start(f32[10,16,128]{2,1,0:T(8,128)S(1)} %get-tuple-element.38), channel_id=1, source_target_pairs={{0,16},{1,2},{2,1},{3,19},{4,20},{5,6},{6,5},{7,23},{8,24},{9,10},... | collective-permute-start | bytes 245768 | tf_op jit(solution)/shard_map/ppermute | solution.py:382
  17.8 4.9 %collective-permute-start.9 = (f32[10,16,128]{2,1,0:T(8,128)S(1)}, f32[10,16,128]{2,1,0:T(8,128)S(1)}, u32[]{:S(2)}, u32[]{:S(2)}) collective-permute-start(f32[10,16,128]{2,1,0:T(8,128)S(1)} %get-tuple-element.37), channel_id=1, source_target_pairs={{0,1},{1,0},{2,3},{3,2},{4,5},{5,4},{6,7},{7,6},{8,9},{9,8},{10,11... | collective-permute-start | bytes 245768 | tf_op jit(solution)/shard_map/ppermute | solution.py:382
  19.4 7.7 %collective-permute-start.14 = (f32[9,16,128]{2,1,0:T(8,128)S(1)}, f32[9,16,128]{2,1,0:T(8,128)S(1)}, u32[]{:S(2)}, u32[]{:S(2)}) collective-permute-start(f32[9,16,128]{2,1,0:T(8,128)S(1)} %get-tuple-element.41.refs_0_), channel_id=1, source_target_pairs={{0,16},{1,17},{2,18},{3,19},{4,20},{5,21},{6,22},{7,23},{8,24},{9,... | collective-permute-start | bytes 221192 | tf_op jit(solution)/shard_map/ppermute | solution.py:382
  19.4 7.7 %collective-permute-start.15 = (f32[9,16,128]{2,1,0:T(8,128)S(1)}, f32[9,16,128]{2,1,0:T(8,128)S(1)}, u32[]{:S(2)}, u32[]{:S(2)}) collective-permute-start(f32[9,16,128]{2,1,0:T(8,128)S(1)} %get-tuple-element.41.refs_0_), channel_id=1, source_target_pairs={{0,16},{1,17},{2,18},{3,19},{4,20},{5,21},{6,22},{7,23},{8,24},{9,... | collective-permute-start | bytes 221192 | tf_op jit(solution)/shard_map/ppermute | solution.py:382
  22.8 5.6 %collective-permute-start.11 = (f32[10,16,128]{2,1,0:T(8,128)S(1)}, f32[10,16,128]{2,1,0:T(8,128)S(1)}, u32[]{:S(2)}, u32[]{:S(2)}) collective-permute-start(f32[10,16,128]{2,1,0:T(8,128)S(1)} %get-tuple-element.39), channel_id=1, source_target_pairs={{0,4},{1,5},{2,6},{3,7},{4,0},{5,1},{6,2},{7,3},{8,24},{9,25},{10,... | collective-permute-start | bytes 245768 | tf_op jit(solution)/shard_map/ppermute | solution.py:382
  22.8 5.6 %collective-permute-start.12 = (f32[10,16,128]{2,1,0:T(8,128)S(1)}, f32[10,16,128]{2,1,0:T(8,128)S(1)}, u32[]{:S(2)}, u32[]{:S(2)}) collective-permute-start(f32[10,16,128]{2,1,0:T(8,128)S(1)} %get-tuple-element.39), channel_id=1, source_target_pairs={{0,16},{1,17},{2,18},{3,19},{4,20},{5,21},{6,22},{7,23},{8,12},{9,... | collective-permute-start | bytes 245768 | tf_op jit(solution)/shard_map/ppermute | solution.py:382
  22.9 6.9 %collective-permute-start.13 = (f32[10,16,128]{2,1,0:T(8,128)S(1)}, f32[10,16,128]{2,1,0:T(8,128)S(1)}, u32[]{:S(2)}, u32[]{:S(2)}) collective-permute-start(f32[10,16,128]{2,1,0:T(8,128)S(1)} %get-tuple-element.40), channel_id=1, source_target_pairs={{0,16},{1,17},{2,18},{3,19},{4,8},{5,9},{6,10},{7,11},{8,4},{9,5},... | collective-permute-start | bytes 245768 | tf_op jit(solution)/shard_map/ppermute | solution.py:382
  27.1 1.3 %collective-permute-start.16 = (f32[9,16,128]{2,1,0:T(8,128)S(1)}, f32[9,16,128]{2,1,0:T(8,128)S(1)}, u32[]{:S(2)}, u32[]{:S(2)}) collective-permute-start(f32[9,16,128]{2,1,0:T(8,128)S(1)} %shard_map.74), channel_id=1, source_target_pairs={{0,16},{1,17},{2,18},{3,19},{4,20},{5,21},{6,22},{7,23},{8,24},{9,... | collective-permute-start | bytes 221192 | tf_op jit(solution)/shard_map/ppermute | solution.py:382

commit v19 on v17

--- a/solution.py
+++ b/solution.py
@@ -304,7 +304,7 @@
     lax.fori_loop(1, extent_x - 1, lambda x, c: (save(x).wait(), c)[1], 0)
 
 
-def outer_kernel(step, adj, vel, solid, first, second, near, two, far, cross, *rest):
+def outer_kernel(last, step, adj, vel, solid, first, second, near, two, far, cross, *rest):
     *rest, made, pulled, sems = rest
     low_in, high_in, _, out, *messages = rest
     extent_x = adj.shape[1]
@@ -312,6 +312,7 @@
     even = is_even("gx")
     interface = lax.axis_index("gx") == lax.axis_size("gx") - 1
 
+    two, far = (far, two) if last else (two, far)
     bottom = lax.axis_index("gx") == 0
     inside = lax.axis_index("gx") < lax.axis_size("gx") - 2
 
@@ -496,9 +497,9 @@
             compiler_params=params,
         )(own, first, second, *others, info, columns[0])
         cross = send(cross, flip)
-        ghosts = (near, two, far)
+        ghosts = (near, far, two) if last else (near, two, far)
         field, *results = make_planes(
-            outer_kernel, 2, (*ghosts, cross, *columns), (new,), () if last else messages
+            lambda *refs: outer_kernel(last, *refs), 2, (*ghosts, cross, *columns), (new,), () if last else messages
         )
         if not last:
             own, first, second = results

time: 28.7 us -> 30.6 us (1.066)
  the two profiles are of different devices: /device:TPU:7 before, /device:TPU:2 now
where the time goes in v19:
time: 30.6 us; the launch traced here: 30.4 us
  starting transfers between devices  15 us (49%)
  Pallas kernels  10.7 us (35%)
  waiting for transfers between devices  4.51 us (15%)
    ppermute x17, starting transfers between devices, send(): lax.ppermute(values, axes, [(flat(*here), flat(*target(*here))) for here...  15 us
    pallas_call x4, Pallas kernels, make_planes(): pl.pallas_call(run, out_shape=(tile_shape(27, extent_x), *extra), in_spec...  5.27 us
    ppermute x17, waiting for transfers between devices, send(): lax.ppermute(values, axes, [(flat(*here), flat(*target(*here))) for here...  4.51 us
    pallas_call x2, Pallas kernels, body(): pl.pallas_call(lambda *refs: velocity_kernel(step, *refs), out_shape=(*(j...  3.34 us
    pallas_call x1, Pallas kernels, body(): pl.pallas_call(pack_kernel, out_shape=(tile_shape(27, extent_x), *message...  1.9 us
  transfers between devices with their start and end apart: 17, of which 6 were waited for; matrix products, arithmetic and copies ran while one was open for 0% of the time, Pallas kernels for 24%

profile of v19, /device:TPU:2, one launch (start us, length us, event | category | flops | bytes accessed | tf_op | source)
XLA Modules:
  0.0 30.4 jit_solution(4385466407794316170)
XLA Ops:
  0.0 1.9 %shard_map.64 = (f32[27,8,16,128]{3,2,1,0:T(8,128)S(1)}, f32[9,16,128]{2,1,0:T(8,128)S(1)}, f32[10,16,128]{2,1,0:T(8,128)S(1)}, f32[10,16,128]{2,1,0:T(8,128)S(1)}) custom-call(f32[27,8,16,128]{3,2,1,0:T(8,128)} %bitcast.14), custom_call_target="tpu_custom_call" | custom-call | tf_op jit(solution)/shard_map/pallas_call | solution.py:426
  1.9 0.1 collective-permute-start
  2.0 3.1 %collective-permute-start.1 = (f32[10,16,128]{2,1,0:T(8,128)S(1)}, f32[10,16,128]{2,1,0:T(8,128)S(1)}, u32[]{:S(2)}, u32[]{:S(2)}) collective-permute-start(f32[10,16,128]{2,1,0:T(8,128)S(1)} %get-tuple-element.31), channel_id=1, source_target_pairs={{0,1},{1,0},{2,3},{3,2},{4,5},{5,4},{6,7},{7,6},{8,9},{9,8},{10,11... | collective-permute-start | bytes 245768 | tf_op jit(solution)/shard_map/ppermute | solution.py:383
  5.1 0.5 %collective-permute-start.7 = (f32[9,16,128]{2,1,0:T(8,128)S(1)}, f32[9,16,128]{2,1,0:T(8,128)S(1)}, u32[]{:S(2)}, u32[]{:S(2)}) collective-permute-start(f32[9,16,128]{2,1,0:T(8,128)S(1)} %get-tuple-element.35.refs_0_), channel_id=1, source_target_pairs={{0,16},{1,17},{2,18},{3,19},{4,20},{5,21},{6,22},{7,23},{8,24},{9,... | collective-permute-start | bytes 221192 | tf_op jit(solution)/shard_map/ppermute | solution.py:383
  5.7 0.1 collective-permute-start.2
  5.8 1.7 %shard_map.65 = (s32[1,8,16,128]{3,2,1,0:T(8,128)S(1)}, f32[3,8,16,128]{3,2,1,0:T(8,128)S(1)}) custom-call(f32[2,1,27,8,16,128]{5,4,3,2,1,0:T(8,128)} %refs_0_.3, s32[1,8,16,128]{3,2,1,0:T(8,128)} %refs_1_.1), custom_call_target="tpu_custom_call" | custom-call | tf_op jit(solution)/shard_map/pallas_call | solution.py:443
  7.6 0.1 shard_map.67
  7.6 0.6 %collective-permute-start.3 = (f32[10,16,128]{2,1,0:T(8,128)S(1)}, f32[10,16,128]{2,1,0:T(8,128)S(1)}, u32[]{:S(2)}, u32[]{:S(2)}) collective-permute-start(f32[10,16,128]{2,1,0:T(8,128)S(1)} %get-tuple-element.32), channel_id=1, source_target_pairs={{0,4},{1,5},{2,6},{3,7},{4,0},{5,1},{6,2},{7,3},{8,24},{9,25},{10,... | collective-permute-start | bytes 245768 | tf_op jit(solution)/shard_map/ppermute | solution.py:383
  8.2 1.4 %collective-permute-start.4 = (f32[10,16,128]{2,1,0:T(8,128)S(1)}, f32[10,16,128]{2,1,0:T(8,128)S(1)}, u32[]{:S(2)}, u32[]{:S(2)}) collective-permute-start(f32[10,16,128]{2,1,0:T(8,128)S(1)} %get-tuple-element.33), channel_id=1, source_target_pairs={{0,16},{1,17},{2,18},{3,19},{4,8},{5,9},{6,10},{7,11},{8,4},{9,5},... | collective-permute-start | bytes 245768 | tf_op jit(solution)/shard_map/ppermute | solution.py:383
  9.6 1.8 %shard_map.68 = (f32[27,8,16,128]{3,2,1,0:T(8,128)S(1)}, f32[16,128]{1,0:T(8,128)S(1)}, f32[16,128]{1,0:T(8,128)S(1)}) custom-call(f32[27,8,16,128]{3,2,1,0:T(8,128)S(1)} %get-tuple-element.27.adj, f32[3,8,16,128]{3,2,1,0:T(8,128)S(1)} %get-tuple-element.28.rest_0_.vel, s32[1,8,16,128]{3,2,1,0:T(8,128)S(1)} %get-tuple-element.29.solid, ...), custom_call_target="tpu_custom_call" | custom-call | tf_op jit(solution)/shard_map/pallas_call | solution.py:476
  11.5 0.6 %collective-permute-start.8 = (f32[9,16,128]{2,1,0:T(8,128)S(1)}, f32[9,16,128]{2,1,0:T(8,128)S(1)}, u32[]{:S(2)}, u32[]{:S(2)}) collective-permute-start(f32[9,16,128]{2,1,0:T(8,128)S(1)} %shard_map.69), channel_id=1, source_target_pairs={{0,16},{1,17},{2,18},{3,19},{4,20},{5,21},{6,22},{7,23},{8,24},{9,... | collective-permute-start | bytes 221192 | tf_op jit(solution)/shard_map/ppermute | solution.py:383
  12.1 0.9 %collective-permute-done.8.refs_5_ = f32[9,16,128]{2,1,0:T(8,128)S(1)} collective-permute-done((f32[9,16,128]{2,1,0:T(8,128)S(1)}, f32[9,16,128]{2,1,0:T(8,128)S(1)}, u32[]{:S(2)}, u32[]{:S(2)}) %collective-permute-start.8) | collective-permute-done | bytes 73760 | tf_op jit(solution)/shard_map/ppermute | solution.py:383
  13.0 0.6 %collective-permute-done.4.refs_3_ = f32[10,16,128]{2,1,0:T(8,128)S(1)} collective-permute-done((f32[10,16,128]{2,1,0:T(8,128)S(1)}, f32[10,16,128]{2,1,0:T(8,128)S(1)}, u32[]{:S(2)}, u32[]{:S(2)}) %collective-permute-start.4) | collective-permute-done | bytes 81952 | tf_op jit(solution)/shard_map/ppermute | solution.py:383
  13.6 0.7 %shard_map.70 = (f32[27,8,16,128]{3,2,1,0:T(8,128)S(1)}, f32[9,16,128]{2,1,0:T(8,128)S(1)}, f32[10,16,128]{2,1,0:T(8,128)S(1)}, f32[10,16,128]{2,1,0:T(8,128)S(1)}) custom-call(f32[27,8,16,128]{3,2,1,0:T(8,128)S(1)} %get-tuple-element.27.adj, f32[3,8,16,128]{3,2,1,0:T(8,128)S(1)} %get-tuple-element.28.rest_0_.vel, ...), custom_call_target="tpu_custom_call", output_to_operand_aliasing={{0}: (11, {})} | custom-call | tf_op jit(solution)/shard_map/pallas_call | solution.py:476
  14.4 3.2 %collective-permute-start.9 = (f32[10,16,128]{2,1,0:T(8,128)S(1)}, f32[10,16,128]{2,1,0:T(8,128)S(1)}, u32[]{:S(2)}, u32[]{:S(2)}) collective-permute-start(f32[10,16,128]{2,1,0:T(8,128)S(1)} %get-tuple-element.40), channel_id=1, source_target_pairs={{0,1},{1,0},{2,3},{3,2},{4,5},{5,4},{6,7},{7,6},{8,9},{9,8},{10,11... | collective-permute-start | bytes 245768 | tf_op jit(solution)/shard_map/ppermute | solution.py:383
  17.5 0.5 %collective-permute-start.15 = (f32[9,16,128]{2,1,0:T(8,128)S(1)}, f32[9,16,128]{2,1,0:T(8,128)S(1)}, u32[]{:S(2)}, u32[]{:S(2)}) collective-permute-start(f32[9,16,128]{2,1,0:T(8,128)S(1)} %get-tuple-element.45.refs_0_), channel_id=1, source_target_pairs={{0,16},{1,17},{2,18},{3,19},{4,20},{5,21},{6,22},{7,23},{8,24},{9,... | collective-permute-start | bytes 221192 | tf_op jit(solution)/shard_map/ppermute | solution.py:383
  18.0 1.6 %shard_map.71.rest_0_.vel = f32[3,8,16,128]{3,2,1,0:T(8,128)S(1)} custom-call(f32[2,1,27,8,16,128]{5,4,3,2,1,0:T(8,128)} %refs_0_.3), custom_call_target="tpu_custom_call" | custom-call | tf_op jit(solution)/shard_map/pallas_call | solution.py:443
  19.7 0.2 collective-permute-done.9.second.refs_0_.refs_2_
  19.9 0.1 shard_map.72
  20.1 4.7 %collective-permute-start.13 = (f32[10,16,128]{2,1,0:T(8,128)S(1)}, f32[10,16,128]{2,1,0:T(8,128)S(1)}, u32[]{:S(2)}, u32[]{:S(2)}) collective-permute-start(f32[10,16,128]{2,1,0:T(8,128)S(1)} %get-tuple-element.44), channel_id=1, source_target_pairs={{0,16},{1,17},{2,18},{3,19},{4,8},{5,9},{6,10},{7,11},{8,4},{9,5},... | collective-permute-start | bytes 245768 | tf_op jit(solution)/shard_map/ppermute | solution.py:383
  24.9 1.7 %shard_map.73 = (f32[27,8,16,128]{3,2,1,0:T(8,128)}, f32[16,128]{1,0:T(8,128)S(1)}, f32[16,128]{1,0:T(8,128)S(1)}) custom-call(f32[27,8,16,128]{3,2,1,0:T(8,128)S(1)} %get-tuple-element.39.adj, f32[3,8,16,128]{3,2,1,0:T(8,128)S(1)} %shard_map.71.rest_0_.vel, s32[1,8,16,128]{3,2,1,0:T(8,128)S(1)} %get-tuple-element.29.solid, ...), custom_call_target="tpu_custom_call" | custom-call | tf_op jit(solution)/shard_map/pallas_call | solution.py:476
  26.8 1.3 %collective-permute-done.16.refs_5_ = f32[9,16,128]{2,1,0:T(8,128)S(1)} collective-permute-done((f32[9,16,128]{2,1,0:T(8,128)S(1)}, f32[9,16,128]{2,1,0:T(8,128)S(1)}, u32[]{:S(2)}, u32[]{:S(2)}) %collective-permute-start.16) | collective-permute-done | bytes 73760 | tf_op jit(solution)/shard_map/ppermute | solution.py:383
  28.0 1.4 %collective-permute-done.13.refs_4_ = f32[10,16,128]{2,1,0:T(8,128)S(1)} collective-permute-done((f32[10,16,128]{2,1,0:T(8,128)S(1)}, f32[10,16,128]{2,1,0:T(8,128)S(1)}, u32[]{:S(2)}, u32[]{:S(2)}) %collective-permute-start.13) | collective-permute-done | bytes 81952 | tf_op jit(solution)/shard_map/ppermute | solution.py:383
  29.4 1.0 %shard_map.75 = f32[27,8,16,128]{3,2,1,0:T(8,128)} custom-call(f32[27,8,16,128]{3,2,1,0:T(8,128)S(1)} %get-tuple-element.39.adj, f32[3,8,16,128]{3,2,1,0:T(8,128)S(1)} %shard_map.71.rest_0_.vel, s32[1,8,16,128]{3,2,1,0:T(8,128)S(1)} %get-tuple-element.29.solid, ...), custom_call_target="tpu_custom_call", output_to_operand_aliasing={{}: (11, {})} | custom-call | tf_op jit(solution)/shard_map/pallas_call | solution.py:476
  (28 shorter events, 0.4 us)
Async XLA Ops:
  0.0 5.7 %copy-start = (s32[1,16,128,2]{2,3,1,0:T(2,128)S(1)}, s32[1,16,128,2]{2,3,1,0:T(2,128)}, u32[]{:S(2)}) copy-start(s32[1,16,128,2]{2,3,1,0:T(2,128)} %param.9) | copy-start | bytes 49156
  0.0 5.7 %copy-start.1 = (s32[1,16,128,2]{2,3,1,0:T(2,128)S(1)}, s32[1,16,128,2]{2,3,1,0:T(2,128)}, u32[]{:S(2)}) copy-start(s32[1,16,128,2]{2,3,1,0:T(2,128)} %param.10) | copy-start | bytes 49156
  0.0 5.7 %copy-start.2 = (f32[1,16,128,2]{2,3,1,0:T(2,128)S(1)}, f32[1,16,128,2]{2,3,1,0:T(2,128)}, u32[]{:S(2)}) copy-start(f32[1,16,128,2]{2,3,1,0:T(2,128)} %param.11) | copy-start | bytes 49156
  1.9 5.6 %collective-permute-start = (f32[10,16,128]{2,1,0:T(8,128)S(1)}, f32[10,16,128]{2,1,0:T(8,128)S(1)}, u32[]{:S(2)}, u32[]{:S(2)}) collective-permute-start(f32[10,16,128]{2,1,0:T(8,128)S(1)} %get-tuple-element.30), channel_id=1, source_target_pairs={{0,16},{1,2},{2,1},{3,19},{4,20},{5,6},{6,5},{7,23},{8,24},{9,10},... | collective-permute-start | bytes 245768 | tf_op jit(solution)/shard_map/ppermute | solution.py:383
  2.0 5.6 %collective-permute-start.1 = (f32[10,16,128]{2,1,0:T(8,128)S(1)}, f32[10,16,128]{2,1,0:T(8,128)S(1)}, u32[]{:S(2)}, u32[]{:S(2)}) collective-permute-start(f32[10,16,128]{2,1,0:T(8,128)S(1)} %get-tuple-element.31), channel_id=1, source_target_pairs={{0,1},{1,0},{2,3},{3,2},{4,5},{5,4},{6,7},{7,6},{8,9},{9,8},{10,11... | collective-permute-start | bytes 245768 | tf_op jit(solution)/shard_map/ppermute | solution.py:383
  5.1 6.3 %collective-permute-start.6 = (f32[9,16,128]{2,1,0:T(8,128)S(1)}, f32[9,16,128]{2,1,0:T(8,128)S(1)}, u32[]{:S(2)}, u32[]{:S(2)}) collective-permute-start(f32[9,16,128]{2,1,0:T(8,128)S(1)} %get-tuple-element.35.refs_0_), channel_id=1, source_target_pairs={{0,16},{1,17},{2,18},{3,19},{4,20},{5,21},{6,22},{7,23},{8,24},{9,... | collective-permute-start | bytes 221192 | tf_op jit(solution)/shard_map/ppermute | solution.py:383
  5.1 6.3 %collective-permute-start.7 = (f32[9,16,128]{2,1,0:T(8,128)S(1)}, f32[9,16,128]{2,1,0:T(8,128)S(1)}, u32[]{:S(2)}, u32[]{:S(2)}) collective-permute-start(f32[9,16,128]{2,1,0:T(8,128)S(1)} %get-tuple-element.35.refs_0_), channel_id=1, source_target_pairs={{0,16},{1,17},{2,18},{3,19},{4,20},{5,21},{6,22},{7,23},{8,24},{9,... | collective-permute-start | bytes 221192 | tf_op jit(solution)/shard_map/ppermute | solution.py:383
  5.7 1.8 %collective-permute-start.2 = (f32[4,16,128]{2,1,0:T(8,128)S(1)}, f32[4,16,128]{2,1,0:T(8,128)S(1)}, u32[]{:S(2)}, u32[]{:S(2)}) collective-permute-start(f32[4,16,128]{2,1,0:T(8,128)S(1)} %shard_map.66), channel_id=1, source_target_pairs={{0,16},{1,17},{2,18},{3,19},{4,20},{5,21},{6,22},{7,23},{8,24},{9,... | collective-permute-start | bytes 98312 | tf_op jit(solution)/shard_map/ppermute | solution.py:383
  7.6 5.3 %collective-permute-start.3 = (f32[10,16,128]{2,1,0:T(8,128)S(1)}, f32[10,16,128]{2,1,0:T(8,128)S(1)}, u32[]{:S(2)}, u32[]{:S(2)}) collective-permute-start(f32[10,16,128]{2,1,0:T(8,128)S(1)} %get-tuple-element.32), channel_id=1, source_target_pairs={{0,4},{1,5},{2,6},{3,7},{4,0},{5,1},{6,2},{7,3},{8,24},{9,25},{10,... | collective-permute-start | bytes 245768 | tf_op jit(solution)/shard_map/ppermute | solution.py:383
  8.2 5.4 %collective-permute-start.4 = (f32[10,16,128]{2,1,0:T(8,128)S(1)}, f32[10,16,128]{2,1,0:T(8,128)S(1)}, u32[]{:S(2)}, u32[]{:S(2)}) collective-permute-start(f32[10,16,128]{2,1,0:T(8,128)S(1)} %get-tuple-element.33), channel_id=1, source_target_pairs={{0,16},{1,17},{2,18},{3,19},{4,8},{5,9},{6,10},{7,11},{8,4},{9,5},... | collective-permute-start | bytes 245768 | tf_op jit(solution)/shard_map/ppermute | solution.py:383
  9.6 4.0 %collective-permute-start.5 = (f32[10,16,128]{2,1,0:T(8,128)S(1)}, f32[10,16,128]{2,1,0:T(8,128)S(1)}, u32[]{:S(2)}, u32[]{:S(2)}) collective-permute-start(f32[10,16,128]{2,1,0:T(8,128)S(1)} %get-tuple-element.34), channel_id=1, source_target_pairs={{0,16},{1,17},{2,18},{3,19},{4,20},{5,21},{6,22},{7,23},{8,12},{9,... | collective-permute-start | bytes 245768 | tf_op jit(solution)/shard_map/ppermute | solution.py:383
  11.5 1.5 %collective-permute-start.8 = (f32[9,16,128]{2,1,0:T(8,128)S(1)}, f32[9,16,128]{2,1,0:T(8,128)S(1)}, u32[]{:S(2)}, u32[]{:S(2)}) collective-permute-start(f32[9,16,128]{2,1,0:T(8,128)S(1)} %shard_map.69), channel_id=1, source_target_pairs={{0,16},{1,17},{2,18},{3,19},{4,20},{5,21},{6,22},{7,23},{8,24},{9,... | collective-permute-start | bytes 221192 | tf_op jit(solution)/shard_map/ppermute | solution.py:383
  14.3 5.4 %collective-permute-start.10 = (f32[10,16,128]{2,1,0:T(8,128)S(1)}, f32[10,16,128]{2,1,0:T(8,128)S(1)}, u32[]{:S(2)}, u32[]{:S(2)}) collective-permute-start(f32[10,16,128]{2,1,0:T(8,128)S(1)} %get-tuple-element.41), channel_id=1, source_target_pairs={{0,16},{1,2},{2,1},{3,19},{4,20},{5,6},{6,5},{7,23},{8,24},{9,10},... | collective-permute-start | bytes 245768 | tf_op jit(solution)/shard_map/ppermute | solution.py:383
  14.4 5.6 %collective-permute-start.9 = (f32[10,16,128]{2,1,0:T(8,128)S(1)}, f32[10,16,128]{2,1,0:T(8,128)S(1)}, u32[]{:S(2)}, u32[]{:S(2)}) collective-permute-start(f32[10,16,128]{2,1,0:T(8,128)S(1)} %get-tuple-element.40), channel_id=1, source_target_pairs={{0,1},{1,0},{2,3},{3,2},{4,5},{5,4},{6,7},{7,6},{8,9},{9,8},{10,11... | collective-permute-start | bytes 245768 | tf_op jit(solution)/shard_map/ppermute | solution.py:383
  17.5 9.1 %collective-permute-start.14 = (f32[9,16,128]{2,1,0:T(8,128)S(1)}, f32[9,16,128]{2,1,0:T(8,128)S(1)}, u32[]{:S(2)}, u32[]{:S(2)}) collective-permute-start(f32[9,16,128]{2,1,0:T(8,128)S(1)} %get-tuple-element.45.refs_0_), channel_id=1, source_target_pairs={{0,16},{1,17},{2,18},{3,19},{4,20},{5,21},{6,22},{7,23},{8,24},{9,... | collective-permute-start | bytes 221192 | tf_op jit(solution)/shard_map/ppermute | solution.py:383
  17.5 9.1 %collective-permute-start.15 = (f32[9,16,128]{2,1,0:T(8,128)S(1)}, f32[9,16,128]{2,1,0:T(8,128)S(1)}, u32[]{:S(2)}, u32[]{:S(2)}) collective-permute-start(f32[9,16,128]{2,1,0:T(8,128)S(1)} %get-tuple-element.45.refs_0_), channel_id=1, source_target_pairs={{0,16},{1,17},{2,18},{3,19},{4,20},{5,21},{6,22},{7,23},{8,24},{9,... | collective-permute-start | bytes 221192 | tf_op jit(solution)/shard_map/ppermute | solution.py:383
  20.0 8.0 %collective-permute-start.11 = (f32[10,16,128]{2,1,0:T(8,128)S(1)}, f32[10,16,128]{2,1,0:T(8,128)S(1)}, u32[]{:S(2)}, u32[]{:S(2)}) collective-permute-start(f32[10,16,128]{2,1,0:T(8,128)S(1)} %get-tuple-element.42), channel_id=1, source_target_pairs={{0,4},{1,5},{2,6},{3,7},{4,0},{5,1},{6,2},{7,3},{8,24},{9,25},{10,... | collective-permute-start | bytes 245768 | tf_op jit(solution)/shard_map/ppermute | solution.py:383
  20.1 8.0 %collective-permute-start.12 = (f32[10,16,128]{2,1,0:T(8,128)S(1)}, f32[10,16,128]{2,1,0:T(8,128)S(1)}, u32[]{:S(2)}, u32[]{:S(2)}) collective-permute-start(f32[10,16,128]{2,1,0:T(8,128)S(1)} %get-tuple-element.43), channel_id=1, source_target_pairs={{0,16},{1,17},{2,18},{3,19},{4,20},{5,21},{6,22},{7,23},{8,12},{9,... | collective-permute-start | bytes 245768 | tf_op jit(solution)/shard_map/ppermute | solution.py:383
  20.1 9.3 %collective-permute-start.13 = (f32[10,16,128]{2,1,0:T(8,128)S(1)}, f32[10,16,128]{2,1,0:T(8,128)S(1)}, u32[]{:S(2)}, u32[]{:S(2)}) collective-permute-start(f32[10,16,128]{2,1,0:T(8,128)S(1)} %get-tuple-element.44), channel_id=1, source_target_pairs={{0,16},{1,17},{2,18},{3,19},{4,8},{5,9},{6,10},{7,11},{8,4},{9,5},... | collective-permute-start | bytes 245768 | tf_op jit(solution)/shard_map/ppermute | solution.py:383
  26.7 1.3 %collective-permute-start.16 = (f32[9,16,128]{2,1,0:T(8,128)S(1)}, f32[9,16,128]{2,1,0:T(8,128)S(1)}, u32[]{:S(2)}, u32[]{:S(2)}) collective-permute-start(f32[9,16,128]{2,1,0:T(8,128)S(1)} %shard_map.74), channel_id=1, source_target_pairs={{0,16},{1,17},{2,18},{3,19},{4,20},{5,21},{6,22},{7,23},{8,24},{9,... | collective-permute-start | bytes 221192 | tf_op jit(solution)/shard_map/ppermute | solution.py:383

commit v20 on v17

--- a/solution.py
+++ b/solution.py
@@ -384,13 +384,16 @@
     def partner_of(place, shift):
         return place + 1 if (place + shift) % 2 == 0 else place - 1
 
+    def stay(zone, gx, yz):
+        return (zone, gx, yz)
+
     def flip(zone, gx, yz):
-        return (1 - zone, gx, yz)
+        return (1 - zone, gx, yz) if gx == widths - 1 else (zone, gx, yz)
 
     def along_z(shift):
         def target(zone, gx, yz):
             to = partner_of(yz, shift)
-            return (zone, gx, to) if 0 <= to < count else flip(zone, gx, yz)
+            return (zone, gx, to) if 0 <= to < count else stay(zone, gx, yz)
 
         return target
 
@@ -398,19 +401,19 @@
         def target(zone, gx, yz):
             if gx == widths - 1:
                 return (zone, gx, (yz + hop) % count)
-            return flip(zone, gx, yz)
+            return stay(zone, gx, yz)
 
         return target
 
     def ends_z(zone, gx, yz):
         if gx == widths - 1 and yz in (0, count - 1):
             return (zone, gx, count - 1 - yz)
-        return flip(zone, gx, yz)
+        return stay(zone, gx, yz)
 
     def along_x(shift, taken):
         def target(zone, gx, yz):
             to = partner_of(gx, shift)
-            return (zone, to, yz) if 0 <= to < widths and taken(gx) else flip(zone, gx, yz)
+            return (zone, to, yz) if 0 <= to < widths and taken(gx) else stay(zone, gx, yz)
 
         return target
 

time: 28.7 us -> 47.7 us (1.66)
  starting transfers between devices: 15 us -> 33.3 us
    ppermute x17, starting transfers between devices: 15 us -> 33.3 us  [send(): lax.ppermute(values, axes, [(flat(*here), flat(*target(*here))) for here...]
  transfers between devices with their start and end apart: 17 -> 17, of which waited for: 2 -> 2; matrix products, arithmetic and copies ran while one was open for 0% -> 0% of each run, Pallas kernels for 27% -> 17%
where the time goes in v20:
time: 47.7 us; the launch traced here: 47.3 us
  starting transfers between devices  33.3 us (70%)
  Pallas kernels  11.5 us (24%)
  waiting for transfers between devices  2.16 us (5%)
    ppermute x17, starting transfers between devices, send(): lax.ppermute(values, axes, [(flat(*here), flat(*target(*here))) for here...  33.3 us
    pallas_call x4, Pallas kernels, make_planes(): pl.pallas_call(run, out_shape=(tile_shape(27, extent_x), *extra), in_spec...  5.31 us
    pallas_call x2, Pallas kernels, body(): pl.pallas_call(lambda *refs: velocity_kernel(step, *refs), out_shape=(*(j...  3.36 us
    ppermute x17, waiting for transfers between devices, send(): lax.ppermute(values, axes, [(flat(*here), flat(*target(*here))) for here...  2.16 us
    pallas_call x1, Pallas kernels, body(): pl.pallas_call(pack_kernel, out_shape=(tile_shape(27, extent_x), *message...  1.9 us
  transfers between devices with their start and end apart: 17, of which 2 were waited for; matrix products, arithmetic and copies ran while one was open for 0% of the time, Pallas kernels for 17%

profile of v20, /device:TPU:7, one launch (start us, length us, event | category | flops | bytes accessed | tf_op | source)
XLA Modules:
  0.0 47.3 jit_solution(15311973477468904461)
XLA Ops:
  0.0 1.9 %shard_map.64 = (f32[27,8,16,128]{3,2,1,0:T(8,128)S(1)}, f32[9,16,128]{2,1,0:T(8,128)S(1)}, f32[10,16,128]{2,1,0:T(8,128)S(1)}, f32[10,16,128]{2,1,0:T(8,128)S(1)}) custom-call(f32[27,8,16,128]{3,2,1,0:T(8,128)} %bitcast.14), custom_call_target="tpu_custom_call" | custom-call | tf_op jit(solution)/shard_map/pallas_call | solution.py:428
  1.9 0.7 %collective-permute-start = (f32[10,16,128]{2,1,0:T(8,128)S(1)}, f32[10,16,128]{2,1,0:T(8,128)S(1)}, u32[]{:S(2)}, u32[]{:S(2)}) collective-permute-start(f32[10,16,128]{2,1,0:T(8,128)S(1)} %get-tuple-element.30), channel_id=1, source_target_pairs={{0,0},{1,2},{2,1},{3,3},{4,4},{5,6},{6,5},{7,7},{8,8},{9,10},{10,9... | collective-permute-start | bytes 245768 | tf_op jit(solution)/shard_map/ppermute | solution.py:382
  2.6 3.9 %collective-permute-start.1 = (f32[10,16,128]{2,1,0:T(8,128)S(1)}, f32[10,16,128]{2,1,0:T(8,128)S(1)}, u32[]{:S(2)}, u32[]{:S(2)}) collective-permute-start(f32[10,16,128]{2,1,0:T(8,128)S(1)} %get-tuple-element.31), channel_id=1, source_target_pairs={{0,1},{1,0},{2,3},{3,2},{4,5},{5,4},{6,7},{7,6},{8,9},{9,8},{10,11... | collective-permute-start | bytes 245768 | tf_op jit(solution)/shard_map/ppermute | solution.py:382
  6.5 1.9 %collective-permute-start.6 = (f32[9,16,128]{2,1,0:T(8,128)S(1)}, f32[9,16,128]{2,1,0:T(8,128)S(1)}, u32[]{:S(2)}, u32[]{:S(2)}) collective-permute-start(f32[9,16,128]{2,1,0:T(8,128)S(1)} %get-tuple-element.35.refs_0_), channel_id=1, source_target_pairs={{0,0},{1,1},{2,2},{3,3},{4,4},{5,5},{6,6},{7,7},{8,8},{9,9},{10,10... | collective-permute-start | bytes 221192 | tf_op jit(solution)/shard_map/ppermute | solution.py:382
  8.4 4.0 %collective-permute-start.7 = (f32[9,16,128]{2,1,0:T(8,128)S(1)}, f32[9,16,128]{2,1,0:T(8,128)S(1)}, u32[]{:S(2)}, u32[]{:S(2)}) collective-permute-start(f32[9,16,128]{2,1,0:T(8,128)S(1)} %get-tuple-element.35.refs_0_), channel_id=1, source_target_pairs={{0,0},{1,1},{2,2},{3,3},{4,4},{5,5},{6,6},{7,7},{8,8},{9,9},{10,10... | collective-permute-start | bytes 221192 | tf_op jit(solution)/shard_map/ppermute | solution.py:382
  12.5 3.4 %collective-permute-start.2 = (f32[4,16,128]{2,1,0:T(8,128)S(1)}, f32[4,16,128]{2,1,0:T(8,128)S(1)}, u32[]{:S(2)}, u32[]{:S(2)}) collective-permute-start(f32[4,16,128]{2,1,0:T(8,128)S(1)} %shard_map.66), channel_id=1, source_target_pairs={{0,0},{1,1},{2,2},{3,3},{4,4},{5,5},{6,6},{7,7},{8,8},{9,9},{10,10... | collective-permute-start | bytes 98312 | tf_op jit(solution)/shard_map/ppermute | solution.py:382
  15.9 1.7 %shard_map.65 = (s32[1,8,16,128]{3,2,1,0:T(8,128)S(1)}, f32[3,8,16,128]{3,2,1,0:T(8,128)S(1)}) custom-call(f32[2,1,27,8,16,128]{5,4,3,2,1,0:T(8,128)} %refs_0_.3, s32[1,8,16,128]{3,2,1,0:T(8,128)} %refs_1_.1), custom_call_target="tpu_custom_call" | custom-call | tf_op jit(solution)/shard_map/pallas_call | solution.py:445
  18.4 0.7 %collective-permute-start.4 = (f32[10,16,128]{2,1,0:T(8,128)S(1)}, f32[10,16,128]{2,1,0:T(8,128)S(1)}, u32[]{:S(2)}, u32[]{:S(2)}) collective-permute-start(f32[10,16,128]{2,1,0:T(8,128)S(1)} %get-tuple-element.33), channel_id=1, source_target_pairs={{0,0},{1,1},{2,2},{3,3},{4,8},{5,9},{6,10},{7,11},{8,4},{9,5},{10,... | collective-permute-start | bytes 245768 | tf_op jit(solution)/shard_map/ppermute | solution.py:382
  19.1 1.9 %collective-permute-start.5 = (f32[10,16,128]{2,1,0:T(8,128)S(1)}, f32[10,16,128]{2,1,0:T(8,128)S(1)}, u32[]{:S(2)}, u32[]{:S(2)}) collective-permute-start(f32[10,16,128]{2,1,0:T(8,128)S(1)} %get-tuple-element.34), channel_id=1, source_target_pairs={{0,0},{1,1},{2,2},{3,3},{4,4},{5,5},{6,6},{7,7},{8,12},{9,13},{10,... | collective-permute-start | bytes 245768 | tf_op jit(solution)/shard_map/ppermute | solution.py:382
  21.0 1.9 %shard_map.68 = (f32[27,8,16,128]{3,2,1,0:T(8,128)S(1)}, f32[16,128]{1,0:T(8,128)S(1)}, f32[16,128]{1,0:T(8,128)S(1)}) custom-call(f32[27,8,16,128]{3,2,1,0:T(8,128)S(1)} %get-tuple-element.27.adj, f32[3,8,16,128]{3,2,1,0:T(8,128)S(1)} %get-tuple-element.28.rest_0_.vel, s32[1,8,16,128]{3,2,1,0:T(8,128)S(1)} %get-tuple-element.29.solid, ...), custom_call_target="tpu_custom_call" | custom-call | tf_op jit(solution)/shard_map/pallas_call | solution.py:478
  23.3 1.9 %collective-permute-start.8 = (f32[9,16,128]{2,1,0:T(8,128)S(1)}, f32[9,16,128]{2,1,0:T(8,128)S(1)}, u32[]{:S(2)}, u32[]{:S(2)}) collective-permute-start(f32[9,16,128]{2,1,0:T(8,128)S(1)} %shard_map.69), channel_id=1, source_target_pairs={{0,0},{1,1},{2,2},{3,3},{4,4},{5,5},{6,6},{7,7},{8,8},{9,9},{10,10... | collective-permute-start | bytes 221192 | tf_op jit(solution)/shard_map/ppermute | solution.py:382
  25.2 1.2 %collective-permute-done.8.refs_5_ = f32[9,16,128]{2,1,0:T(8,128)S(1)} collective-permute-done((f32[9,16,128]{2,1,0:T(8,128)S(1)}, f32[9,16,128]{2,1,0:T(8,128)S(1)}, u32[]{:S(2)}, u32[]{:S(2)}) %collective-permute-start.8) | collective-permute-done | bytes 73760 | tf_op jit(solution)/shard_map/ppermute | solution.py:382
  26.4 0.7 %shard_map.70 = (f32[27,8,16,128]{3,2,1,0:T(8,128)S(1)}, f32[9,16,128]{2,1,0:T(8,128)S(1)}, f32[10,16,128]{2,1,0:T(8,128)S(1)}, f32[10,16,128]{2,1,0:T(8,128)S(1)}) custom-call(f32[27,8,16,128]{3,2,1,0:T(8,128)S(1)} %get-tuple-element.27.adj, f32[3,8,16,128]{3,2,1,0:T(8,128)S(1)} %get-tuple-element.28.rest_0_.vel, ...), custom_call_target="tpu_custom_call", output_to_operand_aliasing={{0}: (11, {})} | custom-call | tf_op jit(solution)/shard_map/pallas_call | solution.py:478
  27.1 0.7 %collective-permute-start.10 = (f32[10,16,128]{2,1,0:T(8,128)S(1)}, f32[10,16,128]{2,1,0:T(8,128)S(1)}, u32[]{:S(2)}, u32[]{:S(2)}) collective-permute-start(f32[10,16,128]{2,1,0:T(8,128)S(1)} %get-tuple-element.41), channel_id=1, source_target_pairs={{0,0},{1,2},{2,1},{3,3},{4,4},{5,6},{6,5},{7,7},{8,8},{9,10},{10,9... | collective-permute-start | bytes 245768 | tf_op jit(solution)/shard_map/ppermute | solution.py:382
  28.4 2.8 %collective-permute-start.14 = (f32[9,16,128]{2,1,0:T(8,128)S(1)}, f32[9,16,128]{2,1,0:T(8,128)S(1)}, u32[]{:S(2)}, u32[]{:S(2)}) collective-permute-start(f32[9,16,128]{2,1,0:T(8,128)S(1)} %get-tuple-element.45.refs_0_), channel_id=1, source_target_pairs={{0,0},{1,1},{2,2},{3,3},{4,4},{5,5},{6,6},{7,7},{8,8},{9,9},{10,10... | collective-permute-start | bytes 221192 | tf_op jit(solution)/shard_map/ppermute | solution.py:382
  31.2 4.0 %collective-permute-start.15 = (f32[9,16,128]{2,1,0:T(8,128)S(1)}, f32[9,16,128]{2,1,0:T(8,128)S(1)}, u32[]{:S(2)}, u32[]{:S(2)}) collective-permute-start(f32[9,16,128]{2,1,0:T(8,128)S(1)} %get-tuple-element.45.refs_0_), channel_id=1, source_target_pairs={{0,0},{1,1},{2,2},{3,3},{4,4},{5,5},{6,6},{7,7},{8,8},{9,9},{10,10... | collective-permute-start | bytes 221192 | tf_op jit(solution)/shard_map/ppermute | solution.py:382
  35.2 1.7 %shard_map.71.rest_0_.vel = f32[3,8,16,128]{3,2,1,0:T(8,128)S(1)} custom-call(f32[2,1,27,8,16,128]{5,4,3,2,1,0:T(8,128)} %refs_0_.3), custom_call_target="tpu_custom_call" | custom-call | tf_op jit(solution)/shard_map/pallas_call | solution.py:445
  37.0 0.7 %collective-permute-start.11 = (f32[10,16,128]{2,1,0:T(8,128)S(1)}, f32[10,16,128]{2,1,0:T(8,128)S(1)}, u32[]{:S(2)}, u32[]{:S(2)}) collective-permute-start(f32[10,16,128]{2,1,0:T(8,128)S(1)} %get-tuple-element.42), channel_id=1, source_target_pairs={{0,4},{1,5},{2,6},{3,7},{4,0},{5,1},{6,2},{7,3},{8,8},{9,9},{10,10... | collective-permute-start | bytes 245768 | tf_op jit(solution)/shard_map/ppermute | solution.py:382
  37.7 0.7 %collective-permute-start.12 = (f32[10,16,128]{2,1,0:T(8,128)S(1)}, f32[10,16,128]{2,1,0:T(8,128)S(1)}, u32[]{:S(2)}, u32[]{:S(2)}) collective-permute-start(f32[10,16,128]{2,1,0:T(8,128)S(1)} %get-tuple-element.43), channel_id=1, source_target_pairs={{0,0},{1,1},{2,2},{3,3},{4,8},{5,9},{6,10},{7,11},{8,4},{9,5},{10,... | collective-permute-start | bytes 245768 | tf_op jit(solution)/shard_map/ppermute | solution.py:382
  38.3 1.9 %collective-permute-start.13 = (f32[10,16,128]{2,1,0:T(8,128)S(1)}, f32[10,16,128]{2,1,0:T(8,128)S(1)}, u32[]{:S(2)}, u32[]{:S(2)}) collective-permute-start(f32[10,16,128]{2,1,0:T(8,128)S(1)} %get-tuple-element.44), channel_id=1, source_target_pairs={{0,0},{1,1},{2,2},{3,3},{4,4},{5,5},{6,6},{7,7},{8,12},{9,13},{10,... | collective-permute-start | bytes 245768 | tf_op jit(solution)/shard_map/ppermute | solution.py:382
  40.3 1.8 %shard_map.73 = (f32[27,8,16,128]{3,2,1,0:T(8,128)}, f32[16,128]{1,0:T(8,128)S(1)}, f32[16,128]{1,0:T(8,128)S(1)}) custom-call(f32[27,8,16,128]{3,2,1,0:T(8,128)S(1)} %get-tuple-element.39.adj, f32[3,8,16,128]{3,2,1,0:T(8,128)S(1)} %shard_map.71.rest_0_.vel, s32[1,8,16,128]{3,2,1,0:T(8,128)S(1)} %get-tuple-element.29.solid, ...), custom_call_target="tpu_custom_call" | custom-call | tf_op jit(solution)/shard_map/pallas_call | solution.py:478
  42.4 2.9 %collective-permute-start.16 = (f32[9,16,128]{2,1,0:T(8,128)S(1)}, f32[9,16,128]{2,1,0:T(8,128)S(1)}, u32[]{:S(2)}, u32[]{:S(2)}) collective-permute-start(f32[9,16,128]{2,1,0:T(8,128)S(1)} %shard_map.74), channel_id=1, source_target_pairs={{0,0},{1,1},{2,2},{3,3},{4,4},{5,5},{6,6},{7,7},{8,8},{9,9},{10,10... | collective-permute-start | bytes 221192 | tf_op jit(solution)/shard_map/ppermute | solution.py:382
  45.3 0.9 %collective-permute-done.16.refs_5_ = f32[9,16,128]{2,1,0:T(8,128)S(1)} collective-permute-done((f32[9,16,128]{2,1,0:T(8,128)S(1)}, f32[9,16,128]{2,1,0:T(8,128)S(1)}, u32[]{:S(2)}, u32[]{:S(2)}) %collective-permute-start.16) | collective-permute-done | bytes 73760 | tf_op jit(solution)/shard_map/ppermute | solution.py:382
  46.2 1.0 %shard_map.75 = f32[27,8,16,128]{3,2,1,0:T(8,128)} custom-call(f32[27,8,16,128]{3,2,1,0:T(8,128)S(1)} %get-tuple-element.39.adj, f32[3,8,16,128]{3,2,1,0:T(8,128)S(1)} %shard_map.71.rest_0_.vel, s32[1,8,16,128]{3,2,1,0:T(8,128)S(1)} %get-tuple-element.29.solid, ...), custom_call_target="tpu_custom_call", output_to_operand_aliasing={{}: (11, {})} | custom-call | tf_op jit(solution)/shard_map/pallas_call | solution.py:478
  (28 shorter events, 2.2 us)
Async XLA Ops:
  0.0 12.4 %copy-start = (s32[1,16,128,2]{2,3,1,0:T(2,128)S(1)}, s32[1,16,128,2]{2,3,1,0:T(2,128)}, u32[]{:S(2)}) copy-start(s32[1,16,128,2]{2,3,1,0:T(2,128)} %param.9) | copy-start | bytes 49156
  0.0 12.4 %copy-start.1 = (s32[1,16,128,2]{2,3,1,0:T(2,128)S(1)}, s32[1,16,128,2]{2,3,1,0:T(2,128)}, u32[]{:S(2)}) copy-start(s32[1,16,128,2]{2,3,1,0:T(2,128)} %param.10) | copy-start | bytes 49156
  0.0 12.4 %copy-start.2 = (f32[1,16,128,2]{2,3,1,0:T(2,128)S(1)}, f32[1,16,128,2]{2,3,1,0:T(2,128)}, u32[]{:S(2)}) copy-start(f32[1,16,128,2]{2,3,1,0:T(2,128)} %param.11) | copy-start | bytes 49156
  1.9 15.7 %collective-permute-start = (f32[10,16,128]{2,1,0:T(8,128)S(1)}, f32[10,16,128]{2,1,0:T(8,128)S(1)}, u32[]{:S(2)}, u32[]{:S(2)}) collective-permute-start(f32[10,16,128]{2,1,0:T(8,128)S(1)} %get-tuple-element.30), channel_id=1, source_target_pairs={{0,0},{1,2},{2,1},{3,3},{4,4},{5,6},{6,5},{7,7},{8,8},{9,10},{10,9... | collective-permute-start | bytes 245768 | tf_op jit(solution)/shard_map/ppermute | solution.py:382
  2.6 15.1 %collective-permute-start.1 = (f32[10,16,128]{2,1,0:T(8,128)S(1)}, f32[10,16,128]{2,1,0:T(8,128)S(1)}, u32[]{:S(2)}, u32[]{:S(2)}) collective-permute-start(f32[10,16,128]{2,1,0:T(8,128)S(1)} %get-tuple-element.31), channel_id=1, source_target_pairs={{0,1},{1,0},{2,3},{3,2},{4,5},{5,4},{6,7},{7,6},{8,9},{9,8},{10,11... | collective-permute-start | bytes 245768 | tf_op jit(solution)/shard_map/ppermute | solution.py:382
  6.5 16.4 %collective-permute-start.6 = (f32[9,16,128]{2,1,0:T(8,128)S(1)}, f32[9,16,128]{2,1,0:T(8,128)S(1)}, u32[]{:S(2)}, u32[]{:S(2)}) collective-permute-start(f32[9,16,128]{2,1,0:T(8,128)S(1)} %get-tuple-element.35.refs_0_), channel_id=1, source_target_pairs={{0,0},{1,1},{2,2},{3,3},{4,4},{5,5},{6,6},{7,7},{8,8},{9,9},{10,10... | collective-permute-start | bytes 221192 | tf_op jit(solution)/shard_map/ppermute | solution.py:382
  8.4 14.5 %collective-permute-start.7 = (f32[9,16,128]{2,1,0:T(8,128)S(1)}, f32[9,16,128]{2,1,0:T(8,128)S(1)}, u32[]{:S(2)}, u32[]{:S(2)}) collective-permute-start(f32[9,16,128]{2,1,0:T(8,128)S(1)} %get-tuple-element.35.refs_0_), channel_id=1, source_target_pairs={{0,0},{1,1},{2,2},{3,3},{4,4},{5,5},{6,6},{7,7},{8,8},{9,9},{10,10... | collective-permute-start | bytes 221192 | tf_op jit(solution)/shard_map/ppermute | solution.py:382
  12.5 5.1 %collective-permute-start.2 = (f32[4,16,128]{2,1,0:T(8,128)S(1)}, f32[4,16,128]{2,1,0:T(8,128)S(1)}, u32[]{:S(2)}, u32[]{:S(2)}) collective-permute-start(f32[4,16,128]{2,1,0:T(8,128)S(1)} %shard_map.66), channel_id=1, source_target_pairs={{0,0},{1,1},{2,2},{3,3},{4,4},{5,5},{6,6},{7,7},{8,8},{9,9},{10,10... | collective-permute-start | bytes 98312 | tf_op jit(solution)/shard_map/ppermute | solution.py:382
  17.8 8.7 %collective-permute-start.3 = (f32[10,16,128]{2,1,0:T(8,128)S(1)}, f32[10,16,128]{2,1,0:T(8,128)S(1)}, u32[]{:S(2)}, u32[]{:S(2)}) collective-permute-start(f32[10,16,128]{2,1,0:T(8,128)S(1)} %get-tuple-element.32), channel_id=1, source_target_pairs={{0,4},{1,5},{2,6},{3,7},{4,0},{5,1},{6,2},{7,3},{8,8},{9,9},{10,10... | collective-permute-start | bytes 245768 | tf_op jit(solution)/shard_map/ppermute | solution.py:382
  18.4 8.0 %collective-permute-start.4 = (f32[10,16,128]{2,1,0:T(8,128)S(1)}, f32[10,16,128]{2,1,0:T(8,128)S(1)}, u32[]{:S(2)}, u32[]{:S(2)}) collective-permute-start(f32[10,16,128]{2,1,0:T(8,128)S(1)} %get-tuple-element.33), channel_id=1, source_target_pairs={{0,0},{1,1},{2,2},{3,3},{4,8},{5,9},{6,10},{7,11},{8,4},{9,5},{10,... | collective-permute-start | bytes 245768 | tf_op jit(solution)/shard_map/ppermute | solution.py:382
  19.1 7.3 %collective-permute-start.5 = (f32[10,16,128]{2,1,0:T(8,128)S(1)}, f32[10,16,128]{2,1,0:T(8,128)S(1)}, u32[]{:S(2)}, u32[]{:S(2)}) collective-permute-start(f32[10,16,128]{2,1,0:T(8,128)S(1)} %get-tuple-element.34), channel_id=1, source_target_pairs={{0,0},{1,1},{2,2},{3,3},{4,4},{5,5},{6,6},{7,7},{8,12},{9,13},{10,... | collective-permute-start | bytes 245768 | tf_op jit(solution)/shard_map/ppermute | solution.py:382
  23.3 3.2 %collective-permute-start.8 = (f32[9,16,128]{2,1,0:T(8,128)S(1)}, f32[9,16,128]{2,1,0:T(8,128)S(1)}, u32[]{:S(2)}, u32[]{:S(2)}) collective-permute-start(f32[9,16,128]{2,1,0:T(8,128)S(1)} %shard_map.69), channel_id=1, source_target_pairs={{0,0},{1,1},{2,2},{3,3},{4,4},{5,5},{6,6},{7,7},{8,8},{9,9},{10,10... | collective-permute-start | bytes 221192 | tf_op jit(solution)/shard_map/ppermute | solution.py:382
  27.1 9.8 %collective-permute-start.10 = (f32[10,16,128]{2,1,0:T(8,128)S(1)}, f32[10,16,128]{2,1,0:T(8,128)S(1)}, u32[]{:S(2)}, u32[]{:S(2)}) collective-permute-start(f32[10,16,128]{2,1,0:T(8,128)S(1)} %get-tuple-element.41), channel_id=1, source_target_pairs={{0,0},{1,2},{2,1},{3,3},{4,4},{5,6},{6,5},{7,7},{8,8},{9,10},{10,9... | collective-permute-start | bytes 245768 | tf_op jit(solution)/shard_map/ppermute | solution.py:382
  27.8 9.1 %collective-permute-start.9 = (f32[10,16,128]{2,1,0:T(8,128)S(1)}, f32[10,16,128]{2,1,0:T(8,128)S(1)}, u32[]{:S(2)}, u32[]{:S(2)}) collective-permute-start(f32[10,16,128]{2,1,0:T(8,128)S(1)} %get-tuple-element.40), channel_id=1, source_target_pairs={{0,1},{1,0},{2,3},{3,2},{4,5},{5,4},{6,7},{7,6},{8,9},{9,8},{10,11... | collective-permute-start | bytes 245768 | tf_op jit(solution)/shard_map/ppermute | solution.py:382
  28.4 13.6 %collective-permute-start.14 = (f32[9,16,128]{2,1,0:T(8,128)S(1)}, f32[9,16,128]{2,1,0:T(8,128)S(1)}, u32[]{:S(2)}, u32[]{:S(2)}) collective-permute-start(f32[9,16,128]{2,1,0:T(8,128)S(1)} %get-tuple-element.45.refs_0_), channel_id=1, source_target_pairs={{0,0},{1,1},{2,2},{3,3},{4,4},{5,5},{6,6},{7,7},{8,8},{9,9},{10,10... | collective-permute-start | bytes 221192 | tf_op jit(solution)/shard_map/ppermute | solution.py:382
  31.2 10.8 %collective-permute-start.15 = (f32[9,16,128]{2,1,0:T(8,128)S(1)}, f32[9,16,128]{2,1,0:T(8,128)S(1)}, u32[]{:S(2)}, u32[]{:S(2)}) collective-permute-start(f32[9,16,128]{2,1,0:T(8,128)S(1)} %get-tuple-element.45.refs_0_), channel_id=1, source_target_pairs={{0,0},{1,1},{2,2},{3,3},{4,4},{5,5},{6,6},{7,7},{8,8},{9,9},{10,10... | collective-permute-start | bytes 221192 | tf_op jit(solution)/shard_map/ppermute | solution.py:382
  37.0 9.2 %collective-permute-start.11 = (f32[10,16,128]{2,1,0:T(8,128)S(1)}, f32[10,16,128]{2,1,0:T(8,128)S(1)}, u32[]{:S(2)}, u32[]{:S(2)}) collective-permute-start(f32[10,16,128]{2,1,0:T(8,128)S(1)} %get-tuple-element.42), channel_id=1, source_target_pairs={{0,4},{1,5},{2,6},{3,7},{4,0},{5,1},{6,2},{7,3},{8,8},{9,9},{10,10... | collective-permute-start | bytes 245768 | tf_op jit(solution)/shard_map/ppermute | solution.py:382
  37.7 8.6 %collective-permute-start.12 = (f32[10,16,128]{2,1,0:T(8,128)S(1)}, f32[10,16,128]{2,1,0:T(8,128)S(1)}, u32[]{:S(2)}, u32[]{:S(2)}) collective-permute-start(f32[10,16,128]{2,1,0:T(8,128)S(1)} %get-tuple-element.43), channel_id=1, source_target_pairs={{0,0},{1,1},{2,2},{3,3},{4,8},{5,9},{6,10},{7,11},{8,4},{9,5},{10,... | collective-permute-start | bytes 245768 | tf_op jit(solution)/shard_map/ppermute | solution.py:382
  38.3 7.9 %collective-permute-start.13 = (f32[10,16,128]{2,1,0:T(8,128)S(1)}, f32[10,16,128]{2,1,0:T(8,128)S(1)}, u32[]{:S(2)}, u32[]{:S(2)}) collective-permute-start(f32[10,16,128]{2,1,0:T(8,128)S(1)} %get-tuple-element.44), channel_id=1, source_target_pairs={{0,0},{1,1},{2,2},{3,3},{4,4},{5,5},{6,6},{7,7},{8,12},{9,13},{10,... | collective-permute-start | bytes 245768 | tf_op jit(solution)/shard_map/ppermute | solution.py:382
  42.4 3.8 %collective-permute-start.16 = (f32[9,16,128]{2,1,0:T(8,128)S(1)}, f32[9,16,128]{2,1,0:T(8,128)S(1)}, u32[]{:S(2)}, u32[]{:S(2)}) collective-permute-start(f32[9,16,128]{2,1,0:T(8,128)S(1)} %shard_map.74), channel_id=1, source_target_pairs={{0,0},{1,1},{2,2},{3,3},{4,4},{5,5},{6,6},{7,7},{8,8},{9,9},{10,10... | collective-permute-start | bytes 221192 | tf_op jit(solution)/shard_map/ppermute | solution.py:382

commit v21 on v17

--- a/solution.py
+++ b/solution.py
@@ -494,7 +494,7 @@
             in_specs=in_vmem(count + 2) + in_any(1),
             out_specs=in_vmem(1)[0],
             compiler_params=params,
-        )(own, first, second, *others, info, columns[0])
+        )(own, first, second, *others, info, vel if last else columns[0])
         cross = send(cross, flip)
         ghosts = (near, two, far)
         field, *results = make_planes(

time: 28.7 us -> 29.6 us (1.031)
  waiting for transfers between devices: 1.86 us -> 2.47 us
  starting transfers between devices: 15 us -> 15.3 us
    ppermute x17, waiting for transfers between devices: 1.86 us -> 2.47 us  [send(): lax.ppermute(values, axes, [(flat(*here), flat(*target(*here))) for here...]
  transfers between devices with their start and end apart: 17 -> 17, of which waited for: 2 -> 3; matrix products, arithmetic and copies ran while one was open for 0% -> 0% of each run, Pallas kernels for 27% -> 27%
where the time goes in v21:
time: 29.6 us; the launch traced here: 29.4 us
  starting transfers between devices  15.3 us (52%)
  Pallas kernels  11.4 us (39%)
  waiting for transfers between devices  2.47 us (8%)
    ppermute x17, starting transfers between devices, send(): lax.ppermute(values, axes, [(flat(*here), flat(*target(*here))) for here...  15.3 us
    pallas_call x4, Pallas kernels, make_planes(): pl.pallas_call(run, out_shape=(tile_shape(27, extent_x), *extra), in_spec...  5.29 us
    pallas_call x2, Pallas kernels, body(): pl.pallas_call(lambda *refs: velocity_kernel(step, *refs), out_shape=(*(j...  3.32 us
    ppermute x17, waiting for transfers between devices, send(): lax.ppermute(values, axes, [(flat(*here), flat(*target(*here))) for here...  2.47 us
    pallas_call x1, Pallas kernels, body(): pl.pallas_call(pack_kernel, out_shape=(tile_shape(27, extent_x), *message...  1.9 us
    pallas_call x2, Pallas kernels, body(): pl.pallas_call(lambda *refs: cross_kernel(count, *refs), out_shape=tile_s...  0.7 us
  transfers between devices with their start and end apart: 17, of which 3 were waited for; matrix products, arithmetic and copies ran while one was open for 0% of the time, Pallas kernels for 27%

profile of v21, /device:TPU:7, one launch (start us, length us, event | category | flops | bytes accessed | tf_op | source)
XLA Modules:
  0.0 29.4 jit_solution(10028015964765755287)
XLA Ops:
  0.0 1.9 %shard_map.64 = (f32[27,8,16,128]{3,2,1,0:T(8,128)S(1)}, f32[9,16,128]{2,1,0:T(8,128)S(1)}, f32[10,16,128]{2,1,0:T(8,128)S(1)}, f32[10,16,128]{2,1,0:T(8,128)S(1)}) custom-call(f32[27,8,16,128]{3,2,1,0:T(8,128)} %bitcast.14), custom_call_target="tpu_custom_call" | custom-call | tf_op jit(solution)/shard_map/pallas_call | solution.py:425
  1.9 0.7 %collective-permute-start = (f32[10,16,128]{2,1,0:T(8,128)S(1)}, f32[10,16,128]{2,1,0:T(8,128)S(1)}, u32[]{:S(2)}, u32[]{:S(2)}) collective-permute-start(f32[10,16,128]{2,1,0:T(8,128)S(1)} %get-tuple-element.30), channel_id=1, source_target_pairs={{0,16},{1,2},{2,1},{3,19},{4,20},{5,6},{6,5},{7,23},{8,24},{9,10},... | collective-permute-start | bytes 245768 | tf_op jit(solution)/shard_map/ppermute | solution.py:382
  2.7 1.9 %collective-permute-start.1 = (f32[10,16,128]{2,1,0:T(8,128)S(1)}, f32[10,16,128]{2,1,0:T(8,128)S(1)}, u32[]{:S(2)}, u32[]{:S(2)}) collective-permute-start(f32[10,16,128]{2,1,0:T(8,128)S(1)} %get-tuple-element.31), channel_id=1, source_target_pairs={{0,1},{1,0},{2,3},{3,2},{4,5},{5,4},{6,7},{7,6},{8,9},{9,8},{10,11... | collective-permute-start | bytes 245768 | tf_op jit(solution)/shard_map/ppermute | solution.py:382
  4.6 1.7 %collective-permute-start.6 = (f32[9,16,128]{2,1,0:T(8,128)S(1)}, f32[9,16,128]{2,1,0:T(8,128)S(1)}, u32[]{:S(2)}, u32[]{:S(2)}) collective-permute-start(f32[9,16,128]{2,1,0:T(8,128)S(1)} %get-tuple-element.35.refs_0_), channel_id=1, source_target_pairs={{0,16},{1,17},{2,18},{3,19},{4,20},{5,21},{6,22},{7,23},{8,24},{9,... | collective-permute-start | bytes 221192 | tf_op jit(solution)/shard_map/ppermute | solution.py:382
  6.3 0.4 %collective-permute-start.7 = (f32[9,16,128]{2,1,0:T(8,128)S(1)}, f32[9,16,128]{2,1,0:T(8,128)S(1)}, u32[]{:S(2)}, u32[]{:S(2)}) collective-permute-start(f32[9,16,128]{2,1,0:T(8,128)S(1)} %get-tuple-element.35.refs_0_), channel_id=1, source_target_pairs={{0,16},{1,17},{2,18},{3,19},{4,20},{5,21},{6,22},{7,23},{8,24},{9,... | collective-permute-start | bytes 221192 | tf_op jit(solution)/shard_map/ppermute | solution.py:382
  6.7 1.6 %collective-permute-start.2 = (f32[4,16,128]{2,1,0:T(8,128)S(1)}, f32[4,16,128]{2,1,0:T(8,128)S(1)}, u32[]{:S(2)}, u32[]{:S(2)}) collective-permute-start(f32[4,16,128]{2,1,0:T(8,128)S(1)} %shard_map.66), channel_id=1, source_target_pairs={{0,16},{1,17},{2,18},{3,19},{4,20},{5,21},{6,22},{7,23},{8,24},{9,... | collective-permute-start | bytes 98312 | tf_op jit(solution)/shard_map/ppermute | solution.py:382
  8.3 1.7 %shard_map.65 = (s32[1,8,16,128]{3,2,1,0:T(8,128)S(1)}, f32[3,8,16,128]{3,2,1,0:T(8,128)S(1)}) custom-call(f32[2,1,27,8,16,128]{5,4,3,2,1,0:T(8,128)} %refs_0_.3, s32[1,8,16,128]{3,2,1,0:T(8,128)} %refs_1_.1), custom_call_target="tpu_custom_call" | custom-call | tf_op jit(solution)/shard_map/pallas_call | solution.py:442
  10.2 0.5 %collective-permute-start.4 = (f32[10,16,128]{2,1,0:T(8,128)S(1)}, f32[10,16,128]{2,1,0:T(8,128)S(1)}, u32[]{:S(2)}, u32[]{:S(2)}) collective-permute-start(f32[10,16,128]{2,1,0:T(8,128)S(1)} %get-tuple-element.33), channel_id=1, source_target_pairs={{0,16},{1,17},{2,18},{3,19},{4,8},{5,9},{6,10},{7,11},{8,4},{9,5},... | collective-permute-start | bytes 245768 | tf_op jit(solution)/shard_map/ppermute | solution.py:382
  10.6 1.8 %shard_map.68 = (f32[27,8,16,128]{3,2,1,0:T(8,128)S(1)}, f32[16,128]{1,0:T(8,128)S(1)}, f32[16,128]{1,0:T(8,128)S(1)}) custom-call(f32[27,8,16,128]{3,2,1,0:T(8,128)S(1)} %get-tuple-element.27.adj, f32[3,8,16,128]{3,2,1,0:T(8,128)S(1)} %get-tuple-element.28.rest_0_.vel, s32[1,8,16,128]{3,2,1,0:T(8,128)S(1)} %get-tuple-element.29.solid, ...), custom_call_target="tpu_custom_call" | custom-call | tf_op jit(solution)/shard_map/pallas_call | solution.py:475
  12.5 0.4 %shard_map.69 = f32[9,16,128]{2,1,0:T(8,128)S(1)} custom-call(f32[9,16,128]{2,1,0:T(8,128)S(1)} %get-tuple-element.35.refs_0_, f32[10,16,128]{2,1,0:T(8,128)S(1)} %collective-permute-done.first.refs_0_.refs_1_, f32[10,16,128]{2,1,0:T(8,128)S(1)} %collective-permute-done.1.second.refs_1_.refs_2_, f32[9,16,128]{2,1,0:T(8,128)S(1)} %collective-permute-done.6.refs_3_, ...), custom_call_target="tpu_custom_call" | custom-call | tf_op jit(solution)/shard_map/pallas_call | solution.py:491
  12.9 0.9 %collective-permute-start.8 = (f32[9,16,128]{2,1,0:T(8,128)S(1)}, f32[9,16,128]{2,1,0:T(8,128)S(1)}, u32[]{:S(2)}, u32[]{:S(2)}) collective-permute-start(f32[9,16,128]{2,1,0:T(8,128)S(1)} %shard_map.69), channel_id=1, source_target_pairs={{0,16},{1,17},{2,18},{3,19},{4,20},{5,21},{6,22},{7,23},{8,24},{9,... | collective-permute-start | bytes 221192 | tf_op jit(solution)/shard_map/ppermute | solution.py:382
  13.8 0.9 %collective-permute-done.8.refs_5_ = f32[9,16,128]{2,1,0:T(8,128)S(1)} collective-permute-done((f32[9,16,128]{2,1,0:T(8,128)S(1)}, f32[9,16,128]{2,1,0:T(8,128)S(1)}, u32[]{:S(2)}, u32[]{:S(2)}) %collective-permute-start.8) | collective-permute-done | bytes 73760 | tf_op jit(solution)/shard_map/ppermute | solution.py:382
  14.7 0.7 %shard_map.70 = (f32[27,8,16,128]{3,2,1,0:T(8,128)S(1)}, f32[9,16,128]{2,1,0:T(8,128)S(1)}, f32[10,16,128]{2,1,0:T(8,128)S(1)}, f32[10,16,128]{2,1,0:T(8,128)S(1)}) custom-call(f32[27,8,16,128]{3,2,1,0:T(8,128)S(1)} %get-tuple-element.27.adj, f32[3,8,16,128]{3,2,1,0:T(8,128)S(1)} %get-tuple-element.28.rest_0_.vel, ...), custom_call_target="tpu_custom_call", output_to_operand_aliasing={{0}: (11, {})} | custom-call | tf_op jit(solution)/shard_map/pallas_call | solution.py:475
  15.3 0.9 %collective-permute-start.10 = (f32[10,16,128]{2,1,0:T(8,128)S(1)}, f32[10,16,128]{2,1,0:T(8,128)S(1)}, u32[]{:S(2)}, u32[]{:S(2)}) collective-permute-start(f32[10,16,128]{2,1,0:T(8,128)S(1)} %get-tuple-element.41), channel_id=1, source_target_pairs={{0,16},{1,2},{2,1},{3,19},{4,20},{5,6},{6,5},{7,23},{8,24},{9,10},... | collective-permute-start | bytes 245768 | tf_op jit(solution)/shard_map/ppermute | solution.py:382
  16.2 0.5 %collective-permute-start.9 = (f32[10,16,128]{2,1,0:T(8,128)S(1)}, f32[10,16,128]{2,1,0:T(8,128)S(1)}, u32[]{:S(2)}, u32[]{:S(2)}) collective-permute-start(f32[10,16,128]{2,1,0:T(8,128)S(1)} %get-tuple-element.40), channel_id=1, source_target_pairs={{0,1},{1,0},{2,3},{3,2},{4,5},{5,4},{6,7},{7,6},{8,9},{9,8},{10,11... | collective-permute-start | bytes 245768 | tf_op jit(solution)/shard_map/ppermute | solution.py:382
  16.7 2.1 %collective-permute-start.14 = (f32[9,16,128]{2,1,0:T(8,128)S(1)}, f32[9,16,128]{2,1,0:T(8,128)S(1)}, u32[]{:S(2)}, u32[]{:S(2)}) collective-permute-start(f32[9,16,128]{2,1,0:T(8,128)S(1)} %get-tuple-element.45.refs_0_), channel_id=1, source_target_pairs={{0,16},{1,17},{2,18},{3,19},{4,20},{5,21},{6,22},{7,23},{8,24},{9,... | collective-permute-start | bytes 221192 | tf_op jit(solution)/shard_map/ppermute | solution.py:382
  18.8 1.0 %collective-permute-start.15 = (f32[9,16,128]{2,1,0:T(8,128)S(1)}, f32[9,16,128]{2,1,0:T(8,128)S(1)}, u32[]{:S(2)}, u32[]{:S(2)}) collective-permute-start(f32[9,16,128]{2,1,0:T(8,128)S(1)} %get-tuple-element.45.refs_0_), channel_id=1, source_target_pairs={{0,16},{1,17},{2,18},{3,19},{4,20},{5,21},{6,22},{7,23},{8,24},{9,... | collective-permute-start | bytes 221192 | tf_op jit(solution)/shard_map/ppermute | solution.py:382
  19.8 1.6 %shard_map.71.rest_0_.refs_6_.vel = f32[3,8,16,128]{3,2,1,0:T(8,128)S(1)} custom-call(f32[2,1,27,8,16,128]{5,4,3,2,1,0:T(8,128)} %refs_0_.3), custom_call_target="tpu_custom_call" | custom-call | tf_op jit(solution)/shard_map/pallas_call | solution.py:442
  21.6 0.9 %collective-permute-start.11 = (f32[10,16,128]{2,1,0:T(8,128)S(1)}, f32[10,16,128]{2,1,0:T(8,128)S(1)}, u32[]{:S(2)}, u32[]{:S(2)}) collective-permute-start(f32[10,16,128]{2,1,0:T(8,128)S(1)} %get-tuple-element.42), channel_id=1, source_target_pairs={{0,4},{1,5},{2,6},{3,7},{4,0},{5,1},{6,2},{7,3},{8,24},{9,25},{10,... | collective-permute-start | bytes 245768 | tf_op jit(solution)/shard_map/ppermute | solution.py:382
  22.7 1.4 %collective-permute-done.15.refs_4_ = f32[9,16,128]{2,1,0:T(8,128)S(1)} collective-permute-done((f32[9,16,128]{2,1,0:T(8,128)S(1)}, f32[9,16,128]{2,1,0:T(8,128)S(1)}, u32[]{:S(2)}, u32[]{:S(2)}) %collective-permute-start.15) | collective-permute-done | bytes 73760 | tf_op jit(solution)/shard_map/ppermute | solution.py:382
  24.1 0.3 %shard_map.73 = f32[9,16,128]{2,1,0:T(8,128)S(1)} custom-call(f32[9,16,128]{2,1,0:T(8,128)S(1)} %get-tuple-element.45.refs_0_, f32[10,16,128]{2,1,0:T(8,128)S(1)} %collective-permute-done.10.first.refs_1_, f32[10,16,128]{2,1,0:T(8,128)S(1)} %collective-permute-done.9.second.refs_2_.refs_0_, f32[9,16,128]{2,1,0:T(8,128)S(1)} %collective-permute-done.14.refs_3_, ...), custom_call_target="tpu_custom_call" | custom-call | tf_op jit(solution)/shard_map/pallas_call | solution.py:491
  24.5 2.1 %collective-permute-start.16 = (f32[9,16,128]{2,1,0:T(8,128)S(1)}, f32[9,16,128]{2,1,0:T(8,128)S(1)}, u32[]{:S(2)}, u32[]{:S(2)}) collective-permute-start(f32[9,16,128]{2,1,0:T(8,128)S(1)} %shard_map.73), channel_id=1, source_target_pairs={{0,16},{1,17},{2,18},{3,19},{4,20},{5,21},{6,22},{7,23},{8,24},{9,... | collective-permute-start | bytes 221192 | tf_op jit(solution)/shard_map/ppermute | solution.py:382
  26.5 1.7 %shard_map.74 = (f32[27,8,16,128]{3,2,1,0:T(8,128)}, f32[16,128]{1,0:T(8,128)S(1)}, f32[16,128]{1,0:T(8,128)S(1)}) custom-call(f32[27,8,16,128]{3,2,1,0:T(8,128)S(1)} %get-tuple-element.39.adj, f32[3,8,16,128]{3,2,1,0:T(8,128)S(1)} %shard_map.71.rest_0_.refs_6_.vel, s32[1,8,16,128]{3,2,1,0:T(8,128)S(1)} %get-tuple-element.29.solid, ...), custom_call_target="tpu_custom_call" | custom-call | tf_op jit(solution)/shard_map/pallas_call | solution.py:475
  28.3 1.0 %shard_map.75 = f32[27,8,16,128]{3,2,1,0:T(8,128)} custom-call(f32[27,8,16,128]{3,2,1,0:T(8,128)S(1)} %get-tuple-element.39.adj, f32[3,8,16,128]{3,2,1,0:T(8,128)S(1)} %shard_map.71.rest_0_.refs_6_.vel, s32[1,8,16,128]{3,2,1,0:T(8,128)S(1)} %get-tuple-element.29.solid, ...), custom_call_target="tpu_custom_call", output_to_operand_aliasing={{}: (11, {})} | custom-call | tf_op jit(solution)/shard_map/pallas_call | solution.py:475
  (28 shorter events, 0.5 us)
Async XLA Ops:
  0.0 6.7 %copy-start = (s32[1,16,128,2]{2,3,1,0:T(2,128)S(1)}, s32[1,16,128,2]{2,3,1,0:T(2,128)}, u32[]{:S(2)}) copy-start(s32[1,16,128,2]{2,3,1,0:T(2,128)} %param.9) | copy-start | bytes 49156
  0.0 6.7 %copy-start.1 = (s32[1,16,128,2]{2,3,1,0:T(2,128)S(1)}, s32[1,16,128,2]{2,3,1,0:T(2,128)}, u32[]{:S(2)}) copy-start(s32[1,16,128,2]{2,3,1,0:T(2,128)} %param.10) | copy-start | bytes 49156
  0.0 6.7 %copy-start.2 = (f32[1,16,128,2]{2,3,1,0:T(2,128)S(1)}, f32[1,16,128,2]{2,3,1,0:T(2,128)}, u32[]{:S(2)}) copy-start(f32[1,16,128,2]{2,3,1,0:T(2,128)} %param.11) | copy-start | bytes 49156
  1.9 8.1 %collective-permute-start = (f32[10,16,128]{2,1,0:T(8,128)S(1)}, f32[10,16,128]{2,1,0:T(8,128)S(1)}, u32[]{:S(2)}, u32[]{:S(2)}) collective-permute-start(f32[10,16,128]{2,1,0:T(8,128)S(1)} %get-tuple-element.30), channel_id=1, source_target_pairs={{0,16},{1,2},{2,1},{3,19},{4,20},{5,6},{6,5},{7,23},{8,24},{9,10},... | collective-permute-start | bytes 245768 | tf_op jit(solution)/shard_map/ppermute | solution.py:382
  2.7 7.3 %collective-permute-start.1 = (f32[10,16,128]{2,1,0:T(8,128)S(1)}, f32[10,16,128]{2,1,0:T(8,128)S(1)}, u32[]{:S(2)}, u32[]{:S(2)}) collective-permute-start(f32[10,16,128]{2,1,0:T(8,128)S(1)} %get-tuple-element.31), channel_id=1, source_target_pairs={{0,1},{1,0},{2,3},{3,2},{4,5},{5,4},{6,7},{7,6},{8,9},{9,8},{10,11... | collective-permute-start | bytes 245768 | tf_op jit(solution)/shard_map/ppermute | solution.py:382
  4.6 7.9 %collective-permute-start.6 = (f32[9,16,128]{2,1,0:T(8,128)S(1)}, f32[9,16,128]{2,1,0:T(8,128)S(1)}, u32[]{:S(2)}, u32[]{:S(2)}) collective-permute-start(f32[9,16,128]{2,1,0:T(8,128)S(1)} %get-tuple-element.35.refs_0_), channel_id=1, source_target_pairs={{0,16},{1,17},{2,18},{3,19},{4,20},{5,21},{6,22},{7,23},{8,24},{9,... | collective-permute-start | bytes 221192 | tf_op jit(solution)/shard_map/ppermute | solution.py:382
  6.3 6.2 %collective-permute-start.7 = (f32[9,16,128]{2,1,0:T(8,128)S(1)}, f32[9,16,128]{2,1,0:T(8,128)S(1)}, u32[]{:S(2)}, u32[]{:S(2)}) collective-permute-start(f32[9,16,128]{2,1,0:T(8,128)S(1)} %get-tuple-element.35.refs_0_), channel_id=1, source_target_pairs={{0,16},{1,17},{2,18},{3,19},{4,20},{5,21},{6,22},{7,23},{8,24},{9,... | collective-permute-start | bytes 221192 | tf_op jit(solution)/shard_map/ppermute | solution.py:382
  6.7 3.3 %collective-permute-start.2 = (f32[4,16,128]{2,1,0:T(8,128)S(1)}, f32[4,16,128]{2,1,0:T(8,128)S(1)}, u32[]{:S(2)}, u32[]{:S(2)}) collective-permute-start(f32[4,16,128]{2,1,0:T(8,128)S(1)} %shard_map.66), channel_id=1, source_target_pairs={{0,16},{1,17},{2,18},{3,19},{4,20},{5,21},{6,22},{7,23},{8,24},{9,... | collective-permute-start | bytes 98312 | tf_op jit(solution)/shard_map/ppermute | solution.py:382
  10.1 4.6 %collective-permute-start.3 = (f32[10,16,128]{2,1,0:T(8,128)S(1)}, f32[10,16,128]{2,1,0:T(8,128)S(1)}, u32[]{:S(2)}, u32[]{:S(2)}) collective-permute-start(f32[10,16,128]{2,1,0:T(8,128)S(1)} %get-tuple-element.32), channel_id=1, source_target_pairs={{0,4},{1,5},{2,6},{3,7},{4,0},{5,1},{6,2},{7,3},{8,24},{9,25},{10,... | collective-permute-start | bytes 245768 | tf_op jit(solution)/shard_map/ppermute | solution.py:382
  10.2 4.5 %collective-permute-start.4 = (f32[10,16,128]{2,1,0:T(8,128)S(1)}, f32[10,16,128]{2,1,0:T(8,128)S(1)}, u32[]{:S(2)}, u32[]{:S(2)}) collective-permute-start(f32[10,16,128]{2,1,0:T(8,128)S(1)} %get-tuple-element.33), channel_id=1, source_target_pairs={{0,16},{1,17},{2,18},{3,19},{4,8},{5,9},{6,10},{7,11},{8,4},{9,5},... | collective-permute-start | bytes 245768 | tf_op jit(solution)/shard_map/ppermute | solution.py:382
  10.6 4.0 %collective-permute-start.5 = (f32[10,16,128]{2,1,0:T(8,128)S(1)}, f32[10,16,128]{2,1,0:T(8,128)S(1)}, u32[]{:S(2)}, u32[]{:S(2)}) collective-permute-start(f32[10,16,128]{2,1,0:T(8,128)S(1)} %get-tuple-element.34), channel_id=1, source_target_pairs={{0,16},{1,17},{2,18},{3,19},{4,20},{5,21},{6,22},{7,23},{8,12},{9,... | collective-permute-start | bytes 245768 | tf_op jit(solution)/shard_map/ppermute | solution.py:382
  12.9 1.8 %collective-permute-start.8 = (f32[9,16,128]{2,1,0:T(8,128)S(1)}, f32[9,16,128]{2,1,0:T(8,128)S(1)}, u32[]{:S(2)}, u32[]{:S(2)}) collective-permute-start(f32[9,16,128]{2,1,0:T(8,128)S(1)} %shard_map.69), channel_id=1, source_target_pairs={{0,16},{1,17},{2,18},{3,19},{4,20},{5,21},{6,22},{7,23},{8,24},{9,... | collective-permute-start | bytes 221192 | tf_op jit(solution)/shard_map/ppermute | solution.py:382
  15.3 6.1 %collective-permute-start.10 = (f32[10,16,128]{2,1,0:T(8,128)S(1)}, f32[10,16,128]{2,1,0:T(8,128)S(1)}, u32[]{:S(2)}, u32[]{:S(2)}) collective-permute-start(f32[10,16,128]{2,1,0:T(8,128)S(1)} %get-tuple-element.41), channel_id=1, source_target_pairs={{0,16},{1,2},{2,1},{3,19},{4,20},{5,6},{6,5},{7,23},{8,24},{9,10},... | collective-permute-start | bytes 245768 | tf_op jit(solution)/shard_map/ppermute | solution.py:382
  16.2 5.2 %collective-permute-start.9 = (f32[10,16,128]{2,1,0:T(8,128)S(1)}, f32[10,16,128]{2,1,0:T(8,128)S(1)}, u32[]{:S(2)}, u32[]{:S(2)}) collective-permute-start(f32[10,16,128]{2,1,0:T(8,128)S(1)} %get-tuple-element.40), channel_id=1, source_target_pairs={{0,1},{1,0},{2,3},{3,2},{4,5},{5,4},{6,7},{7,6},{8,9},{9,8},{10,11... | collective-permute-start | bytes 245768 | tf_op jit(solution)/shard_map/ppermute | solution.py:382
  16.7 6.0 %collective-permute-start.14 = (f32[9,16,128]{2,1,0:T(8,128)S(1)}, f32[9,16,128]{2,1,0:T(8,128)S(1)}, u32[]{:S(2)}, u32[]{:S(2)}) collective-permute-start(f32[9,16,128]{2,1,0:T(8,128)S(1)} %get-tuple-element.45.refs_0_), channel_id=1, source_target_pairs={{0,16},{1,17},{2,18},{3,19},{4,20},{5,21},{6,22},{7,23},{8,24},{9,... | collective-permute-start | bytes 221192 | tf_op jit(solution)/shard_map/ppermute | solution.py:382
  18.8 5.3 %collective-permute-start.15 = (f32[9,16,128]{2,1,0:T(8,128)S(1)}, f32[9,16,128]{2,1,0:T(8,128)S(1)}, u32[]{:S(2)}, u32[]{:S(2)}) collective-permute-start(f32[9,16,128]{2,1,0:T(8,128)S(1)} %get-tuple-element.45.refs_0_), channel_id=1, source_target_pairs={{0,16},{1,17},{2,18},{3,19},{4,20},{5,21},{6,22},{7,23},{8,24},{9,... | collective-permute-start | bytes 221192 | tf_op jit(solution)/shard_map/ppermute | solution.py:382
  21.6 6.7 %collective-permute-start.11 = (f32[10,16,128]{2,1,0:T(8,128)S(1)}, f32[10,16,128]{2,1,0:T(8,128)S(1)}, u32[]{:S(2)}, u32[]{:S(2)}) collective-permute-start(f32[10,16,128]{2,1,0:T(8,128)S(1)} %get-tuple-element.42), channel_id=1, source_target_pairs={{0,4},{1,5},{2,6},{3,7},{4,0},{5,1},{6,2},{7,3},{8,24},{9,25},{10,... | collective-permute-start | bytes 245768 | tf_op jit(solution)/shard_map/ppermute | solution.py:382
  22.5 5.8 %collective-permute-start.12 = (f32[10,16,128]{2,1,0:T(8,128)S(1)}, f32[10,16,128]{2,1,0:T(8,128)S(1)}, u32[]{:S(2)}, u32[]{:S(2)}) collective-permute-start(f32[10,16,128]{2,1,0:T(8,128)S(1)} %get-tuple-element.43), channel_id=1, source_target_pairs={{0,16},{1,17},{2,18},{3,19},{4,8},{5,9},{6,10},{7,11},{8,4},{9,5},... | collective-permute-start | bytes 245768 | tf_op jit(solution)/shard_map/ppermute | solution.py:382
  22.6 5.7 %collective-permute-start.13 = (f32[10,16,128]{2,1,0:T(8,128)S(1)}, f32[10,16,128]{2,1,0:T(8,128)S(1)}, u32[]{:S(2)}, u32[]{:S(2)}) collective-permute-start(f32[10,16,128]{2,1,0:T(8,128)S(1)} %get-tuple-element.44), channel_id=1, source_target_pairs={{0,16},{1,17},{2,18},{3,19},{4,20},{5,21},{6,22},{7,23},{8,12},{9,... | collective-permute-start | bytes 245768 | tf_op jit(solution)/shard_map/ppermute | solution.py:382
  24.5 3.8 %collective-permute-start.16 = (f32[9,16,128]{2,1,0:T(8,128)S(1)}, f32[9,16,128]{2,1,0:T(8,128)S(1)}, u32[]{:S(2)}, u32[]{:S(2)}) collective-permute-start(f32[9,16,128]{2,1,0:T(8,128)S(1)} %shard_map.73), channel_id=1, source_target_pairs={{0,16},{1,17},{2,18},{3,19},{4,20},{5,21},{6,22},{7,23},{8,24},{9,... | collective-permute-start | bytes 221192 | tf_op jit(solution)/shard_map/ppermute | solution.py:382

commit v22 on v17

--- a/solution.py
+++ b/solution.py
@@ -282,7 +282,7 @@
         return pltpu.make_async_copy(made.at[x - 1], out.at[:, x], sems.at[x - 1])
 
     def plane(x, carry):
-        here = pulled.at[lax.rem(x, 2)]
+        here = pulled.at[lax.rem(x, 3)]
         pull_plane(
             lambda i, cx: adj[i, x + cx],
             lambda cx: (low_edge, high_edge, (x + 1 + cx) * 9),
@@ -300,7 +300,7 @@
         return pack_columns(lambda i: made[x - 1, i], x, *carry)
 
     zero = jnp.zeros((16, 128), jnp.float32)
-    low_out[...], high_out[...] = lax.fori_loop(1, extent_x - 1, plane, (zero, zero), unroll=2)
+    low_out[...], high_out[...] = lax.fori_loop(1, extent_x - 1, plane, (zero, zero), unroll=3)
     lax.fori_loop(1, extent_x - 1, lambda x, c: (save(x).wait(), c)[1], 0)
 
 
@@ -479,7 +479,7 @@
                 out_specs=tuple(in_any(1) + in_vmem(len(extra))),
                 scratch_shapes=[
                     pltpu.VMEM((planes, 27, 16, 128), jnp.float32),
-                    pltpu.VMEM((2, 27, 16, 128), jnp.float32),
+                    pltpu.VMEM((3, 27, 16, 128), jnp.float32),
                     pltpu.SemaphoreType.DMA((planes,)),
                 ],
                 input_output_aliases={len(operands): 0} if new else {},

time: 28.7 us -> 28.7 us (level)
  starting transfers between devices: 15 us -> 15.3 us
where the time goes in v22:
time: 28.7 us; the launch traced here: 28.5 us
  starting transfers between devices  15.3 us (53%)
  Pallas kernels  11.2 us (39%)
  waiting for transfers between devices  1.86 us (6%)
    ppermute x17, starting transfers between devices, send(): lax.ppermute(values, axes, [(flat(*here), flat(*target(*here))) for here...  15.3 us
    pallas_call x4, Pallas kernels, make_planes(): pl.pallas_call(run, out_shape=(tile_shape(27, extent_x), *extra), in_spec...  5.05 us
    pallas_call x2, Pallas kernels, body(): pl.pallas_call(lambda *refs: velocity_kernel(step, *refs), out_shape=(*(j...  3.32 us
    pallas_call x1, Pallas kernels, body(): pl.pallas_call(pack_kernel, out_shape=(tile_shape(27, extent_x), *message...  1.9 us
    ppermute x17, waiting for transfers between devices, send(): lax.ppermute(values, axes, [(flat(*here), flat(*target(*here))) for here...  1.86 us
    pallas_call x2, Pallas kernels, body(): pl.pallas_call(lambda *refs: cross_kernel(count, *refs), out_shape=tile_s...  0.71 us
  transfers between devices with their start and end apart: 17, of which 2 were waited for; matrix products, arithmetic and copies ran while one was open for 0% of the time, Pallas kernels for 27%

profile of v22, /device:TPU:7, one launch (start us, length us, event | category | flops | bytes accessed | tf_op | source)
XLA Modules:
  0.0 28.5 jit_solution(12339880637862194503)
XLA Ops:
  0.0 1.9 %shard_map.64 = (f32[27,8,16,128]{3,2,1,0:T(8,128)S(1)}, f32[9,16,128]{2,1,0:T(8,128)S(1)}, f32[10,16,128]{2,1,0:T(8,128)S(1)}, f32[10,16,128]{2,1,0:T(8,128)S(1)}) custom-call(f32[27,8,16,128]{3,2,1,0:T(8,128)} %bitcast.14), custom_call_target="tpu_custom_call" | custom-call | tf_op jit(solution)/shard_map/pallas_call | solution.py:425
  1.9 0.7 %collective-permute-start = (f32[10,16,128]{2,1,0:T(8,128)S(1)}, f32[10,16,128]{2,1,0:T(8,128)S(1)}, u32[]{:S(2)}, u32[]{:S(2)}) collective-permute-start(f32[10,16,128]{2,1,0:T(8,128)S(1)} %get-tuple-element.30), channel_id=1, source_target_pairs={{0,16},{1,2},{2,1},{3,19},{4,20},{5,6},{6,5},{7,23},{8,24},{9,10},... | collective-permute-start | bytes 245768 | tf_op jit(solution)/shard_map/ppermute | solution.py:382
  2.7 1.9 %collective-permute-start.1 = (f32[10,16,128]{2,1,0:T(8,128)S(1)}, f32[10,16,128]{2,1,0:T(8,128)S(1)}, u32[]{:S(2)}, u32[]{:S(2)}) collective-permute-start(f32[10,16,128]{2,1,0:T(8,128)S(1)} %get-tuple-element.31), channel_id=1, source_target_pairs={{0,1},{1,0},{2,3},{3,2},{4,5},{5,4},{6,7},{7,6},{8,9},{9,8},{10,11... | collective-permute-start | bytes 245768 | tf_op jit(solution)/shard_map/ppermute | solution.py:382
  4.6 1.7 %collective-permute-start.6 = (f32[9,16,128]{2,1,0:T(8,128)S(1)}, f32[9,16,128]{2,1,0:T(8,128)S(1)}, u32[]{:S(2)}, u32[]{:S(2)}) collective-permute-start(f32[9,16,128]{2,1,0:T(8,128)S(1)} %get-tuple-element.35.refs_0_), channel_id=1, source_target_pairs={{0,16},{1,17},{2,18},{3,19},{4,20},{5,21},{6,22},{7,23},{8,24},{9,... | collective-permute-start | bytes 221192 | tf_op jit(solution)/shard_map/ppermute | solution.py:382
  6.3 0.4 %collective-permute-start.7 = (f32[9,16,128]{2,1,0:T(8,128)S(1)}, f32[9,16,128]{2,1,0:T(8,128)S(1)}, u32[]{:S(2)}, u32[]{:S(2)}) collective-permute-start(f32[9,16,128]{2,1,0:T(8,128)S(1)} %get-tuple-element.35.refs_0_), channel_id=1, source_target_pairs={{0,16},{1,17},{2,18},{3,19},{4,20},{5,21},{6,22},{7,23},{8,24},{9,... | collective-permute-start | bytes 221192 | tf_op jit(solution)/shard_map/ppermute | solution.py:382
  6.7 1.6 %collective-permute-start.2 = (f32[4,16,128]{2,1,0:T(8,128)S(1)}, f32[4,16,128]{2,1,0:T(8,128)S(1)}, u32[]{:S(2)}, u32[]{:S(2)}) collective-permute-start(f32[4,16,128]{2,1,0:T(8,128)S(1)} %shard_map.66), channel_id=1, source_target_pairs={{0,16},{1,17},{2,18},{3,19},{4,20},{5,21},{6,22},{7,23},{8,24},{9,... | collective-permute-start | bytes 98312 | tf_op jit(solution)/shard_map/ppermute | solution.py:382
  8.3 1.7 %shard_map.65 = (s32[1,8,16,128]{3,2,1,0:T(8,128)S(1)}, f32[3,8,16,128]{3,2,1,0:T(8,128)S(1)}) custom-call(f32[2,1,27,8,16,128]{5,4,3,2,1,0:T(8,128)} %refs_0_.3, s32[1,8,16,128]{3,2,1,0:T(8,128)} %refs_1_.1), custom_call_target="tpu_custom_call" | custom-call | tf_op jit(solution)/shard_map/pallas_call | solution.py:442
  10.2 0.5 %collective-permute-start.4 = (f32[10,16,128]{2,1,0:T(8,128)S(1)}, f32[10,16,128]{2,1,0:T(8,128)S(1)}, u32[]{:S(2)}, u32[]{:S(2)}) collective-permute-start(f32[10,16,128]{2,1,0:T(8,128)S(1)} %get-tuple-element.33), channel_id=1, source_target_pairs={{0,16},{1,17},{2,18},{3,19},{4,8},{5,9},{6,10},{7,11},{8,4},{9,5},... | collective-permute-start | bytes 245768 | tf_op jit(solution)/shard_map/ppermute | solution.py:382
  10.6 1.8 %shard_map.68 = (f32[27,8,16,128]{3,2,1,0:T(8,128)S(1)}, f32[16,128]{1,0:T(8,128)S(1)}, f32[16,128]{1,0:T(8,128)S(1)}) custom-call(f32[27,8,16,128]{3,2,1,0:T(8,128)S(1)} %get-tuple-element.27.adj, f32[3,8,16,128]{3,2,1,0:T(8,128)S(1)} %get-tuple-element.28.rest_0_.vel, s32[1,8,16,128]{3,2,1,0:T(8,128)S(1)} %get-tuple-element.29.solid, ...), custom_call_target="tpu_custom_call" | custom-call | tf_op jit(solution)/shard_map/pallas_call | solution.py:475
  12.4 0.4 %shard_map.69 = f32[9,16,128]{2,1,0:T(8,128)S(1)} custom-call(f32[9,16,128]{2,1,0:T(8,128)S(1)} %get-tuple-element.35.refs_0_, f32[10,16,128]{2,1,0:T(8,128)S(1)} %collective-permute-done.first.refs_0_.refs_1_, f32[10,16,128]{2,1,0:T(8,128)S(1)} %collective-permute-done.1.second.refs_1_.refs_2_, f32[9,16,128]{2,1,0:T(8,128)S(1)} %collective-permute-done.6.refs_3_, ...), custom_call_target="tpu_custom_call" | custom-call | tf_op jit(solution)/shard_map/pallas_call | solution.py:491
  12.8 0.9 %collective-permute-start.8 = (f32[9,16,128]{2,1,0:T(8,128)S(1)}, f32[9,16,128]{2,1,0:T(8,128)S(1)}, u32[]{:S(2)}, u32[]{:S(2)}) collective-permute-start(f32[9,16,128]{2,1,0:T(8,128)S(1)} %shard_map.69), channel_id=1, source_target_pairs={{0,16},{1,17},{2,18},{3,19},{4,20},{5,21},{6,22},{7,23},{8,24},{9,... | collective-permute-start | bytes 221192 | tf_op jit(solution)/shard_map/ppermute | solution.py:382
  13.7 0.9 %collective-permute-done.8.refs_5_ = f32[9,16,128]{2,1,0:T(8,128)S(1)} collective-permute-done((f32[9,16,128]{2,1,0:T(8,128)S(1)}, f32[9,16,128]{2,1,0:T(8,128)S(1)}, u32[]{:S(2)}, u32[]{:S(2)}) %collective-permute-start.8) | collective-permute-done | bytes 73760 | tf_op jit(solution)/shard_map/ppermute | solution.py:382
  14.7 0.7 %shard_map.70 = (f32[27,8,16,128]{3,2,1,0:T(8,128)S(1)}, f32[9,16,128]{2,1,0:T(8,128)S(1)}, f32[10,16,128]{2,1,0:T(8,128)S(1)}, f32[10,16,128]{2,1,0:T(8,128)S(1)}) custom-call(f32[27,8,16,128]{3,2,1,0:T(8,128)S(1)} %get-tuple-element.27.adj, f32[3,8,16,128]{3,2,1,0:T(8,128)S(1)} %get-tuple-element.28.rest_0_.vel, ...), custom_call_target="tpu_custom_call", output_to_operand_aliasing={{0}: (11, {})} | custom-call | tf_op jit(solution)/shard_map/pallas_call | solution.py:475
  15.3 0.9 %collective-permute-start.10 = (f32[10,16,128]{2,1,0:T(8,128)S(1)}, f32[10,16,128]{2,1,0:T(8,128)S(1)}, u32[]{:S(2)}, u32[]{:S(2)}) collective-permute-start(f32[10,16,128]{2,1,0:T(8,128)S(1)} %get-tuple-element.41), channel_id=1, source_target_pairs={{0,16},{1,2},{2,1},{3,19},{4,20},{5,6},{6,5},{7,23},{8,24},{9,10},... | collective-permute-start | bytes 245768 | tf_op jit(solution)/shard_map/ppermute | solution.py:382
  16.2 0.4 %collective-permute-start.9 = (f32[10,16,128]{2,1,0:T(8,128)S(1)}, f32[10,16,128]{2,1,0:T(8,128)S(1)}, u32[]{:S(2)}, u32[]{:S(2)}) collective-permute-start(f32[10,16,128]{2,1,0:T(8,128)S(1)} %get-tuple-element.40), channel_id=1, source_target_pairs={{0,1},{1,0},{2,3},{3,2},{4,5},{5,4},{6,7},{7,6},{8,9},{9,8},{10,11... | collective-permute-start | bytes 245768 | tf_op jit(solution)/shard_map/ppermute | solution.py:382
  16.6 2.2 %collective-permute-start.14 = (f32[9,16,128]{2,1,0:T(8,128)S(1)}, f32[9,16,128]{2,1,0:T(8,128)S(1)}, u32[]{:S(2)}, u32[]{:S(2)}) collective-permute-start(f32[9,16,128]{2,1,0:T(8,128)S(1)} %get-tuple-element.45.refs_0_), channel_id=1, source_target_pairs={{0,16},{1,17},{2,18},{3,19},{4,20},{5,21},{6,22},{7,23},{8,24},{9,... | collective-permute-start | bytes 221192 | tf_op jit(solution)/shard_map/ppermute | solution.py:382
  18.8 1.0 %collective-permute-start.15 = (f32[9,16,128]{2,1,0:T(8,128)S(1)}, f32[9,16,128]{2,1,0:T(8,128)S(1)}, u32[]{:S(2)}, u32[]{:S(2)}) collective-permute-start(f32[9,16,128]{2,1,0:T(8,128)S(1)} %get-tuple-element.45.refs_0_), channel_id=1, source_target_pairs={{0,16},{1,17},{2,18},{3,19},{4,20},{5,21},{6,22},{7,23},{8,24},{9,... | collective-permute-start | bytes 221192 | tf_op jit(solution)/shard_map/ppermute | solution.py:382
  19.8 1.6 %shard_map.71.rest_0_.vel = f32[3,8,16,128]{3,2,1,0:T(8,128)S(1)} custom-call(f32[2,1,27,8,16,128]{5,4,3,2,1,0:T(8,128)} %refs_0_.3), custom_call_target="tpu_custom_call" | custom-call | tf_op jit(solution)/shard_map/pallas_call | solution.py:442
  21.6 0.9 %collective-permute-start.11 = (f32[10,16,128]{2,1,0:T(8,128)S(1)}, f32[10,16,128]{2,1,0:T(8,128)S(1)}, u32[]{:S(2)}, u32[]{:S(2)}) collective-permute-start(f32[10,16,128]{2,1,0:T(8,128)S(1)} %get-tuple-element.42), channel_id=1, source_target_pairs={{0,4},{1,5},{2,6},{3,7},{4,0},{5,1},{6,2},{7,3},{8,24},{9,25},{10,... | collective-permute-start | bytes 245768 | tf_op jit(solution)/shard_map/ppermute | solution.py:382
  22.6 1.6 %shard_map.73 = (f32[27,8,16,128]{3,2,1,0:T(8,128)}, f32[16,128]{1,0:T(8,128)S(1)}, f32[16,128]{1,0:T(8,128)S(1)}) custom-call(f32[27,8,16,128]{3,2,1,0:T(8,128)S(1)} %get-tuple-element.39.adj, f32[3,8,16,128]{3,2,1,0:T(8,128)S(1)} %shard_map.71.rest_0_.vel, s32[1,8,16,128]{3,2,1,0:T(8,128)S(1)} %get-tuple-element.29.solid, ...), custom_call_target="tpu_custom_call" | custom-call | tf_op jit(solution)/shard_map/pallas_call | solution.py:475
  24.2 0.4 %shard_map.74 = f32[9,16,128]{2,1,0:T(8,128)S(1)} custom-call(f32[9,16,128]{2,1,0:T(8,128)S(1)} %get-tuple-element.45.refs_0_, f32[10,16,128]{2,1,0:T(8,128)S(1)} %collective-permute-done.10.first.refs_1_, f32[10,16,128]{2,1,0:T(8,128)S(1)} %collective-permute-done.9.second.refs_0_.refs_2_, f32[9,16,128]{2,1,0:T(8,128)S(1)} %collective-permute-done.14.refs_3_, ...), custom_call_target="tpu_custom_call" | custom-call | tf_op jit(solution)/shard_map/pallas_call | solution.py:491
  24.5 2.0 %collective-permute-start.16 = (f32[9,16,128]{2,1,0:T(8,128)S(1)}, f32[9,16,128]{2,1,0:T(8,128)S(1)}, u32[]{:S(2)}, u32[]{:S(2)}) collective-permute-start(f32[9,16,128]{2,1,0:T(8,128)S(1)} %shard_map.74), channel_id=1, source_target_pairs={{0,16},{1,17},{2,18},{3,19},{4,20},{5,21},{6,22},{7,23},{8,24},{9,... | collective-permute-start | bytes 221192 | tf_op jit(solution)/shard_map/ppermute | solution.py:382
  26.5 0.9 %collective-permute-done.16.refs_5_ = f32[9,16,128]{2,1,0:T(8,128)S(1)} collective-permute-done((f32[9,16,128]{2,1,0:T(8,128)S(1)}, f32[9,16,128]{2,1,0:T(8,128)S(1)}, u32[]{:S(2)}, u32[]{:S(2)}) %collective-permute-start.16) | collective-permute-done | bytes 73760 | tf_op jit(solution)/shard_map/ppermute | solution.py:382
  27.5 1.0 %shard_map.75 = f32[27,8,16,128]{3,2,1,0:T(8,128)} custom-call(f32[27,8,16,128]{3,2,1,0:T(8,128)S(1)} %get-tuple-element.39.adj, f32[3,8,16,128]{3,2,1,0:T(8,128)S(1)} %shard_map.71.rest_0_.vel, s32[1,8,16,128]{3,2,1,0:T(8,128)S(1)} %get-tuple-element.29.solid, ...), custom_call_target="tpu_custom_call", output_to_operand_aliasing={{}: (11, {})} | custom-call | tf_op jit(solution)/shard_map/pallas_call | solution.py:475
  (28 shorter events, 0.4 us)
Async XLA Ops:
  0.0 6.7 %copy-start = (s32[1,16,128,2]{2,3,1,0:T(2,128)S(1)}, s32[1,16,128,2]{2,3,1,0:T(2,128)}, u32[]{:S(2)}) copy-start(s32[1,16,128,2]{2,3,1,0:T(2,128)} %param.9) | copy-start | bytes 49156
  0.0 6.7 %copy-start.1 = (s32[1,16,128,2]{2,3,1,0:T(2,128)S(1)}, s32[1,16,128,2]{2,3,1,0:T(2,128)}, u32[]{:S(2)}) copy-start(s32[1,16,128,2]{2,3,1,0:T(2,128)} %param.10) | copy-start | bytes 49156
  0.0 6.7 %copy-start.2 = (f32[1,16,128,2]{2,3,1,0:T(2,128)S(1)}, f32[1,16,128,2]{2,3,1,0:T(2,128)}, u32[]{:S(2)}) copy-start(f32[1,16,128,2]{2,3,1,0:T(2,128)} %param.11) | copy-start | bytes 49156
  1.9 8.1 %collective-permute-start = (f32[10,16,128]{2,1,0:T(8,128)S(1)}, f32[10,16,128]{2,1,0:T(8,128)S(1)}, u32[]{:S(2)}, u32[]{:S(2)}) collective-permute-start(f32[10,16,128]{2,1,0:T(8,128)S(1)} %get-tuple-element.30), channel_id=1, source_target_pairs={{0,16},{1,2},{2,1},{3,19},{4,20},{5,6},{6,5},{7,23},{8,24},{9,10},... | collective-permute-start | bytes 245768 | tf_op jit(solution)/shard_map/ppermute | solution.py:382
  2.7 7.3 %collective-permute-start.1 = (f32[10,16,128]{2,1,0:T(8,128)S(1)}, f32[10,16,128]{2,1,0:T(8,128)S(1)}, u32[]{:S(2)}, u32[]{:S(2)}) collective-permute-start(f32[10,16,128]{2,1,0:T(8,128)S(1)} %get-tuple-element.31), channel_id=1, source_target_pairs={{0,1},{1,0},{2,3},{3,2},{4,5},{5,4},{6,7},{7,6},{8,9},{9,8},{10,11... | collective-permute-start | bytes 245768 | tf_op jit(solution)/shard_map/ppermute | solution.py:382
  4.6 7.8 %collective-permute-start.6 = (f32[9,16,128]{2,1,0:T(8,128)S(1)}, f32[9,16,128]{2,1,0:T(8,128)S(1)}, u32[]{:S(2)}, u32[]{:S(2)}) collective-permute-start(f32[9,16,128]{2,1,0:T(8,128)S(1)} %get-tuple-element.35.refs_0_), channel_id=1, source_target_pairs={{0,16},{1,17},{2,18},{3,19},{4,20},{5,21},{6,22},{7,23},{8,24},{9,... | collective-permute-start | bytes 221192 | tf_op jit(solution)/shard_map/ppermute | solution.py:382
  6.3 6.1 %collective-permute-start.7 = (f32[9,16,128]{2,1,0:T(8,128)S(1)}, f32[9,16,128]{2,1,0:T(8,128)S(1)}, u32[]{:S(2)}, u32[]{:S(2)}) collective-permute-start(f32[9,16,128]{2,1,0:T(8,128)S(1)} %get-tuple-element.35.refs_0_), channel_id=1, source_target_pairs={{0,16},{1,17},{2,18},{3,19},{4,20},{5,21},{6,22},{7,23},{8,24},{9,... | collective-permute-start | bytes 221192 | tf_op jit(solution)/shard_map/ppermute | solution.py:382
  6.7 3.3 %collective-permute-start.2 = (f32[4,16,128]{2,1,0:T(8,128)S(1)}, f32[4,16,128]{2,1,0:T(8,128)S(1)}, u32[]{:S(2)}, u32[]{:S(2)}) collective-permute-start(f32[4,16,128]{2,1,0:T(8,128)S(1)} %shard_map.66), channel_id=1, source_target_pairs={{0,16},{1,17},{2,18},{3,19},{4,20},{5,21},{6,22},{7,23},{8,24},{9,... | collective-permute-start | bytes 98312 | tf_op jit(solution)/shard_map/ppermute | solution.py:382
  10.1 4.6 %collective-permute-start.3 = (f32[10,16,128]{2,1,0:T(8,128)S(1)}, f32[10,16,128]{2,1,0:T(8,128)S(1)}, u32[]{:S(2)}, u32[]{:S(2)}) collective-permute-start(f32[10,16,128]{2,1,0:T(8,128)S(1)} %get-tuple-element.32), channel_id=1, source_target_pairs={{0,4},{1,5},{2,6},{3,7},{4,0},{5,1},{6,2},{7,3},{8,24},{9,25},{10,... | collective-permute-start | bytes 245768 | tf_op jit(solution)/shard_map/ppermute | solution.py:382
  10.2 4.5 %collective-permute-start.4 = (f32[10,16,128]{2,1,0:T(8,128)S(1)}, f32[10,16,128]{2,1,0:T(8,128)S(1)}, u32[]{:S(2)}, u32[]{:S(2)}) collective-permute-start(f32[10,16,128]{2,1,0:T(8,128)S(1)} %get-tuple-element.33), channel_id=1, source_target_pairs={{0,16},{1,17},{2,18},{3,19},{4,8},{5,9},{6,10},{7,11},{8,4},{9,5},... | collective-permute-start | bytes 245768 | tf_op jit(solution)/shard_map/ppermute | solution.py:382
  10.6 4.0 %collective-permute-start.5 = (f32[10,16,128]{2,1,0:T(8,128)S(1)}, f32[10,16,128]{2,1,0:T(8,128)S(1)}, u32[]{:S(2)}, u32[]{:S(2)}) collective-permute-start(f32[10,16,128]{2,1,0:T(8,128)S(1)} %get-tuple-element.34), channel_id=1, source_target_pairs={{0,16},{1,17},{2,18},{3,19},{4,20},{5,21},{6,22},{7,23},{8,12},{9,... | collective-permute-start | bytes 245768 | tf_op jit(solution)/shard_map/ppermute | solution.py:382
  12.8 1.9 %collective-permute-start.8 = (f32[9,16,128]{2,1,0:T(8,128)S(1)}, f32[9,16,128]{2,1,0:T(8,128)S(1)}, u32[]{:S(2)}, u32[]{:S(2)}) collective-permute-start(f32[9,16,128]{2,1,0:T(8,128)S(1)} %shard_map.69), channel_id=1, source_target_pairs={{0,16},{1,17},{2,18},{3,19},{4,20},{5,21},{6,22},{7,23},{8,24},{9,... | collective-permute-start | bytes 221192 | tf_op jit(solution)/shard_map/ppermute | solution.py:382
  15.3 6.1 %collective-permute-start.10 = (f32[10,16,128]{2,1,0:T(8,128)S(1)}, f32[10,16,128]{2,1,0:T(8,128)S(1)}, u32[]{:S(2)}, u32[]{:S(2)}) collective-permute-start(f32[10,16,128]{2,1,0:T(8,128)S(1)} %get-tuple-element.41), channel_id=1, source_target_pairs={{0,16},{1,2},{2,1},{3,19},{4,20},{5,6},{6,5},{7,23},{8,24},{9,10},... | collective-permute-start | bytes 245768 | tf_op jit(solution)/shard_map/ppermute | solution.py:382
  16.2 5.2 %collective-permute-start.9 = (f32[10,16,128]{2,1,0:T(8,128)S(1)}, f32[10,16,128]{2,1,0:T(8,128)S(1)}, u32[]{:S(2)}, u32[]{:S(2)}) collective-permute-start(f32[10,16,128]{2,1,0:T(8,128)S(1)} %get-tuple-element.40), channel_id=1, source_target_pairs={{0,1},{1,0},{2,3},{3,2},{4,5},{5,4},{6,7},{7,6},{8,9},{9,8},{10,11... | collective-permute-start | bytes 245768 | tf_op jit(solution)/shard_map/ppermute | solution.py:382
  16.6 7.5 %collective-permute-start.14 = (f32[9,16,128]{2,1,0:T(8,128)S(1)}, f32[9,16,128]{2,1,0:T(8,128)S(1)}, u32[]{:S(2)}, u32[]{:S(2)}) collective-permute-start(f32[9,16,128]{2,1,0:T(8,128)S(1)} %get-tuple-element.45.refs_0_), channel_id=1, source_target_pairs={{0,16},{1,17},{2,18},{3,19},{4,20},{5,21},{6,22},{7,23},{8,24},{9,... | collective-permute-start | bytes 221192 | tf_op jit(solution)/shard_map/ppermute | solution.py:382
  18.8 5.4 %collective-permute-start.15 = (f32[9,16,128]{2,1,0:T(8,128)S(1)}, f32[9,16,128]{2,1,0:T(8,128)S(1)}, u32[]{:S(2)}, u32[]{:S(2)}) collective-permute-start(f32[9,16,128]{2,1,0:T(8,128)S(1)} %get-tuple-element.45.refs_0_), channel_id=1, source_target_pairs={{0,16},{1,17},{2,18},{3,19},{4,20},{5,21},{6,22},{7,23},{8,24},{9,... | collective-permute-start | bytes 221192 | tf_op jit(solution)/shard_map/ppermute | solution.py:382
  21.6 5.9 %collective-permute-start.11 = (f32[10,16,128]{2,1,0:T(8,128)S(1)}, f32[10,16,128]{2,1,0:T(8,128)S(1)}, u32[]{:S(2)}, u32[]{:S(2)}) collective-permute-start(f32[10,16,128]{2,1,0:T(8,128)S(1)} %get-tuple-element.42), channel_id=1, source_target_pairs={{0,4},{1,5},{2,6},{3,7},{4,0},{5,1},{6,2},{7,3},{8,24},{9,25},{10,... | collective-permute-start | bytes 245768 | tf_op jit(solution)/shard_map/ppermute | solution.py:382
  22.5 5.0 %collective-permute-start.12 = (f32[10,16,128]{2,1,0:T(8,128)S(1)}, f32[10,16,128]{2,1,0:T(8,128)S(1)}, u32[]{:S(2)}, u32[]{:S(2)}) collective-permute-start(f32[10,16,128]{2,1,0:T(8,128)S(1)} %get-tuple-element.43), channel_id=1, source_target_pairs={{0,16},{1,17},{2,18},{3,19},{4,8},{5,9},{6,10},{7,11},{8,4},{9,5},... | collective-permute-start | bytes 245768 | tf_op jit(solution)/shard_map/ppermute | solution.py:382
  22.6 4.9 %collective-permute-start.13 = (f32[10,16,128]{2,1,0:T(8,128)S(1)}, f32[10,16,128]{2,1,0:T(8,128)S(1)}, u32[]{:S(2)}, u32[]{:S(2)}) collective-permute-start(f32[10,16,128]{2,1,0:T(8,128)S(1)} %get-tuple-element.44), channel_id=1, source_target_pairs={{0,16},{1,17},{2,18},{3,19},{4,20},{5,21},{6,22},{7,23},{8,12},{9,... | collective-permute-start | bytes 245768 | tf_op jit(solution)/shard_map/ppermute | solution.py:382
  24.5 2.9 %collective-permute-start.16 = (f32[9,16,128]{2,1,0:T(8,128)S(1)}, f32[9,16,128]{2,1,0:T(8,128)S(1)}, u32[]{:S(2)}, u32[]{:S(2)}) collective-permute-start(f32[9,16,128]{2,1,0:T(8,128)S(1)} %shard_map.74), channel_id=1, source_target_pairs={{0,16},{1,17},{2,18},{3,19},{4,20},{5,21},{6,22},{7,23},{8,24},{9,... | collective-permute-start | bytes 221192 | tf_op jit(solution)/shard_map/ppermute | solution.py:382
